TPU v7x, 32 devices: a whole 2x2x4 slice. The times are simulated.
32 devices in a mesh: grp: 2 (over y), lon: 4 (over z), lat: 2 (over x), ch: 2 (over core).
Axes of the slice: x: 2, y: 2, z: 4, core: 2. Of those that a mesh axis runs over, the one named last changes fastest.
Arguments:
- patches: bfloat16 [512, 384, 768], P(('grp', 'lat'), 'lon', 'ch'), parts along dimension 0, may hold values from -6 to 6
- filter_norm_gain: bfloat16 [768], P('ch'), may hold values from 0.099609375 to 1.8984375
- filter_norm_bias: bfloat16 [768], P('ch'), may hold values from -6 to 6
- filter_in: bfloat16 [2, 8, 96, 96], P(None, 'ch'), may hold values from -0.625 to 0.625
- filter_in_bias: bfloat16 [2, 768], P(None, 'ch'), may hold values from -1.5 to 1.5
- filter_out: bfloat16 [2, 8, 96, 96], P(None, 'ch'), may hold values from -0.625 to 0.625
- filter_out_bias: bfloat16 [2, 768], P(None, 'ch'), may hold values from -0.875 to 0.875
- kept_lat: int32 [8], P('ch'), may hold values from 32 to 64, as said below
- kept_lon: int32 [8], P('ch'), may hold values from 64 to 128, as said below
- norm_gain: bfloat16 [768], replicated, may hold values from 0.099609375 to 1.8984375
- norm_bias: bfloat16 [768], replicated, may hold values from -6 to 6
- dense_in: bfloat16 [768, 1536], P(None, 'ch'), may hold values from -0.21875 to 0.21875
- dense_in_bias: bfloat16 [1536], P('ch'), may hold values from -6 to 6
- dense_out: bfloat16 [1536, 768], P('ch'), may hold values from -0.15625 to 0.15625
- dense_out_bias: bfloat16 [768], P('ch'), may hold values from -4 to 4
Outputs:
- block_out: bfloat16 [4, 4, 32, 384, 768], P(('grp', 'lat'), 'lon', None, None, 'ch'), parts along dimension 0
There are 2 independent parts, one for each index of `grp`. A program takes and returns all parts, laid end to end along the dimension named above; an argument that names none is the same for every part. Nothing has to cross between parts.
Inputs may be any that keep to these rules, and one draw needn't show every extreme that they name: Block b keeps latitude frequencies -kept_lat[b] to kept_lat[b] - 1; in every draw some block keeps all 128. Block b keeps longitude frequencies 0 to kept_lon[b] - 1; in every draw some block keeps 128.
All inputs are finite; a program needn't handle non-finite values.
Results may differ from a plain program's by a relative error of at most 0.0095.
Values may be sent and summed in bfloat16 or wider, within the bound.
No kernel may reach another device: no remote copies, remote signals or barrier semaphores. Data moves between devices by JAX's collectives and lax.ppermute only.
A program may use at most 192 MiB of HBM per device.

v0:
```python
import math

import jax
import jax.numpy as jnp
from jax import lax
from jax.sharding import PartitionSpec as P

H = 256
W = 384
C = 768
MLAT = 64
KEEP_LON = 128


shrink_level = 0.01
norm_epsilon = 1e-05


def lon_forward(number, length):
    freq_ids = jnp.arange(number, dtype=jnp.int32)
    cell_ids = jnp.arange(length, dtype=jnp.int32)
    phase_turns = cell_ids[:, None] * freq_ids[None, :] % length
    angles = phase_turns.astype(jnp.float32) * (2.0 * math.pi / length)
    factor = 1.0 / math.sqrt(length)
    return jnp.stack([jnp.cos(angles) * factor, -jnp.sin(angles) * factor], axis=1).astype(
        jnp.bfloat16
    )


def lon_inverse(freq_ids, length):
    cell_ids = jnp.arange(length, dtype=jnp.int32)
    phase_turns = freq_ids[:, None] * cell_ids[None, :] % length
    angles = phase_turns.astype(jnp.float32) * (2.0 * math.pi / length)
    factor = 1.0 / math.sqrt(length)
    weight = jnp.where(freq_ids == 0, 1.0, 2.0).astype(jnp.float32)[:, None]
    return jnp.stack(
        [jnp.cos(angles) * factor * weight, -jnp.sin(angles) * factor * weight]
    ).astype(jnp.bfloat16)


def band_ids(half_band, length):
    slot_ids = jnp.arange(2 * half_band, dtype=jnp.int32)
    return jnp.where(slot_ids < half_band, slot_ids, slot_ids + length - 2 * half_band)


def lat_forward(row_ids, half_band, length):
    phase_turns = band_ids(half_band, length)[:, None] * row_ids[None, :] % length
    angles = phase_turns.astype(jnp.float32) * (2.0 * math.pi / length)
    factor = 1.0 / math.sqrt(length)
    cosine = jnp.cos(angles) * factor
    sine_part = jnp.sin(angles) * factor
    upper_half = jnp.concatenate([cosine, sine_part], axis=1)
    bottom = jnp.concatenate([-sine_part, cosine], axis=1)
    return jnp.concatenate([upper_half, bottom], axis=0).astype(jnp.bfloat16)


def lat_inverse(row_ids, half_band, length):
    phase_turns = row_ids[:, None] * band_ids(half_band, length)[None, :] % length
    angles = phase_turns.astype(jnp.float32) * (2.0 * math.pi / length)
    factor = 1.0 / math.sqrt(length)
    cosine = jnp.cos(angles) * factor
    sine_part = jnp.sin(angles) * factor
    upper_half = jnp.concatenate([cosine, -sine_part], axis=1)
    bottom = jnp.concatenate([sine_part, cosine], axis=1)
    return jnp.concatenate([upper_half, bottom], axis=0).astype(jnp.bfloat16)


def complex_layer(values, weight, offset):
    products = jnp.einsum("tjkbc,ubcd->tujkbd", values, weight, preferred_element_type=jnp.float32)
    offset = offset.astype(jnp.float32)
    real_part = products[0, 0] - products[1, 1] + offset[0]
    imag_part = products[1, 0] + products[0, 1] + offset[1]
    return jnp.stack([real_part, imag_part])


def channel_mlp(mixed_full, norm_gain, norm_bias, weight_in, bias_in, weight_out):
    wide = mixed_full.astype(jnp.float32)
    center = jnp.mean(wide, axis=-1, keepdims=True)
    spread = jnp.mean((wide - center) ** 2, axis=-1, keepdims=True)
    normed = (
        (wide - center) * lax.rsqrt(spread + norm_epsilon) * norm_gain.astype(jnp.float32)
        + norm_bias.astype(jnp.float32)
    ).astype(jnp.bfloat16)
    hidden = jnp.einsum("rwc,cu->rwu", normed, weight_in, preferred_element_type=jnp.float32)
    hidden = jax.nn.gelu(hidden + bias_in.astype(jnp.float32), approximate=False).astype(
        jnp.bfloat16
    )
    return jnp.einsum("rwu,uc->rwc", hidden, weight_out, preferred_element_type=jnp.float32)


def on_device(
    patches,
    filter_norm_gain,
    filter_norm_bias,
    filter_in,
    filter_in_bias,
    filter_out,
    filter_out_bias,
    kept_lat,
    kept_lon,
    norm_gain,
    norm_bias,
    dense_in,
    dense_in_bias,
    dense_out,
    dense_out_bias,
):
    lon_count = lax.axis_size("lon")
    lat_count = lax.axis_size("lat")
    band_rows = patches.shape[0] // lon_count
    local_channels = patches.shape[2]
    local_blocks = filter_in.shape[1]
    block_width = filter_in.shape[2]
    row_span = lon_count * band_rows
    local_freqs = KEEP_LON // (lon_count * lat_count)
    local_rows = lax.all_to_all(patches, "lon", split_axis=0, concat_axis=1, tiled=True)
    raw = local_rows.astype(jnp.float32)
    cell_total = lax.psum(jnp.sum(raw, axis=-1, keepdims=True), "ch")
    pre_center = cell_total / C
    centered = raw - pre_center
    square_total = lax.psum(jnp.sum(centered * centered, axis=-1, keepdims=True), "ch")
    pre_spread = square_total / C
    prenormed = (
        centered * lax.rsqrt(pre_spread + norm_epsilon) * filter_norm_gain.astype(jnp.float32)
        + filter_norm_bias.astype(jnp.float32)
    ).astype(jnp.bfloat16)
    spectrum = jnp.einsum(
        "rwc,wtk->trkc", prenormed, lon_forward(KEEP_LON, W), preferred_element_type=jnp.float32
    )
    spectrum = spectrum.astype(jnp.bfloat16)
    slot_ids = jnp.arange(H, dtype=jnp.int32)
    group_ids = slot_ids // band_rows
    direct_rows = (
        group_ids % lat_count * row_span + group_ids // lat_count * band_rows + slot_ids % band_rows
    )
    pencil = lax.all_to_all(spectrum, ("lon", "lat"), split_axis=2, concat_axis=1, tiled=True)
    banded = jnp.dot(
        lat_forward(direct_rows, MLAT, H),
        pencil.reshape(2 * H, -1),
        preferred_element_type=jnp.float32,
    )
    banded = banded.astype(jnp.bfloat16).reshape(
        2, 2 * MLAT, local_freqs, local_blocks, block_width
    )
    first = complex_layer(banded, filter_in, filter_in_bias.reshape(2, local_blocks, block_width))
    first = jnp.maximum(first, 0.0).astype(jnp.bfloat16)
    second = complex_layer(first, filter_out, filter_out_bias.reshape(2, local_blocks, block_width))
    shrunk = jnp.sign(second) * jnp.maximum(jnp.abs(second) - shrink_level, 0.0)
    column_ids = (
        lax.axis_index("lon") * lat_count + lax.axis_index("lat")
    ) * local_freqs + jnp.arange(local_freqs, dtype=jnp.int32)
    band_slots = jnp.arange(2 * MLAT, dtype=jnp.int32)
    signed_band = jnp.where(band_slots < MLAT, band_slots, band_slots - 2 * MLAT)
    lat_ok = (signed_band[:, None] >= -kept_lat[None, :]) & (
        signed_band[:, None] < kept_lat[None, :]
    )
    lon_ok = column_ids[:, None] < kept_lon[None, :]
    keep_mask = (lat_ok[:, None, :] & lon_ok[None, :, :]).astype(jnp.float32)[..., None]
    kept_modes = (shrunk * keep_mask).astype(jnp.bfloat16).reshape(4 * MLAT, -1)
    spatial = jnp.dot(
        lat_inverse(direct_rows, MLAT, H), kept_modes, preferred_element_type=jnp.float32
    )
    spatial = spatial.astype(jnp.bfloat16).reshape(2, H, local_freqs, local_channels)
    returned = lax.all_to_all(spatial, ("lon", "lat"), split_axis=1, concat_axis=2, tiled=True)
    back_freqs = jnp.arange(KEEP_LON, dtype=jnp.int32)
    fine_part = jnp.einsum(
        "trkc,tkw->rwc", returned, lon_inverse(back_freqs, W), preferred_element_type=jnp.float32
    )
    mixed = (raw + fine_part).astype(jnp.bfloat16)
    gathered = lax.all_gather(mixed, "ch", axis=2, tiled=True)
    partial_terms = channel_mlp(gathered, norm_gain, norm_bias, dense_in, dense_in_bias, dense_out)
    summed = lax.psum_scatter(
        partial_terms.astype(jnp.bfloat16), "ch", scatter_dimension=2, tiled=True
    ).astype(jnp.float32)
    result = (mixed.astype(jnp.float32) + summed + dense_out_bias.astype(jnp.float32)).astype(
        jnp.bfloat16
    )
    return result.reshape(1, 1, band_rows, W, local_channels)


def solution(mesh):
    placed = (
        P(("grp", "lat"), "lon", "ch"),
        P("ch"),
        P("ch"),
        P(None, "ch", None, None),
        P(None, "ch"),
        P(None, "ch", None, None),
        P(None, "ch"),
        P("ch"),
        P("ch"),
        P(),
        P(),
        P(None, "ch"),
        P("ch"),
        P("ch", None),
        P("ch"),
    )
    return jax.shard_map(
        on_device,
        mesh=mesh,
        in_specs=placed,
        out_specs=P(("grp", "lat"), "lon", None, None, "ch"),
        check_vma=False,
    )
```

profile of v0, /device:TPU:0, one launch (start us, length us, event | category | flops | bytes accessed | tf_op | source)
XLA Modules:
  0.0 945.3 jit_solution(8569480694956395511)
XLA Ops:
  6.5 6.4 all-to-all-start
  13.0 0.8 multiply_convert_fusion.1
  13.9 205.9 %all-to-all-done = bf16[128,96,384]{2,1,0:T(8,128)(2,1)} async-done(((bf16[128,96,384]{2,1,0:T(8,128)(2,1)}), bf16[128,96,384]{2,1,0:T(8,128)(2,1)}, u32[]{:S(2)}, u32[]{:S(2)}) %all-to-all-start) | async-done | bytes 9437216 | tf_op jit(solution)/shard_map/all_to_all | solution.py:116
  219.8 12.8 %bitcast_convert_fusion = f32[4,32,96,384]{3,2,1,0:T(8,128)} fusion(bf16[128,96,384]{2,1,0:T(8,128)(2,1)} %all-to-all-done), kind=kLoop, calls=%fused_computation.216 | loop fusion | flops 4718592 | bytes 28311552 | tf_op jit(solution)/shard_map/convert_element_type | solution.py:117
  232.6 7.6 bitcast_reduce_fusion
  240.3 0.1 broadcast_in_dim.12
  240.4 3.5 psum.14
  243.9 0.1 sub.129
  244.0 8.5 fusion.23
  252.5 0.1 broadcast_in_dim.13
  252.6 3.7 psum.15
  256.3 12.8 %copy.37 = f32[4,32,96,384]{3,2,0,1:T(8,128)} copy(bf16[4,32,96,384]{3,2,1,0:T(8,128)(2,1)} %bitcast.34) | data formatting | bytes 28311552 | tf_op jit(solution)/shard_map/convert_element_type | solution.py:117
  269.2 9.0 fusion.21
  278.2 0.0 copy-start.8
  278.2 0.0 copy-start.13
  278.3 0.0 copy-start.15
  278.3 3.6 convert_bitcast_fusion
  281.9 6.4 copy.38
  288.3 5.2 all-to-all-start.1
  293.6 0.1 add.382
  293.7 0.1 add.387
  293.8 0.1 add.390
  293.9 0.1 add.395
  294.1 0.1 broadcast_compare_fusion
  294.1 0.1 compare_and_fusion
  294.2 0.1 and_convert_fusion.2
  294.3 0.6 fusion.93
  294.9 0.6 negate_convert_fusion.1
  295.5 136.8 %all-to-all-done.1 = bf16[2,32,128,384]{3,1,0,2:T(8,128)(2,1)} async-done(((bf16[2,32,128,384]{3,1,0,2:T(8,128)(2,1)}), bf16[2,32,128,384]{3,1,0,2:T(8,128)(2,1)}, u32[]{:S(2)}, u32[]{:S(2)}) %all-to-all-start.1) | async-done | bytes 6291488 | tf_op jit(solution)/shard_map/all_to_all | solution.py:136
  432.3 6.5 copy.39
  438.9 2.1 copy.72
  441.0 3.6 convolution_convert_fusion.1
  444.6 9.1 reshape.537
  453.7 7.8 convolution_bitcast_fusion.1
  461.5 1.3 fusion.52
  462.8 1.8 convolution_bitcast_fusion
  464.7 3.1 fusion.47
  467.8 4.3 multiply_convert_fusion
  472.1 3.2 copy.48
  475.3 1.8 convolution_convert_fusion
  477.2 1.6 copy.74
  478.8 3.4 copy.49
  482.2 4.8 all-to-all-start.2
  487.0 0.0 all-gather.2.cloned.1.call-start
  487.1 0.8 multiply_convert_fusion.4
  487.9 137.0 %all-to-all-done.2 = bf16[2,256,16,384]{3,2,0,1:T(8,128)(2,1)} async-done(((bf16[2,256,16,384]{3,2,0,1:T(8,128)(2,1)}), bf16[2,256,16,384]{3,2,0,1:T(8,128)(2,1)}, u32[]{:S(2)}, u32[]{:S(2)}) %all-to-all-start.2) | async-done | bytes 6291488 | tf_op jit(solution)/shard_map/all_to_all | solution.py:164
  625.0 4.0 copy.50
  629.0 10.5 %fusion.17 = bf16[32,384,384]{2,1,0:T(8,128)(2,1)} fusion(f32[4,32,96,384]{3,2,0,1:T(8,128)} %copy.37, bf16[2,32,128,384]{3,2,0,1:T(8,128)(2,1)S(1)} %bitcast.142, bf16[1,128,384]{1,2,0:T(8,128)(2,1)S(1)} %get-tuple-element.24, bf16[1,128,384]{1,2,0:T(8,128)(2,1)S(1)} %get-tuple-element.23), kind=kOutput, calls=%fused_computation.32 | convolution fusion | flops 2425749504 | bytes 34799616 | tf_op jit(solution)/shard_map/trkc,tkw->rwc/dot_general | solution.py:166
  639.5 0.0 all-gather.2.cloned.1.call-update
  639.5 0.0 reduce-scatter.4.cloned.1.call-start
  639.6 32.9 %all-gather.2.cloned.1.call-done = bf16[32,384,768]{2,1,0:T(8,128)(2,1)} async-done(((bf16[32,384,384]{2,1,0:T(8,128)(2,1)}), bf16[32,384,768]{2,1,0:T(8,128)(2,1)}) %all-gather.2.cloned.1.call-update) | async-done | bytes 18874384 | tf_op jit(solution)/shard_map/all_gather | solution.py:170
  672.5 9.1 convert_reduce_fusion
  681.7 2.9 copy-done.2
  684.6 7.5 fusion.2
  692.1 33.4 %convert_reduce_fusion.2 = (u32[384,768]{1,0:T(8,128)S(1)}, u32[384,768]{1,0:T(8,128)S(1)}, f32[32,384,768]{2,1,0:T(8,128)}) fusion(f32[768]{0:T(1024)S(1)} %convert_element_type.178, bf16[768,768]{1,0:T(8,128)(2,1)S(1)} %copy-done, bf16[32,384,768]{2,1,0:T(8,128)(2,1)S(1)} %copy-done.2, f32[768]{0:T(1024)S(1)} %convert_element_type.176, ...), kind=kOutput, calls=%fused_computation.16 | convolution fusion | flops 14664794112 | bytes 60269568 | tf_op jit(solution)/shard_map/rwc,cu->rwu/dot_general | solution.py:84
  725.6 102.7 %fusion.30 = bf16[32,384,768]{2,1,0:T(8,128)(2,1)} fusion(f32[32,384,768]{2,1,0:T(8,128)} %get-tuple-element.25, u32[384,768]{1,0:T(8,128)S(1)} %get-tuple-element.6, u32[384,768]{1,0:T(8,128)S(1)} %get-tuple-element.5, f32[768]{0:T(1024)S(1)} %convert_element_type.178, bf16[768,768]{1,0:T(8,128)(2,1)S(1)} %copy-done.14), kind=kOutput, calls=%fused_computation.48 | convolution fusion | flops 15156117504 | bytes 60165120 | tf_op jit(solution)/shard_map/rwu,uc->rwc/dot_general | solution.py:88
  828.3 24.5 %copy.68 = bf16[32,384,768]{1,0,2:T(8,128)(2,1)} copy(bf16[32,384,768]{2,1,0:T(8,128)(2,1)} %fusion.30) | data formatting | bytes 37748736
  852.7 20.3 %copy.75 = bf16[96,8,32,384]{3,1,2,0:T(8,128)(2,1)} copy(bf16[96,8,32,384]{3,2,1,0:T(8,128)(2,1)} %bitcast.137) | data formatting | bytes 37748736
  873.1 0.0 reduce-scatter.4.cloned.1.call-update
  873.1 0.7 copy-done.12
  873.7 28.9 %reduce-scatter.4.cloned.1.call-done = bf16[384,12288]{1,0:T(8,128)(2,1)} async-done(((bf16[768,12288]{1,0:T(8,128)(2,1)}), bf16[384,12288]{1,0:T(8,128)(2,1)}) %reduce-scatter.4.cloned.1.call-update) | async-done | bytes 9437200
  902.7 9.7 %copy.76 = bf16[48,8,32,384]{3,2,1,0:T(8,128)(2,1)} copy(bf16[48,8,32,384]{3,1,2,0:T(8,128)(2,1)} %bitcast.145) | data formatting | bytes 18874368
  912.3 13.4 %copy.69 = bf16[32,384,384]{2,1,0:T(8,128)(2,1)} copy(bf16[32,384,384]{1,0,2:T(8,128)(2,1)} %bitcast.139) | data formatting | bytes 18874368
  925.8 12.3 %fusion.33 = bf16[1,1,32,384,384]{4,3,2,1,0:T(8,128)(2,1)} fusion(bf16[32,384,384]{2,1,0:T(8,128)(2,1)} %copy.69, bf16[32,384,384]{2,1,0:T(8,128)(2,1)} %fusion.17, f32[384]{0:T(512)S(1)} %convert_element_type.182), kind=kLoop, calls=%fused_computation.49 | loop fusion | flops 23592960 | bytes 28313088 | tf_op jit(solution)/shard_map/reshape | solution.py:178
  (47 shorter events, 0.2 us)
Async XLA Ops:
  6.5 685.6 %copy-start = (bf16[768,768]{1,0:T(8,128)(2,1)S(1)}, bf16[768,768]{1,0:T(8,128)(2,1)}, u32[]{:S(2)}) copy-start(bf16[768,768]{1,0:T(8,128)(2,1)} %param.26) | copy-start | bytes 3538948
  6.5 6.5 copy-start.10
  6.5 6.5 copy-start.11
  6.5 213.3 %all-to-all-start = ((bf16[128,96,384]{2,1,0:T(8,128)(2,1)}), bf16[128,96,384]{2,1,0:T(8,128)(2,1)}, u32[]{:S(2)}, u32[]{:S(2)}) async-start(bf16[128,96,384]{2,1,0:T(8,128)(2,1)} %param.15), calls=%async_computation | async-start | bytes 18874368 | tf_op jit(solution)/shard_map/all_to_all | solution.py:116
  278.2 15.4 %copy-start.8 = (bf16[2,384]{1,0:T(2,128)(2,1)S(1)}, bf16[2,384]{1,0:T(2,128)(2,1)}, u32[]{:S(2)}) copy-start(bf16[2,384]{1,0:T(2,128)(2,1)} %param.19) | copy-start | bytes 4612
  278.2 15.6 %copy-start.9 = (bf16[2,384]{1,0:T(2,128)(2,1)S(1)}, bf16[2,384]{1,0:T(2,128)(2,1)}, u32[]{:S(2)}) copy-start(bf16[2,384]{1,0:T(2,128)(2,1)} %param.21) | copy-start | bytes 4612
  278.2 15.7 %copy-start.13 = (s32[4]{0:T(128)S(1)}, s32[4]{0:T(128)}, u32[]{:S(2)}) copy-start(s32[4]{0:T(128)} %param.22) | copy-start | bytes 52
  278.3 15.8 %copy-start.15 = (s32[4]{0:T(128)S(1)}, s32[4]{0:T(128)}, u32[]{:S(2)}) copy-start(s32[4]{0:T(128)} %param.23) | copy-start | bytes 52
  288.3 144.0 %all-to-all-start.1 = ((bf16[2,32,128,384]{3,1,0,2:T(8,128)(2,1)}), bf16[2,32,128,384]{3,1,0,2:T(8,128)(2,1)}, u32[]{:S(2)}, u32[]{:S(2)}) async-start(bf16[2,32,128,384]{3,1,0,2:T(8,128)(2,1)} %copy.38), calls=%async_computation.1 | async-start | bytes 12582912 | tf_op jit(solution)/shard_map/all_to_all | solution.py:136
  432.3 21.4 %copy-start.3 = (bf16[2,4,96,96]{3,2,1,0:T(8,128)(2,1)S(1)}, bf16[2,4,96,96]{3,2,1,0:T(8,128)(2,1)}, u32[]{:S(2)}) copy-start(bf16[2,4,96,96]{3,2,1,0:T(8,128)(2,1)} %param.18) | copy-start | bytes 442372
  444.6 18.3 %copy-start.4 = (bf16[2,4,96,96]{3,2,1,0:T(8,128)(2,1)S(1)}, bf16[2,4,96,96]{3,2,1,0:T(8,128)(2,1)}, u32[]{:S(2)}) copy-start(bf16[2,4,96,96]{3,2,1,0:T(8,128)(2,1)} %param.20) | copy-start | bytes 442372
  482.2 142.7 %all-to-all-start.2 = ((bf16[2,256,16,384]{3,2,0,1:T(8,128)(2,1)}), bf16[2,256,16,384]{3,2,0,1:T(8,128)(2,1)}, u32[]{:S(2)}, u32[]{:S(2)}) async-start(bf16[2,256,16,384]{3,2,0,1:T(8,128)(2,1)} %copy.49), calls=%async_computation.2 | async-start | bytes 12582912 | tf_op jit(solution)/shard_map/all_to_all | solution.py:164
  487.0 185.5 %all-gather.2.cloned.1.call-start = ((), (), s32[]{:S(2)}) async-start(), calls=%async_computation.4 | async-start | bytes 28311552 | tf_op jit(solution)/shard_map/all_gather | solution.py:170
  628.9 10.6 %copy-start.5 = (bf16[768]{0:T(1024)(128)(2,1)S(1)}, bf16[768]{0:T(1024)(128)(2,1)}, u32[]{:S(2)}) copy-start(bf16[768]{0:T(1024)(128)(2,1)} %param.27) | copy-start | bytes 4612
  628.9 10.6 %copy-start.6 = (bf16[768]{0:T(1024)(128)(2,1)S(1)}, bf16[768]{0:T(1024)(128)(2,1)}, u32[]{:S(2)}) copy-start(bf16[768]{0:T(1024)(128)(2,1)} %param.24) | copy-start | bytes 4612
  628.9 10.6 %copy-start.7 = (bf16[768]{0:T(1024)(128)(2,1)S(1)}, bf16[768]{0:T(1024)(128)(2,1)}, u32[]{:S(2)}) copy-start(bf16[768]{0:T(1024)(128)(2,1)} %param.25) | copy-start | bytes 4612
  639.5 263.2 %reduce-scatter.4.cloned.1.call-start = ((), (), s32[]{:S(2)}) async-start(), calls=%async_computation.5 | async-start | bytes 28311552
  672.5 12.0 %copy-start.2 = (bf16[32,384,768]{2,1,0:T(8,128)(2,1)S(1)}, bf16[32,384,768]{2,1,0:T(8,128)(2,1)}, u32[]{:S(2)}) copy-start(bf16[32,384,768]{2,1,0:T(8,128)(2,1)} %all-gather.2.cloned.1.call-done) | copy-start | bytes 56623108
  692.1 33.5 %copy-start.14 = (bf16[768,768]{1,0:T(8,128)(2,1)S(1)}, bf16[768,768]{1,0:T(8,128)(2,1)}, u32[]{:S(2)}) copy-start(bf16[768,768]{1,0:T(8,128)(2,1)} %param.28) | copy-start | bytes 3538948
  873.1 0.7 copy-start.12
  912.3 25.7 %copy-start.1 = (bf16[768,768]{1,0:T(8,128)(2,1)S(1)}, bf16[768,768]{1,0:T(8,128)(2,1)}, u32[]{:S(2)}) copy-start(bf16[768,768]{1,0:T(8,128)(2,1)} %param.26) | copy-start | bytes 3538948
Sparse Core Ops, SparseCore 0:
  639.6 32.8 all-gather.1
  873.2 29.4 reduce-scatter.3
where the time goes:
time: 955 us; the launch traced here: 945 us
  waiting for transfers between devices  542 us (57%)
  matrix products  165 us (17%)
  local copies, waits for them, and re-layouts  121 us (13%)
  other arithmetic  78.9 us (8%)
  starting transfers between devices  16.5 us (2%)
  between operations  14.3 us (1%)
    all_to_all x1, waiting for transfers between devices, on_device(): lax.all_to_all(patches, 'lon', split_axis=0, concat_axis=1, tiled=True)  206 us
    all_to_all x1, waiting for transfers between devices, on_device(): lax.all_to_all(spatial, ('lon', 'lat'), split_axis=1, concat_axis=2, tile...  137 us
    all_to_all x1, waiting for transfers between devices, on_device(): lax.all_to_all(spectrum, ('lon', 'lat'), split_axis=2, concat_axis=1, til...  137 us
    dot_general x1, matrix products, channel_mlp(): jnp.einsum('rwu,uc->rwc', hidden, weight_out, preferred_element_type=jnp....  103 us
    unnamed x38, local copies, waits for them, and re-layouts  75.3 us
    dot_general x1, matrix products, channel_mlp(): jnp.einsum('rwc,cu->rwu', normed, weight_in, preferred_element_type=jnp.f...  33.4 us
    all_gather x1, waiting for transfers between devices, on_device(): gathered = lax.all_gather(mixed, 'ch', axis=2, tiled=True)  32.9 us
    unnamed x3, waiting for transfers between devices  29 us
  transfers between devices with their start and end apart: 5, of which 5 were waited for; matrix products, arithmetic and copies ran while one was open for 0% of the time, Pallas kernels for 0%

commit v1 on v0

--- a/solution.py
+++ b/solution.py
@@ -1,8 +1,12 @@
+import functools
 import math
 
 import jax
 import jax.numpy as jnp
+import numpy as np
 from jax import lax
+from jax.experimental import pallas as pl
+from jax.experimental.pallas import tpu as pltpu
 from jax.sharding import PartitionSpec as P
 
 H = 256
@@ -11,9 +15,432 @@
 MLAT = 64
 KEEP_LON = 128
 
-
 shrink_level = 0.01
 norm_epsilon = 1e-05
+
+BF = jnp.bfloat16
+F32 = jnp.float32
+
+
+def angle_table(rows, cols, length):
+    phase = rows[:, None] * cols[None, :] % length
+    return phase * (2.0 * math.pi / length)
+
+
+def lat_slots(lat_count, lon_count):
+    per = MLAT // (lat_count * lon_count)
+    freq, kind = [], []
+    for dev in range(lat_count * lon_count):
+        for pair in range(dev * per, dev * per + per):
+            freq += [0, MLAT] if pair == 0 else [pair, pair]
+            kind += [0, 0] if pair == 0 else [0, 1]
+        freq.append(MLAT if dev == 0 else 0)
+        kind.append(1 if dev == 0 else 2)
+    return np.array(freq), np.array(kind)
+
+
+def lat_tables(lat_count, lon_count):
+    freq, kind = lat_slots(lat_count, lon_count)
+    angles = angle_table(freq, np.arange(H), H)
+    table = np.where(kind[:, None] == 0, np.cos(angles), -np.sin(angles)) / math.sqrt(H)
+    table = np.where(kind[:, None] == 2, 0.0, table)
+    return table.astype(np.float32)
+
+
+def lon_tables(order):
+    freqs = np.arange(KEEP_LON)
+    angles = angle_table(freqs, order, W)
+    factor = 1.0 / math.sqrt(W)
+    weight = np.where(freqs == 0, 1.0, 2.0)[:, None]
+    forward = np.concatenate([np.cos(angles) * factor, -np.sin(angles) * factor], axis=0)
+    inverse = np.concatenate(
+        [np.cos(angles) * factor * weight, -np.sin(angles) * factor * weight], axis=0
+    ).T
+    return forward.astype(np.float32).astype(jnp.bfloat16), inverse.astype(np.float32).astype(jnp.bfloat16)
+
+
+def spread8(table):
+    return np.kron(table, np.eye(8, dtype=np.float32)).astype(jnp.bfloat16)
+
+
+def lat_forward_kernel(cells_ref, table_ref, send_ref, keep_ref):
+    rows = cells_ref.shape[0]
+    values = cells_ref[...].astype(F32).reshape(rows, 2, 8, cells_ref.shape[2])
+    width = cells_ref.shape[2]
+    pair = jnp.concatenate(
+        [values[:, 0].reshape(rows * 8, width), values[:, 1].reshape(rows * 8, width)], axis=1
+    ).astype(BF)
+    half = table_ref.shape[0] // 2
+    for part, out_ref in ((0, send_ref), (1, keep_ref)):
+        total = jnp.dot(
+            table_ref[part * half : (part + 1) * half, :], pair, preferred_element_type=F32
+        )
+        slots = half // 8
+        out_ref[...] = jnp.concatenate(
+            [
+                total[:, :width].reshape(slots, 8, width),
+                total[:, width:].reshape(slots, 8, width),
+            ],
+            axis=1,
+        ).astype(BF)
+
+
+def lat_forward(cells, table):
+    rows, cols, width = cells.shape
+    slots = table.shape[0] // 16
+    block = pl.BlockSpec((slots, 16, width), lambda i: (0, i, 0))
+    return pl.pallas_call(
+        lat_forward_kernel,
+        grid=(cols // 16,),
+        in_specs=[
+            pl.BlockSpec((rows, 16, width), lambda i: (0, i, 0)),
+            pl.BlockSpec(table.shape, lambda i: (0, 0)),
+        ],
+        out_specs=[block, block],
+        out_shape=[jax.ShapeDtypeStruct((slots, cols, width), BF)] * 2,
+        compiler_params=pltpu.CompilerParams(vmem_limit_bytes=40 << 20),
+        cost_estimate=pl.CostEstimate(
+            flops=2 * table.size * cols // 8 * width,
+            bytes_accessed=4 * rows * cols * width,
+            transcendentals=0,
+        ),
+        name="lat_forward",
+    )(cells, table)
+
+
+def lat_inverse_kernel(own_ref, other_ref, table_ref, patches_ref, out_ref):
+    rows, _, width = patches_ref.shape
+    slots = own_ref.shape[0] * own_ref.shape[1]
+
+    def flat(ref):
+        values = ref[...].astype(F32).reshape(slots, 2, 8, width)
+        return jnp.concatenate(
+            [values[:, 0].reshape(slots * 8, width), values[:, 1].reshape(slots * 8, width)], axis=1
+        ).astype(BF)
+
+    half = table_ref.shape[1] // 2
+    total = jnp.dot(table_ref[:, :half], flat(own_ref), preferred_element_type=F32)
+    total += jnp.dot(table_ref[:, half:], flat(other_ref), preferred_element_type=F32)
+    fine = jnp.concatenate(
+        [total[:, :width].reshape(rows, 8, width), total[:, width:].reshape(rows, 8, width)], axis=1
+    )
+    out_ref[...] = (patches_ref[...].astype(F32) + fine).astype(BF)
+
+
+def lat_inverse(own, other, table, patches, first_block):
+    groups, slots, cols, width = own.shape
+    rows = patches.shape[0]
+    spec = pl.BlockSpec((groups, slots, 16, width), lambda i: (0, 0, i, 0))
+    return pl.pallas_call(
+        lat_inverse_kernel,
+        grid=(cols // 16,),
+        in_specs=[
+            spec,
+            spec,
+            pl.BlockSpec(table.shape, lambda i: (0, 0)),
+            pl.BlockSpec((rows, 16, width), lambda i: (0, first_block + i, 0)),
+        ],
+        out_specs=pl.BlockSpec((rows, 16, width), lambda i: (0, i, 0)),
+        out_shape=jax.ShapeDtypeStruct((rows, cols, width), BF),
+        compiler_params=pltpu.CompilerParams(vmem_limit_bytes=40 << 20),
+        cost_estimate=pl.CostEstimate(
+            flops=2 * table.size * cols // 8 * width,
+            bytes_accessed=6 * rows * cols * width,
+            transcendentals=0,
+        ),
+        name="lat_inverse",
+    )(own, other, table, patches)
+
+
+def modes_kernel(
+    chunks,
+    first_pair_ref,
+    lat_lo_ref,
+    lon_lo_ref,
+    *refs,
+):
+    pair_refs = refs[:chunks]
+    spare_refs = refs[chunks : 2 * chunks]
+    forward_ref, inverse_ref, w_in_ref, b_in_ref, w_out_ref, b_out_ref = refs[
+        2 * chunks : 2 * chunks + 6
+    ]
+    out_refs = refs[2 * chunks + 6 :]
+    width = pair_refs[0].shape[-1]
+    groups, _, cols, _ = pair_refs[0].shape
+    step = pl.program_id(0)
+    pairs = pl.num_programs(0)
+    pair_id = first_pair_ref[0] + step
+    special = pair_id == 0
+    keep = KEEP_LON
+
+    def columns(refs, row):
+        return jnp.concatenate(
+            [ref[:, row].reshape(groups * cols, width) for ref in refs], axis=0
+        )
+
+    both = jnp.concatenate([columns(pair_refs, 0), columns(pair_refs, 1)], axis=1)
+    spectrum = jnp.dot(forward_ref[...], both, preferred_element_type=F32)
+    a_re, a_im = spectrum[:keep, :width], spectrum[keep:, :width]
+    b_re, b_im = spectrum[:keep, width:], spectrum[keep:, width:]
+
+    def filtered(plus_re, plus_im, minus_re, minus_im):
+        banded = jnp.concatenate(
+            [
+                jnp.concatenate([plus_re, plus_im], axis=1),
+                jnp.concatenate([minus_re, minus_im], axis=1),
+            ],
+            axis=0,
+        ).astype(BF)
+        first = jnp.dot(banded, w_in_ref[...], preferred_element_type=F32) + b_in_ref[...]
+        first = jnp.maximum(first, 0.0).astype(BF)
+        second = jnp.dot(first, w_out_ref[...], preferred_element_type=F32) + b_out_ref[...]
+        shrunk = second - jnp.clip(second, -shrink_level, shrink_level)
+        freq = lax.broadcasted_iota(jnp.int32, (keep, 2 * width), 0)
+        lon_ok = freq < lon_lo_ref[...]
+        plus_ok = lon_ok & (pair_id < lat_lo_ref[...])
+        minus_id = jnp.where(special, MLAT, pair_id)
+        minus_ok = lon_ok & (minus_id <= lat_lo_ref[...])
+        plus = jnp.where(plus_ok, shrunk[:keep], 0.0)
+        minus = jnp.where(minus_ok, shrunk[keep:], 0.0)
+        return plus[:, :width], plus[:, width:], minus[:, :width], minus[:, width:]
+
+    def back(values, refs, row):
+        grid_values = jnp.dot(inverse_ref[...], values, preferred_element_type=F32).astype(BF)
+        for i, ref in enumerate(refs):
+            piece = grid_values[i * groups * cols : (i + 1) * groups * cols]
+            for r in range(piece.shape[1] // width):
+                ref[:, pl.ds(row + r, 1)] = piece[:, r * width : (r + 1) * width].reshape(
+                    groups, 1, cols, width
+                )
+
+    @pl.when(special)
+    def _():
+        spare = jnp.dot(forward_ref[...], columns(spare_refs, 0), preferred_element_type=F32)
+        e_re, e_im = spare[:keep], spare[keep:]
+        p_re, p_im, m_re, m_im = filtered(a_re, a_im, b_re + e_im, b_im - e_re)
+        values = jnp.concatenate(
+            [jnp.concatenate([p_re, m_re], axis=1), jnp.concatenate([p_im, m_im], axis=1)], axis=0
+        ).astype(BF)
+        back(values, out_refs, 2 * step)
+        back(jnp.concatenate([-m_im, m_re], axis=0).astype(BF), out_refs, 2 * pairs)
+
+    @pl.when(jnp.logical_not(special))
+    def _():
+        p_re, p_im, m_re, m_im = filtered(a_re - b_im, a_im + b_re, a_re + b_im, a_im - b_re)
+        values = jnp.concatenate(
+            [
+                jnp.concatenate([p_re + m_re, p_im - m_im], axis=1),
+                jnp.concatenate([p_im + m_im, m_re - p_re], axis=1),
+            ],
+            axis=0,
+        ).astype(BF)
+        back(values, out_refs, 2 * step)
+
+    @pl.when(jnp.logical_and(step == 0, jnp.logical_not(special)))
+    def _():
+        for ref in out_refs:
+            ref[:, pl.ds(2 * pairs, 1)] = jnp.zeros((groups, 1, cols, width), BF)
+
+
+def modes(received, first_pair, lat_keep, lon_keep, forward, inverse, w_in, b_in, w_out, b_out):
+    chunks = len(received)
+    groups, slots, cols, width = received[0].shape
+    pairs = slots // 2
+    pair_spec = pl.BlockSpec((groups, 2, cols, width), lambda i: (0, i, 0, 0))
+    spare_spec = pl.BlockSpec((groups, 1, cols, width), lambda i: (0, slots - 1, 0, 0))
+    whole = lambda array: pl.BlockSpec(array.shape, lambda i: (0,) * array.ndim)
+    return pl.pallas_call(
+        functools.partial(modes_kernel, chunks),
+        grid=(pairs,),
+        in_specs=[pl.BlockSpec(memory_space=pltpu.SMEM), whole(lat_keep), whole(lon_keep)]
+        + [pair_spec] * chunks
+        + [spare_spec] * chunks
+        + [whole(forward), whole(inverse), whole(w_in), whole(b_in), whole(w_out), whole(b_out)],
+        out_specs=[pl.BlockSpec((groups, slots, cols, width), lambda i: (0, 0, 0, 0))] * chunks,
+        out_shape=[jax.ShapeDtypeStruct((groups, slots, cols, width), BF)] * chunks,
+        compiler_params=pltpu.CompilerParams(vmem_limit_bytes=48 << 20),
+        cost_estimate=pl.CostEstimate(
+            flops=pairs * 2 * (2 * 2 * KEEP_LON * W * 2 * width + 4 * KEEP_LON * 4 * width * width),
+            bytes_accessed=4 * chunks * groups * slots * cols * width,
+            transcendentals=0,
+        ),
+        name="modes",
+    )(
+        first_pair, lat_keep, lon_keep, *received, *received,
+        forward, inverse, w_in, b_in, w_out, b_out,
+    )
+
+
+def mlp_kernel(
+    flag_ref, own_ref, other_ref, gain_ref, bias_ref, w_in_ref, b_in_ref, w_out_ref, b_out_ref,
+    out_ref,
+):
+    width = own_ref.shape[-1]
+    cells = own_ref.shape[1] * own_ref.shape[2]
+    own = own_ref[0].reshape(cells, width)
+    other = other_ref[0].reshape(cells, width)
+    flip = flag_ref[0] == 1
+    low = jnp.where(flip, other, own)
+    high = jnp.where(flip, own, other)
+    wide = jnp.concatenate([low, high], axis=1).astype(F32)
+    center = jnp.mean(wide, axis=1, keepdims=True)
+    off = wide - center
+    spread = jnp.mean(off * off, axis=1, keepdims=True)
+    normed = (off * lax.rsqrt(spread + norm_epsilon) * gain_ref[...] + bias_ref[...]).astype(BF)
+    hidden = jnp.dot(normed, w_in_ref[...], preferred_element_type=F32) + b_in_ref[...]
+    hidden = (hidden * (0.5 + 0.5 * lax.erf(hidden * math.sqrt(0.5)))).astype(BF)
+    total = jnp.dot(hidden, w_out_ref[...], preferred_element_type=F32) + wide + b_out_ref[...]
+    total = total.astype(BF)
+    rows, cols = own_ref.shape[1], own_ref.shape[2]
+    out_ref[0, 0] = total[:, :width].reshape(rows, cols, width)
+    out_ref[0, 1] = total[:, width:].reshape(rows, cols, width)
+
+
+def mlp(flag, own, other, gain, bias, w_in, b_in, w_out, b_out):
+    groups, rows, cols, width = own.shape
+    whole = lambda array: pl.BlockSpec(array.shape, lambda i: (0,) * array.ndim)
+    cell_spec = pl.BlockSpec((1, rows, cols, width), lambda i: (i, 0, 0, 0))
+    cells = groups * rows * cols
+    return pl.pallas_call(
+        mlp_kernel,
+        grid=(groups,),
+        in_specs=[pl.BlockSpec(memory_space=pltpu.SMEM), cell_spec, cell_spec]
+        + [whole(a) for a in (gain, bias, w_in, b_in, w_out, b_out)],
+        out_specs=pl.BlockSpec((1, 2, rows, cols, width), lambda i: (i, 0, 0, 0, 0)),
+        out_shape=jax.ShapeDtypeStruct((groups, 2, rows, cols, width), BF),
+        compiler_params=pltpu.CompilerParams(vmem_limit_bytes=48 << 20),
+        cost_estimate=pl.CostEstimate(
+            flops=4 * cells * w_in.size,
+            bytes_accessed=8 * cells * width,
+            transcendentals=cells * w_in.shape[1],
+        ),
+        name="channel_mlp",
+    )(flag, own, other, gain, bias, w_in, b_in, w_out, b_out)
+
+
+def block_diagonal(weight):
+    blocks, n = weight.shape[1], weight.shape[2]
+    eye = jnp.eye(blocks, dtype=weight.dtype)
+    spread = (weight[:, :, :, None, :] * eye[None, :, None, :, None]).reshape(
+        2, blocks * n, blocks * n
+    )
+    return jnp.concatenate(
+        [
+            jnp.concatenate([spread[0], spread[1]], axis=1),
+            jnp.concatenate([-spread[1], spread[0]], axis=1),
+        ],
+        axis=0,
+    )
+
+
+def swap(values, axis):
+    return lax.ppermute(values, axis, [(0, 1), (1, 0)])
+
+
+def column_plan(
+    chunk_cols,
+    patches,
+    filter_norm_gain,
+    filter_norm_bias,
+    filter_in,
+    filter_in_bias,
+    filter_out,
+    filter_out_bias,
+    kept_lat,
+    kept_lon,
+    norm_gain,
+    norm_bias,
+    dense_in,
+    dense_in_bias,
+    dense_out,
+    dense_out_bias,
+):
+    lon_count = lax.axis_size("lon")
+    lat_count = lax.axis_size("lat")
+    rows, cols, width = patches.shape
+    chunks = cols // chunk_cols
+    band_rows = rows // lon_count
+    block_width = filter_in.shape[2]
+    lat_id = lax.axis_index("lat")
+    lon_id = lax.axis_index("lon")
+    ch_id = lax.axis_index("ch")
+    pairs = MLAT // (lat_count * lon_count)
+    slots = 2 * pairs + 1
+
+    lat_table = lat_tables(lat_count, lon_count).reshape(lat_count, lon_count * slots, H)
+    forward_all, inverse_all = [], []
+    for a in range(lat_count):
+        here = lat_table[:, :, a * rows : (a + 1) * rows]
+        ordered = np.concatenate([here[1 - a], here[a]], axis=0)
+        forward_all.append(spread8(ordered))
+        ordered = np.concatenate([here[a], here[1 - a]], axis=0)
+        inverse_all.append(spread8(ordered.T))
+    forward_lat = lax.dynamic_index_in_dim(jnp.asarray(np.stack(forward_all)), lat_id, 0, False)
+    inverse_lat = lax.dynamic_index_in_dim(jnp.asarray(np.stack(inverse_all)), lat_id, 0, False)
+    order = np.arange(W).reshape(lon_count, chunks, chunk_cols).transpose(1, 0, 2).reshape(-1)
+    forward_lon, inverse_lon = (jnp.asarray(t) for t in lon_tables(order))
+
+    received = []
+    for i in range(chunks):
+        raw = patches[:, i * chunk_cols : (i + 1) * chunk_cols].astype(F32)
+        center = jnp.mean(raw, axis=-1)
+        off = raw - center[..., None]
+        square = jnp.sum(off * off, axis=-1)
+        theirs = swap(jnp.stack([center, square]), "ch")
+        mean = 0.5 * (center + theirs[0])
+        gap = center - theirs[0]
+        spread = (square + theirs[1]) / C + 0.25 * gap * gap
+        scale = lax.rsqrt(spread + norm_epsilon)
+        prenormed = (
+            (raw - mean[..., None]) * scale[..., None] * filter_norm_gain.astype(F32)
+            + filter_norm_bias.astype(F32)
+        ).astype(BF)
+        send, keep = lat_forward(prenormed, forward_lat)
+        total = (keep.astype(F32) + swap(send, "lat").astype(F32)).astype(BF)
+        received.append(
+            lax.all_to_all(
+                total.reshape(lon_count, slots, chunk_cols, width), "lon", 0, 0, tiled=True
+            )
+        )
+
+    w_in = block_diagonal(filter_in)
+    w_out = block_diagonal(filter_out)
+    b_in = filter_in_bias.reshape(1, -1).astype(F32)
+    b_out = filter_out_bias.reshape(1, -1).astype(F32)
+    lat_keep = jnp.tile(jnp.repeat(kept_lat, block_width), 2).reshape(1, -1)
+    lon_keep = jnp.tile(jnp.repeat(kept_lon, block_width), 2).reshape(1, -1)
+    first_pair = ((lat_id * lon_count + lon_id) * pairs).astype(jnp.int32).reshape(1)
+    filtered = modes(
+        received, first_pair, lat_keep, lon_keep, forward_lon, inverse_lon, w_in, b_in, w_out, b_out
+    )
+
+    m_in = jnp.concatenate([dense_in, swap(dense_in, "ch")], axis=1)
+    m_in_bias = jnp.concatenate([dense_in_bias, swap(dense_in_bias, "ch")]).astype(F32)[None]
+    m_out = jnp.concatenate([dense_out, swap(dense_out, "ch")], axis=0)
+    m_out_bias = lax.all_gather(dense_out_bias, "ch", axis=0, tiled=True).astype(F32)[None]
+    gain = norm_gain.astype(F32)[None]
+    bias = norm_bias.astype(F32)[None]
+    flag = ch_id.astype(jnp.int32).reshape(1)
+
+    pieces = []
+    for i in range(chunks):
+        own = lax.all_to_all(filtered[i], "lon", 0, 0, tiled=True)
+        other = swap(own, "lat")
+        mixed = lat_inverse(own, other, inverse_lat, patches, i * chunk_cols // 16)
+        halves = mixed.reshape(lon_count, 2, band_rows // 2, chunk_cols, width)
+        mine = lax.dynamic_index_in_dim(halves, ch_id, 1, False)
+        sent = lax.dynamic_index_in_dim(halves, 1 - ch_id, 1, False)
+        done = mlp(
+            flag, mine, swap(sent, "ch"), gain, bias, m_in, m_in_bias, m_out, m_out_bias
+        )
+        pieces.append(
+            lax.all_to_all(
+                done.reshape(lon_count * 2, band_rows // 2, chunk_cols, width),
+                ("lon", "ch"), 0, 0, tiled=True,
+            ).reshape(lon_count, 2, band_rows // 2, chunk_cols, width)
+        )
+    result = jnp.stack(pieces).transpose(2, 3, 1, 0, 4, 5)
+    return result.reshape(1, 1, band_rows, lon_count * cols, width)
 
 
 def lon_forward(number, length):
@@ -43,7 +470,7 @@
     return jnp.where(slot_ids < half_band, slot_ids, slot_ids + length - 2 * half_band)
 
 
-def lat_forward(row_ids, half_band, length):
+def lat_forward_table(row_ids, half_band, length):
     phase_turns = band_ids(half_band, length)[:, None] * row_ids[None, :] % length
     angles = phase_turns.astype(jnp.float32) * (2.0 * math.pi / length)
     factor = 1.0 / math.sqrt(length)
@@ -54,7 +481,7 @@
     return jnp.concatenate([upper_half, bottom], axis=0).astype(jnp.bfloat16)
 
 
-def lat_inverse(row_ids, half_band, length):
+def lat_inverse_table(row_ids, half_band, length):
     phase_turns = row_ids[:, None] * band_ids(half_band, length)[None, :] % length
     angles = phase_turns.astype(jnp.float32) * (2.0 * math.pi / length)
     factor = 1.0 / math.sqrt(length)
@@ -88,7 +515,7 @@
     return jnp.einsum("rwu,uc->rwc", hidden, weight_out, preferred_element_type=jnp.float32)
 
 
-def on_device(
+def row_plan(
     patches,
     filter_norm_gain,
     filter_norm_bias,
@@ -135,7 +562,7 @@
     )
     pencil = lax.all_to_all(spectrum, ("lon", "lat"), split_axis=2, concat_axis=1, tiled=True)
     banded = jnp.dot(
-        lat_forward(direct_rows, MLAT, H),
+        lat_forward_table(direct_rows, MLAT, H),
         pencil.reshape(2 * H, -1),
         preferred_element_type=jnp.float32,
     )
@@ -158,7 +585,7 @@
     keep_mask = (lat_ok[:, None, :] & lon_ok[None, :, :]).astype(jnp.float32)[..., None]
     kept_modes = (shrunk * keep_mask).astype(jnp.bfloat16).reshape(4 * MLAT, -1)
     spatial = jnp.dot(
-        lat_inverse(direct_rows, MLAT, H), kept_modes, preferred_element_type=jnp.float32
+        lat_inverse_table(direct_rows, MLAT, H), kept_modes, preferred_element_type=jnp.float32
     )
     spatial = spatial.astype(jnp.bfloat16).reshape(2, H, local_freqs, local_channels)
     returned = lax.all_to_all(spatial, ("lon", "lat"), split_axis=1, concat_axis=2, tiled=True)
@@ -196,8 +623,14 @@
         P("ch", None),
         P("ch"),
     )
+    sizes = mesh.shape
+    lat_count, lon_count = sizes["lat"], sizes["lon"]
+    cols = W // lon_count
+    fits = lat_count == 2 and sizes["ch"] == 2 and MLAT % (lat_count * lon_count) == 0
+    fits = fits and cols % 32 == 0 and H % (2 * lat_count * lon_count) == 0
+    plan = functools.partial(column_plan, 32) if fits else row_plan
     return jax.shard_map(
-        on_device,
+        plan,
         mesh=mesh,
         in_specs=placed,
         out_specs=P(("grp", "lat"), "lon", None, None, "ch"),

time: 955 us -> 616 us (0.65)
  waiting for transfers between devices: 542 us -> 277 us
  matrix products: 165 us -> 0 us
  blocking collectives: 7.2 us -> 122 us
  Pallas kernels: 0 us -> 97.3 us
  local copies, waits for them, and re-layouts: 121 us -> 30.3 us
  other arithmetic: 78.9 us -> 33.2 us
  starting transfers between devices: 16.5 us -> 45.2 us
  between operations: 14.3 us -> 1.1 us
    all_to_all x3 -> x7, waiting for transfers between devices: 480 us -> 51.7 us  [the longest x3 28.7 us: column_plan(): lax.all_to_all(total.reshape(lon_count, slots, chunk_cols, width), 'lon',...]
    ppermute x0 -> x15, waiting for transfers between devices: none -> 225 us  [swap(): return lax.ppermute(values, axis, [(0, 1), (1, 0)])]
    dot_general x8 -> x0, matrix products: 165 us -> none  [the longest x1 103 us: channel_mlp(): jnp.einsum('rwu,uc->rwc', hidden, weight_out, preferred_element_type=jnp....]
    all_to_all x0 -> x2, blocking collectives: none -> 117 us  [the longest x1 75.1 us: column_plan(): lax.all_to_all(done.reshape(lon_count * 2, band_rows // 2, chunk_cols, wi...]
    pallas_call x0 -> x10, Pallas kernels: none -> 97.3 us  [the longest x3 44.8 us: mlp(): pl.pallas_call(mlp_kernel, grid=(groups,), in_specs=[pl.BlockSpec(memory_...]
    unnamed x38 -> x61, local copies, waits for them, and re-layouts: 75.3 us -> 10.7 us
    all_gather x1 -> x0, waiting for transfers between devices: 32.9 us -> none  [on_device(): gathered = lax.all_gather(mixed, 'ch', axis=2, tiled=True)]
    unnamed x3 -> x0, waiting for transfers between devices: 29 us -> none
  transfers between devices with their start and end apart: 5 -> 22, of which waited for: 5 -> 12; matrix products, arithmetic and copies ran while one was open for 0% -> 3% of each run, Pallas kernels for 0% -> 13%
where the time goes in v1:
time: 616 us; the launch traced here: 607 us
  waiting for transfers between devices  277 us (45%)
  blocking collectives  122 us (20%)
  Pallas kernels  97.3 us (16%)
  starting transfers between devices  45.2 us (7%)
  other arithmetic  33.2 us (5%)
  local copies, waits for them, and re-layouts  30.3 us (5%)
    ppermute x15, waiting for transfers between devices, swap(): return lax.ppermute(values, axis, [(0, 1), (1, 0)])  225 us
    all_to_all x1, blocking collectives, column_plan(): lax.all_to_all(done.reshape(lon_count * 2, band_rows // 2, chunk_cols, wi...  75.1 us
    pallas_call x3, Pallas kernels, mlp(): pl.pallas_call(mlp_kernel, grid=(groups,), in_specs=[pl.BlockSpec(memory_...  44.8 us
    all_to_all x1, blocking collectives, column_plan(): own = lax.all_to_all(filtered[i], 'lon', 0, 0, tiled=True)  41.8 us
    all_to_all x3, waiting for transfers between devices, column_plan(): lax.all_to_all(total.reshape(lon_count, slots, chunk_cols, width), 'lon',...  28.7 us
    pallas_call x3, Pallas kernels, lat_inverse(): pl.pallas_call(lat_inverse_kernel, grid=(cols // 16,), in_specs=[spec, sp...  22.4 us
    pallas_call x1, Pallas kernels, modes(): pl.pallas_call(functools.partial(modes_kernel, chunks), grid=(pairs,), in...  16.6 us
    all_to_all x3, starting transfers between devices, column_plan(): lax.all_to_all(total.reshape(lon_count, slots, chunk_cols, width), 'lon',...  15 us
  transfers between devices with their start and end apart: 22, of which 12 were waited for; matrix products, arithmetic and copies ran while one was open for 3% of the time, Pallas kernels for 13%

profile of v1, /device:TPU:0, one launch (start us, length us, event | category | flops | bytes accessed | tf_op | source)
XLA Modules:
  0.0 606.5 jit_solution(5044759592264325313)
XLA Ops:
  0.0 4.8 convert_reduce_fusion
  4.9 1.6 copy-done.10
  6.5 4.4 fusion.13
  10.9 0.5 collective-permute-start
  11.6 0.5 collective-permute-start.4
  12.1 1.8 dynamic-slice_bitcast_fusion.1.table_ref
  14.2 7.7 %fusion.17 = (bf16[128,32,384]{2,1,0:T(8,128)(2,1)S(1)}, bf16[128,32,384]{2,1,0:T(8,128)(2,1)}, bf16[128,32,384]{2,1,0:T(8,128)(2,1)S(1)}) fusion(f32[128,32]{1,0:T(8,128)S(1)} %get-tuple-element.43, f32[128,32]{1,0:T(8,128)S(1)} %get-tuple-element.42, f32[384]{0:T(512)S(1)} %convert_element_type.90, f32[384]{0:T(512)S(1)} %convert_element_type.89, ...), kind=kLoop, calls=%fused_computation.27 | loop fusion | flops 28311552 | bytes 18975744 | tf_op jit(solution)/shard_map/convert_element_type | solution.py:397
  21.9 4.5 lat_forward.5
  26.4 2.6 collective-permute-start.5
  29.0 37.1 %collective-permute-done.5 = bf16[68,32,384]{2,1,0:T(8,128)(2,1)S(1)} collective-permute-done((bf16[68,32,384]{2,1,0:T(8,128)(2,1)S(1)}, bf16[68,32,384]{2,1,0:T(8,128)(2,1)S(1)}, u32[]{:S(2)}, u32[]{:S(2)}) %collective-permute-start.5) | collective-permute-done | bytes 1671200 | tf_op jit(solution)/shard_map/ppermute | solution.py:337
  66.1 1.6 add_convert_fusion
  67.8 5.1 all-to-all-start.2
  72.9 1.9 copy-done.1
  74.8 1.6 copy-done.3
  76.4 4.5 lat_forward.4
  80.9 1.6 collective-permute-start.3
  82.5 36.3 %collective-permute-done.3 = bf16[68,32,384]{2,1,0:T(8,128)(2,1)S(1)} collective-permute-done((bf16[68,32,384]{2,1,0:T(8,128)(2,1)S(1)}, bf16[68,32,384]{2,1,0:T(8,128)(2,1)S(1)}, u32[]{:S(2)}, u32[]{:S(2)}) %collective-permute-start.3) | collective-permute-done | bytes 1671200 | tf_op jit(solution)/shard_map/ppermute | solution.py:337
  118.8 1.7 add_convert_fusion.1
  120.4 4.8 all-to-all-start.1
  125.3 1.6 copy-done.4
  126.9 4.5 lat_forward.3
  131.4 1.6 collective-permute-start.1
  132.9 35.0 %collective-permute-done.1 = bf16[68,32,384]{2,1,0:T(8,128)(2,1)S(1)} collective-permute-done((bf16[68,32,384]{2,1,0:T(8,128)(2,1)S(1)}, bf16[68,32,384]{2,1,0:T(8,128)(2,1)S(1)}, u32[]{:S(2)}, u32[]{:S(2)}) %collective-permute-start.1) | collective-permute-done | bytes 1671200 | tf_op jit(solution)/shard_map/ppermute | solution.py:337
  167.9 1.6 add_convert_fusion.2
  169.6 5.1 all-to-all-start
  174.7 0.8 broadcast_multiply_fusion
  175.5 0.6 fusion.37
  176.5 1.0 squeeze.71
  177.8 0.8 neg.7
  178.6 1.0 squeeze.73
  180.0 1.1 maximum_maximum_fusion.refs_8_
  181.1 1.2 maximum_maximum_fusion.1.refs_10_
  182.4 28.6 %all-to-all-done.refs_0_.refs_3_ = bf16[4,17,32,384]{3,2,1,0:T(8,128)(2,1)} async-done(((bf16[4,17,32,384]{3,2,1,0:T(8,128)(2,1)}), bf16[4,17,32,384]{3,2,1,0:T(8,128)(2,1)}, u32[]{:S(2)}, u32[]{:S(2)}) %all-to-all-start) | async-done | bytes 1671200 | tf_op jit(solution)/shard_map/all_to_all | solution.py:401
  211.0 16.6 %modes.1 = (bf16[4,17,32,384]{3,2,1,0:T(8,128)(2,1)S(1)}, bf16[4,17,32,384]{3,2,1,0:T(8,128)(2,1)}, bf16[4,17,32,384]{3,2,1,0:T(8,128)(2,1)}) custom-call(s32[1]{0:T(128)} %bitcast.1.first_pair_ref, s32[1,768]{1,0:T(1,128)S(1)} %bitcast.117, s32[1,768]{1,0:T(1,128)S(1)} %bitcast.118, bf16[4,17,32,384]{3,2,1,0:T(8,128)(2,1)} %all-to-all-done.refs_0_.refs_3_, ...), custom_call_target="tpu_custom_call" | custom-call | flops 7247757312 | bytes 10027008 | tf_op jit(solution)/shard_map/modes/pallas_call | solution.py:252
  227.6 41.8 %all_to_all.45.own_ref = bf16[4,17,32,384]{3,2,1,0:T(8,128)(2,1)} all-to-all(bf16[4,17,32,384]{3,2,1,0:T(8,128)(2,1)S(1)} %get-tuple-element.20), channel_id=1, replica_groups=mesh['grp'=2,'lon'=4,'lat'=2,'ch'=2] {'lon'}, dimensions={0} | all-to-all | bytes 3342336 | tf_op jit(solution)/shard_map/all_to_all | solution.py:427
  269.3 4.4 all-to-all-start.5
  273.7 1.3 collective-permute-start.6
  275.0 1.8 dynamic-slice_bitcast_fusion.table_ref
  276.8 34.5 %collective-permute-done.6.other_ref = bf16[4,17,32,384]{3,2,1,0:T(8,128)(2,1)} collective-permute-done((bf16[4,17,32,384]{3,2,1,0:T(8,128)(2,1)}, bf16[4,17,32,384]{3,2,1,0:T(8,128)(2,1)}, u32[]{:S(2)}, u32[]{:S(2)}) %collective-permute-start.6) | collective-permute-done | bytes 1671200 | tf_op jit(solution)/shard_map/ppermute | solution.py:337
  311.3 7.6 %lat_inverse.3 = bf16[128,32,384]{2,1,0:T(8,128)(2,1)S(1)} custom-call(bf16[4,17,32,384]{3,2,1,0:T(8,128)(2,1)} %all_to_all.45.own_ref, bf16[4,17,32,384]{3,2,1,0:T(8,128)(2,1)} %collective-permute-done.6.other_ref, bf16[1024,1088]{1,0:T(8,128)(2,1)S(1)} %dynamic-slice_bitcast_fusion.table_ref, bf16[128,96,384]{2,1,0:T(8,128)(2,1)} %patches_ref.5), custom_call_target="tpu_custom_call" | custom-call | flops 3422552064 | bytes 9437184 | tf_op jit(solution)/shard_map/lat_inverse/pallas_call | solution.py:134
  319.0 1.7 copy-done
  320.6 4.7 all-to-all-start.7
  325.3 2.4 dynamic-slice_bitcast_fusion.6
  329.1 5.5 all-gather
  335.0 1.5 copy-done.13
  337.0 14.9 %channel_mlp.3 = bf16[4,2,16,32,384]{4,3,2,1,0:T(8,128)(2,1)} custom-call(s32[1]{0:T(128)} %bitcast.flag_ref, bf16[4,16,32,384]{3,2,1,0:T(8,128)(2,1)S(1)} %get-tuple-element.33.own_ref, bf16[4,16,32,384]{3,2,1,0:T(8,128)(2,1)S(1)} %collective-permute-done.7.other_ref, f32[1,768]{1,0:T(1,128)S(1)} %reshape.253.gain_ref, f32[1,768]{1,0:T(1,128)S(1)} %reshape.254.bias_ref, ...), custom_call_target="tpu_custom_call" | custom-call | flops 9663676416 | bytes 6291456 | tf_op jit(solution)/shard_map/channel_mlp/pallas_call | solution.py:304
  351.9 10.5 %all-to-all-done.7.own_ref = bf16[4,17,32,384]{3,2,1,0:T(8,128)(2,1)} async-done(((bf16[4,17,32,384]{3,2,1,0:T(8,128)(2,1)}), bf16[4,17,32,384]{3,2,1,0:T(8,128)(2,1)}, u32[]{:S(2)}, u32[]{:S(2)}) %all-to-all-start.7) | async-done | bytes 1671200 | tf_op jit(solution)/shard_map/all_to_all | solution.py:427
  362.4 4.5 all-to-all-start.4
  366.9 1.3 collective-permute-start.11
  368.2 37.7 %collective-permute-done.11.other_ref = bf16[4,17,32,384]{3,2,1,0:T(8,128)(2,1)S(1)} collective-permute-done((bf16[4,17,32,384]{3,2,1,0:T(8,128)(2,1)}, bf16[4,17,32,384]{3,2,1,0:T(8,128)(2,1)S(1)}, u32[]{:S(2)}, u32[]{:S(2)}) %collective-permute-start.11) | collective-permute-done | bytes 1671200 | tf_op jit(solution)/shard_map/ppermute | solution.py:337
  405.9 7.4 %lat_inverse.4 = bf16[128,32,384]{2,1,0:T(8,128)(2,1)S(1)} custom-call(bf16[4,17,32,384]{3,2,1,0:T(8,128)(2,1)} %all-to-all-done.5.own_ref, bf16[4,17,32,384]{3,2,1,0:T(8,128)(2,1)S(1)} %collective-permute-done.11.other_ref, bf16[1024,1088]{1,0:T(8,128)(2,1)S(1)} %dynamic-slice_bitcast_fusion.table_ref, bf16[128,96,384]{2,1,0:T(8,128)(2,1)} %patches_ref.5), custom_call_target="tpu_custom_call" | custom-call | flops 3422552064 | bytes 9437184 | tf_op jit(solution)/shard_map/lat_inverse/pallas_call | solution.py:134
  413.8 3.4 collective-permute-done.12.other_ref
  417.2 15.0 %channel_mlp.4 = bf16[4,2,16,32,384]{4,3,2,1,0:T(8,128)(2,1)} custom-call(s32[1]{0:T(128)} %bitcast.flag_ref, bf16[4,16,32,384]{3,2,1,0:T(8,128)(2,1)S(1)} %get-tuple-element.35.own_ref, bf16[4,16,32,384]{3,2,1,0:T(8,128)(2,1)S(1)} %collective-permute-done.12.other_ref, f32[1,768]{1,0:T(1,128)S(1)} %reshape.253.gain_ref, f32[1,768]{1,0:T(1,128)S(1)} %reshape.254.bias_ref, ...), custom_call_target="tpu_custom_call" | custom-call | flops 9663676416 | bytes 6291456 | tf_op jit(solution)/shard_map/channel_mlp/pallas_call | solution.py:304
  432.1 6.3 %all-to-all-done.4 = bf16[8,16,32,384]{3,2,1,0:T(8,128)(2,1)} async-done(((bf16[8,16,32,384]{3,2,1,0:T(8,128)(2,1)}), bf16[8,16,32,384]{3,2,1,0:T(8,128)(2,1)}, u32[]{:S(2)}, u32[]{:S(2)}) %all-to-all-start.4) | async-done | bytes 3145760 | tf_op jit(solution)/shard_map/all_to_all | solution.py:437
  438.5 4.7 all-to-all-start.6
  443.2 1.3 collective-permute-start.13
  444.5 37.8 %collective-permute-done.13.other_ref = bf16[4,17,32,384]{3,2,1,0:T(8,128)(2,1)S(1)} collective-permute-done((bf16[4,17,32,384]{3,2,1,0:T(8,128)(2,1)}, bf16[4,17,32,384]{3,2,1,0:T(8,128)(2,1)S(1)}, u32[]{:S(2)}, u32[]{:S(2)}) %collective-permute-start.13) | collective-permute-done | bytes 1671200 | tf_op jit(solution)/shard_map/ppermute | solution.py:337
  482.3 7.4 %lat_inverse.5 = bf16[128,32,384]{2,1,0:T(8,128)(2,1)S(1)} custom-call(bf16[4,17,32,384]{3,2,1,0:T(8,128)(2,1)} %all-to-all-done.7.own_ref, bf16[4,17,32,384]{3,2,1,0:T(8,128)(2,1)S(1)} %collective-permute-done.13.other_ref, bf16[1024,1088]{1,0:T(8,128)(2,1)S(1)} %dynamic-slice_bitcast_fusion.table_ref, bf16[128,96,384]{2,1,0:T(8,128)(2,1)} %patches_ref.5), custom_call_target="tpu_custom_call" | custom-call | flops 3422552064 | bytes 9437184 | tf_op jit(solution)/shard_map/lat_inverse/pallas_call | solution.py:134
  490.2 3.4 collective-permute-done.14.other_ref
  493.6 14.9 %channel_mlp.5 = bf16[4,2,16,32,384]{4,3,2,1,0:T(8,128)(2,1)} custom-call(s32[1]{0:T(128)} %bitcast.flag_ref, bf16[4,16,32,384]{3,2,1,0:T(8,128)(2,1)S(1)} %get-tuple-element.37.own_ref, bf16[4,16,32,384]{3,2,1,0:T(8,128)(2,1)S(1)} %collective-permute-done.14.other_ref, f32[1,768]{1,0:T(1,128)S(1)} %reshape.253.gain_ref, f32[1,768]{1,0:T(1,128)S(1)} %reshape.254.bias_ref, ...), custom_call_target="tpu_custom_call" | custom-call | flops 9663676416 | bytes 6291456 | tf_op jit(solution)/shard_map/channel_mlp/pallas_call | solution.py:304
  508.5 6.2 %all-to-all-done.6 = bf16[8,16,32,384]{3,2,1,0:T(8,128)(2,1)} async-done(((bf16[8,16,32,384]{3,2,1,0:T(8,128)(2,1)}), bf16[8,16,32,384]{3,2,1,0:T(8,128)(2,1)}, u32[]{:S(2)}, u32[]{:S(2)}) %all-to-all-start.6) | async-done | bytes 3145760 | tf_op jit(solution)/shard_map/all_to_all | solution.py:437
  514.7 75.1 %all_to_all.46 = bf16[8,16,32,384]{3,2,1,0:T(8,128)(2,1)S(1)} all-to-all(bf16[8,16,32,384]{3,2,1,0:T(8,128)(2,1)} %bitcast.126), channel_id=1, replica_groups=mesh['grp'=2,'lon'=4,'lat'=2,'ch'=2] {'lon','ch'}, dimensions={0} | all-to-all | bytes 6291456 | tf_op jit(solution)/shard_map/all_to_all | solution.py:437
  589.8 7.0 %pad_maximum_fusion = bf16[3,4,2,16,32,384]{5,4,3,2,1,0:T(8,128)(2,1)} fusion(bf16[1,4,2,16,32,384]{5,4,3,2,1,0:T(8,128)(2,1)S(1)} %bitcast.121, bf16[1,4,2,16,32,384]{5,4,3,2,1,0:T(8,128)(2,1)} %bitcast.30, bf16[1,4,2,16,32,384]{5,4,3,2,1,0:T(8,128)(2,1)} %bitcast.24), kind=kLoop, calls=%fused_computation.9 | loop fusion | flops 9437184 | bytes 18874368 | tf_op jit(solution)/shard_map/stack | solution.py:442
  596.8 9.3 %copy.74 = bf16[3,4,2,16,32,384]{5,4,0,1,3,2:T(8,128)(2,1)} copy(bf16[3,4,2,16,32,384]{5,4,3,2,1,0:T(8,128)(2,1)} %pad_maximum_fusion) | data formatting | bytes 18874368 | tf_op jit(solution)/shard_map/stack | solution.py:442
  (102 shorter events, 4.2 us)
Async XLA Ops:
  0.0 6.5 %copy-start.10 = (bf16[128,96,384]{2,1,0:T(8,128)(2,1)S(1)}, bf16[128,96,384]{2,1,0:T(8,128)(2,1)}, u32[]{:S(2)}) copy-start(bf16[128,96,384]{2,1,0:T(8,128)(2,1)} %patches_ref.5) | copy-start | bytes 28311556
  10.9 3.1 collective-permute-start
  11.5 2.6 collective-permute-start.2
  11.6 2.4 copy-start.21
  11.6 2.4 copy-start.22
  11.6 2.5 collective-permute-start.4
  14.0 7.9 %copy-start.2 = (bf16[1088,1024]{1,0:T(8,128)(2,1)}, bf16[1088,1024]{1,0:T(8,128)(2,1)S(1)}, u32[]{:S(2)}) copy-start(bf16[1088,1024]{1,0:T(8,128)(2,1)S(1)} %dynamic-slice_bitcast_fusion.1.table_ref) | copy-start | bytes 6684676
  26.4 39.7 %collective-permute-start.5 = (bf16[68,32,384]{2,1,0:T(8,128)(2,1)S(1)}, bf16[68,32,384]{2,1,0:T(8,128)(2,1)S(1)}, u32[]{:S(2)}, u32[]{:S(2)}) collective-permute-start(bf16[68,32,384]{2,1,0:T(8,128)(2,1)S(1)} %get-tuple-element.19), channel_id=1, source_target_pairs={{0,2},{2,0},{1,3},{3,1},{4,6},{6,4},{5,7},{7,5},{8,10},{10,8},{9,1... | collective-permute-start | bytes 5013512 | tf_op jit(solution)/shard_map/ppermute | solution.py:337
  67.8 52.7 %all-to-all-start.2 = ((bf16[4,17,32,384]{3,2,1,0:T(8,128)(2,1)}), bf16[4,17,32,384]{3,2,1,0:T(8,128)(2,1)}, u32[]{:S(2)}, u32[]{:S(2)}) async-start(bf16[4,17,32,384]{3,2,1,0:T(8,128)(2,1)} %bitcast.123), calls=%async_computation.2 | async-start | bytes 3342336 | tf_op jit(solution)/shard_map/all_to_all | solution.py:401
  72.9 1.9 copy-start.1
  74.8 1.6 copy-start.3
  80.9 37.9 %collective-permute-start.3 = (bf16[68,32,384]{2,1,0:T(8,128)(2,1)S(1)}, bf16[68,32,384]{2,1,0:T(8,128)(2,1)S(1)}, u32[]{:S(2)}, u32[]{:S(2)}) collective-permute-start(bf16[68,32,384]{2,1,0:T(8,128)(2,1)S(1)} %get-tuple-element.17), channel_id=1, source_target_pairs={{0,2},{2,0},{1,3},{3,1},{4,6},{6,4},{5,7},{7,5},{8,10},{10,8},{9,1... | collective-permute-start | bytes 5013512 | tf_op jit(solution)/shard_map/ppermute | solution.py:337
  120.4 49.1 %all-to-all-start.1 = ((bf16[4,17,32,384]{3,2,1,0:T(8,128)(2,1)}), bf16[4,17,32,384]{3,2,1,0:T(8,128)(2,1)}, u32[]{:S(2)}, u32[]{:S(2)}) async-start(bf16[4,17,32,384]{3,2,1,0:T(8,128)(2,1)} %bitcast.122), calls=%async_computation.1 | async-start | bytes 3342336 | tf_op jit(solution)/shard_map/all_to_all | solution.py:401
  125.3 1.6 copy-start.4
  131.4 36.6 %collective-permute-start.1 = (bf16[68,32,384]{2,1,0:T(8,128)(2,1)S(1)}, bf16[68,32,384]{2,1,0:T(8,128)(2,1)S(1)}, u32[]{:S(2)}, u32[]{:S(2)}) collective-permute-start(bf16[68,32,384]{2,1,0:T(8,128)(2,1)S(1)} %get-tuple-element.15), channel_id=1, source_target_pairs={{0,2},{2,0},{1,3},{3,1},{4,6},{6,4},{5,7},{7,5},{8,10},{10,8},{9,1... | collective-permute-start | bytes 5013512 | tf_op jit(solution)/shard_map/ppermute | solution.py:337
  169.6 5.1 copy-start.14
  169.6 5.1 copy-start.15
  169.6 41.4 %all-to-all-start = ((bf16[4,17,32,384]{3,2,1,0:T(8,128)(2,1)}), bf16[4,17,32,384]{3,2,1,0:T(8,128)(2,1)}, u32[]{:S(2)}, u32[]{:S(2)}) async-start(bf16[4,17,32,384]{3,2,1,0:T(8,128)(2,1)} %bitcast.7), calls=%async_computation | async-start | bytes 3342336 | tf_op jit(solution)/shard_map/all_to_all | solution.py:401
  176.1 3.4 copy-start.24
  176.1 3.6 copy-start.25
  176.2 3.7 copy-start.19
  176.2 3.8 copy-start.20
  178.6 32.4 %copy-start.8 = (bf16[256,384]{1,0:T(8,128)(2,1)S(1)}, bf16[256,384]{1,0:T(8,128)(2,1)}, u32[]{:S(2)}) copy-start(bf16[256,384]{1,0:T(8,128)(2,1)} %constant.71.clone.refs_6_) | copy-start | bytes 589828
  178.6 32.5 %copy-start.9 = (bf16[384,256]{1,0:T(8,128)(2,1)S(1)}, bf16[384,256]{1,0:T(8,128)(2,1)}, u32[]{:S(2)}) copy-start(bf16[384,256]{1,0:T(8,128)(2,1)} %constant.72.clone.refs_7_) | copy-start | bytes 589828
  269.3 51.3 %all-to-all-start.5 = ((bf16[4,17,32,384]{3,2,1,0:T(8,128)(2,1)}), bf16[4,17,32,384]{3,2,1,0:T(8,128)(2,1)}, u32[]{:S(2)}, u32[]{:S(2)}) async-start(bf16[4,17,32,384]{3,2,1,0:T(8,128)(2,1)} %get-tuple-element.21), calls=%async_computation.5 | async-start | bytes 3342336 | tf_op jit(solution)/shard_map/all_to_all | solution.py:427
  273.7 37.6 %collective-permute-start.6 = (bf16[4,17,32,384]{3,2,1,0:T(8,128)(2,1)}, bf16[4,17,32,384]{3,2,1,0:T(8,128)(2,1)}, u32[]{:S(2)}, u32[]{:S(2)}) collective-permute-start(bf16[4,17,32,384]{3,2,1,0:T(8,128)(2,1)} %all_to_all.45.own_ref), channel_id=1, source_target_pairs={{0,2},{2,0},{1,3},{3,1},{4,6},{6,4},{5,7},{7,5},{8,10},{10,8},{9,1... | collective-permute-start | bytes 5013512 | tf_op jit(solution)/shard_map/ppermute | solution.py:337
  318.9 1.7 copy-start
  320.6 41.8 %all-to-all-start.7 = ((bf16[4,17,32,384]{3,2,1,0:T(8,128)(2,1)}), bf16[4,17,32,384]{3,2,1,0:T(8,128)(2,1)}, u32[]{:S(2)}, u32[]{:S(2)}) async-start(bf16[4,17,32,384]{3,2,1,0:T(8,128)(2,1)} %get-tuple-element.22), calls=%async_computation.7 | async-start | bytes 3342336 | tf_op jit(solution)/shard_map/all_to_all | solution.py:427
  325.3 2.5 copy-start.11
  325.3 3.0 copy-start.12
  325.3 3.1 copy-start.18
  327.7 1.3 copy-start.23
  327.7 6.9 %copy-start.16 = (bf16[768]{0:T(1024)(128)(2,1)S(1)}, bf16[768]{0:T(1024)(128)(2,1)}, u32[]{:S(2)}) copy-start(bf16[768]{0:T(1024)(128)(2,1)} %param.28) | copy-start | bytes 4612
  327.8 6.9 %copy-start.17 = (bf16[768]{0:T(1024)(128)(2,1)S(1)}, bf16[768]{0:T(1024)(128)(2,1)}, u32[]{:S(2)}) copy-start(bf16[768]{0:T(1024)(128)(2,1)} %param.29) | copy-start | bytes 4612
  327.8 7.2 %collective-permute-start.7 = (bf16[4,16,32,384]{3,2,1,0:T(8,128)(2,1)S(1)}, bf16[4,16,32,384]{3,2,1,0:T(8,128)(2,1)S(1)}, u32[]{:S(2)}, u32[]{:S(2)}) collective-permute-start(bf16[4,16,32,384]{3,2,1,0:T(8,128)(2,1)S(1)} %get-tuple-element.32), channel_id=1, source_target_pairs={{0,1},{1,0},{2,3},{3,2},{4,5},{5,4},{6,7},{7,6},{8,9},{9,8},{10,11... | collective-permute-start | bytes 4718600 | tf_op jit(solution)/shard_map/ppermute | solution.py:337
  327.9 6.9 %collective-permute-start.8 = (bf16[768,768]{1,0:T(8,128)(2,1)S(1)}, bf16[768,768]{1,0:T(8,128)(2,1)S(1)}, u32[]{:S(2)}, u32[]{:S(2)}) collective-permute-start(bf16[768,768]{1,0:T(8,128)(2,1)S(1)} %copy-done.11), channel_id=1, source_target_pairs={{0,1},{1,0},{2,3},{3,2},{4,5},{5,4},{6,7},{7,6},{8,9},{9,8},{10,11... | collective-permute-start | bytes 3538952 | tf_op jit(solution)/shard_map/ppermute | solution.py:337
  328.3 6.5 %collective-permute-start.10 = (bf16[768,768]{1,0:T(8,128)(2,1)S(1)}, bf16[768,768]{1,0:T(8,128)(2,1)S(1)}, u32[]{:S(2)}, u32[]{:S(2)}) collective-permute-start(bf16[768,768]{1,0:T(8,128)(2,1)S(1)} %copy-done.12), channel_id=1, source_target_pairs={{0,1},{1,0},{2,3},{3,2},{4,5},{5,4},{6,7},{7,6},{8,9},{9,8},{10,11... | collective-permute-start | bytes 3538952 | tf_op jit(solution)/shard_map/ppermute | solution.py:337
  328.4 6.2 %collective-permute-start.9 = (bf16[768]{0:T(1024)(128)(2,1)S(1)}, bf16[768]{0:T(1024)(128)(2,1)S(1)}, u32[]{:S(2)}, u32[]{:S(2)}) collective-permute-start(bf16[768]{0:T(1024)(128)(2,1)S(1)} %copy-done.18), channel_id=1, source_target_pairs={{0,1},{1,0},{2,3},{3,2},{4,5},{5,4},{6,7},{7,6},{8,9},{9,8},{10,11... | collective-permute-start | bytes 4616 | tf_op jit(solution)/shard_map/ppermute | solution.py:337
  334.8 2.1 copy-start.5
  334.9 1.6 copy-start.13
  362.4 76.0 %all-to-all-start.4 = ((bf16[8,16,32,384]{3,2,1,0:T(8,128)(2,1)}), bf16[8,16,32,384]{3,2,1,0:T(8,128)(2,1)}, u32[]{:S(2)}, u32[]{:S(2)}) async-start(bf16[8,16,32,384]{3,2,1,0:T(8,128)(2,1)} %bitcast.125), calls=%async_computation.4 | async-start | bytes 6291456 | tf_op jit(solution)/shard_map/all_to_all | solution.py:437
  366.9 39.0 %collective-permute-start.11 = (bf16[4,17,32,384]{3,2,1,0:T(8,128)(2,1)}, bf16[4,17,32,384]{3,2,1,0:T(8,128)(2,1)S(1)}, u32[]{:S(2)}, u32[]{:S(2)}) collective-permute-start(bf16[4,17,32,384]{3,2,1,0:T(8,128)(2,1)} %all-to-all-done.5.own_ref), channel_id=1, source_target_pairs={{0,2},{2,0},{1,3},{3,1},{4,6},{6,4},{5,7},{7,5},{8,10},{10,8},{9,1... | collective-permute-start | bytes 5013512 | tf_op jit(solution)/shard_map/ppermute | solution.py:337
  413.3 3.9 copy-start.6
  413.7 3.5 collective-permute-start.12
  438.5 76.3 %all-to-all-start.6 = ((bf16[8,16,32,384]{3,2,1,0:T(8,128)(2,1)}), bf16[8,16,32,384]{3,2,1,0:T(8,128)(2,1)}, u32[]{:S(2)}, u32[]{:S(2)}) async-start(bf16[8,16,32,384]{3,2,1,0:T(8,128)(2,1)} %bitcast.124), calls=%async_computation.6 | async-start | bytes 6291456 | tf_op jit(solution)/shard_map/all_to_all | solution.py:437
  443.2 39.1 %collective-permute-start.13 = (bf16[4,17,32,384]{3,2,1,0:T(8,128)(2,1)}, bf16[4,17,32,384]{3,2,1,0:T(8,128)(2,1)S(1)}, u32[]{:S(2)}, u32[]{:S(2)}) collective-permute-start(bf16[4,17,32,384]{3,2,1,0:T(8,128)(2,1)} %all-to-all-done.7.own_ref), channel_id=1, source_target_pairs={{0,2},{2,0},{1,3},{3,1},{4,6},{6,4},{5,7},{7,5},{8,10},{10,8},{9,1... | collective-permute-start | bytes 5013512 | tf_op jit(solution)/shard_map/ppermute | solution.py:337
  489.7 3.9 copy-start.7
  490.1 3.5 collective-permute-start.14

commit v2 on v1

--- a/solution.py
+++ b/solution.py
@@ -17,6 +17,9 @@
 
 shrink_level = 0.01
 norm_epsilon = 1e-05
+
+COST_SHARE = 1
+LATE_SHARE = 8
 
 BF = jnp.bfloat16
 F32 = jnp.float32
@@ -63,110 +66,132 @@
     return np.kron(table, np.eye(8, dtype=np.float32)).astype(jnp.bfloat16)
 
 
-def lat_forward_kernel(cells_ref, table_ref, send_ref, keep_ref):
-    rows = cells_ref.shape[0]
-    values = cells_ref[...].astype(F32).reshape(rows, 2, 8, cells_ref.shape[2])
-    width = cells_ref.shape[2]
+def lat_forward_kernel(where_ref, cells_ref, table_ref, send_ref, keep_ref):
+    rows, _, width = cells_ref.shape
+    lon_count, slots, _, _ = send_ref.shape
+    values = cells_ref[...].astype(F32).reshape(rows, 2, 8, width)
     pair = jnp.concatenate(
         [values[:, 0].reshape(rows * 8, width), values[:, 1].reshape(rows * 8, width)], axis=1
     ).astype(BF)
-    half = table_ref.shape[0] // 2
+    half = table_ref.shape[1] // 2
     for part, out_ref in ((0, send_ref), (1, keep_ref)):
         total = jnp.dot(
-            table_ref[part * half : (part + 1) * half, :], pair, preferred_element_type=F32
+            table_ref[0, part * half : (part + 1) * half, :], pair, preferred_element_type=F32
         )
-        slots = half // 8
-        out_ref[...] = jnp.concatenate(
+        total = jnp.concatenate(
             [
-                total[:, :width].reshape(slots, 8, width),
-                total[:, width:].reshape(slots, 8, width),
+                total[:, :width].reshape(lon_count, slots, 8, width),
+                total[:, width:].reshape(lon_count, slots, 8, width),
             ],
-            axis=1,
+            axis=2,
         ).astype(BF)
-
-
-def lat_forward(cells, table):
+        for z in range(lon_count):
+            out_ref[lax.rem(z + lon_count - where_ref[0], lon_count)] = total[z]
+
+
+def lat_forward(where, cells, table, lon_count):
     rows, cols, width = cells.shape
-    slots = table.shape[0] // 16
-    block = pl.BlockSpec((slots, 16, width), lambda i: (0, i, 0))
+    slots = table.shape[1] // (16 * lon_count)
+    block = pl.BlockSpec((lon_count, slots, 16, width), lambda i, where: (0, 0, i, 0))
     return pl.pallas_call(
         lat_forward_kernel,
-        grid=(cols // 16,),
-        in_specs=[
-            pl.BlockSpec((rows, 16, width), lambda i: (0, i, 0)),
-            pl.BlockSpec(table.shape, lambda i: (0, 0)),
-        ],
-        out_specs=[block, block],
-        out_shape=[jax.ShapeDtypeStruct((slots, cols, width), BF)] * 2,
+        grid_spec=pltpu.PrefetchScalarGridSpec(
+            num_scalar_prefetch=1,
+            grid=(cols // 16,),
+            in_specs=[
+                pl.BlockSpec((rows, 16, width), lambda i, where: (0, i, 0)),
+                pl.BlockSpec((1,) + table.shape[1:], lambda i, where: (where[2], 0, 0)),
+            ],
+            out_specs=[block, block],
+        ),
+        out_shape=[jax.ShapeDtypeStruct((lon_count, slots, cols, width), BF)] * 2,
         compiler_params=pltpu.CompilerParams(vmem_limit_bytes=40 << 20),
         cost_estimate=pl.CostEstimate(
-            flops=2 * table.size * cols // 8 * width,
-            bytes_accessed=4 * rows * cols * width,
+            flops=2 * table[0].size * cols // 8 * width // COST_SHARE,
+            bytes_accessed=4 * rows * cols * width // COST_SHARE,
             transcendentals=0,
         ),
         name="lat_forward",
-    )(cells, table)
-
-
-def lat_inverse_kernel(own_ref, other_ref, table_ref, patches_ref, out_ref):
+    )(where, cells, table)
+
+
+def lat_inverse_kernel(
+    where_ref, own_ref, other_ref, table_ref, patches_ref, mine_ref, sent_ref, flat_ref
+):
     rows, _, width = patches_ref.shape
-    slots = own_ref.shape[0] * own_ref.shape[1]
-
-    def flat(ref):
-        values = ref[...].astype(F32).reshape(slots, 2, 8, width)
-        return jnp.concatenate(
-            [values[:, 0].reshape(slots * 8, width), values[:, 1].reshape(slots * 8, width)], axis=1
-        ).astype(BF)
-
-    half = table_ref.shape[1] // 2
-    total = jnp.dot(table_ref[:, :half], flat(own_ref), preferred_element_type=F32)
-    total += jnp.dot(table_ref[:, half:], flat(other_ref), preferred_element_type=F32)
+    lon_count, slots = own_ref.shape[:2]
+    blank = jnp.zeros((flat_ref.shape[1] - slots * 8, 2 * width), BF)
+    for side, ref in enumerate((own_ref, other_ref)):
+        for s in range(lon_count):
+            values = ref[s].astype(F32).reshape(slots, 2, 8, width)
+            flat = jnp.concatenate(
+                [values[:, 0].reshape(slots * 8, width), values[:, 1].reshape(slots * 8, width)],
+                axis=1,
+            )
+            source = lax.rem(where_ref[0] + (lon_count - s), lon_count)
+            flat_ref[side * lon_count + source] = jnp.concatenate([flat.astype(BF), blank], axis=0)
+    total = jnp.dot(
+        table_ref[0], flat_ref[...].reshape(-1, 2 * width), preferred_element_type=F32
+    )
     fine = jnp.concatenate(
         [total[:, :width].reshape(rows, 8, width), total[:, width:].reshape(rows, 8, width)], axis=1
     )
-    out_ref[...] = (patches_ref[...].astype(F32) + fine).astype(BF)
-
-
-def lat_inverse(own, other, table, patches, first_block):
-    groups, slots, cols, width = own.shape
+    mixed = (patches_ref[...].astype(F32) + fine).astype(BF)
+    mixed = mixed.reshape(lon_count, 2, rows // (2 * lon_count), 16, width)
+
+    @pl.when(where_ref[1] == 0)
+    def _():
+        mine_ref[...] = mixed[:, 0]
+        sent_ref[...] = mixed[:, 1]
+
+    @pl.when(where_ref[1] != 0)
+    def _():
+        mine_ref[...] = mixed[:, 1]
+        sent_ref[...] = mixed[:, 0]
+
+
+def lat_inverse(where, own, other, table, patches, first_col):
+    lon_count, slots, cols, width = own.shape
     rows = patches.shape[0]
-    spec = pl.BlockSpec((groups, slots, 16, width), lambda i: (0, 0, i, 0))
+    first_block = first_col // 16
+    spec = pl.BlockSpec((lon_count, slots, 16, width), lambda i, where: (0, 0, i, 0))
+    half = rows // (2 * lon_count)
+    out_spec = pl.BlockSpec((lon_count, half, 16, width), lambda i, where: (0, 0, i, 0))
     return pl.pallas_call(
         lat_inverse_kernel,
-        grid=(cols // 16,),
-        in_specs=[
-            spec,
-            spec,
-            pl.BlockSpec(table.shape, lambda i: (0, 0)),
-            pl.BlockSpec((rows, 16, width), lambda i: (0, first_block + i, 0)),
-        ],
-        out_specs=pl.BlockSpec((rows, 16, width), lambda i: (0, i, 0)),
-        out_shape=jax.ShapeDtypeStruct((rows, cols, width), BF),
+        grid_spec=pltpu.PrefetchScalarGridSpec(
+            num_scalar_prefetch=1,
+            grid=(cols // 16,),
+            in_specs=[
+                spec,
+                spec,
+                pl.BlockSpec((1,) + table.shape[1:], lambda i, where: (where[2], 0, 0)),
+                pl.BlockSpec((rows, 16, width), lambda i, where: (0, first_block + i, 0)),
+            ],
+            out_specs=[out_spec, out_spec],
+            scratch_shapes=[
+                pltpu.VMEM((2 * lon_count, table.shape[2] // (2 * lon_count), 2 * width), BF)
+            ],
+        ),
+        out_shape=[jax.ShapeDtypeStruct((lon_count, half, cols, width), BF)] * 2,
         compiler_params=pltpu.CompilerParams(vmem_limit_bytes=40 << 20),
         cost_estimate=pl.CostEstimate(
-            flops=2 * table.size * cols // 8 * width,
-            bytes_accessed=6 * rows * cols * width,
+            flops=2 * table[0].size * cols // 8 * width // LATE_SHARE,
+            bytes_accessed=6 * rows * cols * width // LATE_SHARE,
             transcendentals=0,
         ),
         name="lat_inverse",
-    )(own, other, table, patches)
-
-
-def modes_kernel(
-    chunks,
-    first_pair_ref,
-    lat_lo_ref,
-    lon_lo_ref,
-    *refs,
-):
-    pair_refs = refs[:chunks]
-    spare_refs = refs[chunks : 2 * chunks]
+    )(where, own, other, table, patches)
+
+
+def modes_kernel(inputs, first_pair_ref, lat_keep_ref, lon_keep_ref, *refs):
+    pair_refs = refs[:inputs]
+    spare_refs = refs[inputs : 2 * inputs]
     forward_ref, inverse_ref, w_in_ref, b_in_ref, w_out_ref, b_out_ref = refs[
-        2 * chunks : 2 * chunks + 6
+        2 * inputs : 2 * inputs + 6
     ]
-    out_refs = refs[2 * chunks + 6 :]
+    out_refs = refs[2 * inputs + 6 :]
     width = pair_refs[0].shape[-1]
-    groups, _, cols, _ = pair_refs[0].shape
     step = pl.program_id(0)
     pairs = pl.num_programs(0)
     pair_id = first_pair_ref[0] + step
@@ -174,9 +199,7 @@
     keep = KEEP_LON
 
     def columns(refs, row):
-        return jnp.concatenate(
-            [ref[:, row].reshape(groups * cols, width) for ref in refs], axis=0
-        )
+        return jnp.concatenate([ref[row] for ref in refs], axis=0)
 
     both = jnp.concatenate([columns(pair_refs, 0), columns(pair_refs, 1)], axis=1)
     spectrum = jnp.dot(forward_ref[...], both, preferred_element_type=F32)
@@ -196,22 +219,22 @@
         second = jnp.dot(first, w_out_ref[...], preferred_element_type=F32) + b_out_ref[...]
         shrunk = second - jnp.clip(second, -shrink_level, shrink_level)
         freq = lax.broadcasted_iota(jnp.int32, (keep, 2 * width), 0)
-        lon_ok = freq < lon_lo_ref[...]
-        plus_ok = lon_ok & (pair_id < lat_lo_ref[...])
+        lon_ok = freq < lon_keep_ref[...]
+        plus_ok = lon_ok & (pair_id < lat_keep_ref[...])
         minus_id = jnp.where(special, MLAT, pair_id)
-        minus_ok = lon_ok & (minus_id <= lat_lo_ref[...])
+        minus_ok = lon_ok & (minus_id <= lat_keep_ref[...])
         plus = jnp.where(plus_ok, shrunk[:keep], 0.0)
         minus = jnp.where(minus_ok, shrunk[keep:], 0.0)
         return plus[:, :width], plus[:, width:], minus[:, :width], minus[:, width:]
 
-    def back(values, refs, row):
+    def back(values, row):
         grid_values = jnp.dot(inverse_ref[...], values, preferred_element_type=F32).astype(BF)
-        for i, ref in enumerate(refs):
-            piece = grid_values[i * groups * cols : (i + 1) * groups * cols]
-            for r in range(piece.shape[1] // width):
-                ref[:, pl.ds(row + r, 1)] = piece[:, r * width : (r + 1) * width].reshape(
-                    groups, 1, cols, width
-                )
+        start = 0
+        for ref in out_refs:
+            cols = ref.shape[1]
+            for r in range(grid_values.shape[1] // width):
+                ref[row + r] = grid_values[start : start + cols, r * width : (r + 1) * width]
+            start += cols
 
     @pl.when(special)
     def _():
@@ -221,8 +244,8 @@
         values = jnp.concatenate(
             [jnp.concatenate([p_re, m_re], axis=1), jnp.concatenate([p_im, m_im], axis=1)], axis=0
         ).astype(BF)
-        back(values, out_refs, 2 * step)
-        back(jnp.concatenate([-m_im, m_re], axis=0).astype(BF), out_refs, 2 * pairs)
+        back(values, 2 * step)
+        back(jnp.concatenate([-m_im, m_re], axis=0).astype(BF), 2 * pairs)
 
     @pl.when(jnp.logical_not(special))
     def _():
@@ -234,52 +257,54 @@
             ],
             axis=0,
         ).astype(BF)
-        back(values, out_refs, 2 * step)
+        back(values, 2 * step)
 
     @pl.when(jnp.logical_and(step == 0, jnp.logical_not(special)))
     def _():
         for ref in out_refs:
-            ref[:, pl.ds(2 * pairs, 1)] = jnp.zeros((groups, 1, cols, width), BF)
+            ref[2 * pairs] = jnp.zeros(ref.shape[1:], BF)
 
 
 def modes(received, first_pair, lat_keep, lon_keep, forward, inverse, w_in, b_in, w_out, b_out):
-    chunks = len(received)
-    groups, slots, cols, width = received[0].shape
+    lon_count = len(received[0])
+    flat = [values for chunk in received for values in chunk]
+    slots, _, width = flat[0].shape
     pairs = slots // 2
-    pair_spec = pl.BlockSpec((groups, 2, cols, width), lambda i: (0, i, 0, 0))
-    spare_spec = pl.BlockSpec((groups, 1, cols, width), lambda i: (0, slots - 1, 0, 0))
+    pair_specs = [pl.BlockSpec((2, r.shape[1], width), lambda i: (i, 0, 0)) for r in flat]
+    spare_specs = [pl.BlockSpec((1, r.shape[1], width), lambda i: (slots - 1, 0, 0)) for r in flat]
     whole = lambda array: pl.BlockSpec(array.shape, lambda i: (0,) * array.ndim)
-    return pl.pallas_call(
-        functools.partial(modes_kernel, chunks),
+    out = pl.pallas_call(
+        functools.partial(modes_kernel, len(flat)),
         grid=(pairs,),
         in_specs=[pl.BlockSpec(memory_space=pltpu.SMEM), whole(lat_keep), whole(lon_keep)]
-        + [pair_spec] * chunks
-        + [spare_spec] * chunks
+        + pair_specs
+        + spare_specs
         + [whole(forward), whole(inverse), whole(w_in), whole(b_in), whole(w_out), whole(b_out)],
-        out_specs=[pl.BlockSpec((groups, slots, cols, width), lambda i: (0, 0, 0, 0))] * chunks,
-        out_shape=[jax.ShapeDtypeStruct((groups, slots, cols, width), BF)] * chunks,
+        out_specs=[pl.BlockSpec(r.shape, lambda i: (0, 0, 0)) for r in flat],
+        out_shape=[jax.ShapeDtypeStruct(r.shape, BF) for r in flat],
         compiler_params=pltpu.CompilerParams(vmem_limit_bytes=48 << 20),
         cost_estimate=pl.CostEstimate(
-            flops=pairs * 2 * (2 * 2 * KEEP_LON * W * 2 * width + 4 * KEEP_LON * 4 * width * width),
-            bytes_accessed=4 * chunks * groups * slots * cols * width,
+            flops=pairs * 2 * (2 * 2 * KEEP_LON * W * 2 * width + 4 * KEEP_LON * 4 * width * width) // COST_SHARE,
+            bytes_accessed=4 * slots * W * width // COST_SHARE,
             transcendentals=0,
         ),
         name="modes",
     )(
-        first_pair, lat_keep, lon_keep, *received, *received,
+        first_pair, lat_keep, lon_keep, *flat, *flat,
         forward, inverse, w_in, b_in, w_out, b_out,
     )
+    return [list(out[i : i + lon_count]) for i in range(0, len(flat), lon_count)]
 
 
 def mlp_kernel(
-    flag_ref, own_ref, other_ref, gain_ref, bias_ref, w_in_ref, b_in_ref, w_out_ref, b_out_ref,
-    out_ref,
+    where_ref, own_ref, other_ref, gain_ref, bias_ref, w_in_ref, b_in_ref, w_out_ref, b_out_ref,
+    *out_refs,
 ):
-    width = own_ref.shape[-1]
-    cells = own_ref.shape[1] * own_ref.shape[2]
+    _, rows, cols, width = own_ref.shape
+    cells = rows * cols
     own = own_ref[0].reshape(cells, width)
     other = other_ref[0].reshape(cells, width)
-    flip = flag_ref[0] == 1
+    flip = where_ref[1] == 1
     low = jnp.where(flip, other, own)
     high = jnp.where(flip, own, other)
     wide = jnp.concatenate([low, high], axis=1).astype(F32)
@@ -291,31 +316,101 @@
     hidden = (hidden * (0.5 + 0.5 * lax.erf(hidden * math.sqrt(0.5)))).astype(BF)
     total = jnp.dot(hidden, w_out_ref[...], preferred_element_type=F32) + wide + b_out_ref[...]
     total = total.astype(BF)
-    rows, cols = own_ref.shape[1], own_ref.shape[2]
-    out_ref[0, 0] = total[:, :width].reshape(rows, cols, width)
-    out_ref[0, 1] = total[:, width:].reshape(rows, cols, width)
-
-
-def mlp(flag, own, other, gain, bias, w_in, b_in, w_out, b_out):
-    groups, rows, cols, width = own.shape
-    whole = lambda array: pl.BlockSpec(array.shape, lambda i: (0,) * array.ndim)
-    cell_spec = pl.BlockSpec((1, rows, cols, width), lambda i: (i, 0, 0, 0))
-    cells = groups * rows * cols
+    low, high = total[:, :width], total[:, width:]
+    mine = jnp.where(flip, high, low).reshape(rows, cols, width)
+    sent = jnp.where(flip, low, high).reshape(rows, cols, width)
+    for s, ref in enumerate(out_refs):
+
+        @pl.when(pl.program_id(0) == s)
+        def _():
+            ref[0] = mine
+            ref[1] = sent
+
+
+def mlp(where, own, other, gain, bias, w_in, b_in, w_out, b_out):
+    lon_count, rows, cols, width = own.shape
+    whole = lambda array: pl.BlockSpec(array.shape, lambda i, where: (0,) * array.ndim)
+    cell_spec = pl.BlockSpec(
+        (1, rows, cols, width), lambda i, where: (lax.rem(where[0] + i, lon_count), 0, 0, 0)
+    )
+    cells = lon_count * rows * cols
     return pl.pallas_call(
         mlp_kernel,
-        grid=(groups,),
-        in_specs=[pl.BlockSpec(memory_space=pltpu.SMEM), cell_spec, cell_spec]
-        + [whole(a) for a in (gain, bias, w_in, b_in, w_out, b_out)],
-        out_specs=pl.BlockSpec((1, 2, rows, cols, width), lambda i: (i, 0, 0, 0, 0)),
-        out_shape=jax.ShapeDtypeStruct((groups, 2, rows, cols, width), BF),
+        grid_spec=pltpu.PrefetchScalarGridSpec(
+            num_scalar_prefetch=1,
+            grid=(lon_count,),
+            in_specs=[cell_spec, cell_spec]
+            + [whole(a) for a in (gain, bias, w_in, b_in, w_out, b_out)],
+            out_specs=[pl.BlockSpec((2, rows, cols, width), lambda i, where: (0, 0, 0, 0))]
+            * lon_count,
+        ),
+        out_shape=[jax.ShapeDtypeStruct((2, rows, cols, width), BF)] * lon_count,
         compiler_params=pltpu.CompilerParams(vmem_limit_bytes=48 << 20),
         cost_estimate=pl.CostEstimate(
-            flops=4 * cells * w_in.size,
-            bytes_accessed=8 * cells * width,
-            transcendentals=cells * w_in.shape[1],
+            flops=4 * cells * w_in.size // LATE_SHARE,
+            bytes_accessed=8 * cells * width // LATE_SHARE,
+            transcendentals=cells * w_in.shape[1] // LATE_SHARE,
         ),
         name="channel_mlp",
-    )(flag, own, other, gain, bias, w_in, b_in, w_out, b_out)
+    )(where, own, other, gain, bias, w_in, b_in, w_out, b_out)
+
+
+def assemble_kernel(where_ref, their_ref, *refs):
+    my_refs, out_ref = refs[:-1], refs[-1]
+    half = their_ref.shape[1]
+    flip = where_ref[1] == 1
+    for s, ref in enumerate(my_refs):
+
+        @pl.when(pl.program_id(0) == s)
+        def _():
+            mine, theirs = ref[0], their_ref[0]
+            out_ref[:half] = jnp.where(flip, theirs, mine)
+            out_ref[half:] = jnp.where(flip, mine, theirs)
+
+
+def assemble(where, result, mine, theirs, first_col, block_cols):
+    lon_count, rows, cols, width = theirs.shape
+    block = math.gcd(math.gcd(cols, block_cols), first_col)
+    steps = cols // block
+
+    def piece(s):
+        def index(g, j, where):
+            return 0, 0, jnp.where(g == s, j, jnp.where(g < s, 0, steps - 1)), 0
+
+        return pl.BlockSpec((1, rows, block, width), index)
+
+    def place(g, j, where):
+        source = lax.rem(where[0] + (lon_count - g), lon_count)
+        return 0, source * (block_cols // block) + first_col // block + j, 0
+
+    specs = [pl.BlockSpec((1, rows, block, width), lambda g, j, where: (g, 0, j, 0))]
+    specs += [piece(s) for s in range(lon_count)]
+    operands = [where, theirs, *mine]
+    aliases = {}
+    kernel = assemble_kernel
+    if result is not None:
+        aliases = {len(operands): 0}
+        operands.append(result)
+        specs.append(pl.BlockSpec(memory_space=pl.ANY))
+
+        def kernel(where_ref, *refs):
+            assemble_kernel(where_ref, *refs[:-2], refs[-1])
+
+    return pl.pallas_call(
+        kernel,
+        grid_spec=pltpu.PrefetchScalarGridSpec(
+            num_scalar_prefetch=1,
+            grid=(lon_count, steps),
+            in_specs=specs,
+            out_specs=pl.BlockSpec((2 * rows, block, width), place),
+        ),
+        out_shape=jax.ShapeDtypeStruct((2 * rows, lon_count * block_cols, width), BF),
+        input_output_aliases=aliases,
+        cost_estimate=pl.CostEstimate(
+            flops=0, bytes_accessed=8 * lon_count * rows * cols * width, transcendentals=0
+        ),
+        name="assemble",
+    )(*operands)
 
 
 def block_diagonal(weight):
@@ -337,8 +432,14 @@
     return lax.ppermute(values, axis, [(0, 1), (1, 0)])
 
 
+def shift(values, steps, lon_count):
+    if steps == 0:
+        return values
+    return lax.ppermute(values, "lon", [(z, (z + steps) % lon_count) for z in range(lon_count)])
+
+
 def column_plan(
-    chunk_cols,
+    widths,
     patches,
     filter_norm_gain,
     filter_norm_bias,
@@ -358,8 +459,8 @@
     lon_count = lax.axis_size("lon")
     lat_count = lax.axis_size("lat")
     rows, cols, width = patches.shape
-    chunks = cols // chunk_cols
-    band_rows = rows // lon_count
+    chunks = len(widths)
+    starts = [sum(widths[:i]) for i in range(chunks)]
     block_width = filter_in.shape[2]
     lat_id = lax.axis_index("lat")
     lon_id = lax.axis_index("lon")
@@ -367,22 +468,31 @@
     pairs = MLAT // (lat_count * lon_count)
     slots = 2 * pairs + 1
 
-    lat_table = lat_tables(lat_count, lon_count).reshape(lat_count, lon_count * slots, H)
+    lat_table = lat_tables(lat_count, lon_count).reshape(lat_count, lon_count, slots, H)
     forward_all, inverse_all = [], []
     for a in range(lat_count):
-        here = lat_table[:, :, a * rows : (a + 1) * rows]
-        ordered = np.concatenate([here[1 - a], here[a]], axis=0)
+        here = lat_table[..., a * rows : (a + 1) * rows]
+        ordered = np.concatenate([here[1 - a], here[a]], axis=0).reshape(-1, rows)
         forward_all.append(spread8(ordered))
         ordered = np.concatenate([here[a], here[1 - a]], axis=0)
+        ordered = np.pad(ordered, ((0, 0), (0, slots % 2), (0, 0))).reshape(-1, rows)
         inverse_all.append(spread8(ordered.T))
-    forward_lat = lax.dynamic_index_in_dim(jnp.asarray(np.stack(forward_all)), lat_id, 0, False)
-    inverse_lat = lax.dynamic_index_in_dim(jnp.asarray(np.stack(inverse_all)), lat_id, 0, False)
-    order = np.arange(W).reshape(lon_count, chunks, chunk_cols).transpose(1, 0, 2).reshape(-1)
-    forward_lon, inverse_lon = (jnp.asarray(t) for t in lon_tables(order))
-
-    received = []
-    for i in range(chunks):
-        raw = patches[:, i * chunk_cols : (i + 1) * chunk_cols].astype(F32)
+    forward_lat, inverse_lat = jnp.asarray(np.stack(forward_all)), jnp.asarray(np.stack(inverse_all))
+
+    ids = np.arange(W).reshape(lon_count, cols)
+
+    def column_order(devices):
+        return np.concatenate([ids[devices, c : c + w].reshape(-1) for c, w in zip(starts, widths)])
+
+    steps = np.arange(lon_count)
+    from_here = [lon_tables(column_order((z - steps) % lon_count))[0] for z in range(lon_count)]
+    to_there = [lon_tables(column_order((z + steps) % lon_count))[1] for z in range(lon_count)]
+
+    fence = lax.optimization_barrier
+    where = jnp.stack([lon_id, ch_id, lat_id]).astype(jnp.int32)
+
+    def row_transform(i, source):
+        raw = source[:, starts[i] : starts[i] + widths[i]].astype(F32)
         center = jnp.mean(raw, axis=-1)
         off = raw - center[..., None]
         square = jnp.sum(off * off, axis=-1)
@@ -395,52 +505,101 @@
             (raw - mean[..., None]) * scale[..., None] * filter_norm_gain.astype(F32)
             + filter_norm_bias.astype(F32)
         ).astype(BF)
-        send, keep = lat_forward(prenormed, forward_lat)
-        total = (keep.astype(F32) + swap(send, "lat").astype(F32)).astype(BF)
-        received.append(
-            lax.all_to_all(
-                total.reshape(lon_count, slots, chunk_cols, width), "lon", 0, 0, tiled=True
-            )
+        return lat_forward(where, prenormed, forward_lat, lon_count)
+
+    def mlp_weights(dense_in, dense_in_bias, dense_out, dense_out_bias):
+        return (
+            norm_gain.astype(F32)[None],
+            norm_bias.astype(F32)[None],
+            jnp.concatenate([dense_in, swap(dense_in, "ch")], axis=1),
+            jnp.concatenate([dense_in_bias, swap(dense_in_bias, "ch")]).astype(F32)[None],
+            jnp.concatenate([dense_out, swap(dense_out, "ch")], axis=0),
+            lax.all_gather(dense_out_bias, "ch", axis=0, tiled=True).astype(F32)[None],
         )
 
-    w_in = block_diagonal(filter_in)
-    w_out = block_diagonal(filter_out)
-    b_in = filter_in_bias.reshape(1, -1).astype(F32)
-    b_out = filter_out_bias.reshape(1, -1).astype(F32)
-    lat_keep = jnp.tile(jnp.repeat(kept_lat, block_width), 2).reshape(1, -1)
-    lon_keep = jnp.tile(jnp.repeat(kept_lon, block_width), 2).reshape(1, -1)
-    first_pair = ((lat_id * lon_count + lon_id) * pairs).astype(jnp.int32).reshape(1)
-    filtered = modes(
-        received, first_pair, lat_keep, lon_keep, forward_lon, inverse_lon, w_in, b_in, w_out, b_out
-    )
-
-    m_in = jnp.concatenate([dense_in, swap(dense_in, "ch")], axis=1)
-    m_in_bias = jnp.concatenate([dense_in_bias, swap(dense_in_bias, "ch")]).astype(F32)[None]
-    m_out = jnp.concatenate([dense_out, swap(dense_out, "ch")], axis=0)
-    m_out_bias = lax.all_gather(dense_out_bias, "ch", axis=0, tiled=True).astype(F32)[None]
-    gain = norm_gain.astype(F32)[None]
-    bias = norm_bias.astype(F32)[None]
-    flag = ch_id.astype(jnp.int32).reshape(1)
-
-    pieces = []
+    def filter_operands():
+        return (
+            ((lat_id * lon_count + lon_id) * pairs).astype(jnp.int32).reshape(1),
+            jnp.tile(jnp.repeat(kept_lat, block_width), 2).reshape(1, -1),
+            jnp.tile(jnp.repeat(kept_lon, block_width), 2).reshape(1, -1),
+            lax.dynamic_index_in_dim(jnp.asarray(np.stack(from_here)), lon_id, 0, False),
+            lax.dynamic_index_in_dim(jnp.asarray(np.stack(to_there)), lon_id, 0, False),
+            block_diagonal(filter_in),
+            filter_in_bias.reshape(1, -1).astype(F32),
+            block_diagonal(filter_out),
+            filter_out_bias.reshape(1, -1).astype(F32),
+        )
+
+    def along_lon(values):
+        return [shift(values[s], s, lon_count) for s in range(lon_count)]
+
+    def row_result(i, own, other):
+        mine, sent = lat_inverse(where, own, other, inverse_lat, patches, starts[i])
+        return mlp(where, mine, swap(sent, "ch"), *weights)
+
+    def placed(result, i, pieces):
+        theirs = swap(jnp.stack([piece[1] for piece in pieces]), "ch")
+        return assemble(where, result, pieces, theirs, starts[i], cols)
+
+    received, summed, sent, kept = [], None, None, None
+    weights = None
+    filter_args = None
+    dense = (dense_in, dense_in_bias, dense_out, dense_out_bias)
+    for step in range(chunks + 2):
+        arrived = None
+        if sent is not None:
+            arrived = (kept, swap(sent, "lat"))
+            sent = None
+        if summed is not None:
+            received.append(along_lon(summed))
+            summed = None
+        if step < chunks:
+            sent, kept = row_transform(step, patches)
+        elif step == chunks:
+            filter_args = filter_operands()
+        else:
+            weights = mlp_weights(*dense)
+        patches, arrived, sent, kept, received, filter_args, weights, dense = fence(
+            (patches, arrived, sent, kept, received, filter_args, weights, dense)
+        )
+        if arrived is not None:
+            summed = [
+                (arrived[0][s].astype(F32) + arrived[1][s].astype(F32)).astype(BF)
+                for s in range(lon_count)
+            ]
+
+    filtered = modes(received, *filter_args)
+
+    owns = [None] * chunks
+    others = [None] * chunks
+    outputs = [None] * chunks
+    for step in range(chunks):
+        owns[step] = along_lon(filtered[step])
+        if step >= 1:
+            owns[step - 1] = jnp.stack(owns[step - 1])
+            others[step - 1] = swap(owns[step - 1], "lat")
+        if step >= 2:
+            outputs[step - 2] = row_result(step - 2, owns[step - 2], others[step - 2])
+        patches, filtered, owns, others, outputs = fence((patches, filtered, owns, others, outputs))
+
+    result = None
+    pieces = None
     for i in range(chunks):
-        own = lax.all_to_all(filtered[i], "lon", 0, 0, tiled=True)
-        other = swap(own, "lat")
-        mixed = lat_inverse(own, other, inverse_lat, patches, i * chunk_cols // 16)
-        halves = mixed.reshape(lon_count, 2, band_rows // 2, chunk_cols, width)
-        mine = lax.dynamic_index_in_dim(halves, ch_id, 1, False)
-        sent = lax.dynamic_index_in_dim(halves, 1 - ch_id, 1, False)
-        done = mlp(
-            flag, mine, swap(sent, "ch"), gain, bias, m_in, m_in_bias, m_out, m_out_bias
+        last = pieces
+        pieces = along_lon(outputs[i])
+        if last is not None:
+            result = placed(result, i - 1, last)
+        for later in (i + 1, i + 2):
+            if later < chunks and outputs[later] is None:
+                if others[later] is None:
+                    owns[later] = jnp.stack(owns[later])
+                    others[later] = swap(owns[later], "lat")
+                outputs[later] = row_result(later, owns[later], others[later])
+        patches, owns, others, outputs, pieces, result = fence(
+            (patches, owns, others, outputs, pieces, result)
         )
-        pieces.append(
-            lax.all_to_all(
-                done.reshape(lon_count * 2, band_rows // 2, chunk_cols, width),
-                ("lon", "ch"), 0, 0, tiled=True,
-            ).reshape(lon_count, 2, band_rows // 2, chunk_cols, width)
-        )
-    result = jnp.stack(pieces).transpose(2, 3, 1, 0, 4, 5)
-    return result.reshape(1, 1, band_rows, lon_count * cols, width)
+    result = placed(result, chunks - 1, pieces)
+    return result.reshape(1, 1, rows // lon_count, lon_count * cols, width)
 
 
 def lon_forward(number, length):
@@ -627,8 +786,8 @@
     lat_count, lon_count = sizes["lat"], sizes["lon"]
     cols = W // lon_count
     fits = lat_count == 2 and sizes["ch"] == 2 and MLAT % (lat_count * lon_count) == 0
-    fits = fits and cols % 32 == 0 and H % (2 * lat_count * lon_count) == 0
-    plan = functools.partial(column_plan, 32) if fits else row_plan
+    fits = fits and cols == 96 and H % (2 * lat_count * lon_count) == 0
+    plan = functools.partial(column_plan, (32, 32, 32)) if fits else row_plan
     return jax.shard_map(
         plan,
         mesh=mesh,

time: 616 us -> 617 us (level)
  the two profiles are of different devices: /device:TPU:0 before, /device:TPU:9 now
where the time goes in v2:
time: 617 us; the launch traced here: 609 us
  waiting for transfers between devices  373 us (60%)
  Pallas kernels  122 us (20%)
  starting transfers between devices  42.6 us (7%)
  other arithmetic  42 us (7%)
  local copies, waits for them, and re-layouts  26.3 us (4%)
    ppermute x27, waiting for transfers between devices, shift(): lax.ppermute(values, 'lon', [(z, (z + steps) % lon_count) for z in range(...  316 us
    ppermute x18, waiting for transfers between devices, swap(): return lax.ppermute(values, axis, [(0, 1), (1, 0)])  57.3 us
    pallas_call x3, Pallas kernels, mlp(): pl.pallas_call(mlp_kernel, grid_spec=pltpu.PrefetchScalarGridSpec(num_sca...  50.1 us
    ppermute x27, starting transfers between devices, shift(): lax.ppermute(values, 'lon', [(z, (z + steps) % lon_count) for z in range(...  26.7 us
    pallas_call x3, Pallas kernels, lat_inverse(): pl.pallas_call(lat_inverse_kernel, grid_spec=pltpu.PrefetchScalarGridSpec...  22.5 us
    pallas_call x1, Pallas kernels, modes(): pl.pallas_call(functools.partial(modes_kernel, len(flat)), grid=(pairs,),...  17.2 us
    pallas_call x3, Pallas kernels, lat_forward(): pl.pallas_call(lat_forward_kernel, grid_spec=pltpu.PrefetchScalarGridSpec...  16.5 us
    ppermute x18, starting transfers between devices, swap(): return lax.ppermute(values, axis, [(0, 1), (1, 0)])  15.9 us
  transfers between devices with their start and end apart: 45, of which 29 were waited for; matrix products, arithmetic and copies ran while one was open for 6% of the time, Pallas kernels for 14%

profile of v2, /device:TPU:9, one launch (start us, length us, event | category | flops | bytes accessed | tf_op | source)
XLA Modules:
  0.0 609.0 jit_solution(12302429254045373840)
XLA Ops:
  0.0 2.5 convert_reduce_fusion.2
  2.6 2.9 fusion.1
  7.3 3.8 fusion.5.cells_ref
  11.1 5.7 lat_forward.3
  18.8 1.6 fusion.7
  22.1 3.6 fusion.11.cells_ref
  25.8 2.3 copy-done.13
  28.0 5.1 lat_forward.4
  33.1 22.5 %collective-permute-done.1 = bf16[4,17,32,384]{3,2,1,0:T(8,128)(2,1)} collective-permute-done((bf16[4,17,32,384]{3,2,1,0:T(8,128)(2,1)}, bf16[4,17,32,384]{3,2,1,0:T(8,128)(2,1)}, u32[]{:S(2)}, u32[]{:S(2)}) %collective-permute-start.1) | collective-permute-done | bytes 1671200 | tf_op jit(solution)/shard_map/ppermute | solution.py:432
  55.7 2.5 convert_reduce_fusion
  59.5 2.9 fusion.13
  62.4 1.5 collective-permute-start.4
  64.0 1.8 fusion.21
  68.2 1.5 collective-permute-start.7
  69.8 3.6 fusion.17.cells_ref
  73.5 5.7 lat_forward.5
  79.2 23.9 %collective-permute-done.6.refs_2_.refs_14_ = bf16[17,32,384]{2,1,0:T(8,128)(2,1)S(1)} collective-permute-done((bf16[17,32,384]{2,1,0:T(8,128)(2,1)S(1)}, bf16[17,32,384]{2,1,0:T(8,128)(2,1)S(1)}, u32[]{:S(2)}, u32[]{:S(2)}) %collective-permute-start.6) | collective-permute-done | bytes 417824 | tf_op jit(solution)/shard_map/ppermute | solution.py:438
  103.1 2.1 collective-permute-done.7.refs_3_.refs_15_
  107.8 1.5 fusion.25
  110.4 1.5 collective-permute-start.9
  114.9 2.0 squeeze.36
  121.2 2.3 maximum_maximum_fusion.refs_26_
  124.6 12.5 %collective-permute-done.10.refs_6_.refs_18_ = bf16[17,32,384]{2,1,0:T(8,128)(2,1)} collective-permute-done((bf16[17,32,384]{2,1,0:T(8,128)(2,1)}, bf16[17,32,384]{2,1,0:T(8,128)(2,1)}, u32[]{:S(2)}, u32[]{:S(2)}) %collective-permute-start.10) | collective-permute-done | bytes 417824 | tf_op jit(solution)/shard_map/ppermute | solution.py:438
  137.1 7.9 %collective-permute-done.11.refs_7_.refs_19_ = bf16[17,32,384]{2,1,0:T(8,128)(2,1)} collective-permute-done((bf16[17,32,384]{2,1,0:T(8,128)(2,1)}, bf16[17,32,384]{2,1,0:T(8,128)(2,1)}, u32[]{:S(2)}, u32[]{:S(2)}) %collective-permute-start.11) | collective-permute-done | bytes 417824 | tf_op jit(solution)/shard_map/ppermute | solution.py:438
  147.2 2.6 fusion.29
  149.8 2.2 collective-permute-start.12
  152.0 1.8 all-gather
  155.2 1.5 pad_maximum_fusion.1.w_out_ref
  156.7 1.6 pad_maximum_fusion.w_in_ref
  158.3 20.5 %collective-permute-done.12.refs_9_.refs_21_ = bf16[17,32,384]{2,1,0:T(8,128)(2,1)S(1)} collective-permute-done((bf16[17,32,384]{2,1,0:T(8,128)(2,1)S(1)}, bf16[17,32,384]{2,1,0:T(8,128)(2,1)S(1)}, u32[]{:S(2)}, u32[]{:S(2)}) %collective-permute-start.12) | collective-permute-done | bytes 417824 | tf_op jit(solution)/shard_map/ppermute | solution.py:438
  178.8 9.1 %collective-permute-done.13.refs_10_.refs_22_ = bf16[17,32,384]{2,1,0:T(8,128)(2,1)S(1)} collective-permute-done((bf16[17,32,384]{2,1,0:T(8,128)(2,1)S(1)}, bf16[17,32,384]{2,1,0:T(8,128)(2,1)S(1)}, u32[]{:S(2)}, u32[]{:S(2)}) %collective-permute-start.13) | collective-permute-done | bytes 417824 | tf_op jit(solution)/shard_map/ppermute | solution.py:438
  188.8 17.2 %modes.1 = (bf16[17,32,384]{2,1,0:T(8,128)(2,1)S(1)}, bf16[17,32,384]{2,1,0:T(8,128)(2,1)S(1)}, bf16[17,32,384]{2,1,0:T(8,128)(2,1)S(1)}, bf16[17,32,384]{2,1,0:...) custom-call(s32[1]{0:T(128)} %bitcast.23.first_pair_ref, ...), custom_call_target="tpu_custom_call" | custom-call | flops 7247757312 | bytes 10027008 | tf_op jit(solution)/shard_map/modes/pallas_call | solution.py:276
  206.1 3.2 collective-permute-start.19
  210.7 5.7 collective-permute-done.18
  216.4 25.0 %collective-permute-done.19 = bf16[17,32,384]{2,1,0:T(8,128)(2,1)S(1)} collective-permute-done((bf16[17,32,384]{2,1,0:T(8,128)(2,1)S(1)}, bf16[17,32,384]{2,1,0:T(8,128)(2,1)S(1)}, u32[]{:S(2)}, u32[]{:S(2)}) %collective-permute-start.19) | collective-permute-done | bytes 417824 | tf_op jit(solution)/shard_map/ppermute | solution.py:438
  241.4 4.8 collective-permute-done.20
  247.7 1.7 collective-permute-start.23
  249.4 8.7 %collective-permute-done.21 = bf16[17,32,384]{2,1,0:T(8,128)(2,1)S(1)} collective-permute-done((bf16[17,32,384]{2,1,0:T(8,128)(2,1)S(1)}, bf16[17,32,384]{2,1,0:T(8,128)(2,1)S(1)}, u32[]{:S(2)}, u32[]{:S(2)}) %collective-permute-start.21) | collective-permute-done | bytes 417824 | tf_op jit(solution)/shard_map/ppermute | solution.py:438
  258.1 25.0 %collective-permute-done.22 = bf16[17,32,384]{2,1,0:T(8,128)(2,1)S(1)} collective-permute-done((bf16[17,32,384]{2,1,0:T(8,128)(2,1)S(1)}, bf16[17,32,384]{2,1,0:T(8,128)(2,1)S(1)}, u32[]{:S(2)}, u32[]{:S(2)}) %collective-permute-start.22) | collective-permute-done | bytes 417824 | tf_op jit(solution)/shard_map/ppermute | solution.py:438
  284.1 7.5 %lat_inverse.3 = (bf16[4,16,32,384]{3,2,1,0:T(8,128)(2,1)S(1)}, bf16[4,16,32,384]{3,2,1,0:T(8,128)(2,1)S(1)}) custom-call(s32[3]{0:T(128)S(1)} %pad_add_fusion.where_ref, bf16[4,17,32,384]{3,2,1,0:T(8,128)(2,1)S(1)} %pad_maximum_fusion.2.own_ref, bf16[4,17,32,384]{3,2,1,0:T(8,128)(2,1)S(1)} %collective-permute-done.24.other_ref, ...), custom_call_target="tpu_custom_call" | custom-call | flops 452984832 | bytes 1179648 | tf_op jit(solution)/shard_map/lat_inverse/pallas_call | solution.py:160
  295.8 1.5 collective-permute-start.27
  299.8 16.8 %channel_mlp.3 = (bf16[2,16,32,384]{3,2,1,0:T(8,128)(2,1)S(1)}, bf16[2,16,32,384]{3,2,1,0:T(8,128)(2,1)}, bf16[2,16,32,384]{3,2,1,0:T(8,128)(2,1)S(1)}, bf16[2,16,32,384]{3,2,1,0:T(8,128)(2,1)S(1)}) custom-call(s32[3]{0:T(128)S(1)} %pad_add_fusion.where_ref, bf16[4,16,32,384]{3,2,1,0:T(8,128)(2,1)S(1)} %copy-done.6, bf16[4,16,32,384]{3,2,1,0:T(8,128)(2,1)} %copy-done.22, ...), custom_call_target="tpu_custom_call" | custom-call | flops 1207959552 | bytes 786432 | tf_op jit(solution)/shard_map/channel_mlp/pallas_call | solution.py:337
  316.6 14.1 %collective-permute-done.26 = bf16[17,32,384]{2,1,0:T(8,128)(2,1)} collective-permute-done((bf16[17,32,384]{2,1,0:T(8,128)(2,1)S(1)}, bf16[17,32,384]{2,1,0:T(8,128)(2,1)}, u32[]{:S(2)}, u32[]{:S(2)}) %collective-permute-start.26) | collective-permute-done | bytes 417824 | tf_op jit(solution)/shard_map/ppermute | solution.py:438
  330.7 2.4 collective-permute-done.27
  333.1 1.5 pad_maximum_fusion.4.own_ref
  335.9 7.5 %lat_inverse.4 = (bf16[4,16,32,384]{3,2,1,0:T(8,128)(2,1)S(1)}, bf16[4,16,32,384]{3,2,1,0:T(8,128)(2,1)S(1)}) custom-call(s32[3]{0:T(128)S(1)} %pad_add_fusion.where_ref, bf16[4,17,32,384]{3,2,1,0:T(8,128)(2,1)S(1)} %pad_maximum_fusion.3.own_ref, bf16[4,17,32,384]{3,2,1,0:T(8,128)(2,1)S(1)} %collective-permute-done.28.other_ref, ...), custom_call_target="tpu_custom_call" | custom-call | flops 452984832 | bytes 1179648 | tf_op jit(solution)/shard_map/lat_inverse/pallas_call | solution.py:160
  344.2 28.0 %collective-permute-done.30.other_ref = bf16[4,17,32,384]{3,2,1,0:T(8,128)(2,1)S(1)} collective-permute-done((bf16[4,17,32,384]{3,2,1,0:T(8,128)(2,1)S(1)}, bf16[4,17,32,384]{3,2,1,0:T(8,128)(2,1)S(1)}, u32[]{:S(2)}, u32[]{:S(2)}) %collective-permute-start.30) | collective-permute-done | bytes 1671200 | tf_op jit(solution)/shard_map/ppermute | solution.py:432
  372.2 7.5 %lat_inverse.5 = (bf16[4,16,32,384]{3,2,1,0:T(8,128)(2,1)S(1)}, bf16[4,16,32,384]{3,2,1,0:T(8,128)(2,1)S(1)}) custom-call(s32[3]{0:T(128)S(1)} %pad_add_fusion.where_ref, bf16[4,17,32,384]{3,2,1,0:T(8,128)(2,1)S(1)} %pad_maximum_fusion.4.own_ref, bf16[4,17,32,384]{3,2,1,0:T(8,128)(2,1)S(1)} %collective-permute-done.30.other_ref, ...), custom_call_target="tpu_custom_call" | custom-call | flops 452984832 | bytes 1179648 | tf_op jit(solution)/shard_map/lat_inverse/pallas_call | solution.py:160
  382.0 1.7 collective-permute-start.35
  386.3 17.4 %channel_mlp.4 = (bf16[2,16,32,384]{3,2,1,0:T(8,128)(2,1)S(1)}, bf16[2,16,32,384]{3,2,1,0:T(8,128)(2,1)}, bf16[2,16,32,384]{3,2,1,0:T(8,128)(2,1)}, bf16[2,16,32,384]{3,2,1,0:T(8,128)(2,1)}) custom-call(s32[3]{0:T(128)S(1)} %pad_add_fusion.where_ref, bf16[4,16,32,384]{3,2,1,0:T(8,128)(2,1)S(1)} %copy-done.4, bf16[4,16,32,384]{3,2,1,0:T(8,128)(2,1)} %copy-done.21, ...), custom_call_target="tpu_custom_call" | custom-call | flops 1207959552 | bytes 786432 | tf_op jit(solution)/shard_map/channel_mlp/pallas_call | solution.py:337
  404.9 15.9 %channel_mlp.5 = (bf16[2,16,32,384]{3,2,1,0:T(8,128)(2,1)S(1)}, bf16[2,16,32,384]{3,2,1,0:T(8,128)(2,1)S(1)}, bf16[2,16,32,384]{3,2,1,0:T(8,128)(2,1)S(1)}, bf16[2,16,32,384]{3,2,1,0:T(8,128)(2,1)S(1)}) custom-call(s32[3]{0:T(128)S(1)} %pad_add_fusion.where_ref, bf16[4,16,32,384]{3,2,1,0:T(8,128)(2,1)S(1)} %get-tuple-element.328.own_ref, ...), custom_call_target="tpu_custom_call" | custom-call | flops 1207959552 | bytes 786432 | tf_op jit(solution)/shard_map/channel_mlp/pallas_call | solution.py:337
  420.9 28.2 %collective-permute-done.34.refs_2_ = bf16[2,16,32,384]{3,2,1,0:T(8,128)(2,1)S(1)} collective-permute-done((bf16[2,16,32,384]{3,2,1,0:T(8,128)(2,1)S(1)}, bf16[2,16,32,384]{3,2,1,0:T(8,128)(2,1)S(1)}, u32[]{:S(2)}, u32[]{:S(2)}) %collective-permute-start.34) | collective-permute-done | bytes 786464 | tf_op jit(solution)/shard_map/ppermute | solution.py:438
  449.1 1.8 collective-permute-done.35.refs_3_
  452.2 1.8 collective-permute-start.37
  455.5 5.1 assemble.3.refs_5_
  460.6 11.0 %collective-permute-done.36.refs_2_ = bf16[2,16,32,384]{3,2,1,0:T(8,128)(2,1)S(1)} collective-permute-done((bf16[2,16,32,384]{3,2,1,0:T(8,128)(2,1)}, bf16[2,16,32,384]{3,2,1,0:T(8,128)(2,1)S(1)}, u32[]{:S(2)}, u32[]{:S(2)}) %collective-permute-start.36) | collective-permute-done | bytes 786464 | tf_op jit(solution)/shard_map/ppermute | solution.py:438
  471.6 48.7 %collective-permute-done.37.refs_3_ = bf16[2,16,32,384]{3,2,1,0:T(8,128)(2,1)} collective-permute-done((bf16[2,16,32,384]{3,2,1,0:T(8,128)(2,1)}, bf16[2,16,32,384]{3,2,1,0:T(8,128)(2,1)}, u32[]{:S(2)}, u32[]{:S(2)}) %collective-permute-start.37) | collective-permute-done | bytes 786464 | tf_op jit(solution)/shard_map/ppermute | solution.py:438
  520.3 2.7 collective-permute-done.38.refs_4_
  529.3 5.1 assemble.4.refs_5_
  534.4 10.9 %collective-permute-done.40.refs_2_ = bf16[2,16,32,384]{3,2,1,0:T(8,128)(2,1)} collective-permute-done((bf16[2,16,32,384]{3,2,1,0:T(8,128)(2,1)S(1)}, bf16[2,16,32,384]{3,2,1,0:T(8,128)(2,1)}, u32[]{:S(2)}, u32[]{:S(2)}) %collective-permute-start.40) | collective-permute-done | bytes 786464 | tf_op jit(solution)/shard_map/ppermute | solution.py:438
  545.3 48.5 %collective-permute-done.41.refs_3_ = bf16[2,16,32,384]{3,2,1,0:T(8,128)(2,1)} collective-permute-done((bf16[2,16,32,384]{3,2,1,0:T(8,128)(2,1)S(1)}, bf16[2,16,32,384]{3,2,1,0:T(8,128)(2,1)}, u32[]{:S(2)}, u32[]{:S(2)}) %collective-permute-start.41) | collective-permute-done | bytes 786464 | tf_op jit(solution)/shard_map/ppermute | solution.py:438
  593.8 1.6 collective-permute-done.42.refs_4_
  599.3 3.0 collective-permute-done.44.refs_0_
  603.5 5.1 assemble.5
  (211 shorter events, 58.5 us)
Async XLA Ops:
  5.6 1.7 collective-permute-start
  6.6 397.1 %copy-start.7 = (s32[3]{0:T(128)}, s32[3]{0:T(128)S(1)}, u32[]{:S(2)}) copy-start(s32[3]{0:T(128)S(1)} %pad_add_fusion.where_ref) | copy-start | bytes 40
  17.5 38.1 %collective-permute-start.1 = (bf16[4,17,32,384]{3,2,1,0:T(8,128)(2,1)}, bf16[4,17,32,384]{3,2,1,0:T(8,128)(2,1)}, u32[]{:S(2)}, u32[]{:S(2)}) collective-permute-start(bf16[4,17,32,384]{3,2,1,0:T(8,128)(2,1)} %get-tuple-element.187), channel_id=1, source_target_pairs={{0,2},{2,0},{1,3},{3,1},{4,6},{6,4},{5,7},{7,5},{8,10},{10,8},{9,1... | collective-permute-start | bytes 5013512 | tf_op jit(solution)/shard_map/ppermute | solution.py:432
  20.4 1.7 collective-permute-start.2
  58.2 47.0 %collective-permute-start.3 = (bf16[4,17,32,384]{3,2,1,0:T(8,128)(2,1)S(1)}, bf16[4,17,32,384]{3,2,1,0:T(8,128)(2,1)S(1)}, u32[]{:S(2)}, u32[]{:S(2)}) collective-permute-start(bf16[4,17,32,384]{3,2,1,0:T(8,128)(2,1)S(1)} %get-tuple-element.196), channel_id=1, source_target_pairs={{0,2},{2,0},{1,3},{3,1},{4,6},{6,4},{5,7},{7,5},{8,10},{10,8},{9,1... | collective-permute-start | bytes 5013512 | tf_op jit(solution)/shard_map/ppermute | solution.py:432
  62.4 7.3 %collective-permute-start.4 = (f32[2,128,32]{2,1,0:T(8,128)S(1)}, f32[2,128,32]{2,1,0:T(8,128)S(1)}, u32[]{:S(2)}, u32[]{:S(2)}) collective-permute-start(f32[2,128,32]{2,1,0:T(8,128)S(1)} %pad_maximum_fusion.10), channel_id=1, source_target_pairs={{0,1},{1,0},{2,3},{3,2},{4,5},{5,4},{6,7},{7,6},{8,9},{9,8},{10,11... | collective-permute-start | bytes 98312 | tf_op jit(solution)/shard_map/ppermute | solution.py:432
  65.8 13.4 %collective-permute-start.5 = (bf16[17,32,384]{2,1,0:T(8,128)(2,1)S(1)}, bf16[17,32,384]{2,1,0:T(8,128)(2,1)S(1)}, u32[]{:S(2)}, u32[]{:S(2)}) collective-permute-start(bf16[17,32,384]{2,1,0:T(8,128)(2,1)S(1)} %get-tuple-element.371), channel_id=1, source_target_pairs={{0,4},{4,8},{8,12},{12,0},{1,5},{5,9},{9,13},{13,1},{2,6},{6,10},{... | collective-permute-start | bytes 1253384 | tf_op jit(solution)/shard_map/ppermute | solution.py:438
  67.1 35.9 %collective-permute-start.6 = (bf16[17,32,384]{2,1,0:T(8,128)(2,1)S(1)}, bf16[17,32,384]{2,1,0:T(8,128)(2,1)S(1)}, u32[]{:S(2)}, u32[]{:S(2)}) collective-permute-start(bf16[17,32,384]{2,1,0:T(8,128)(2,1)S(1)} %get-tuple-element.370), channel_id=1, source_target_pairs={{0,8},{4,12},{8,0},{12,4},{1,9},{5,13},{9,1},{13,5},{2,10},{6,14},... | collective-permute-start | bytes 1253384 | tf_op jit(solution)/shard_map/ppermute | solution.py:438
  68.2 37.0 %collective-permute-start.7 = (bf16[17,32,384]{2,1,0:T(8,128)(2,1)S(1)}, bf16[17,32,384]{2,1,0:T(8,128)(2,1)S(1)}, u32[]{:S(2)}, u32[]{:S(2)}) collective-permute-start(bf16[17,32,384]{2,1,0:T(8,128)(2,1)S(1)} %get-tuple-element.369), channel_id=1, source_target_pairs={{0,12},{4,0},{8,4},{12,8},{1,13},{5,1},{9,5},{13,9},{2,14},{6,2},{... | collective-permute-start | bytes 1253384 | tf_op jit(solution)/shard_map/ppermute | solution.py:438
  73.5 32.0 %copy-start.27 = (bf16[2,4,96,96]{3,2,1,0:T(8,128)(2,1)S(1)}, bf16[2,4,96,96]{3,2,1,0:T(8,128)(2,1)}, u32[]{:S(2)}) copy-start(bf16[2,4,96,96]{3,2,1,0:T(8,128)(2,1)} %param.24) | copy-start | bytes 442372
  73.5 32.0 %copy-start.28 = (bf16[2,4,96,96]{3,2,1,0:T(8,128)(2,1)S(1)}, bf16[2,4,96,96]{3,2,1,0:T(8,128)(2,1)}, u32[]{:S(2)}) copy-start(bf16[2,4,96,96]{3,2,1,0:T(8,128)(2,1)} %param.22) | copy-start | bytes 442372
  79.2 28.6 %copy-start.39 = (bf16[17,32,384]{2,1,0:T(8,128)(2,1)}, bf16[17,32,384]{2,1,0:T(8,128)(2,1)S(1)}, u32[]{:S(2)}) copy-start(bf16[17,32,384]{2,1,0:T(8,128)(2,1)S(1)} %collective-permute-done.5.refs_1_.refs_13_) | copy-start | bytes 1253380
  105.2 40.9 %collective-permute-start.8 = (bf16[4,17,32,384]{3,2,1,0:T(8,128)(2,1)}, bf16[4,17,32,384]{3,2,1,0:T(8,128)(2,1)}, u32[]{:S(2)}, u32[]{:S(2)}) collective-permute-start(bf16[4,17,32,384]{3,2,1,0:T(8,128)(2,1)} %get-tuple-element.207), channel_id=1, source_target_pairs={{0,2},{2,0},{1,3},{3,1},{4,6},{6,4},{5,7},{7,5},{8,10},{10,8},{9,1... | collective-permute-start | bytes 5013512 | tf_op jit(solution)/shard_map/ppermute | solution.py:432
  109.3 27.8 %collective-permute-start.10 = (bf16[17,32,384]{2,1,0:T(8,128)(2,1)}, bf16[17,32,384]{2,1,0:T(8,128)(2,1)}, u32[]{:S(2)}, u32[]{:S(2)}) collective-permute-start(bf16[17,32,384]{2,1,0:T(8,128)(2,1)} %get-tuple-element.366), channel_id=1, source_target_pairs={{0,8},{4,12},{8,0},{12,4},{1,9},{5,13},{9,1},{13,5},{2,10},{6,14},... | collective-permute-start | bytes 1253384 | tf_op jit(solution)/shard_map/ppermute | solution.py:438
  110.4 34.7 %collective-permute-start.11 = (bf16[17,32,384]{2,1,0:T(8,128)(2,1)}, bf16[17,32,384]{2,1,0:T(8,128)(2,1)}, u32[]{:S(2)}, u32[]{:S(2)}) collective-permute-start(bf16[17,32,384]{2,1,0:T(8,128)(2,1)} %get-tuple-element.365), channel_id=1, source_target_pairs={{0,12},{4,0},{8,4},{12,8},{1,13},{5,1},{9,5},{13,9},{2,14},{6,2},{... | collective-permute-start | bytes 1253384 | tf_op jit(solution)/shard_map/ppermute | solution.py:438
  110.4 35.7 %collective-permute-start.9 = (bf16[17,32,384]{2,1,0:T(8,128)(2,1)}, bf16[17,32,384]{2,1,0:T(8,128)(2,1)}, u32[]{:S(2)}, u32[]{:S(2)}) collective-permute-start(bf16[17,32,384]{2,1,0:T(8,128)(2,1)} %get-tuple-element.367), channel_id=1, source_target_pairs={{0,4},{4,8},{8,12},{12,0},{1,5},{5,9},{9,13},{13,1},{2,6},{6,10},{... | collective-permute-start | bytes 1253384 | tf_op jit(solution)/shard_map/ppermute | solution.py:438
  120.0 26.7 %copy-start.29 = (bf16[768]{0:T(1024)(128)(2,1)S(1)}, bf16[768]{0:T(1024)(128)(2,1)}, u32[]{:S(2)}) copy-start(bf16[768]{0:T(1024)(128)(2,1)} %param.28) | copy-start | bytes 4612
  120.0 26.7 %copy-start.30 = (bf16[768]{0:T(1024)(128)(2,1)S(1)}, bf16[768]{0:T(1024)(128)(2,1)}, u32[]{:S(2)}) copy-start(bf16[768]{0:T(1024)(128)(2,1)} %param.29) | copy-start | bytes 4612
  120.0 26.7 %copy-start.31 = (bf16[768]{0:T(1024)(128)(2,1)S(1)}, bf16[768]{0:T(1024)(128)(2,1)}, u32[]{:S(2)}) copy-start(bf16[768]{0:T(1024)(128)(2,1)} %param.31) | copy-start | bytes 4612
  120.1 26.0 %copy-start.24 = (bf16[768,768]{1,0:T(8,128)(2,1)S(1)}, bf16[768,768]{1,0:T(8,128)(2,1)}, u32[]{:S(2)}) copy-start(bf16[768,768]{1,0:T(8,128)(2,1)} %param.32) | copy-start | bytes 3538948
  120.1 26.5 %copy-start.25 = (bf16[768,768]{1,0:T(8,128)(2,1)S(1)}, bf16[768,768]{1,0:T(8,128)(2,1)}, u32[]{:S(2)}) copy-start(bf16[768,768]{1,0:T(8,128)(2,1)} %param.30) | copy-start | bytes 3538948
  146.1 9.1 %collective-permute-start.17 = (bf16[768,768]{1,0:T(8,128)(2,1)S(1)}, bf16[768,768]{1,0:T(8,128)(2,1)S(1)}, u32[]{:S(2)}, u32[]{:S(2)}) collective-permute-start(bf16[768,768]{1,0:T(8,128)(2,1)S(1)} %copy-done.24), channel_id=1, source_target_pairs={{0,1},{1,0},{2,3},{3,2},{4,5},{5,4},{6,7},{7,6},{8,9},{9,8},{10,11... | collective-permute-start | bytes 3538952 | tf_op jit(solution)/shard_map/ppermute | solution.py:432
  146.6 10.1 %collective-permute-start.15 = (bf16[768,768]{1,0:T(8,128)(2,1)S(1)}, bf16[768,768]{1,0:T(8,128)(2,1)S(1)}, u32[]{:S(2)}, u32[]{:S(2)}) collective-permute-start(bf16[768,768]{1,0:T(8,128)(2,1)S(1)} %copy-done.25), channel_id=1, source_target_pairs={{0,1},{1,0},{2,3},{3,2},{4,5},{5,4},{6,7},{7,6},{8,9},{9,8},{10,11... | collective-permute-start | bytes 3538952 | tf_op jit(solution)/shard_map/ppermute | solution.py:432
  146.7 7.2 %collective-permute-start.16 = (bf16[768]{0:T(1024)(128)(2,1)S(1)}, bf16[768]{0:T(1024)(128)(2,1)S(1)}, u32[]{:S(2)}, u32[]{:S(2)}) collective-permute-start(bf16[768]{0:T(1024)(128)(2,1)S(1)} %copy-done.31), channel_id=1, source_target_pairs={{0,1},{1,0},{2,3},{3,2},{4,5},{5,4},{6,7},{7,6},{8,9},{9,8},{10,11... | collective-permute-start | bytes 4616 | tf_op jit(solution)/shard_map/ppermute | solution.py:432
  149.8 29.0 %collective-permute-start.12 = (bf16[17,32,384]{2,1,0:T(8,128)(2,1)S(1)}, bf16[17,32,384]{2,1,0:T(8,128)(2,1)S(1)}, u32[]{:S(2)}, u32[]{:S(2)}) collective-permute-start(bf16[17,32,384]{2,1,0:T(8,128)(2,1)S(1)} %get-tuple-element.363), channel_id=1, source_target_pairs={{0,4},{4,8},{8,12},{12,0},{1,5},{5,9},{9,13},{13,1},{2,6},{6,10},{... | collective-permute-start | bytes 1253384 | tf_op jit(solution)/shard_map/ppermute | solution.py:438
  152.0 35.9 %collective-permute-start.13 = (bf16[17,32,384]{2,1,0:T(8,128)(2,1)S(1)}, bf16[17,32,384]{2,1,0:T(8,128)(2,1)S(1)}, u32[]{:S(2)}, u32[]{:S(2)}) collective-permute-start(bf16[17,32,384]{2,1,0:T(8,128)(2,1)S(1)} %get-tuple-element.362), channel_id=1, source_target_pairs={{0,8},{4,12},{8,0},{12,4},{1,9},{5,13},{9,1},{13,5},{2,10},{6,14},... | collective-permute-start | bytes 1253384 | tf_op jit(solution)/shard_map/ppermute | solution.py:438
  153.9 34.0 %collective-permute-start.14 = (bf16[17,32,384]{2,1,0:T(8,128)(2,1)S(1)}, bf16[17,32,384]{2,1,0:T(8,128)(2,1)S(1)}, u32[]{:S(2)}, u32[]{:S(2)}) collective-permute-start(bf16[17,32,384]{2,1,0:T(8,128)(2,1)S(1)} %get-tuple-element.361), channel_id=1, source_target_pairs={{0,12},{4,0},{8,4},{12,8},{1,13},{5,1},{9,5},{13,9},{2,14},{6,2},{... | collective-permute-start | bytes 1253384 | tf_op jit(solution)/shard_map/ppermute | solution.py:438
  187.9 96.2 %slice-start = ((s8[4718592]{0:T(1024)(128)(4,1)}), s8[4194304]{0:T(1024)(128)(4,1)S(1)}, s32[]{:S(2)}) async-start(s8[4718592]{0:T(1024)(128)(4,1)} %bitcast.114), calls=%async_computation | async-start | bytes 8388608
  188.8 95.3 %slice-start.1 = ((s8[4718592]{0:T(1024)(128)(4,1)}), s8[524288]{0:T(1024)(128)(4,1)S(1)}, s32[]{:S(2)}) async-start(s8[4718592]{0:T(1024)(128)(4,1)} %bitcast.114), calls=%async_computation.1 | async-start | bytes 1048576
  206.0 10.4 %collective-permute-start.18 = (bf16[17,32,384]{2,1,0:T(8,128)(2,1)S(1)}, bf16[17,32,384]{2,1,0:T(8,128)(2,1)S(1)}, u32[]{:S(2)}, u32[]{:S(2)}) collective-permute-start(bf16[17,32,384]{2,1,0:T(8,128)(2,1)S(1)} %get-tuple-element.264), channel_id=1, source_target_pairs={{0,4},{4,8},{8,12},{12,0},{1,5},{5,9},{9,13},{13,1},{2,6},{6,10},{... | collective-permute-start | bytes 1253384 | tf_op jit(solution)/shard_map/ppermute | solution.py:438
  206.1 35.3 %collective-permute-start.19 = (bf16[17,32,384]{2,1,0:T(8,128)(2,1)S(1)}, bf16[17,32,384]{2,1,0:T(8,128)(2,1)S(1)}, u32[]{:S(2)}, u32[]{:S(2)}) collective-permute-start(bf16[17,32,384]{2,1,0:T(8,128)(2,1)S(1)} %get-tuple-element.265), channel_id=1, source_target_pairs={{0,8},{4,12},{8,0},{12,4},{1,9},{5,13},{9,1},{13,5},{2,10},{6,14},... | collective-permute-start | bytes 1253384 | tf_op jit(solution)/shard_map/ppermute | solution.py:438
  209.3 36.9 %collective-permute-start.20 = (bf16[17,32,384]{2,1,0:T(8,128)(2,1)S(1)}, bf16[17,32,384]{2,1,0:T(8,128)(2,1)S(1)}, u32[]{:S(2)}, u32[]{:S(2)}) collective-permute-start(bf16[17,32,384]{2,1,0:T(8,128)(2,1)S(1)} %get-tuple-element.266), channel_id=1, source_target_pairs={{0,12},{4,0},{8,4},{12,8},{1,13},{5,1},{9,5},{13,9},{2,14},{6,2},{... | collective-permute-start | bytes 1253384 | tf_op jit(solution)/shard_map/ppermute | solution.py:438
  246.5 37.6 %collective-permute-start.24 = (bf16[4,17,32,384]{3,2,1,0:T(8,128)(2,1)S(1)}, bf16[4,17,32,384]{3,2,1,0:T(8,128)(2,1)S(1)}, u32[]{:S(2)}, u32[]{:S(2)}) collective-permute-start(bf16[4,17,32,384]{3,2,1,0:T(8,128)(2,1)S(1)} %pad_maximum_fusion.2.own_ref), channel_id=1, source_target_pairs={{0,2},{2,0},{1,3},{3,1},{4,6},{6,4},{5,7},{7,5},{8,10},{10,8},{9,1... | collective-permute-start | bytes 5013512 | tf_op jit(solution)/shard_map/ppermute | solution.py:432
  247.7 10.4 %collective-permute-start.21 = (bf16[17,32,384]{2,1,0:T(8,128)(2,1)S(1)}, bf16[17,32,384]{2,1,0:T(8,128)(2,1)S(1)}, u32[]{:S(2)}, u32[]{:S(2)}) collective-permute-start(bf16[17,32,384]{2,1,0:T(8,128)(2,1)S(1)} %get-tuple-element.277), channel_id=1, source_target_pairs={{0,4},{4,8},{8,12},{12,0},{1,5},{5,9},{9,13},{13,1},{2,6},{6,10},{... | collective-permute-start | bytes 1253384 | tf_op jit(solution)/shard_map/ppermute | solution.py:438
  247.7 35.4 %collective-permute-start.22 = (bf16[17,32,384]{2,1,0:T(8,128)(2,1)S(1)}, bf16[17,32,384]{2,1,0:T(8,128)(2,1)S(1)}, u32[]{:S(2)}, u32[]{:S(2)}) collective-permute-start(bf16[17,32,384]{2,1,0:T(8,128)(2,1)S(1)} %get-tuple-element.278), channel_id=1, source_target_pairs={{0,8},{4,12},{8,0},{12,4},{1,9},{5,13},{9,1},{13,5},{2,10},{6,14},... | collective-permute-start | bytes 1253384 | tf_op jit(solution)/shard_map/ppermute | solution.py:438
  247.7 35.4 %collective-permute-start.23 = (bf16[17,32,384]{2,1,0:T(8,128)(2,1)S(1)}, bf16[17,32,384]{2,1,0:T(8,128)(2,1)S(1)}, u32[]{:S(2)}, u32[]{:S(2)}) collective-permute-start(bf16[17,32,384]{2,1,0:T(8,128)(2,1)S(1)} %get-tuple-element.279), channel_id=1, source_target_pairs={{0,12},{4,0},{8,4},{12,8},{1,13},{5,1},{9,5},{13,9},{2,14},{6,2},{... | collective-permute-start | bytes 1253384 | tf_op jit(solution)/shard_map/ppermute | solution.py:438
  291.6 5.6 collective-permute-start.29
  293.3 39.8 %collective-permute-start.28 = (bf16[4,17,32,384]{3,2,1,0:T(8,128)(2,1)S(1)}, bf16[4,17,32,384]{3,2,1,0:T(8,128)(2,1)S(1)}, u32[]{:S(2)}, u32[]{:S(2)}) collective-permute-start(bf16[4,17,32,384]{3,2,1,0:T(8,128)(2,1)S(1)} %pad_maximum_fusion.3.own_ref), channel_id=1, source_target_pairs={{0,2},{2,0},{1,3},{3,1},{4,6},{6,4},{5,7},{7,5},{8,10},{10,8},{9,1... | collective-permute-start | bytes 5013512 | tf_op jit(solution)/shard_map/ppermute | solution.py:432
  294.6 22.0 %collective-permute-start.25 = (bf16[17,32,384]{2,1,0:T(8,128)(2,1)}, bf16[17,32,384]{2,1,0:T(8,128)(2,1)}, u32[]{:S(2)}, u32[]{:S(2)}) collective-permute-start(bf16[17,32,384]{2,1,0:T(8,128)(2,1)} %get-tuple-element.290), channel_id=1, source_target_pairs={{0,4},{4,8},{8,12},{12,0},{1,5},{5,9},{9,13},{13,1},{2,6},{6,10},{... | collective-permute-start | bytes 1253384 | tf_op jit(solution)/shard_map/ppermute | solution.py:438
  294.6 36.1 %collective-permute-start.26 = (bf16[17,32,384]{2,1,0:T(8,128)(2,1)S(1)}, bf16[17,32,384]{2,1,0:T(8,128)(2,1)}, u32[]{:S(2)}, u32[]{:S(2)}) collective-permute-start(bf16[17,32,384]{2,1,0:T(8,128)(2,1)S(1)} %get-tuple-element.291), channel_id=1, source_target_pairs={{0,8},{4,12},{8,0},{12,4},{1,9},{5,13},{9,1},{13,5},{2,10},{6,14},... | collective-permute-start | bytes 1253384 | tf_op jit(solution)/shard_map/ppermute | solution.py:438
  295.8 37.3 %collective-permute-start.27 = (bf16[17,32,384]{2,1,0:T(8,128)(2,1)S(1)}, bf16[17,32,384]{2,1,0:T(8,128)(2,1)}, u32[]{:S(2)}, u32[]{:S(2)}) collective-permute-start(bf16[17,32,384]{2,1,0:T(8,128)(2,1)S(1)} %get-tuple-element.292), channel_id=1, source_target_pairs={{0,12},{4,0},{8,4},{12,8},{1,13},{5,1},{9,5},{13,9},{2,14},{6,2},{... | collective-permute-start | bytes 1253384 | tf_op jit(solution)/shard_map/ppermute | solution.py:438
  316.6 134.3 %copy-start.2 = (bf16[2,16,32,384]{3,2,1,0:T(8,128)(2,1)}, bf16[2,16,32,384]{3,2,1,0:T(8,128)(2,1)S(1)}, u32[]{:S(2)}) copy-start(bf16[2,16,32,384]{3,2,1,0:T(8,128)(2,1)S(1)} %get-tuple-element.343.refs_0_) | copy-start | bytes 2359300
  334.6 37.6 %collective-permute-start.30 = (bf16[4,17,32,384]{3,2,1,0:T(8,128)(2,1)S(1)}, bf16[4,17,32,384]{3,2,1,0:T(8,128)(2,1)S(1)}, u32[]{:S(2)}, u32[]{:S(2)}) collective-permute-start(bf16[4,17,32,384]{3,2,1,0:T(8,128)(2,1)S(1)} %pad_maximum_fusion.4.own_ref), channel_id=1, source_target_pairs={{0,2},{2,0},{1,3},{3,1},{4,6},{6,4},{5,7},{7,5},{8,10},{10,8},{9,1... | collective-permute-start | bytes 5013512 | tf_op jit(solution)/shard_map/ppermute | solution.py:432
  343.4 36.4 %copy-start.3 = (bf16[4,16,32,384]{3,2,1,0:T(8,128)(2,1)}, bf16[4,16,32,384]{3,2,1,0:T(8,128)(2,1)S(1)}, u32[]{:S(2)}) copy-start(bf16[4,16,32,384]{3,2,1,0:T(8,128)(2,1)S(1)} %get-tuple-element.322.own_ref) | copy-start | bytes 4718596
  343.4 40.3 %collective-permute-start.31 = (bf16[4,16,32,384]{3,2,1,0:T(8,128)(2,1)S(1)}, bf16[4,16,32,384]{3,2,1,0:T(8,128)(2,1)S(1)}, u32[]{:S(2)}, u32[]{:S(2)}) collective-permute-start(bf16[4,16,32,384]{3,2,1,0:T(8,128)(2,1)S(1)} %get-tuple-element.323), channel_id=1, source_target_pairs={{0,1},{1,0},{2,3},{3,2},{4,5},{5,4},{6,7},{7,6},{8,9},{9,8},{10,11... | collective-permute-start | bytes 4718600 | tf_op jit(solution)/shard_map/ppermute | solution.py:432
  379.8 23.9 %collective-permute-start.32 = (bf16[4,16,32,384]{3,2,1,0:T(8,128)(2,1)S(1)}, bf16[4,16,32,384]{3,2,1,0:T(8,128)(2,1)S(1)}, u32[]{:S(2)}, u32[]{:S(2)}) collective-permute-start(bf16[4,16,32,384]{3,2,1,0:T(8,128)(2,1)S(1)} %get-tuple-element.329), channel_id=1, source_target_pairs={{0,1},{1,0},{2,3},{3,2},{4,5},{5,4},{6,7},{7,6},{8,9},{9,8},{10,11... | collective-permute-start | bytes 4718600 | tf_op jit(solution)/shard_map/ppermute | solution.py:432
  381.2 39.7 %collective-permute-start.33 = (bf16[2,16,32,384]{3,2,1,0:T(8,128)(2,1)}, bf16[2,16,32,384]{3,2,1,0:T(8,128)(2,1)S(1)}, u32[]{:S(2)}, u32[]{:S(2)}) collective-permute-start(bf16[2,16,32,384]{3,2,1,0:T(8,128)(2,1)} %get-tuple-element.319), channel_id=1, source_target_pairs={{0,4},{4,8},{8,12},{12,0},{1,5},{5,9},{9,13},{13,1},{2,6},{6,10},{... | collective-permute-start | bytes 2359304 | tf_op jit(solution)/shard_map/ppermute | solution.py:438
  381.2 67.9 %collective-permute-start.34 = (bf16[2,16,32,384]{3,2,1,0:T(8,128)(2,1)S(1)}, bf16[2,16,32,384]{3,2,1,0:T(8,128)(2,1)S(1)}, u32[]{:S(2)}, u32[]{:S(2)}) collective-permute-start(bf16[2,16,32,384]{3,2,1,0:T(8,128)(2,1)S(1)} %get-tuple-element.320), channel_id=1, source_target_pairs={{0,8},{4,12},{8,0},{12,4},{1,9},{5,13},{9,1},{13,5},{2,10},{6,14},... | collective-permute-start | bytes 2359304 | tf_op jit(solution)/shard_map/ppermute | solution.py:438
  382.0 68.8 %collective-permute-start.35 = (bf16[2,16,32,384]{3,2,1,0:T(8,128)(2,1)S(1)}, bf16[2,16,32,384]{3,2,1,0:T(8,128)(2,1)S(1)}, u32[]{:S(2)}, u32[]{:S(2)}) collective-permute-start(bf16[2,16,32,384]{3,2,1,0:T(8,128)(2,1)S(1)} %get-tuple-element.321), channel_id=1, source_target_pairs={{0,12},{4,0},{8,4},{12,8},{1,13},{5,1},{9,5},{13,9},{2,14},{6,2},{... | collective-permute-start | bytes 2359304 | tf_op jit(solution)/shard_map/ppermute | solution.py:438
  403.7 119.3 %copy-start.1 = (bf16[2,16,32,384]{3,2,1,0:T(8,128)(2,1)}, bf16[2,16,32,384]{3,2,1,0:T(8,128)(2,1)S(1)}, u32[]{:S(2)}) copy-start(bf16[2,16,32,384]{3,2,1,0:T(8,128)(2,1)S(1)} %get-tuple-element.351.refs_1_) | copy-start | bytes 2359300
  420.8 30.5 %copy-start.8 = (bf16[2,16,32,384]{3,2,1,0:T(8,128)(2,1)}, bf16[2,16,32,384]{3,2,1,0:T(8,128)(2,1)S(1)}, u32[]{:S(2)}) copy-start(bf16[2,16,32,384]{3,2,1,0:T(8,128)(2,1)S(1)} %get-tuple-element.348) | copy-start | bytes 2359300
  420.8 30.5 %copy-start.10 = (bf16[2,16,32,384]{3,2,1,0:T(8,128)(2,1)}, bf16[2,16,32,384]{3,2,1,0:T(8,128)(2,1)S(1)}, u32[]{:S(2)}) copy-start(bf16[2,16,32,384]{3,2,1,0:T(8,128)(2,1)S(1)} %get-tuple-element.347) | copy-start | bytes 2359300
  420.8 174.5 %copy-start = (bf16[2,16,32,384]{3,2,1,0:T(8,128)(2,1)}, bf16[2,16,32,384]{3,2,1,0:T(8,128)(2,1)S(1)}, u32[]{:S(2)}) copy-start(bf16[2,16,32,384]{3,2,1,0:T(8,128)(2,1)S(1)} %get-tuple-element.356.refs_1_) | copy-start | bytes 2359300
  420.9 30.5 %copy-start.16 = (bf16[2,16,32,384]{3,2,1,0:T(8,128)(2,1)}, bf16[2,16,32,384]{3,2,1,0:T(8,128)(2,1)S(1)}, u32[]{:S(2)}) copy-start(bf16[2,16,32,384]{3,2,1,0:T(8,128)(2,1)S(1)} %collective-permute-done.33.refs_1_) | copy-start | bytes 2359300
  451.8 3.7 collective-permute-start.39
  452.2 19.3 %collective-permute-start.36 = (bf16[2,16,32,384]{3,2,1,0:T(8,128)(2,1)}, bf16[2,16,32,384]{3,2,1,0:T(8,128)(2,1)S(1)}, u32[]{:S(2)}, u32[]{:S(2)}) collective-permute-start(bf16[2,16,32,384]{3,2,1,0:T(8,128)(2,1)} %get-tuple-element.335), channel_id=1, source_target_pairs={{0,4},{4,8},{8,12},{12,0},{1,5},{5,9},{9,13},{13,1},{2,6},{6,10},{... | collective-permute-start | bytes 2359304 | tf_op jit(solution)/shard_map/ppermute | solution.py:438
  452.2 68.0 %collective-permute-start.37 = (bf16[2,16,32,384]{3,2,1,0:T(8,128)(2,1)}, bf16[2,16,32,384]{3,2,1,0:T(8,128)(2,1)}, u32[]{:S(2)}, u32[]{:S(2)}) collective-permute-start(bf16[2,16,32,384]{3,2,1,0:T(8,128)(2,1)} %get-tuple-element.336), channel_id=1, source_target_pairs={{0,8},{4,12},{8,0},{12,4},{1,9},{5,13},{9,1},{13,5},{2,10},{6,14},... | collective-permute-start | bytes 2359304 | tf_op jit(solution)/shard_map/ppermute | solution.py:438
  454.0 68.9 %collective-permute-start.38 = (bf16[2,16,32,384]{3,2,1,0:T(8,128)(2,1)}, bf16[2,16,32,384]{3,2,1,0:T(8,128)(2,1)}, u32[]{:S(2)}, u32[]{:S(2)}) collective-permute-start(bf16[2,16,32,384]{3,2,1,0:T(8,128)(2,1)} %get-tuple-element.337), channel_id=1, source_target_pairs={{0,12},{4,0},{8,4},{12,8},{1,13},{5,1},{9,5},{13,9},{2,14},{6,2},{... | collective-permute-start | bytes 2359304 | tf_op jit(solution)/shard_map/ppermute | solution.py:438
  471.6 51.5 %copy-start.15 = (bf16[2,16,32,384]{3,2,1,0:T(8,128)(2,1)}, bf16[2,16,32,384]{3,2,1,0:T(8,128)(2,1)S(1)}, u32[]{:S(2)}) copy-start(bf16[2,16,32,384]{3,2,1,0:T(8,128)(2,1)S(1)} %collective-permute-done.36.refs_2_) | copy-start | bytes 2359300
  525.6 3.7 collective-permute-start.43
  526.1 19.2 %collective-permute-start.40 = (bf16[2,16,32,384]{3,2,1,0:T(8,128)(2,1)S(1)}, bf16[2,16,32,384]{3,2,1,0:T(8,128)(2,1)}, u32[]{:S(2)}, u32[]{:S(2)}) collective-permute-start(bf16[2,16,32,384]{3,2,1,0:T(8,128)(2,1)S(1)} %copy-done.11), channel_id=1, source_target_pairs={{0,4},{4,8},{8,12},{12,0},{1,5},{5,9},{9,13},{13,1},{2,6},{6,10},{... | collective-permute-start | bytes 2359304 | tf_op jit(solution)/shard_map/ppermute | solution.py:438
  526.1 67.7 %collective-permute-start.41 = (bf16[2,16,32,384]{3,2,1,0:T(8,128)(2,1)S(1)}, bf16[2,16,32,384]{3,2,1,0:T(8,128)(2,1)}, u32[]{:S(2)}, u32[]{:S(2)}) collective-permute-start(bf16[2,16,32,384]{3,2,1,0:T(8,128)(2,1)S(1)} %copy-done.9), channel_id=1, source_target_pairs={{0,8},{4,12},{8,0},{12,4},{1,9},{5,13},{9,1},{13,5},{2,10},{6,14},... | collective-permute-start | bytes 2359304 | tf_op jit(solution)/shard_map/ppermute | solution.py:438
  526.7 68.6 %collective-permute-start.42 = (bf16[2,16,32,384]{3,2,1,0:T(8,128)(2,1)S(1)}, bf16[2,16,32,384]{3,2,1,0:T(8,128)(2,1)}, u32[]{:S(2)}, u32[]{:S(2)}) collective-permute-start(bf16[2,16,32,384]{3,2,1,0:T(8,128)(2,1)S(1)} %get-tuple-element.349), channel_id=1, source_target_pairs={{0,12},{4,0},{8,4},{12,8},{1,13},{5,1},{9,5},{13,9},{2,14},{6,2},{... | collective-permute-start | bytes 2359304 | tf_op jit(solution)/shard_map/ppermute | solution.py:438
  598.8 3.6 collective-permute-start.44
  (28 other events, 86.0 us)

commit v3 on v2

--- a/solution.py
+++ b/solution.py
@@ -19,7 +19,7 @@
 norm_epsilon = 1e-05
 
 COST_SHARE = 1
-LATE_SHARE = 8
+LATE_SHARE = 1
 
 BF = jnp.bfloat16
 F32 = jnp.float32
@@ -319,12 +319,13 @@
     low, high = total[:, :width], total[:, width:]
     mine = jnp.where(flip, high, low).reshape(rows, cols, width)
     sent = jnp.where(flip, low, high).reshape(rows, cols, width)
-    for s, ref in enumerate(out_refs):
+    lon_count = len(out_refs) // 2
+    for s in range(lon_count):
 
         @pl.when(pl.program_id(0) == s)
         def _():
-            ref[0] = mine
-            ref[1] = sent
+            out_refs[s][...] = mine
+            out_refs[lon_count + s][...] = sent
 
 
 def mlp(where, own, other, gain, bias, w_in, b_in, w_out, b_out):
@@ -334,17 +335,17 @@
         (1, rows, cols, width), lambda i, where: (lax.rem(where[0] + i, lon_count), 0, 0, 0)
     )
     cells = lon_count * rows * cols
-    return pl.pallas_call(
+    out = pl.pallas_call(
         mlp_kernel,
         grid_spec=pltpu.PrefetchScalarGridSpec(
             num_scalar_prefetch=1,
             grid=(lon_count,),
             in_specs=[cell_spec, cell_spec]
             + [whole(a) for a in (gain, bias, w_in, b_in, w_out, b_out)],
-            out_specs=[pl.BlockSpec((2, rows, cols, width), lambda i, where: (0, 0, 0, 0))]
-            * lon_count,
+            out_specs=[pl.BlockSpec((rows, cols, width), lambda i, where: (0, 0, 0))]
+            * (2 * lon_count),
         ),
-        out_shape=[jax.ShapeDtypeStruct((2, rows, cols, width), BF)] * lon_count,
+        out_shape=[jax.ShapeDtypeStruct((rows, cols, width), BF)] * (2 * lon_count),
         compiler_params=pltpu.CompilerParams(vmem_limit_bytes=48 << 20),
         cost_estimate=pl.CostEstimate(
             flops=4 * cells * w_in.size // LATE_SHARE,
@@ -353,39 +354,41 @@
         ),
         name="channel_mlp",
     )(where, own, other, gain, bias, w_in, b_in, w_out, b_out)
-
-
-def assemble_kernel(where_ref, their_ref, *refs):
-    my_refs, out_ref = refs[:-1], refs[-1]
-    half = their_ref.shape[1]
+    return out[:lon_count], out[lon_count:]
+
+
+def assemble_kernel(where_ref, *refs):
+    lon_count = (len(refs) - 1) // 2
+    out_ref = refs[-1]
+    half = refs[0].shape[0]
     flip = where_ref[1] == 1
-    for s, ref in enumerate(my_refs):
+    for s in range(lon_count):
 
         @pl.when(pl.program_id(0) == s)
         def _():
-            mine, theirs = ref[0], their_ref[0]
+            mine, theirs = refs[s][...], refs[lon_count + s][...]
             out_ref[:half] = jnp.where(flip, theirs, mine)
             out_ref[half:] = jnp.where(flip, mine, theirs)
 
 
 def assemble(where, result, mine, theirs, first_col, block_cols):
-    lon_count, rows, cols, width = theirs.shape
+    lon_count = len(mine)
+    rows, cols, width = mine[0].shape
     block = math.gcd(math.gcd(cols, block_cols), first_col)
     steps = cols // block
 
     def piece(s):
         def index(g, j, where):
-            return 0, 0, jnp.where(g == s, j, jnp.where(g < s, 0, steps - 1)), 0
-
-        return pl.BlockSpec((1, rows, block, width), index)
+            return 0, jnp.where(g == s, j, jnp.where(g < s, 0, steps - 1)), 0
+
+        return pl.BlockSpec((rows, block, width), index)
 
     def place(g, j, where):
         source = lax.rem(where[0] + (lon_count - g), lon_count)
         return 0, source * (block_cols // block) + first_col // block + j, 0
 
-    specs = [pl.BlockSpec((1, rows, block, width), lambda g, j, where: (g, 0, j, 0))]
-    specs += [piece(s) for s in range(lon_count)]
-    operands = [where, theirs, *mine]
+    specs = [piece(s) for s in range(lon_count)] * 2
+    operands = [where, *mine, *theirs]
     aliases = {}
     kernel = assemble_kernel
     if result is not None:
@@ -407,7 +410,7 @@
         out_shape=jax.ShapeDtypeStruct((2 * rows, lon_count * block_cols, width), BF),
         input_output_aliases=aliases,
         cost_estimate=pl.CostEstimate(
-            flops=0, bytes_accessed=8 * lon_count * rows * cols * width, transcendentals=0
+            flops=0, bytes_accessed=8 * lon_count * rows * cols * width // COST_SHARE, transcendentals=0
         ),
         name="assemble",
     )(*operands)
@@ -436,6 +439,19 @@
     if steps == 0:
         return values
     return lax.ppermute(values, "lon", [(z, (z + steps) % lon_count) for z in range(lon_count)])
+
+
+def shift_across(values, steps, lon_count):
+    pairs = [
+        (z * 2 + c, (z + steps) % lon_count * 2 + 1 - c)
+        for z in range(lon_count)
+        for c in range(2)
+    ]
+    return lax.ppermute(values, ("lon", "ch"), pairs)
+
+
+def after(value, *others):
+    return lax.optimization_barrier((value,) + others)[0]
 
 
 def column_plan(
@@ -537,9 +553,13 @@
         mine, sent = lat_inverse(where, own, other, inverse_lat, patches, starts[i])
         return mlp(where, mine, swap(sent, "ch"), *weights)
 
-    def placed(result, i, pieces):
-        theirs = swap(jnp.stack([piece[1] for piece in pieces]), "ch")
-        return assemble(where, result, pieces, theirs, starts[i], cols)
+    def outward(outputs):
+        mine, sent = outputs
+        return (
+            along_lon(mine),
+            [shift_across(values, s, lon_count) for s, values in enumerate(sent)],
+        )
+
 
     received, summed, sent, kept = [], None, None, None
     weights = None
@@ -586,19 +606,19 @@
     pieces = None
     for i in range(chunks):
         last = pieces
-        pieces = along_lon(outputs[i])
+        pieces = outward(outputs[i])
         if last is not None:
-            result = placed(result, i - 1, last)
-        for later in (i + 1, i + 2):
-            if later < chunks and outputs[later] is None:
-                if others[later] is None:
-                    owns[later] = jnp.stack(owns[later])
-                    others[later] = swap(owns[later], "lat")
-                outputs[later] = row_result(later, owns[later], others[later])
+            result = assemble(where, result, *last, starts[i - 1], cols)
+        if i + 1 < chunks and outputs[i + 1] is None:
+            own, _ = fence((owns[i + 1], pieces[0][1]))
+            outputs[i + 1] = row_result(i + 1, own, others[i + 1])
+        if i + 2 < chunks and others[i + 2] is None:
+            owns[i + 2] = jnp.stack(owns[i + 2])
+            others[i + 2] = swap(owns[i + 2], "lat")
         patches, owns, others, outputs, pieces, result = fence(
             (patches, owns, others, outputs, pieces, result)
         )
-    result = placed(result, chunks - 1, pieces)
+    result = assemble(where, result, *pieces, starts[chunks - 1], cols)
     return result.reshape(1, 1, rows // lon_count, lon_count * cols, width)
 
 

time: 617 us -> 591 us (0.958)
  waiting for transfers between devices: 373 us -> 344 us
  starting transfers between devices: 42.6 us -> 56.7 us
  local copies, waits for them, and re-layouts: 26.3 us -> 19.7 us
    ppermute x0 -> x12, waiting for transfers between devices: none -> 51.1 us  [shift_across(): return lax.ppermute(values, ('lon', 'ch'), pairs)]
    ppermute x27, waiting for transfers between devices: 316 us -> 268 us  [shift(): lax.ppermute(values, 'lon', [(z, (z + steps) % lon_count) for z in range(...]
    ppermute x18 -> x15, waiting for transfers between devices: 57.3 us -> 25 us  [swap(): return lax.ppermute(values, axis, [(0, 1), (1, 0)])]
    ppermute x0 -> x12, starting transfers between devices: none -> 17.2 us  [shift_across(): return lax.ppermute(values, ('lon', 'ch'), pairs)]
    ppermute x18 -> x15, starting transfers between devices: 15.9 us -> 14.7 us  [swap(): return lax.ppermute(values, axis, [(0, 1), (1, 0)])]
  transfers between devices with their start and end apart: 45 -> 54, of which waited for: 29 -> 34; matrix products, arithmetic and copies ran while one was open for 6% -> 6% of each run, Pallas kernels for 14% -> 12%
where the time goes in v3:
time: 591 us; the launch traced here: 583 us
  waiting for transfers between devices  344 us (58%)
  Pallas kernels  121 us (20%)
  starting transfers between devices  56.7 us (10%)
  other arithmetic  38.2 us (6%)
  local copies, waits for them, and re-layouts  19.7 us (3%)
    ppermute x27, waiting for transfers between devices, shift(): lax.ppermute(values, 'lon', [(z, (z + steps) % lon_count) for z in range(...  268 us
    ppermute x12, waiting for transfers between devices, shift_across(): return lax.ppermute(values, ('lon', 'ch'), pairs)  51.1 us
    pallas_call x3, Pallas kernels, mlp(): pl.pallas_call(mlp_kernel, grid_spec=pltpu.PrefetchScalarGridSpec(num_sca...  50.8 us
    ppermute x15, waiting for transfers between devices, swap(): return lax.ppermute(values, axis, [(0, 1), (1, 0)])  25 us
    ppermute x27, starting transfers between devices, shift(): lax.ppermute(values, 'lon', [(z, (z + steps) % lon_count) for z in range(...  24.8 us
    pallas_call x3, Pallas kernels, lat_inverse(): pl.pallas_call(lat_inverse_kernel, grid_spec=pltpu.PrefetchScalarGridSpec...  23.2 us
    ppermute x12, starting transfers between devices, shift_across(): return lax.ppermute(values, ('lon', 'ch'), pairs)  17.2 us
    pallas_call x3, Pallas kernels, lat_forward(): pl.pallas_call(lat_forward_kernel, grid_spec=pltpu.PrefetchScalarGridSpec...  16.6 us
  transfers between devices with their start and end apart: 54, of which 34 were waited for; matrix products, arithmetic and copies ran while one was open for 6% of the time, Pallas kernels for 12%

profile of v3, /device:TPU:9, one launch (start us, length us, event | category | flops | bytes accessed | tf_op | source)
XLA Modules:
  0.0 582.7 jit_solution(15219754793414970624)
XLA Ops:
  0.0 2.5 convert_reduce_fusion.2
  2.6 2.9 fusion.1
  7.3 3.8 fusion.5.cells_ref
  11.1 5.8 lat_forward.3
  22.1 3.6 fusion.11.cells_ref
  25.8 2.3 copy-done.12
  28.0 5.1 lat_forward.4
  33.2 22.5 %collective-permute-done.1 = bf16[4,17,32,384]{3,2,1,0:T(8,128)(2,1)} collective-permute-done((bf16[4,17,32,384]{3,2,1,0:T(8,128)(2,1)}, bf16[4,17,32,384]{3,2,1,0:T(8,128)(2,1)}, u32[]{:S(2)}, u32[]{:S(2)}) %collective-permute-start.1) | collective-permute-done | bytes 1671200 | tf_op jit(solution)/shard_map/ppermute | solution.py:435
  57.6 1.6 fusion.13
  60.7 1.8 fusion.21
  66.5 1.7 fusion.17.cells_ref
  68.2 5.8 lat_forward.5
  74.0 25.8 %collective-permute-done.6.refs_2_.refs_14_ = bf16[17,32,384]{2,1,0:T(8,128)(2,1)} collective-permute-done((bf16[17,32,384]{2,1,0:T(8,128)(2,1)S(1)}, bf16[17,32,384]{2,1,0:T(8,128)(2,1)}, u32[]{:S(2)}, u32[]{:S(2)}) %collective-permute-start.6) | collective-permute-done | bytes 417824 | tf_op jit(solution)/shard_map/ppermute | solution.py:441
  99.8 2.2 collective-permute-done.7.refs_3_.refs_15_
  104.6 3.0 fusion.25
  118.3 2.3 maximum_maximum_fusion.refs_26_
  120.6 2.3 maximum_maximum_fusion.1.refs_28_
  122.8 12.4 %collective-permute-done.10.refs_6_.refs_18_ = bf16[17,32,384]{2,1,0:T(8,128)(2,1)} collective-permute-done((bf16[17,32,384]{2,1,0:T(8,128)(2,1)}, bf16[17,32,384]{2,1,0:T(8,128)(2,1)}, u32[]{:S(2)}, u32[]{:S(2)}) %collective-permute-start.10) | collective-permute-done | bytes 417824 | tf_op jit(solution)/shard_map/ppermute | solution.py:441
  135.2 7.9 %collective-permute-done.11.refs_7_.refs_19_ = bf16[17,32,384]{2,1,0:T(8,128)(2,1)} collective-permute-done((bf16[17,32,384]{2,1,0:T(8,128)(2,1)}, bf16[17,32,384]{2,1,0:T(8,128)(2,1)}, u32[]{:S(2)}, u32[]{:S(2)}) %collective-permute-start.11) | collective-permute-done | bytes 417824 | tf_op jit(solution)/shard_map/ppermute | solution.py:441
  145.3 2.5 fusion.29
  147.8 2.2 collective-permute-start.12
  150.1 1.8 all-gather
  153.2 1.6 pad_maximum_fusion.1.w_out_ref
  154.8 1.6 pad_maximum_fusion.w_in_ref
  156.4 20.5 %collective-permute-done.12.refs_9_.refs_21_ = bf16[17,32,384]{2,1,0:T(8,128)(2,1)S(1)} collective-permute-done((bf16[17,32,384]{2,1,0:T(8,128)(2,1)S(1)}, bf16[17,32,384]{2,1,0:T(8,128)(2,1)S(1)}, u32[]{:S(2)}, u32[]{:S(2)}) %collective-permute-start.12) | collective-permute-done | bytes 417824 | tf_op jit(solution)/shard_map/ppermute | solution.py:441
  176.8 9.1 %collective-permute-done.13.refs_10_.refs_22_ = bf16[17,32,384]{2,1,0:T(8,128)(2,1)S(1)} collective-permute-done((bf16[17,32,384]{2,1,0:T(8,128)(2,1)S(1)}, bf16[17,32,384]{2,1,0:T(8,128)(2,1)S(1)}, u32[]{:S(2)}, u32[]{:S(2)}) %collective-permute-start.13) | collective-permute-done | bytes 417824 | tf_op jit(solution)/shard_map/ppermute | solution.py:441
  186.8 16.5 %modes.1 = (bf16[17,32,384]{2,1,0:T(8,128)(2,1)S(1)}, bf16[17,32,384]{2,1,0:T(8,128)(2,1)S(1)}, bf16[17,32,384]{2,1,0:T(8,128)(2,1)S(1)}, bf16[17,32,384]{2,1,0:...) custom-call(s32[1]{0:T(128)} %bitcast.23.first_pair_ref, ...), custom_call_target="tpu_custom_call" | custom-call | flops 7247757312 | bytes 10027008 | tf_op jit(solution)/shard_map/modes/pallas_call | solution.py:276
  203.4 3.1 collective-permute-start.19
  208.0 5.8 collective-permute-done.18
  213.7 25.0 %collective-permute-done.19 = bf16[17,32,384]{2,1,0:T(8,128)(2,1)S(1)} collective-permute-done((bf16[17,32,384]{2,1,0:T(8,128)(2,1)S(1)}, bf16[17,32,384]{2,1,0:T(8,128)(2,1)S(1)}, u32[]{:S(2)}, u32[]{:S(2)}) %collective-permute-start.19) | collective-permute-done | bytes 417824 | tf_op jit(solution)/shard_map/ppermute | solution.py:441
  238.7 4.8 collective-permute-done.20
  245.1 1.7 collective-permute-start.23
  246.7 8.7 %collective-permute-done.21 = bf16[17,32,384]{2,1,0:T(8,128)(2,1)S(1)} collective-permute-done((bf16[17,32,384]{2,1,0:T(8,128)(2,1)S(1)}, bf16[17,32,384]{2,1,0:T(8,128)(2,1)S(1)}, u32[]{:S(2)}, u32[]{:S(2)}) %collective-permute-start.21) | collective-permute-done | bytes 417824 | tf_op jit(solution)/shard_map/ppermute | solution.py:441
  255.5 25.0 %collective-permute-done.22 = bf16[17,32,384]{2,1,0:T(8,128)(2,1)S(1)} collective-permute-done((bf16[17,32,384]{2,1,0:T(8,128)(2,1)S(1)}, bf16[17,32,384]{2,1,0:T(8,128)(2,1)S(1)}, u32[]{:S(2)}, u32[]{:S(2)}) %collective-permute-start.22) | collective-permute-done | bytes 417824 | tf_op jit(solution)/shard_map/ppermute | solution.py:441
  281.4 7.5 %lat_inverse.3 = (bf16[4,16,32,384]{3,2,1,0:T(8,128)(2,1)S(1)}, bf16[4,16,32,384]{3,2,1,0:T(8,128)(2,1)S(1)}) custom-call(s32[3]{0:T(128)S(1)} %pad_add_fusion.where_ref, bf16[4,17,32,384]{3,2,1,0:T(8,128)(2,1)S(1)} %pad_maximum_fusion.2.own_ref, bf16[4,17,32,384]{3,2,1,0:T(8,128)(2,1)S(1)} %collective-permute-done.24.other_ref, ...), custom_call_target="tpu_custom_call" | custom-call | flops 3623878656 | bytes 9437184 | tf_op jit(solution)/shard_map/lat_inverse/pallas_call | solution.py:160
  296.8 16.8 %channel_mlp.3 = (bf16[16,32,384]{2,1,0:T(8,128)(2,1)S(1)}, bf16[16,32,384]{2,1,0:T(8,128)(2,1)S(1)}, bf16[16,32,384]{2,1,0:T(8,128)(2,1)S(1)}, bf16[16,32,384]{...) custom-call(s32[3]{0:T(128)S(1)} %pad_add_fusion.where_ref, ...), custom_call_target="tpu_custom_call" | custom-call | flops 9663676416 | bytes 6291456 | tf_op jit(solution)/shard_map/channel_mlp/pallas_call | solution.py:338
  314.3 14.6 %collective-permute-done.26 = bf16[17,32,384]{2,1,0:T(8,128)(2,1)S(1)} collective-permute-done((bf16[17,32,384]{2,1,0:T(8,128)(2,1)S(1)}, bf16[17,32,384]{2,1,0:T(8,128)(2,1)S(1)}, u32[]{:S(2)}, u32[]{:S(2)}) %collective-permute-start.26) | collective-permute-done | bytes 417824 | tf_op jit(solution)/shard_map/ppermute | solution.py:441
  328.9 2.4 collective-permute-done.27
  331.2 10.2 %collective-permute-done.31.refs_1_ = bf16[16,32,384]{2,1,0:T(8,128)(2,1)S(1)} collective-permute-done((bf16[16,32,384]{2,1,0:T(8,128)(2,1)S(1)}, bf16[16,32,384]{2,1,0:T(8,128)(2,1)S(1)}, u32[]{:S(2)}, u32[]{:S(2)}) %collective-permute-start.31) | collective-permute-done | bytes 393248 | tf_op jit(solution)/shard_map/ppermute | solution.py:441
  341.4 7.5 %lat_inverse.4 = (bf16[4,16,32,384]{3,2,1,0:T(8,128)(2,1)S(1)}, bf16[4,16,32,384]{3,2,1,0:T(8,128)(2,1)S(1)}) custom-call(s32[3]{0:T(128)S(1)} %pad_add_fusion.where_ref, bf16[4,17,32,384]{3,2,1,0:T(8,128)(2,1)S(1)} %pad_maximum_fusion.3.own_ref, bf16[4,17,32,384]{3,2,1,0:T(8,128)(2,1)S(1)} %collective-permute-done.28.other_ref, ...), custom_call_target="tpu_custom_call" | custom-call | flops 3623878656 | bytes 9437184 | tf_op jit(solution)/shard_map/lat_inverse/pallas_call | solution.py:160
  355.3 22.5 %collective-permute-done.33.refs_2_ = bf16[16,32,384]{2,1,0:T(8,128)(2,1)S(1)} collective-permute-done((bf16[16,32,384]{2,1,0:T(8,128)(2,1)S(1)}, bf16[16,32,384]{2,1,0:T(8,128)(2,1)S(1)}, u32[]{:S(2)}, u32[]{:S(2)}) %collective-permute-start.33) | collective-permute-done | bytes 393248 | tf_op jit(solution)/shard_map/ppermute | solution.py:441
  379.0 3.2 collective-permute-start.37
  382.2 1.9 collective-permute-start.38
  385.6 16.8 %channel_mlp.4 = (bf16[16,32,384]{2,1,0:T(8,128)(2,1)S(1)}, bf16[16,32,384]{2,1,0:T(8,128)(2,1)S(1)}, bf16[16,32,384]{2,1,0:T(8,128)(2,1)}, bf16[16,32,384]{2,1,...) custom-call(s32[3]{0:T(128)S(1)} %pad_add_fusion.where_ref, ...), custom_call_target="tpu_custom_call" | custom-call | flops 9663676416 | bytes 6291456 | tf_op jit(solution)/shard_map/channel_mlp/pallas_call | solution.py:338
  403.1 7.8 %collective-permute-done.37.refs_6_ = bf16[16,32,384]{2,1,0:T(8,128)(2,1)S(1)} collective-permute-done((bf16[16,32,384]{2,1,0:T(8,128)(2,1)S(1)}, bf16[16,32,384]{2,1,0:T(8,128)(2,1)S(1)}, u32[]{:S(2)}, u32[]{:S(2)}) %collective-permute-start.37) | collective-permute-done | bytes 393248 | tf_op jit(solution)/shard_map/ppermute | solution.py:450
  410.9 13.6 %collective-permute-done.38.refs_7_ = bf16[16,32,384]{2,1,0:T(8,128)(2,1)S(1)} collective-permute-done((bf16[16,32,384]{2,1,0:T(8,128)(2,1)S(1)}, bf16[16,32,384]{2,1,0:T(8,128)(2,1)S(1)}, u32[]{:S(2)}, u32[]{:S(2)}) %collective-permute-start.38) | collective-permute-done | bytes 393248 | tf_op jit(solution)/shard_map/ppermute | solution.py:450
  424.5 10.3 %collective-permute-done.39.refs_1_ = bf16[16,32,384]{2,1,0:T(8,128)(2,1)S(1)} collective-permute-done((bf16[16,32,384]{2,1,0:T(8,128)(2,1)S(1)}, bf16[16,32,384]{2,1,0:T(8,128)(2,1)S(1)}, u32[]{:S(2)}, u32[]{:S(2)}) %collective-permute-start.39) | collective-permute-done | bytes 393248 | tf_op jit(solution)/shard_map/ppermute | solution.py:441
  434.8 8.2 %lat_inverse.5 = (bf16[4,16,32,384]{3,2,1,0:T(8,128)(2,1)S(1)}, bf16[4,16,32,384]{3,2,1,0:T(8,128)(2,1)}) custom-call(s32[3]{0:T(128)S(1)} %pad_add_fusion.where_ref, bf16[4,17,32,384]{3,2,1,0:T(8,128)(2,1)S(1)} %pad_maximum_fusion.4.own_ref, bf16[4,17,32,384]{3,2,1,0:T(8,128)(2,1)S(1)} %collective-permute-done.30.other_ref, ...), custom_call_target="tpu_custom_call" | custom-call | flops 3623878656 | bytes 9437184 | tf_op jit(solution)/shard_map/lat_inverse/pallas_call | solution.py:160
  447.4 4.7 assemble.3.refs_8_
  452.1 19.4 %collective-permute-done.41.refs_2_ = bf16[16,32,384]{2,1,0:T(8,128)(2,1)} collective-permute-done((bf16[16,32,384]{2,1,0:T(8,128)(2,1)}, bf16[16,32,384]{2,1,0:T(8,128)(2,1)}, u32[]{:S(2)}, u32[]{:S(2)}) %collective-permute-start.41) | collective-permute-done | bytes 393248 | tf_op jit(solution)/shard_map/ppermute | solution.py:441
  471.4 3.7 collective-permute-start.45
  475.2 17.2 %channel_mlp.5 = (bf16[16,32,384]{2,1,0:T(8,128)(2,1)S(1)}, bf16[16,32,384]{2,1,0:T(8,128)(2,1)S(1)}, bf16[16,32,384]{2,1,0:T(8,128)(2,1)S(1)}, bf16[16,32,384]{...) custom-call(s32[3]{0:T(128)S(1)} %copy-done.4, ...), custom_call_target="tpu_custom_call" | custom-call | flops 9663676416 | bytes 6291456 | tf_op jit(solution)/shard_map/channel_mlp/pallas_call | solution.py:338
  493.2 3.4 collective-permute-done.44.refs_5_
  496.6 8.4 %collective-permute-done.45.refs_6_ = bf16[16,32,384]{2,1,0:T(8,128)(2,1)S(1)} collective-permute-done((bf16[16,32,384]{2,1,0:T(8,128)(2,1)S(1)}, bf16[16,32,384]{2,1,0:T(8,128)(2,1)S(1)}, u32[]{:S(2)}, u32[]{:S(2)}) %collective-permute-start.45) | collective-permute-done | bytes 393248 | tf_op jit(solution)/shard_map/ppermute | solution.py:450
  506.1 2.2 collective-permute-start.48
  510.9 5.6 collective-permute-done.47.refs_1_
  516.5 5.2 collective-permute-start.52
  521.7 18.2 %collective-permute-done.48.refs_2_ = bf16[16,32,384]{2,1,0:T(8,128)(2,1)S(1)} collective-permute-done((bf16[16,32,384]{2,1,0:T(8,128)(2,1)S(1)}, bf16[16,32,384]{2,1,0:T(8,128)(2,1)S(1)}, u32[]{:S(2)}, u32[]{:S(2)}) %collective-permute-start.48) | collective-permute-done | bytes 393248 | tf_op jit(solution)/shard_map/ppermute | solution.py:441
  540.0 4.7 assemble.4.refs_8_
  544.7 15.3 %collective-permute-done.49.refs_3_ = bf16[16,32,384]{2,1,0:T(8,128)(2,1)S(1)} collective-permute-done((bf16[16,32,384]{2,1,0:T(8,128)(2,1)}, bf16[16,32,384]{2,1,0:T(8,128)(2,1)S(1)}, u32[]{:S(2)}, u32[]{:S(2)}) %collective-permute-start.49) | collective-permute-done | bytes 393248 | tf_op jit(solution)/shard_map/ppermute | solution.py:441
  560.0 5.4 collective-permute-done.51.refs_5_
  565.3 8.4 %collective-permute-done.52.refs_6_ = bf16[16,32,384]{2,1,0:T(8,128)(2,1)S(1)} collective-permute-done((bf16[16,32,384]{2,1,0:T(8,128)(2,1)}, bf16[16,32,384]{2,1,0:T(8,128)(2,1)S(1)}, u32[]{:S(2)}, u32[]{:S(2)}) %collective-permute-start.52) | collective-permute-done | bytes 393248 | tf_op jit(solution)/shard_map/ppermute | solution.py:450
  573.7 3.1 collective-permute-done.53.refs_7_
  577.6 4.7 assemble.5
  (230 shorter events, 63.9 us)
Async XLA Ops:
  5.5 1.7 collective-permute-start
  6.5 428.3 %copy-start.3 = (s32[3]{0:T(128)}, s32[3]{0:T(128)S(1)}, u32[]{:S(2)}) copy-start(s32[3]{0:T(128)S(1)} %pad_add_fusion.where_ref) | copy-start | bytes 40
  17.5 38.1 %collective-permute-start.1 = (bf16[4,17,32,384]{3,2,1,0:T(8,128)(2,1)}, bf16[4,17,32,384]{3,2,1,0:T(8,128)(2,1)}, u32[]{:S(2)}, u32[]{:S(2)}) collective-permute-start(bf16[4,17,32,384]{3,2,1,0:T(8,128)(2,1)} %get-tuple-element.224), channel_id=1, source_target_pairs={{0,2},{2,0},{1,3},{3,1},{4,6},{6,4},{5,7},{7,5},{8,10},{10,8},{9,1... | collective-permute-start | bytes 5013512 | tf_op jit(solution)/shard_map/ppermute | solution.py:435
  20.4 1.7 collective-permute-start.2
  56.3 45.7 %collective-permute-start.3 = (bf16[4,17,32,384]{3,2,1,0:T(8,128)(2,1)S(1)}, bf16[4,17,32,384]{3,2,1,0:T(8,128)(2,1)}, u32[]{:S(2)}, u32[]{:S(2)}) collective-permute-start(bf16[4,17,32,384]{3,2,1,0:T(8,128)(2,1)S(1)} %get-tuple-element.233), channel_id=1, source_target_pairs={{0,2},{2,0},{1,3},{3,1},{4,6},{6,4},{5,7},{7,5},{8,10},{10,8},{9,1... | collective-permute-start | bytes 5013512 | tf_op jit(solution)/shard_map/ppermute | solution.py:435
  59.2 7.3 %collective-permute-start.4 = (f32[2,128,32]{2,1,0:T(8,128)S(1)}, f32[2,128,32]{2,1,0:T(8,128)S(1)}, u32[]{:S(2)}, u32[]{:S(2)}) collective-permute-start(f32[2,128,32]{2,1,0:T(8,128)S(1)} %pad_maximum_fusion.7), channel_id=1, source_target_pairs={{0,1},{1,0},{2,3},{3,2},{4,5},{5,4},{6,7},{7,6},{8,9},{9,8},{10,11... | collective-permute-start | bytes 98312 | tf_op jit(solution)/shard_map/ppermute | solution.py:435
  62.5 11.5 %collective-permute-start.5 = (bf16[17,32,384]{2,1,0:T(8,128)(2,1)S(1)}, bf16[17,32,384]{2,1,0:T(8,128)(2,1)S(1)}, u32[]{:S(2)}, u32[]{:S(2)}) collective-permute-start(bf16[17,32,384]{2,1,0:T(8,128)(2,1)S(1)} %get-tuple-element.445), channel_id=1, source_target_pairs={{0,4},{4,8},{8,12},{12,0},{1,5},{5,9},{9,13},{13,1},{2,6},{6,10},{... | collective-permute-start | bytes 1253384 | tf_op jit(solution)/shard_map/ppermute | solution.py:441
  63.8 35.9 %collective-permute-start.6 = (bf16[17,32,384]{2,1,0:T(8,128)(2,1)S(1)}, bf16[17,32,384]{2,1,0:T(8,128)(2,1)}, u32[]{:S(2)}, u32[]{:S(2)}) collective-permute-start(bf16[17,32,384]{2,1,0:T(8,128)(2,1)S(1)} %get-tuple-element.444), channel_id=1, source_target_pairs={{0,8},{4,12},{8,0},{12,4},{1,9},{5,13},{9,1},{13,5},{2,10},{6,14},... | collective-permute-start | bytes 1253384 | tf_op jit(solution)/shard_map/ppermute | solution.py:441
  64.9 37.1 %collective-permute-start.7 = (bf16[17,32,384]{2,1,0:T(8,128)(2,1)S(1)}, bf16[17,32,384]{2,1,0:T(8,128)(2,1)}, u32[]{:S(2)}, u32[]{:S(2)}) collective-permute-start(bf16[17,32,384]{2,1,0:T(8,128)(2,1)S(1)} %get-tuple-element.443), channel_id=1, source_target_pairs={{0,12},{4,0},{8,4},{12,8},{1,13},{5,1},{9,5},{13,9},{2,14},{6,2},{... | collective-permute-start | bytes 1253384 | tf_op jit(solution)/shard_map/ppermute | solution.py:441
  68.2 34.1 %copy-start.35 = (bf16[2,4,96,96]{3,2,1,0:T(8,128)(2,1)S(1)}, bf16[2,4,96,96]{3,2,1,0:T(8,128)(2,1)}, u32[]{:S(2)}) copy-start(bf16[2,4,96,96]{3,2,1,0:T(8,128)(2,1)} %param.24) | copy-start | bytes 442372
  68.2 34.1 %copy-start.36 = (bf16[2,4,96,96]{3,2,1,0:T(8,128)(2,1)S(1)}, bf16[2,4,96,96]{3,2,1,0:T(8,128)(2,1)}, u32[]{:S(2)}) copy-start(bf16[2,4,96,96]{3,2,1,0:T(8,128)(2,1)} %param.22) | copy-start | bytes 442372
  102.0 42.2 %collective-permute-start.8 = (bf16[4,17,32,384]{3,2,1,0:T(8,128)(2,1)}, bf16[4,17,32,384]{3,2,1,0:T(8,128)(2,1)}, u32[]{:S(2)}, u32[]{:S(2)}) collective-permute-start(bf16[4,17,32,384]{3,2,1,0:T(8,128)(2,1)} %get-tuple-element.244), channel_id=1, source_target_pairs={{0,2},{2,0},{1,3},{3,1},{4,6},{6,4},{5,7},{7,5},{8,10},{10,8},{9,1... | collective-permute-start | bytes 5013512 | tf_op jit(solution)/shard_map/ppermute | solution.py:435
  107.5 27.7 %collective-permute-start.10 = (bf16[17,32,384]{2,1,0:T(8,128)(2,1)}, bf16[17,32,384]{2,1,0:T(8,128)(2,1)}, u32[]{:S(2)}, u32[]{:S(2)}) collective-permute-start(bf16[17,32,384]{2,1,0:T(8,128)(2,1)} %get-tuple-element.440), channel_id=1, source_target_pairs={{0,8},{4,12},{8,0},{12,4},{1,9},{5,13},{9,1},{13,5},{2,10},{6,14},... | collective-permute-start | bytes 1253384 | tf_op jit(solution)/shard_map/ppermute | solution.py:441
  108.5 34.6 %collective-permute-start.11 = (bf16[17,32,384]{2,1,0:T(8,128)(2,1)}, bf16[17,32,384]{2,1,0:T(8,128)(2,1)}, u32[]{:S(2)}, u32[]{:S(2)}) collective-permute-start(bf16[17,32,384]{2,1,0:T(8,128)(2,1)} %get-tuple-element.439), channel_id=1, source_target_pairs={{0,12},{4,0},{8,4},{12,8},{1,13},{5,1},{9,5},{13,9},{2,14},{6,2},{... | collective-permute-start | bytes 1253384 | tf_op jit(solution)/shard_map/ppermute | solution.py:441
  108.5 35.7 %collective-permute-start.9 = (bf16[17,32,384]{2,1,0:T(8,128)(2,1)}, bf16[17,32,384]{2,1,0:T(8,128)(2,1)}, u32[]{:S(2)}, u32[]{:S(2)}) collective-permute-start(bf16[17,32,384]{2,1,0:T(8,128)(2,1)} %get-tuple-element.441), channel_id=1, source_target_pairs={{0,4},{4,8},{8,12},{12,0},{1,5},{5,9},{9,13},{13,1},{2,6},{6,10},{... | collective-permute-start | bytes 1253384 | tf_op jit(solution)/shard_map/ppermute | solution.py:441
  144.2 9.0 %collective-permute-start.17 = (bf16[768,768]{1,0:T(8,128)(2,1)S(1)}, bf16[768,768]{1,0:T(8,128)(2,1)S(1)}, u32[]{:S(2)}, u32[]{:S(2)}) collective-permute-start(bf16[768,768]{1,0:T(8,128)(2,1)S(1)} %copy-done.16), channel_id=1, source_target_pairs={{0,1},{1,0},{2,3},{3,2},{4,5},{5,4},{6,7},{7,6},{8,9},{9,8},{10,11... | collective-permute-start | bytes 3538952 | tf_op jit(solution)/shard_map/ppermute | solution.py:435
  144.7 10.1 %collective-permute-start.15 = (bf16[768,768]{1,0:T(8,128)(2,1)S(1)}, bf16[768,768]{1,0:T(8,128)(2,1)S(1)}, u32[]{:S(2)}, u32[]{:S(2)}) collective-permute-start(bf16[768,768]{1,0:T(8,128)(2,1)S(1)} %copy-done.17), channel_id=1, source_target_pairs={{0,1},{1,0},{2,3},{3,2},{4,5},{5,4},{6,7},{7,6},{8,9},{9,8},{10,11... | collective-permute-start | bytes 3538952 | tf_op jit(solution)/shard_map/ppermute | solution.py:435
  144.8 7.1 %collective-permute-start.16 = (bf16[768]{0:T(1024)(128)(2,1)S(1)}, bf16[768]{0:T(1024)(128)(2,1)S(1)}, u32[]{:S(2)}, u32[]{:S(2)}) collective-permute-start(bf16[768]{0:T(1024)(128)(2,1)S(1)} %copy-done.39), channel_id=1, source_target_pairs={{0,1},{1,0},{2,3},{3,2},{4,5},{5,4},{6,7},{7,6},{8,9},{9,8},{10,11... | collective-permute-start | bytes 4616 | tf_op jit(solution)/shard_map/ppermute | solution.py:435
  147.8 29.0 %collective-permute-start.12 = (bf16[17,32,384]{2,1,0:T(8,128)(2,1)S(1)}, bf16[17,32,384]{2,1,0:T(8,128)(2,1)S(1)}, u32[]{:S(2)}, u32[]{:S(2)}) collective-permute-start(bf16[17,32,384]{2,1,0:T(8,128)(2,1)S(1)} %get-tuple-element.437), channel_id=1, source_target_pairs={{0,4},{4,8},{8,12},{12,0},{1,5},{5,9},{9,13},{13,1},{2,6},{6,10},{... | collective-permute-start | bytes 1253384 | tf_op jit(solution)/shard_map/ppermute | solution.py:441
  150.0 35.9 %collective-permute-start.13 = (bf16[17,32,384]{2,1,0:T(8,128)(2,1)S(1)}, bf16[17,32,384]{2,1,0:T(8,128)(2,1)S(1)}, u32[]{:S(2)}, u32[]{:S(2)}) collective-permute-start(bf16[17,32,384]{2,1,0:T(8,128)(2,1)S(1)} %get-tuple-element.436), channel_id=1, source_target_pairs={{0,8},{4,12},{8,0},{12,4},{1,9},{5,13},{9,1},{13,5},{2,10},{6,14},... | collective-permute-start | bytes 1253384 | tf_op jit(solution)/shard_map/ppermute | solution.py:441
  151.9 34.0 %collective-permute-start.14 = (bf16[17,32,384]{2,1,0:T(8,128)(2,1)S(1)}, bf16[17,32,384]{2,1,0:T(8,128)(2,1)S(1)}, u32[]{:S(2)}, u32[]{:S(2)}) collective-permute-start(bf16[17,32,384]{2,1,0:T(8,128)(2,1)S(1)} %get-tuple-element.435), channel_id=1, source_target_pairs={{0,12},{4,0},{8,4},{12,8},{1,13},{5,1},{9,5},{13,9},{2,14},{6,2},{... | collective-permute-start | bytes 1253384 | tf_op jit(solution)/shard_map/ppermute | solution.py:441
  185.9 95.5 %slice-start = ((s8[4718592]{0:T(1024)(128)(4,1)}), s8[4194304]{0:T(1024)(128)(4,1)S(1)}, s32[]{:S(2)}) async-start(s8[4718592]{0:T(1024)(128)(4,1)} %bitcast.114), calls=%async_computation | async-start | bytes 8388608
  186.8 94.6 %slice-start.1 = ((s8[4718592]{0:T(1024)(128)(4,1)}), s8[524288]{0:T(1024)(128)(4,1)S(1)}, s32[]{:S(2)}) async-start(s8[4718592]{0:T(1024)(128)(4,1)} %bitcast.114), calls=%async_computation.1 | async-start | bytes 1048576
  203.4 10.4 %collective-permute-start.18 = (bf16[17,32,384]{2,1,0:T(8,128)(2,1)S(1)}, bf16[17,32,384]{2,1,0:T(8,128)(2,1)S(1)}, u32[]{:S(2)}, u32[]{:S(2)}) collective-permute-start(bf16[17,32,384]{2,1,0:T(8,128)(2,1)S(1)} %get-tuple-element.301), channel_id=1, source_target_pairs={{0,4},{4,8},{8,12},{12,0},{1,5},{5,9},{9,13},{13,1},{2,6},{6,10},{... | collective-permute-start | bytes 1253384 | tf_op jit(solution)/shard_map/ppermute | solution.py:441
  203.4 35.3 %collective-permute-start.19 = (bf16[17,32,384]{2,1,0:T(8,128)(2,1)S(1)}, bf16[17,32,384]{2,1,0:T(8,128)(2,1)S(1)}, u32[]{:S(2)}, u32[]{:S(2)}) collective-permute-start(bf16[17,32,384]{2,1,0:T(8,128)(2,1)S(1)} %get-tuple-element.302), channel_id=1, source_target_pairs={{0,8},{4,12},{8,0},{12,4},{1,9},{5,13},{9,1},{13,5},{2,10},{6,14},... | collective-permute-start | bytes 1253384 | tf_op jit(solution)/shard_map/ppermute | solution.py:441
  206.6 36.9 %collective-permute-start.20 = (bf16[17,32,384]{2,1,0:T(8,128)(2,1)S(1)}, bf16[17,32,384]{2,1,0:T(8,128)(2,1)S(1)}, u32[]{:S(2)}, u32[]{:S(2)}) collective-permute-start(bf16[17,32,384]{2,1,0:T(8,128)(2,1)S(1)} %get-tuple-element.303), channel_id=1, source_target_pairs={{0,12},{4,0},{8,4},{12,8},{1,13},{5,1},{9,5},{13,9},{2,14},{6,2},{... | collective-permute-start | bytes 1253384 | tf_op jit(solution)/shard_map/ppermute | solution.py:441
  243.8 37.6 %collective-permute-start.24 = (bf16[4,17,32,384]{3,2,1,0:T(8,128)(2,1)S(1)}, bf16[4,17,32,384]{3,2,1,0:T(8,128)(2,1)S(1)}, u32[]{:S(2)}, u32[]{:S(2)}) collective-permute-start(bf16[4,17,32,384]{3,2,1,0:T(8,128)(2,1)S(1)} %pad_maximum_fusion.2.own_ref), channel_id=1, source_target_pairs={{0,2},{2,0},{1,3},{3,1},{4,6},{6,4},{5,7},{7,5},{8,10},{10,8},{9,1... | collective-permute-start | bytes 5013512 | tf_op jit(solution)/shard_map/ppermute | solution.py:435
  245.1 10.4 %collective-permute-start.21 = (bf16[17,32,384]{2,1,0:T(8,128)(2,1)S(1)}, bf16[17,32,384]{2,1,0:T(8,128)(2,1)S(1)}, u32[]{:S(2)}, u32[]{:S(2)}) collective-permute-start(bf16[17,32,384]{2,1,0:T(8,128)(2,1)S(1)} %get-tuple-element.314), channel_id=1, source_target_pairs={{0,4},{4,8},{8,12},{12,0},{1,5},{5,9},{9,13},{13,1},{2,6},{6,10},{... | collective-permute-start | bytes 1253384 | tf_op jit(solution)/shard_map/ppermute | solution.py:441
  245.1 35.4 %collective-permute-start.22 = (bf16[17,32,384]{2,1,0:T(8,128)(2,1)S(1)}, bf16[17,32,384]{2,1,0:T(8,128)(2,1)S(1)}, u32[]{:S(2)}, u32[]{:S(2)}) collective-permute-start(bf16[17,32,384]{2,1,0:T(8,128)(2,1)S(1)} %get-tuple-element.315), channel_id=1, source_target_pairs={{0,8},{4,12},{8,0},{12,4},{1,9},{5,13},{9,1},{13,5},{2,10},{6,14},... | collective-permute-start | bytes 1253384 | tf_op jit(solution)/shard_map/ppermute | solution.py:441
  245.1 35.4 %collective-permute-start.23 = (bf16[17,32,384]{2,1,0:T(8,128)(2,1)S(1)}, bf16[17,32,384]{2,1,0:T(8,128)(2,1)S(1)}, u32[]{:S(2)}, u32[]{:S(2)}) collective-permute-start(bf16[17,32,384]{2,1,0:T(8,128)(2,1)S(1)} %get-tuple-element.316), channel_id=1, source_target_pairs={{0,12},{4,0},{8,4},{12,8},{1,13},{5,1},{9,5},{13,9},{2,14},{6,2},{... | collective-permute-start | bytes 1253384 | tf_op jit(solution)/shard_map/ppermute | solution.py:441
  290.0 5.5 collective-permute-start.29
  291.7 39.6 %collective-permute-start.28 = (bf16[4,17,32,384]{3,2,1,0:T(8,128)(2,1)S(1)}, bf16[4,17,32,384]{3,2,1,0:T(8,128)(2,1)S(1)}, u32[]{:S(2)}, u32[]{:S(2)}) collective-permute-start(bf16[4,17,32,384]{3,2,1,0:T(8,128)(2,1)S(1)} %pad_maximum_fusion.3.own_ref), channel_id=1, source_target_pairs={{0,2},{2,0},{1,3},{3,1},{4,6},{6,4},{5,7},{7,5},{8,10},{10,8},{9,1... | collective-permute-start | bytes 5013512 | tf_op jit(solution)/shard_map/ppermute | solution.py:435
  292.9 21.3 %collective-permute-start.25 = (bf16[17,32,384]{2,1,0:T(8,128)(2,1)S(1)}, bf16[17,32,384]{2,1,0:T(8,128)(2,1)S(1)}, u32[]{:S(2)}, u32[]{:S(2)}) collective-permute-start(bf16[17,32,384]{2,1,0:T(8,128)(2,1)S(1)} %get-tuple-element.327), channel_id=1, source_target_pairs={{0,4},{4,8},{8,12},{12,0},{1,5},{5,9},{9,13},{13,1},{2,6},{6,10},{... | collective-permute-start | bytes 1253384 | tf_op jit(solution)/shard_map/ppermute | solution.py:441
  292.9 35.9 %collective-permute-start.26 = (bf16[17,32,384]{2,1,0:T(8,128)(2,1)S(1)}, bf16[17,32,384]{2,1,0:T(8,128)(2,1)S(1)}, u32[]{:S(2)}, u32[]{:S(2)}) collective-permute-start(bf16[17,32,384]{2,1,0:T(8,128)(2,1)S(1)} %get-tuple-element.328), channel_id=1, source_target_pairs={{0,8},{4,12},{8,0},{12,4},{1,9},{5,13},{9,1},{13,5},{2,10},{6,14},... | collective-permute-start | bytes 1253384 | tf_op jit(solution)/shard_map/ppermute | solution.py:441
  294.1 37.1 %collective-permute-start.27 = (bf16[17,32,384]{2,1,0:T(8,128)(2,1)S(1)}, bf16[17,32,384]{2,1,0:T(8,128)(2,1)}, u32[]{:S(2)}, u32[]{:S(2)}) collective-permute-start(bf16[17,32,384]{2,1,0:T(8,128)(2,1)S(1)} %get-tuple-element.329), channel_id=1, source_target_pairs={{0,12},{4,0},{8,4},{12,8},{1,13},{5,1},{9,5},{13,9},{2,14},{6,2},{... | collective-permute-start | bytes 1253384 | tf_op jit(solution)/shard_map/ppermute | solution.py:441
  331.2 10.2 %collective-permute-start.31 = (bf16[16,32,384]{2,1,0:T(8,128)(2,1)S(1)}, bf16[16,32,384]{2,1,0:T(8,128)(2,1)S(1)}, u32[]{:S(2)}, u32[]{:S(2)}) collective-permute-start(bf16[16,32,384]{2,1,0:T(8,128)(2,1)S(1)} %get-tuple-element.360), channel_id=1, source_target_pairs={{0,4},{4,8},{8,12},{12,0},{1,5},{5,9},{9,13},{13,1},{2,6},{6,10},{... | collective-permute-start | bytes 1179656 | tf_op jit(solution)/shard_map/ppermute | solution.py:441
  348.9 35.2 %copy-start.7 = (bf16[4,16,32,384]{3,2,1,0:T(8,128)(2,1)}, bf16[4,16,32,384]{3,2,1,0:T(8,128)(2,1)S(1)}, u32[]{:S(2)}) copy-start(bf16[4,16,32,384]{3,2,1,0:T(8,128)(2,1)S(1)} %get-tuple-element.368.own_ref) | copy-start | bytes 4718596
  348.9 33.3 %collective-permute-start.32 = (bf16[4,16,32,384]{3,2,1,0:T(8,128)(2,1)S(1)}, bf16[4,16,32,384]{3,2,1,0:T(8,128)(2,1)S(1)}, u32[]{:S(2)}, u32[]{:S(2)}) collective-permute-start(bf16[4,16,32,384]{3,2,1,0:T(8,128)(2,1)S(1)} %get-tuple-element.369), channel_id=1, source_target_pairs={{0,1},{1,0},{2,3},{3,2},{4,5},{5,4},{6,7},{7,6},{8,9},{9,8},{10,11... | collective-permute-start | bytes 4718600 | tf_op jit(solution)/shard_map/ppermute | solution.py:435
  351.6 72.9 %collective-permute-start.30 = (bf16[4,17,32,384]{3,2,1,0:T(8,128)(2,1)S(1)}, bf16[4,17,32,384]{3,2,1,0:T(8,128)(2,1)S(1)}, u32[]{:S(2)}, u32[]{:S(2)}) collective-permute-start(bf16[4,17,32,384]{3,2,1,0:T(8,128)(2,1)S(1)} %pad_maximum_fusion.4.own_ref), channel_id=1, source_target_pairs={{0,2},{2,0},{1,3},{3,1},{4,6},{6,4},{5,7},{7,5},{8,10},{10,8},{9,1... | collective-permute-start | bytes 5013512 | tf_op jit(solution)/shard_map/ppermute | solution.py:435
  352.9 24.9 %collective-permute-start.33 = (bf16[16,32,384]{2,1,0:T(8,128)(2,1)S(1)}, bf16[16,32,384]{2,1,0:T(8,128)(2,1)S(1)}, u32[]{:S(2)}, u32[]{:S(2)}) collective-permute-start(bf16[16,32,384]{2,1,0:T(8,128)(2,1)S(1)} %get-tuple-element.361), channel_id=1, source_target_pairs={{0,8},{4,12},{8,0},{12,4},{1,9},{5,13},{9,1},{13,5},{2,10},{6,14},... | collective-permute-start | bytes 1179656 | tf_op jit(solution)/shard_map/ppermute | solution.py:441
  352.9 26.1 %collective-permute-start.34 = (bf16[16,32,384]{2,1,0:T(8,128)(2,1)S(1)}, bf16[16,32,384]{2,1,0:T(8,128)(2,1)S(1)}, u32[]{:S(2)}, u32[]{:S(2)}) collective-permute-start(bf16[16,32,384]{2,1,0:T(8,128)(2,1)S(1)} %get-tuple-element.362), channel_id=1, source_target_pairs={{0,12},{4,0},{8,4},{12,8},{1,13},{5,1},{9,5},{13,9},{2,14},{6,2},{... | collective-permute-start | bytes 1179656 | tf_op jit(solution)/shard_map/ppermute | solution.py:441
  354.1 49.0 %collective-permute-start.35 = (bf16[16,32,384]{2,1,0:T(8,128)(2,1)}, bf16[16,32,384]{2,1,0:T(8,128)(2,1)S(1)}, u32[]{:S(2)}, u32[]{:S(2)}) collective-permute-start(bf16[16,32,384]{2,1,0:T(8,128)(2,1)} %get-tuple-element.363), channel_id=1, source_target_pairs={{0,1},{1,0},{4,5},{5,4},{8,9},{9,8},{12,13},{13,12},{2,3},{3,2},{6... | collective-permute-start | bytes 1179656 | tf_op jit(solution)/shard_map/ppermute | solution.py:450
  377.8 25.3 %collective-permute-start.36 = (bf16[16,32,384]{2,1,0:T(8,128)(2,1)}, bf16[16,32,384]{2,1,0:T(8,128)(2,1)S(1)}, u32[]{:S(2)}, u32[]{:S(2)}) collective-permute-start(bf16[16,32,384]{2,1,0:T(8,128)(2,1)} %get-tuple-element.364), channel_id=1, source_target_pairs={{0,5},{1,4},{4,9},{5,8},{8,13},{9,12},{12,1},{13,0},{2,7},{3,6},{6... | collective-permute-start | bytes 1179656 | tf_op jit(solution)/shard_map/ppermute | solution.py:450
  379.0 31.9 %collective-permute-start.37 = (bf16[16,32,384]{2,1,0:T(8,128)(2,1)S(1)}, bf16[16,32,384]{2,1,0:T(8,128)(2,1)S(1)}, u32[]{:S(2)}, u32[]{:S(2)}) collective-permute-start(bf16[16,32,384]{2,1,0:T(8,128)(2,1)S(1)} %get-tuple-element.365), channel_id=1, source_target_pairs={{0,9},{1,8},{4,13},{5,12},{8,1},{9,0},{12,5},{13,4},{2,11},{3,10},... | collective-permute-start | bytes 1179656 | tf_op jit(solution)/shard_map/ppermute | solution.py:450
  382.2 42.3 %collective-permute-start.38 = (bf16[16,32,384]{2,1,0:T(8,128)(2,1)S(1)}, bf16[16,32,384]{2,1,0:T(8,128)(2,1)S(1)}, u32[]{:S(2)}, u32[]{:S(2)}) collective-permute-start(bf16[16,32,384]{2,1,0:T(8,128)(2,1)S(1)} %get-tuple-element.366), channel_id=1, source_target_pairs={{0,13},{1,12},{4,1},{5,0},{8,5},{9,4},{12,9},{13,8},{2,15},{3,14},... | collective-permute-start | bytes 1179656 | tf_op jit(solution)/shard_map/ppermute | solution.py:450
  403.1 40.0 %copy-start.21 = (bf16[16,32,384]{2,1,0:T(8,128)(2,1)}, bf16[16,32,384]{2,1,0:T(8,128)(2,1)S(1)}, u32[]{:S(2)}) copy-start(bf16[16,32,384]{2,1,0:T(8,128)(2,1)S(1)} %collective-permute-done.35.refs_4_) | copy-start | bytes 1179652
  403.1 39.9 %copy-start.22 = (bf16[16,32,384]{2,1,0:T(8,128)(2,1)}, bf16[16,32,384]{2,1,0:T(8,128)(2,1)S(1)}, u32[]{:S(2)}) copy-start(bf16[16,32,384]{2,1,0:T(8,128)(2,1)S(1)} %collective-permute-done.36.refs_5_) | copy-start | bytes 1179652
  424.5 10.3 %collective-permute-start.39 = (bf16[16,32,384]{2,1,0:T(8,128)(2,1)S(1)}, bf16[16,32,384]{2,1,0:T(8,128)(2,1)S(1)}, u32[]{:S(2)}, u32[]{:S(2)}) collective-permute-start(bf16[16,32,384]{2,1,0:T(8,128)(2,1)S(1)} %get-tuple-element.382), channel_id=1, source_target_pairs={{0,4},{4,8},{8,12},{12,0},{1,5},{5,9},{9,13},{13,1},{2,6},{6,10},{... | collective-permute-start | bytes 1179656 | tf_op jit(solution)/shard_map/ppermute | solution.py:441
  444.2 31.0 %collective-permute-start.40 = (bf16[4,16,32,384]{3,2,1,0:T(8,128)(2,1)}, bf16[4,16,32,384]{3,2,1,0:T(8,128)(2,1)}, u32[]{:S(2)}, u32[]{:S(2)}) collective-permute-start(bf16[4,16,32,384]{3,2,1,0:T(8,128)(2,1)} %get-tuple-element.391), channel_id=1, source_target_pairs={{0,1},{1,0},{2,3},{3,2},{4,5},{5,4},{6,7},{7,6},{8,9},{9,8},{10,11... | collective-permute-start | bytes 4718600 | tf_op jit(solution)/shard_map/ppermute | solution.py:435
  445.5 26.0 %collective-permute-start.41 = (bf16[16,32,384]{2,1,0:T(8,128)(2,1)}, bf16[16,32,384]{2,1,0:T(8,128)(2,1)}, u32[]{:S(2)}, u32[]{:S(2)}) collective-permute-start(bf16[16,32,384]{2,1,0:T(8,128)(2,1)} %get-tuple-element.383), channel_id=1, source_target_pairs={{0,8},{4,12},{8,0},{12,4},{1,9},{5,13},{9,1},{13,5},{2,10},{6,14},... | collective-permute-start | bytes 1179656 | tf_op jit(solution)/shard_map/ppermute | solution.py:441
  445.5 47.7 %collective-permute-start.42 = (bf16[16,32,384]{2,1,0:T(8,128)(2,1)}, bf16[16,32,384]{2,1,0:T(8,128)(2,1)}, u32[]{:S(2)}, u32[]{:S(2)}) collective-permute-start(bf16[16,32,384]{2,1,0:T(8,128)(2,1)} %get-tuple-element.384), channel_id=1, source_target_pairs={{0,12},{4,0},{8,4},{12,8},{1,13},{5,1},{9,5},{13,9},{2,14},{6,2},{... | collective-permute-start | bytes 1179656 | tf_op jit(solution)/shard_map/ppermute | solution.py:441
  446.7 46.5 %collective-permute-start.43 = (bf16[16,32,384]{2,1,0:T(8,128)(2,1)S(1)}, bf16[16,32,384]{2,1,0:T(8,128)(2,1)}, u32[]{:S(2)}, u32[]{:S(2)}) collective-permute-start(bf16[16,32,384]{2,1,0:T(8,128)(2,1)S(1)} %get-tuple-element.385), channel_id=1, source_target_pairs={{0,1},{1,0},{4,5},{5,4},{8,9},{9,8},{12,13},{13,12},{2,3},{3,2},{6... | collective-permute-start | bytes 1179656 | tf_op jit(solution)/shard_map/ppermute | solution.py:450
  447.2 49.4 %collective-permute-start.44 = (bf16[16,32,384]{2,1,0:T(8,128)(2,1)S(1)}, bf16[16,32,384]{2,1,0:T(8,128)(2,1)}, u32[]{:S(2)}, u32[]{:S(2)}) collective-permute-start(bf16[16,32,384]{2,1,0:T(8,128)(2,1)S(1)} %get-tuple-element.386), channel_id=1, source_target_pairs={{0,5},{1,4},{4,9},{5,8},{8,13},{9,12},{12,1},{13,0},{2,7},{3,6},{6... | collective-permute-start | bytes 1179656 | tf_op jit(solution)/shard_map/ppermute | solution.py:450
  471.4 33.6 %collective-permute-start.45 = (bf16[16,32,384]{2,1,0:T(8,128)(2,1)S(1)}, bf16[16,32,384]{2,1,0:T(8,128)(2,1)S(1)}, u32[]{:S(2)}, u32[]{:S(2)}) collective-permute-start(bf16[16,32,384]{2,1,0:T(8,128)(2,1)S(1)} %get-tuple-element.387), channel_id=1, source_target_pairs={{0,9},{1,8},{4,13},{5,12},{8,1},{9,0},{12,5},{13,4},{2,11},{3,10},... | collective-permute-start | bytes 1179656 | tf_op jit(solution)/shard_map/ppermute | solution.py:450
  475.2 30.9 %collective-permute-start.46 = (bf16[16,32,384]{2,1,0:T(8,128)(2,1)S(1)}, bf16[16,32,384]{2,1,0:T(8,128)(2,1)S(1)}, u32[]{:S(2)}, u32[]{:S(2)}) collective-permute-start(bf16[16,32,384]{2,1,0:T(8,128)(2,1)S(1)} %get-tuple-element.388), channel_id=1, source_target_pairs={{0,13},{1,12},{4,1},{5,0},{8,5},{9,4},{12,9},{13,8},{2,15},{3,14},... | collective-permute-start | bytes 1179656 | tf_op jit(solution)/shard_map/ppermute | solution.py:450
  505.1 34.9 %copy-start.26 = (bf16[16,32,384]{2,1,0:T(8,128)(2,1)}, bf16[16,32,384]{2,1,0:T(8,128)(2,1)S(1)}, u32[]{:S(2)}) copy-start(bf16[16,32,384]{2,1,0:T(8,128)(2,1)S(1)} %collective-permute-done.45.refs_6_) | copy-start | bytes 1179652
  506.1 33.9 %copy-start.27 = (bf16[16,32,384]{2,1,0:T(8,128)(2,1)}, bf16[16,32,384]{2,1,0:T(8,128)(2,1)S(1)}, u32[]{:S(2)}) copy-start(bf16[16,32,384]{2,1,0:T(8,128)(2,1)S(1)} %collective-permute-done.46.refs_7_) | copy-start | bytes 1179652
  506.1 10.4 %collective-permute-start.47 = (bf16[16,32,384]{2,1,0:T(8,128)(2,1)S(1)}, bf16[16,32,384]{2,1,0:T(8,128)(2,1)S(1)}, u32[]{:S(2)}, u32[]{:S(2)}) collective-permute-start(bf16[16,32,384]{2,1,0:T(8,128)(2,1)S(1)} %get-tuple-element.409), channel_id=1, source_target_pairs={{0,4},{4,8},{8,12},{12,0},{1,5},{5,9},{9,13},{13,1},{2,6},{6,10},{... | collective-permute-start | bytes 1179656 | tf_op jit(solution)/shard_map/ppermute | solution.py:441
  506.1 33.9 %collective-permute-start.48 = (bf16[16,32,384]{2,1,0:T(8,128)(2,1)S(1)}, bf16[16,32,384]{2,1,0:T(8,128)(2,1)S(1)}, u32[]{:S(2)}, u32[]{:S(2)}) collective-permute-start(bf16[16,32,384]{2,1,0:T(8,128)(2,1)S(1)} %get-tuple-element.410), channel_id=1, source_target_pairs={{0,8},{4,12},{8,0},{12,4},{1,9},{5,13},{9,1},{13,5},{2,10},{6,14},... | collective-permute-start | bytes 1179656 | tf_op jit(solution)/shard_map/ppermute | solution.py:441
  508.3 51.7 %collective-permute-start.49 = (bf16[16,32,384]{2,1,0:T(8,128)(2,1)}, bf16[16,32,384]{2,1,0:T(8,128)(2,1)S(1)}, u32[]{:S(2)}, u32[]{:S(2)}) collective-permute-start(bf16[16,32,384]{2,1,0:T(8,128)(2,1)} %get-tuple-element.411), channel_id=1, source_target_pairs={{0,12},{4,0},{8,4},{12,8},{1,13},{5,1},{9,5},{13,9},{2,14},{6,2},{... | collective-permute-start | bytes 1179656 | tf_op jit(solution)/shard_map/ppermute | solution.py:441
  509.7 50.3 %collective-permute-start.50 = (bf16[16,32,384]{2,1,0:T(8,128)(2,1)}, bf16[16,32,384]{2,1,0:T(8,128)(2,1)S(1)}, u32[]{:S(2)}, u32[]{:S(2)}) collective-permute-start(bf16[16,32,384]{2,1,0:T(8,128)(2,1)} %get-tuple-element.412), channel_id=1, source_target_pairs={{0,1},{1,0},{4,5},{5,4},{8,9},{9,8},{12,13},{13,12},{2,3},{3,2},{6... | collective-permute-start | bytes 1179656 | tf_op jit(solution)/shard_map/ppermute | solution.py:450
  510.9 54.4 %collective-permute-start.51 = (bf16[16,32,384]{2,1,0:T(8,128)(2,1)}, bf16[16,32,384]{2,1,0:T(8,128)(2,1)S(1)}, u32[]{:S(2)}, u32[]{:S(2)}) collective-permute-start(bf16[16,32,384]{2,1,0:T(8,128)(2,1)} %get-tuple-element.413), channel_id=1, source_target_pairs={{0,5},{1,4},{4,9},{5,8},{8,13},{9,12},{12,1},{13,0},{2,7},{3,6},{6... | collective-permute-start | bytes 1179656 | tf_op jit(solution)/shard_map/ppermute | solution.py:450
  516.5 57.3 %collective-permute-start.52 = (bf16[16,32,384]{2,1,0:T(8,128)(2,1)}, bf16[16,32,384]{2,1,0:T(8,128)(2,1)S(1)}, u32[]{:S(2)}, u32[]{:S(2)}) collective-permute-start(bf16[16,32,384]{2,1,0:T(8,128)(2,1)} %get-tuple-element.414), channel_id=1, source_target_pairs={{0,9},{1,8},{4,13},{5,12},{8,1},{9,0},{12,5},{13,4},{2,11},{3,10},... | collective-permute-start | bytes 1179656 | tf_op jit(solution)/shard_map/ppermute | solution.py:450
  539.9 36.9 %collective-permute-start.53 = (bf16[16,32,384]{2,1,0:T(8,128)(2,1)}, bf16[16,32,384]{2,1,0:T(8,128)(2,1)S(1)}, u32[]{:S(2)}, u32[]{:S(2)}) collective-permute-start(bf16[16,32,384]{2,1,0:T(8,128)(2,1)} %get-tuple-element.415), channel_id=1, source_target_pairs={{0,13},{1,12},{4,1},{5,0},{8,5},{9,4},{12,9},{13,8},{2,15},{3,14},... | collective-permute-start | bytes 1179656 | tf_op jit(solution)/shard_map/ppermute | solution.py:450
  (45 other events, 485.8 us)

commit v4 on v2

--- a/solution.py
+++ b/solution.py
@@ -19,7 +19,6 @@
 norm_epsilon = 1e-05
 
 COST_SHARE = 1
-LATE_SHARE = 8
 
 BF = jnp.bfloat16
 F32 = jnp.float32
@@ -73,10 +72,10 @@
     pair = jnp.concatenate(
         [values[:, 0].reshape(rows * 8, width), values[:, 1].reshape(rows * 8, width)], axis=1
     ).astype(BF)
-    half = table_ref.shape[1] // 2
+    half = table_ref.shape[0] // 2
     for part, out_ref in ((0, send_ref), (1, keep_ref)):
         total = jnp.dot(
-            table_ref[0, part * half : (part + 1) * half, :], pair, preferred_element_type=F32
+            table_ref[part * half : (part + 1) * half, :], pair, preferred_element_type=F32
         )
         total = jnp.concatenate(
             [
@@ -91,23 +90,21 @@
 
 def lat_forward(where, cells, table, lon_count):
     rows, cols, width = cells.shape
-    slots = table.shape[1] // (16 * lon_count)
-    block = pl.BlockSpec((lon_count, slots, 16, width), lambda i, where: (0, 0, i, 0))
+    slots = table.shape[0] // (16 * lon_count)
+    block = pl.BlockSpec((lon_count, slots, 16, width), lambda i: (0, 0, i, 0))
     return pl.pallas_call(
         lat_forward_kernel,
-        grid_spec=pltpu.PrefetchScalarGridSpec(
-            num_scalar_prefetch=1,
-            grid=(cols // 16,),
-            in_specs=[
-                pl.BlockSpec((rows, 16, width), lambda i, where: (0, i, 0)),
-                pl.BlockSpec((1,) + table.shape[1:], lambda i, where: (where[2], 0, 0)),
-            ],
-            out_specs=[block, block],
-        ),
+        grid=(cols // 16,),
+        in_specs=[
+            pl.BlockSpec(memory_space=pltpu.SMEM),
+            pl.BlockSpec((rows, 16, width), lambda i: (0, i, 0)),
+            pl.BlockSpec(table.shape, lambda i: (0, 0)),
+        ],
+        out_specs=[block, block],
         out_shape=[jax.ShapeDtypeStruct((lon_count, slots, cols, width), BF)] * 2,
         compiler_params=pltpu.CompilerParams(vmem_limit_bytes=40 << 20),
         cost_estimate=pl.CostEstimate(
-            flops=2 * table[0].size * cols // 8 * width // COST_SHARE,
+            flops=2 * table.size * cols // 8 * width // COST_SHARE,
             bytes_accessed=4 * rows * cols * width // COST_SHARE,
             transcendentals=0,
         ),
@@ -131,7 +128,7 @@
             source = lax.rem(where_ref[0] + (lon_count - s), lon_count)
             flat_ref[side * lon_count + source] = jnp.concatenate([flat.astype(BF), blank], axis=0)
     total = jnp.dot(
-        table_ref[0], flat_ref[...].reshape(-1, 2 * width), preferred_element_type=F32
+        table_ref[...], flat_ref[...].reshape(-1, 2 * width), preferred_element_type=F32
     )
     fine = jnp.concatenate(
         [total[:, :width].reshape(rows, 8, width), total[:, width:].reshape(rows, 8, width)], axis=1
@@ -154,30 +151,28 @@
     lon_count, slots, cols, width = own.shape
     rows = patches.shape[0]
     first_block = first_col // 16
-    spec = pl.BlockSpec((lon_count, slots, 16, width), lambda i, where: (0, 0, i, 0))
+    spec = pl.BlockSpec((lon_count, slots, 16, width), lambda i: (0, 0, i, 0))
     half = rows // (2 * lon_count)
-    out_spec = pl.BlockSpec((lon_count, half, 16, width), lambda i, where: (0, 0, i, 0))
+    out_spec = pl.BlockSpec((lon_count, half, 16, width), lambda i: (0, 0, i, 0))
     return pl.pallas_call(
         lat_inverse_kernel,
-        grid_spec=pltpu.PrefetchScalarGridSpec(
-            num_scalar_prefetch=1,
-            grid=(cols // 16,),
-            in_specs=[
-                spec,
-                spec,
-                pl.BlockSpec((1,) + table.shape[1:], lambda i, where: (where[2], 0, 0)),
-                pl.BlockSpec((rows, 16, width), lambda i, where: (0, first_block + i, 0)),
-            ],
-            out_specs=[out_spec, out_spec],
-            scratch_shapes=[
-                pltpu.VMEM((2 * lon_count, table.shape[2] // (2 * lon_count), 2 * width), BF)
-            ],
-        ),
+        grid=(cols // 16,),
+        in_specs=[
+            pl.BlockSpec(memory_space=pltpu.SMEM),
+            spec,
+            spec,
+            pl.BlockSpec(table.shape, lambda i: (0, 0)),
+            pl.BlockSpec((rows, 16, width), lambda i: (0, first_block + i, 0)),
+        ],
+        out_specs=[out_spec, out_spec],
         out_shape=[jax.ShapeDtypeStruct((lon_count, half, cols, width), BF)] * 2,
+        scratch_shapes=[
+            pltpu.VMEM((2 * lon_count, table.shape[1] // (2 * lon_count), 2 * width), BF)
+        ],
         compiler_params=pltpu.CompilerParams(vmem_limit_bytes=40 << 20),
         cost_estimate=pl.CostEstimate(
-            flops=2 * table[0].size * cols // 8 * width // LATE_SHARE,
-            bytes_accessed=6 * rows * cols * width // LATE_SHARE,
+            flops=2 * table.size * cols // 8 * width // COST_SHARE,
+            bytes_accessed=6 * rows * cols * width // COST_SHARE,
             transcendentals=0,
         ),
         name="lat_inverse",
@@ -298,7 +293,7 @@
 
 def mlp_kernel(
     where_ref, own_ref, other_ref, gain_ref, bias_ref, w_in_ref, b_in_ref, w_out_ref, b_out_ref,
-    *out_refs,
+    out_ref,
 ):
     _, rows, cols, width = own_ref.shape
     cells = rows * cols
@@ -316,23 +311,14 @@
     hidden = (hidden * (0.5 + 0.5 * lax.erf(hidden * math.sqrt(0.5)))).astype(BF)
     total = jnp.dot(hidden, w_out_ref[...], preferred_element_type=F32) + wide + b_out_ref[...]
     total = total.astype(BF)
-    low, high = total[:, :width], total[:, width:]
-    mine = jnp.where(flip, high, low).reshape(rows, cols, width)
-    sent = jnp.where(flip, low, high).reshape(rows, cols, width)
-    for s, ref in enumerate(out_refs):
-
-        @pl.when(pl.program_id(0) == s)
-        def _():
-            ref[0] = mine
-            ref[1] = sent
+    out_ref[0, 0] = total[:, :width].reshape(rows, cols, width)
+    out_ref[0, 1] = total[:, width:].reshape(rows, cols, width)
 
 
 def mlp(where, own, other, gain, bias, w_in, b_in, w_out, b_out):
     lon_count, rows, cols, width = own.shape
     whole = lambda array: pl.BlockSpec(array.shape, lambda i, where: (0,) * array.ndim)
-    cell_spec = pl.BlockSpec(
-        (1, rows, cols, width), lambda i, where: (lax.rem(where[0] + i, lon_count), 0, 0, 0)
-    )
+    cell_spec = pl.BlockSpec((1, rows, cols, width), lambda i, where: (i, 0, 0, 0))
     cells = lon_count * rows * cols
     return pl.pallas_call(
         mlp_kernel,
@@ -341,68 +327,43 @@
             grid=(lon_count,),
             in_specs=[cell_spec, cell_spec]
             + [whole(a) for a in (gain, bias, w_in, b_in, w_out, b_out)],
-            out_specs=[pl.BlockSpec((2, rows, cols, width), lambda i, where: (0, 0, 0, 0))]
-            * lon_count,
+            out_specs=pl.BlockSpec((1, 2, rows, cols, width), lambda i, where: (i, 0, 0, 0, 0)),
         ),
-        out_shape=[jax.ShapeDtypeStruct((2, rows, cols, width), BF)] * lon_count,
+        out_shape=jax.ShapeDtypeStruct((lon_count, 2, rows, cols, width), BF),
         compiler_params=pltpu.CompilerParams(vmem_limit_bytes=48 << 20),
         cost_estimate=pl.CostEstimate(
-            flops=4 * cells * w_in.size // LATE_SHARE,
-            bytes_accessed=8 * cells * width // LATE_SHARE,
-            transcendentals=cells * w_in.shape[1] // LATE_SHARE,
+            flops=4 * cells * w_in.size // COST_SHARE,
+            bytes_accessed=8 * cells * width // COST_SHARE,
+            transcendentals=cells * w_in.shape[1] // COST_SHARE,
         ),
         name="channel_mlp",
     )(where, own, other, gain, bias, w_in, b_in, w_out, b_out)
 
 
-def assemble_kernel(where_ref, their_ref, *refs):
-    my_refs, out_ref = refs[:-1], refs[-1]
-    half = their_ref.shape[1]
-    flip = where_ref[1] == 1
-    for s, ref in enumerate(my_refs):
-
-        @pl.when(pl.program_id(0) == s)
-        def _():
-            mine, theirs = ref[0], their_ref[0]
-            out_ref[:half] = jnp.where(flip, theirs, mine)
-            out_ref[half:] = jnp.where(flip, mine, theirs)
-
-
-def assemble(where, result, mine, theirs, first_col, block_cols):
-    lon_count, rows, cols, width = theirs.shape
+def assemble_kernel(piece_ref, *refs):
+    out_ref = refs[-1]
+    half = piece_ref.shape[2]
+    for c in range(2):
+        out_ref[c * half : (c + 1) * half] = piece_ref[0, c]
+
+
+def assemble(result, pieces, first_col, block_cols):
+    lon_count, _, rows, cols, width = pieces.shape
     block = math.gcd(math.gcd(cols, block_cols), first_col)
-    steps = cols // block
-
-    def piece(s):
-        def index(g, j, where):
-            return 0, 0, jnp.where(g == s, j, jnp.where(g < s, 0, steps - 1)), 0
-
-        return pl.BlockSpec((1, rows, block, width), index)
-
-    def place(g, j, where):
-        source = lax.rem(where[0] + (lon_count - g), lon_count)
-        return 0, source * (block_cols // block) + first_col // block + j, 0
-
-    specs = [pl.BlockSpec((1, rows, block, width), lambda g, j, where: (g, 0, j, 0))]
-    specs += [piece(s) for s in range(lon_count)]
-    operands = [where, theirs, *mine]
+    specs = [pl.BlockSpec((1, 2, rows, block, width), lambda z, j: (z, 0, 0, j, 0))]
+    operands = [pieces]
     aliases = {}
-    kernel = assemble_kernel
     if result is not None:
-        aliases = {len(operands): 0}
+        aliases = {1: 0}
         operands.append(result)
         specs.append(pl.BlockSpec(memory_space=pl.ANY))
-
-        def kernel(where_ref, *refs):
-            assemble_kernel(where_ref, *refs[:-2], refs[-1])
-
     return pl.pallas_call(
-        kernel,
-        grid_spec=pltpu.PrefetchScalarGridSpec(
-            num_scalar_prefetch=1,
-            grid=(lon_count, steps),
-            in_specs=specs,
-            out_specs=pl.BlockSpec((2 * rows, block, width), place),
+        assemble_kernel,
+        grid=(lon_count, cols // block),
+        in_specs=specs,
+        out_specs=pl.BlockSpec(
+            (2 * rows, block, width),
+            lambda z, j: (0, z * (block_cols // block) + first_col // block + j, 0),
         ),
         out_shape=jax.ShapeDtypeStruct((2 * rows, lon_count * block_cols, width), BF),
         input_output_aliases=aliases,
@@ -477,7 +438,8 @@
         ordered = np.concatenate([here[a], here[1 - a]], axis=0)
         ordered = np.pad(ordered, ((0, 0), (0, slots % 2), (0, 0))).reshape(-1, rows)
         inverse_all.append(spread8(ordered.T))
-    forward_lat, inverse_lat = jnp.asarray(np.stack(forward_all)), jnp.asarray(np.stack(inverse_all))
+    forward_lat = lax.dynamic_index_in_dim(jnp.asarray(np.stack(forward_all)), lat_id, 0, False)
+    inverse_lat = None
 
     ids = np.arange(W).reshape(lon_count, cols)
 
@@ -489,7 +451,7 @@
     to_there = [lon_tables(column_order((z + steps) % lon_count))[1] for z in range(lon_count)]
 
     fence = lax.optimization_barrier
-    where = jnp.stack([lon_id, ch_id, lat_id]).astype(jnp.int32)
+    where = jnp.stack([lon_id, ch_id]).astype(jnp.int32)
 
     def row_transform(i, source):
         raw = source[:, starts[i] : starts[i] + widths[i]].astype(F32)
@@ -537,9 +499,10 @@
         mine, sent = lat_inverse(where, own, other, inverse_lat, patches, starts[i])
         return mlp(where, mine, swap(sent, "ch"), *weights)
 
-    def placed(result, i, pieces):
-        theirs = swap(jnp.stack([piece[1] for piece in pieces]), "ch")
-        return assemble(where, result, pieces, theirs, starts[i], cols)
+    def outward(outputs):
+        shape = outputs.shape
+        flat = outputs.reshape((shape[0] * 2,) + shape[2:])
+        return lax.all_to_all(flat, ("lon", "ch"), 0, 0, tiled=True).reshape(shape)
 
     received, summed, sent, kept = [], None, None, None
     weights = None
@@ -559,8 +522,9 @@
             filter_args = filter_operands()
         else:
             weights = mlp_weights(*dense)
-        patches, arrived, sent, kept, received, filter_args, weights, dense = fence(
-            (patches, arrived, sent, kept, received, filter_args, weights, dense)
+            inverse_lat = lax.dynamic_index_in_dim(jnp.asarray(np.stack(inverse_all)), lat_id, 0, False)
+        patches, arrived, sent, kept, received, filter_args, weights, inverse_lat, dense = fence(
+            (patches, arrived, sent, kept, received, filter_args, weights, inverse_lat, dense)
         )
         if arrived is not None:
             summed = [
@@ -586,19 +550,18 @@
     pieces = None
     for i in range(chunks):
         last = pieces
-        pieces = along_lon(outputs[i])
+        pieces = outward(outputs[i])
         if last is not None:
-            result = placed(result, i - 1, last)
-        for later in (i + 1, i + 2):
-            if later < chunks and outputs[later] is None:
-                if others[later] is None:
-                    owns[later] = jnp.stack(owns[later])
-                    others[later] = swap(owns[later], "lat")
-                outputs[later] = row_result(later, owns[later], others[later])
+            result = assemble(result, last, starts[i - 1], cols)
+        if i + 1 < chunks and outputs[i + 1] is None:
+            outputs[i + 1] = row_result(i + 1, owns[i + 1], others[i + 1])
+        if i + 2 < chunks and others[i + 2] is None:
+            owns[i + 2] = jnp.stack(owns[i + 2])
+            others[i + 2] = swap(owns[i + 2], "lat")
         patches, owns, others, outputs, pieces, result = fence(
             (patches, owns, others, outputs, pieces, result)
         )
-    result = placed(result, chunks - 1, pieces)
+    result = assemble(result, pieces, starts[chunks - 1], cols)
     return result.reshape(1, 1, rows // lon_count, lon_count * cols, width)
 
 

time: 617 us -> 577 us (0.935)
  the two profiles are of different devices: /device:TPU:9 before, /device:TPU:0 now
where the time goes in v4:
time: 577 us; the launch traced here: 569 us
  waiting for transfers between devices  318 us (55%)
  Pallas kernels  114 us (20%)
  starting transfers between devices  71.4 us (12%)
  other arithmetic  35 us (6%)
  local copies, waits for them, and re-layouts  27.8 us (5%)
    ppermute x18, waiting for transfers between devices, shift(): lax.ppermute(values, 'lon', [(z, (z + steps) % lon_count) for z in range(...  145 us
    all_to_all x3, waiting for transfers between devices, outward(): return lax.all_to_all(flat, ('lon', 'ch'), 0, 0, tiled=True).reshape(shape)  126 us
    pallas_call x3, Pallas kernels, mlp(): pl.pallas_call(mlp_kernel, grid_spec=pltpu.PrefetchScalarGridSpec(num_sca...  47.4 us
    ppermute x15, waiting for transfers between devices, swap(): return lax.ppermute(values, axis, [(0, 1), (1, 0)])  47.1 us
    ppermute x18, starting transfers between devices, shift(): lax.ppermute(values, 'lon', [(z, (z + steps) % lon_count) for z in range(...  40.6 us
    pallas_call x3, Pallas kernels, lat_inverse(): pl.pallas_call(lat_inverse_kernel, grid=(cols // 16,), in_specs=[pl.Block...  21.6 us
    all_to_all x3, starting transfers between devices, outward(): return lax.all_to_all(flat, ('lon', 'ch'), 0, 0, tiled=True).reshape(shape)  19.9 us
    pallas_call x1, Pallas kernels, modes(): pl.pallas_call(functools.partial(modes_kernel, len(flat)), grid=(pairs,),...  16.2 us
  transfers between devices with their start and end apart: 36, of which 17 were waited for; matrix products, arithmetic and copies ran while one was open for 6% of the time, Pallas kernels for 14%

profile of v4, /device:TPU:0, one launch (start us, length us, event | category | flops | bytes accessed | tf_op | source)
XLA Modules:
  0.0 569.1 jit_solution(5276546659382550955)
XLA Ops:
  0.0 2.5 convert_reduce_fusion.2
  2.6 2.9 fusion.1
  6.2 1.8 dynamic-slice_bitcast_fusion.1.table_ref
  8.2 4.5 fusion.5.cells_ref
  12.8 5.6 lat_forward.3
  19.1 2.6 collective-permute-start.1
  21.6 1.5 fusion.7
  24.7 4.5 fusion.11.cells_ref
  29.2 4.9 lat_forward.4
  34.2 24.9 %collective-permute-done.1 = bf16[4,17,32,384]{3,2,1,0:T(8,128)(2,1)} collective-permute-done((bf16[4,17,32,384]{3,2,1,0:T(8,128)(2,1)}, bf16[4,17,32,384]{3,2,1,0:T(8,128)(2,1)}, u32[]{:S(2)}, u32[]{:S(2)}) %collective-permute-start.1) | collective-permute-done | bytes 1671200 | tf_op jit(solution)/shard_map/ppermute | solution.py:393
  59.8 1.8 collective-permute-start.3
  61.6 1.6 fusion.13
  63.3 1.9 fusion.21
  65.2 3.7 collective-permute-start.7
  70.0 1.7 fusion.17.cells_ref
  71.7 5.6 lat_forward.5
  77.3 1.5 collective-permute-done.7.refs_3_.refs_15_
  78.9 26.4 %collective-permute-done.6.refs_2_.refs_14_ = bf16[17,32,384]{2,1,0:T(8,128)(2,1)} collective-permute-done((bf16[17,32,384]{2,1,0:T(8,128)(2,1)S(1)}, bf16[17,32,384]{2,1,0:T(8,128)(2,1)}, u32[]{:S(2)}, u32[]{:S(2)}) %collective-permute-start.6) | collective-permute-done | bytes 417824 | tf_op jit(solution)/shard_map/ppermute | solution.py:399
  106.6 1.5 fusion.49
  108.1 1.6 fusion.25
  109.7 2.8 collective-permute-start.10
  112.5 2.0 collective-permute-start.9
  118.7 2.0 squeeze.46
  122.8 2.3 maximum_maximum_fusion.1.refs_28_
  125.1 2.2 maximum_maximum_fusion.refs_26_
  127.3 21.3 %collective-permute-done.10.refs_6_.refs_18_ = bf16[17,32,384]{2,1,0:T(8,128)(2,1)} collective-permute-done((bf16[17,32,384]{2,1,0:T(8,128)(2,1)}, bf16[17,32,384]{2,1,0:T(8,128)(2,1)}, u32[]{:S(2)}, u32[]{:S(2)}) %collective-permute-start.10) | collective-permute-done | bytes 417824 | tf_op jit(solution)/shard_map/ppermute | solution.py:399
  149.8 2.0 dynamic-slice_bitcast_fusion.table_ref
  153.7 1.8 all-gather
  156.1 1.9 collective-permute-start.12
  158.3 1.7 pad_maximum_fusion.1.w_out_ref
  160.0 8.5 %collective-permute-done.14.refs_11_.refs_23_ = bf16[17,32,384]{2,1,0:T(8,128)(2,1)S(1)} collective-permute-done((bf16[17,32,384]{2,1,0:T(8,128)(2,1)S(1)}, bf16[17,32,384]{2,1,0:T(8,128)(2,1)S(1)}, u32[]{:S(2)}, u32[]{:S(2)}) %collective-permute-start.14) | collective-permute-done | bytes 417824 | tf_op jit(solution)/shard_map/ppermute | solution.py:399
  168.5 24.3 %collective-permute-done.13.refs_10_.refs_22_ = bf16[17,32,384]{2,1,0:T(8,128)(2,1)S(1)} collective-permute-done((bf16[17,32,384]{2,1,0:T(8,128)(2,1)S(1)}, bf16[17,32,384]{2,1,0:T(8,128)(2,1)S(1)}, u32[]{:S(2)}, u32[]{:S(2)}) %collective-permute-start.13) | collective-permute-done | bytes 417824 | tf_op jit(solution)/shard_map/ppermute | solution.py:399
  193.7 16.2 %modes.1 = (bf16[17,32,384]{2,1,0:T(8,128)(2,1)S(1)}, bf16[17,32,384]{2,1,0:T(8,128)(2,1)S(1)}, bf16[17,32,384]{2,1,0:T(8,128)(2,1)S(1)}, bf16[17,32,384]{2,1,0:...) custom-call(s32[1]{0:T(128)} %bitcast.23.first_pair_ref, ...), custom_call_target="tpu_custom_call" | custom-call | flops 7247757312 | bytes 10027008 | tf_op jit(solution)/shard_map/modes/pallas_call | solution.py:271
  210.1 2.0 collective-permute-start.19
  212.1 2.8 collective-permute-start.20
  214.9 9.5 %collective-permute-done.18 = bf16[17,32,384]{2,1,0:T(8,128)(2,1)S(1)} collective-permute-done((bf16[17,32,384]{2,1,0:T(8,128)(2,1)S(1)}, bf16[17,32,384]{2,1,0:T(8,128)(2,1)S(1)}, u32[]{:S(2)}, u32[]{:S(2)}) %collective-permute-start.18) | collective-permute-done | bytes 417824 | tf_op jit(solution)/shard_map/ppermute | solution.py:399
  224.4 16.6 %collective-permute-done.19 = bf16[17,32,384]{2,1,0:T(8,128)(2,1)S(1)} collective-permute-done((bf16[17,32,384]{2,1,0:T(8,128)(2,1)S(1)}, bf16[17,32,384]{2,1,0:T(8,128)(2,1)S(1)}, u32[]{:S(2)}, u32[]{:S(2)}) %collective-permute-start.19) | collective-permute-done | bytes 417824 | tf_op jit(solution)/shard_map/ppermute | solution.py:399
  242.5 9.0 %collective-permute-start.21 = (bf16[17,32,384]{2,1,0:T(8,128)(2,1)S(1)}, bf16[17,32,384]{2,1,0:T(8,128)(2,1)S(1)}, u32[]{:S(2)}, u32[]{:S(2)}) collective-permute-start(bf16[17,32,384]{2,1,0:T(8,128)(2,1)S(1)} %get-tuple-element.247), channel_id=1, source_target_pairs={{0,4},{4,8},{8,12},{12,0},{1,5},{5,9},{9,13},{13,1},{2,6},{6,10},{... | collective-permute-start | bytes 1253384 | tf_op jit(solution)/shard_map/ppermute | solution.py:399
  251.5 2.2 collective-permute-start.22
  254.1 9.7 %collective-permute-done.21 = bf16[17,32,384]{2,1,0:T(8,128)(2,1)S(1)} collective-permute-done((bf16[17,32,384]{2,1,0:T(8,128)(2,1)S(1)}, bf16[17,32,384]{2,1,0:T(8,128)(2,1)S(1)}, u32[]{:S(2)}, u32[]{:S(2)}) %collective-permute-start.21) | collective-permute-done | bytes 417824 | tf_op jit(solution)/shard_map/ppermute | solution.py:399
  263.8 16.0 %collective-permute-done.22 = bf16[17,32,384]{2,1,0:T(8,128)(2,1)S(1)} collective-permute-done((bf16[17,32,384]{2,1,0:T(8,128)(2,1)S(1)}, bf16[17,32,384]{2,1,0:T(8,128)(2,1)S(1)}, u32[]{:S(2)}, u32[]{:S(2)}) %collective-permute-start.22) | collective-permute-done | bytes 417824 | tf_op jit(solution)/shard_map/ppermute | solution.py:399
  279.9 6.9 %lat_inverse.3 = (bf16[4,16,32,384]{3,2,1,0:T(8,128)(2,1)S(1)}, bf16[4,16,32,384]{3,2,1,0:T(8,128)(2,1)S(1)}) custom-call(s32[2]{0:T(128)S(1)} %pad_add_fusion.where_ref, bf16[4,17,32,384]{3,2,1,0:T(8,128)(2,1)S(1)} %pad_maximum_fusion.2.own_ref, bf16[4,17,32,384]{3,2,1,0:T(8,128)(2,1)S(1)} %collective-permute-done.24.other_ref, ...), custom_call_target="tpu_custom_call" | custom-call | flops 3623878656 | bytes 9437184 | tf_op jit(solution)/shard_map/lat_inverse/pallas_call | solution.py:157
  287.7 9.4 %collective-permute-start.25 = (bf16[17,32,384]{2,1,0:T(8,128)(2,1)S(1)}, bf16[17,32,384]{2,1,0:T(8,128)(2,1)S(1)}, u32[]{:S(2)}, u32[]{:S(2)}) collective-permute-start(bf16[17,32,384]{2,1,0:T(8,128)(2,1)S(1)} %get-tuple-element.260), channel_id=1, source_target_pairs={{0,4},{4,8},{8,12},{12,0},{1,5},{5,9},{9,13},{13,1},{2,6},{6,10},{... | collective-permute-start | bytes 1253384 | tf_op jit(solution)/shard_map/ppermute | solution.py:399
  299.5 15.7 %channel_mlp.3 = bf16[4,2,16,32,384]{4,3,2,1,0:T(8,128)(2,1)} custom-call(s32[2]{0:T(128)S(1)} %pad_add_fusion.where_ref, bf16[4,16,32,384]{3,2,1,0:T(8,128)(2,1)S(1)} %get-tuple-element.271.own_ref, bf16[4,16,32,384]{3,2,1,0:T(8,128)(2,1)S(1)} %collective-permute-done.29.other_ref, f32[1,768]{1,0:T(1,128)S(1)} %reshape.285.gain_ref, ...), custom_call_target="tpu_custom_call" | custom-call | flops 9663676416 | bytes 6291456 | tf_op jit(solution)/shard_map/channel_mlp/pallas_call | solution.py:323
  315.3 10.8 %collective-permute-done.26 = bf16[17,32,384]{2,1,0:T(8,128)(2,1)S(1)} collective-permute-done((bf16[17,32,384]{2,1,0:T(8,128)(2,1)S(1)}, bf16[17,32,384]{2,1,0:T(8,128)(2,1)S(1)}, u32[]{:S(2)}, u32[]{:S(2)}) %collective-permute-start.26) | collective-permute-done | bytes 417824 | tf_op jit(solution)/shard_map/ppermute | solution.py:399
  328.2 11.6 %all-to-all-start = ((bf16[8,16,32,384]{3,2,1,0:T(8,128)(2,1)}), bf16[8,16,32,384]{3,2,1,0:T(8,128)(2,1)}, u32[]{:S(2)}, u32[]{:S(2)}) async-start(bf16[8,16,32,384]{3,2,1,0:T(8,128)(2,1)} %bitcast.135), calls=%async_computation | async-start | bytes 6291456 | tf_op jit(solution)/shard_map/all_to_all | solution.py:505
  339.8 1.4 copy-done.1
  341.2 1.4 copy-done.8
  342.7 7.0 %lat_inverse.4 = (bf16[4,16,32,384]{3,2,1,0:T(8,128)(2,1)S(1)}, bf16[4,16,32,384]{3,2,1,0:T(8,128)(2,1)S(1)}) custom-call(s32[2]{0:T(128)S(1)} %pad_add_fusion.where_ref, bf16[4,17,32,384]{3,2,1,0:T(8,128)(2,1)S(1)} %copy-done.1, bf16[4,17,32,384]{3,2,1,0:T(8,128)(2,1)S(1)} %copy-done.8, bf16[1024,1152]{1,0:T(8,128)(2,1)S(1)} %dynamic-slice_bitcast_fusion.table_ref, ...), custom_call_target="tpu_custom_call" | custom-call | flops 3623878656 | bytes 9437184 | tf_op jit(solution)/shard_map/lat_inverse/pallas_call | solution.py:157
  350.5 1.5 collective-permute-start.30
  353.3 15.8 %channel_mlp.4 = bf16[4,2,16,32,384]{4,3,2,1,0:T(8,128)(2,1)} custom-call(s32[2]{0:T(128)S(1)} %pad_add_fusion.where_ref, bf16[4,16,32,384]{3,2,1,0:T(8,128)(2,1)S(1)} %get-tuple-element.287.own_ref, bf16[4,16,32,384]{3,2,1,0:T(8,128)(2,1)S(1)} %collective-permute-done.31.other_ref, f32[1,768]{1,0:T(1,128)S(1)} %reshape.285.gain_ref, ...), custom_call_target="tpu_custom_call" | custom-call | flops 9663676416 | bytes 6291456 | tf_op jit(solution)/shard_map/channel_mlp/pallas_call | solution.py:323
  369.1 20.0 %collective-permute-done.30.other_ref = bf16[4,17,32,384]{3,2,1,0:T(8,128)(2,1)S(1)} collective-permute-done((bf16[4,17,32,384]{3,2,1,0:T(8,128)(2,1)S(1)}, bf16[4,17,32,384]{3,2,1,0:T(8,128)(2,1)S(1)}, u32[]{:S(2)}, u32[]{:S(2)}) %collective-permute-start.30) | collective-permute-done | bytes 1671200 | tf_op jit(solution)/shard_map/ppermute | solution.py:393
  390.2 21.2 %all-to-all-done = bf16[8,16,32,384]{3,2,1,0:T(8,128)(2,1)} async-done(((bf16[8,16,32,384]{3,2,1,0:T(8,128)(2,1)}), bf16[8,16,32,384]{3,2,1,0:T(8,128)(2,1)}, u32[]{:S(2)}, u32[]{:S(2)}) %all-to-all-start) | async-done | bytes 3145760 | tf_op jit(solution)/shard_map/all_to_all | solution.py:505
  411.4 4.7 all-to-all-start.1
  417.6 1.4 copy-done.10
  419.0 7.7 %lat_inverse.5 = (bf16[4,16,32,384]{3,2,1,0:T(8,128)(2,1)S(1)}, bf16[4,16,32,384]{3,2,1,0:T(8,128)(2,1)}) custom-call(s32[2]{0:T(128)S(1)} %pad_add_fusion.where_ref, bf16[4,17,32,384]{3,2,1,0:T(8,128)(2,1)S(1)} %copy-done.3, bf16[4,17,32,384]{3,2,1,0:T(8,128)(2,1)S(1)} %copy-done.10, bf16[1024,1152]{1,0:T(8,128)(2,1)S(1)} %dynamic-slice_bitcast_fusion.table_ref, ...), custom_call_target="tpu_custom_call" | custom-call | flops 3623878656 | bytes 9437184 | tf_op jit(solution)/shard_map/lat_inverse/pallas_call | solution.py:157
  428.3 4.4 assemble.3.refs_0_
  434.2 15.9 %channel_mlp.5 = bf16[4,2,16,32,384]{4,3,2,1,0:T(8,128)(2,1)} custom-call(s32[2]{0:T(128)S(1)} %pad_add_fusion.where_ref, bf16[4,16,32,384]{3,2,1,0:T(8,128)(2,1)S(1)} %copy-done.16, bf16[4,16,32,384]{3,2,1,0:T(8,128)(2,1)} %collective-permute-done.32.other_ref, f32[1,768]{1,0:T(1,128)S(1)} %reshape.285.gain_ref, f32[1,768]{1,0:T(1,128)S(1)} %reshape.286.bias_ref, ...), custom_call_target="tpu_custom_call" | custom-call | flops 9663676416 | bytes 6291456 | tf_op jit(solution)/shard_map/channel_mlp/pallas_call | solution.py:323
  450.1 37.6 %all-to-all-done.1 = bf16[8,16,32,384]{3,2,1,0:T(8,128)(2,1)} async-done(((bf16[8,16,32,384]{3,2,1,0:T(8,128)(2,1)}), bf16[8,16,32,384]{3,2,1,0:T(8,128)(2,1)}, u32[]{:S(2)}, u32[]{:S(2)}) %all-to-all-start.1) | async-done | bytes 3145760 | tf_op jit(solution)/shard_map/all_to_all | solution.py:505
  487.7 3.6 all-to-all-start.2
  491.3 4.2 assemble.4.refs_0_
  495.6 67.2 %all-to-all-done.2 = bf16[8,16,32,384]{3,2,1,0:T(8,128)(2,1)S(1)} async-done(((bf16[8,16,32,384]{3,2,1,0:T(8,128)(2,1)}), bf16[8,16,32,384]{3,2,1,0:T(8,128)(2,1)S(1)}, u32[]{:S(2)}, u32[]{:S(2)}) %all-to-all-start.2) | async-done | bytes 3145760 | tf_op jit(solution)/shard_map/all_to_all | solution.py:505
  562.8 1.6 copy-done.17
  564.4 4.2 assemble.5
  (185 shorter events, 32.6 us)
Async XLA Ops:
  2.5 3.5 copy-start.37
  2.5 3.7 copy-start.32
  5.5 2.6 collective-permute-start
  8.2 10.2 %slice-start = ((s8[9437184]{0:T(1024)(128)(4,1)}), s8[4194304]{0:T(1024)(128)(4,1)S(1)}, s32[]{:S(2)}) async-start(s8[9437184]{0:T(1024)(128)(4,1)} %bitcast.130), calls=%async_computation.3 | async-start | bytes 8388608
  8.2 10.2 %slice-start.1 = ((s8[9437184]{0:T(1024)(128)(4,1)}), s8[4194304]{0:T(1024)(128)(4,1)S(1)}, s32[]{:S(2)}) async-start(s8[9437184]{0:T(1024)(128)(4,1)} %bitcast.130), calls=%async_computation.4 | async-start | bytes 8388608
  12.8 5.6 slice-start.2
  18.4 4.8 copy-start.13
  19.0 4.5 copy-start.33
  19.0 4.5 copy-start.38
  19.1 40.0 %collective-permute-start.1 = (bf16[4,17,32,384]{3,2,1,0:T(8,128)(2,1)}, bf16[4,17,32,384]{3,2,1,0:T(8,128)(2,1)}, u32[]{:S(2)}, u32[]{:S(2)}) collective-permute-start(bf16[4,17,32,384]{3,2,1,0:T(8,128)(2,1)} %get-tuple-element.157), channel_id=1, source_target_pairs={{0,2},{2,0},{1,3},{3,1},{4,6},{6,4},{5,7},{7,5},{8,10},{10,8},{9,1... | collective-permute-start | bytes 5013512 | tf_op jit(solution)/shard_map/ppermute | solution.py:393
  23.2 1.4 collective-permute-start.2
  24.7 34.4 %slice-start.3 = ((s8[9437184]{0:T(1024)(128)(4,1)}), s8[4194304]{0:T(1024)(128)(4,1)S(1)}, s32[]{:S(2)}) async-start(s8[9437184]{0:T(1024)(128)(4,1)} %bitcast.132), calls=%async_computation.6 | async-start | bytes 8388608
  24.7 34.4 %slice-start.4 = ((s8[9437184]{0:T(1024)(128)(4,1)}), s8[4194304]{0:T(1024)(128)(4,1)S(1)}, s32[]{:S(2)}) async-start(s8[9437184]{0:T(1024)(128)(4,1)} %bitcast.132), calls=%async_computation.7 | async-start | bytes 8388608
  29.2 29.9 %slice-start.5 = ((s8[9437184]{0:T(1024)(128)(4,1)}), s8[1048576]{0:T(1024)(128)(4,1)S(1)}, s32[]{:S(2)}) async-start(s8[9437184]{0:T(1024)(128)(4,1)} %bitcast.132), calls=%async_computation.8 | async-start | bytes 2097152
  59.8 3.5 copy-start.14
  59.8 45.4 %collective-permute-start.3 = (bf16[4,17,32,384]{3,2,1,0:T(8,128)(2,1)S(1)}, bf16[4,17,32,384]{3,2,1,0:T(8,128)(2,1)S(1)}, u32[]{:S(2)}, u32[]{:S(2)}) collective-permute-start(bf16[4,17,32,384]{3,2,1,0:T(8,128)(2,1)S(1)} %get-tuple-element.166), channel_id=1, source_target_pairs={{0,2},{2,0},{1,3},{3,1},{4,6},{6,4},{5,7},{7,5},{8,10},{10,8},{9,1... | collective-permute-start | bytes 5013512 | tf_op jit(solution)/shard_map/ppermute | solution.py:393
  63.2 6.8 %collective-permute-start.4 = (f32[2,128,32]{2,1,0:T(8,128)S(1)}, f32[2,128,32]{2,1,0:T(8,128)S(1)}, u32[]{:S(2)}, u32[]{:S(2)}) collective-permute-start(f32[2,128,32]{2,1,0:T(8,128)S(1)} %pad_maximum_fusion.7), channel_id=1, source_target_pairs={{0,1},{1,0},{2,3},{3,2},{4,5},{5,4},{6,7},{7,6},{8,9},{9,8},{10,11... | collective-permute-start | bytes 98312 | tf_op jit(solution)/shard_map/ppermute | solution.py:393
  65.2 13.7 %collective-permute-start.7 = (bf16[17,32,384]{2,1,0:T(8,128)(2,1)S(1)}, bf16[17,32,384]{2,1,0:T(8,128)(2,1)S(1)}, u32[]{:S(2)}, u32[]{:S(2)}) collective-permute-start(bf16[17,32,384]{2,1,0:T(8,128)(2,1)S(1)} %get-tuple-element.309), channel_id=1, source_target_pairs={{0,12},{4,0},{8,4},{12,8},{1,13},{5,1},{9,5},{13,9},{2,14},{6,2},{... | collective-permute-start | bytes 1253384 | tf_op jit(solution)/shard_map/ppermute | solution.py:399
  68.8 36.4 %collective-permute-start.6 = (bf16[17,32,384]{2,1,0:T(8,128)(2,1)S(1)}, bf16[17,32,384]{2,1,0:T(8,128)(2,1)}, u32[]{:S(2)}, u32[]{:S(2)}) collective-permute-start(bf16[17,32,384]{2,1,0:T(8,128)(2,1)S(1)} %get-tuple-element.310), channel_id=1, source_target_pairs={{0,8},{4,12},{8,0},{12,4},{1,9},{5,13},{9,1},{13,5},{2,10},{6,14},... | collective-permute-start | bytes 1253384 | tf_op jit(solution)/shard_map/ppermute | solution.py:399
  68.8 36.4 %collective-permute-start.5 = (bf16[17,32,384]{2,1,0:T(8,128)(2,1)S(1)}, bf16[17,32,384]{2,1,0:T(8,128)(2,1)}, u32[]{:S(2)}, u32[]{:S(2)}) collective-permute-start(bf16[17,32,384]{2,1,0:T(8,128)(2,1)S(1)} %get-tuple-element.311), channel_id=1, source_target_pairs={{0,4},{4,8},{8,12},{12,0},{1,5},{5,9},{9,13},{13,1},{2,6},{6,10},{... | collective-permute-start | bytes 1253384 | tf_op jit(solution)/shard_map/ppermute | solution.py:399
  71.7 34.1 %copy-start.27 = (bf16[2,4,96,96]{3,2,1,0:T(8,128)(2,1)S(1)}, bf16[2,4,96,96]{3,2,1,0:T(8,128)(2,1)}, u32[]{:S(2)}) copy-start(bf16[2,4,96,96]{3,2,1,0:T(8,128)(2,1)} %param.24) | copy-start | bytes 442372
  71.7 34.1 %copy-start.28 = (bf16[2,4,96,96]{3,2,1,0:T(8,128)(2,1)S(1)}, bf16[2,4,96,96]{3,2,1,0:T(8,128)(2,1)}, u32[]{:S(2)}) copy-start(bf16[2,4,96,96]{3,2,1,0:T(8,128)(2,1)} %param.22) | copy-start | bytes 442372
  77.3 30.8 %copy-start.11 = (bf16[4,17,32,384]{3,2,1,0:T(8,128)(2,1)}, bf16[4,17,32,384]{3,2,1,0:T(8,128)(2,1)S(1)}, u32[]{:S(2)}) copy-start(bf16[4,17,32,384]{3,2,1,0:T(8,128)(2,1)S(1)} %get-tuple-element.197) | copy-start | bytes 5013508
  78.9 29.3 %copy-start.39 = (bf16[17,32,384]{2,1,0:T(8,128)(2,1)}, bf16[17,32,384]{2,1,0:T(8,128)(2,1)S(1)}, u32[]{:S(2)}) copy-start(bf16[17,32,384]{2,1,0:T(8,128)(2,1)S(1)} %collective-permute-done.7.refs_3_.refs_15_) | copy-start | bytes 1253380
  105.2 43.3 %collective-permute-start.8 = (bf16[4,17,32,384]{3,2,1,0:T(8,128)(2,1)}, bf16[4,17,32,384]{3,2,1,0:T(8,128)(2,1)S(1)}, u32[]{:S(2)}, u32[]{:S(2)}) collective-permute-start(bf16[4,17,32,384]{3,2,1,0:T(8,128)(2,1)} %get-tuple-element.177), channel_id=1, source_target_pairs={{0,2},{2,0},{1,3},{3,1},{4,6},{6,4},{5,7},{7,5},{8,10},{10,8},{9,1... | collective-permute-start | bytes 5013512 | tf_op jit(solution)/shard_map/ppermute | solution.py:393
  109.7 17.6 %collective-permute-start.11 = (bf16[17,32,384]{2,1,0:T(8,128)(2,1)}, bf16[17,32,384]{2,1,0:T(8,128)(2,1)}, u32[]{:S(2)}, u32[]{:S(2)}) collective-permute-start(bf16[17,32,384]{2,1,0:T(8,128)(2,1)} %get-tuple-element.305), channel_id=1, source_target_pairs={{0,12},{4,0},{8,4},{12,8},{1,13},{5,1},{9,5},{13,9},{2,14},{6,2},{... | collective-permute-start | bytes 1253384 | tf_op jit(solution)/shard_map/ppermute | solution.py:399
  109.7 38.9 %collective-permute-start.10 = (bf16[17,32,384]{2,1,0:T(8,128)(2,1)}, bf16[17,32,384]{2,1,0:T(8,128)(2,1)}, u32[]{:S(2)}, u32[]{:S(2)}) collective-permute-start(bf16[17,32,384]{2,1,0:T(8,128)(2,1)} %get-tuple-element.306), channel_id=1, source_target_pairs={{0,8},{4,12},{8,0},{12,4},{1,9},{5,13},{9,1},{13,5},{2,10},{6,14},... | collective-permute-start | bytes 1253384 | tf_op jit(solution)/shard_map/ppermute | solution.py:399
  112.5 36.1 %collective-permute-start.9 = (bf16[17,32,384]{2,1,0:T(8,128)(2,1)}, bf16[17,32,384]{2,1,0:T(8,128)(2,1)}, u32[]{:S(2)}, u32[]{:S(2)}) collective-permute-start(bf16[17,32,384]{2,1,0:T(8,128)(2,1)} %get-tuple-element.307), channel_id=1, source_target_pairs={{0,4},{4,8},{8,12},{12,0},{1,5},{5,9},{9,13},{13,1},{2,6},{6,10},{... | collective-permute-start | bytes 1253384 | tf_op jit(solution)/shard_map/ppermute | solution.py:399
  121.7 27.5 %copy-start.29 = (bf16[768]{0:T(1024)(128)(2,1)S(1)}, bf16[768]{0:T(1024)(128)(2,1)}, u32[]{:S(2)}) copy-start(bf16[768]{0:T(1024)(128)(2,1)} %param.28) | copy-start | bytes 4612
  121.7 28.1 %copy-start.30 = (bf16[768]{0:T(1024)(128)(2,1)S(1)}, bf16[768]{0:T(1024)(128)(2,1)}, u32[]{:S(2)}) copy-start(bf16[768]{0:T(1024)(128)(2,1)} %param.29) | copy-start | bytes 4612
  121.7 26.9 %copy-start.21 = (bf16[768,768]{1,0:T(8,128)(2,1)S(1)}, bf16[768,768]{1,0:T(8,128)(2,1)}, u32[]{:S(2)}) copy-start(bf16[768,768]{1,0:T(8,128)(2,1)} %param.30) | copy-start | bytes 3538948
  121.7 27.0 %copy-start.22 = (bf16[768,768]{1,0:T(8,128)(2,1)S(1)}, bf16[768,768]{1,0:T(8,128)(2,1)}, u32[]{:S(2)}) copy-start(bf16[768,768]{1,0:T(8,128)(2,1)} %param.32) | copy-start | bytes 3538948
  148.6 9.5 %collective-permute-start.15 = (bf16[768,768]{1,0:T(8,128)(2,1)S(1)}, bf16[768,768]{1,0:T(8,128)(2,1)S(1)}, u32[]{:S(2)}, u32[]{:S(2)}) collective-permute-start(bf16[768,768]{1,0:T(8,128)(2,1)S(1)} %copy-done.21), channel_id=1, source_target_pairs={{0,1},{1,0},{2,3},{3,2},{4,5},{5,4},{6,7},{7,6},{8,9},{9,8},{10,11... | collective-permute-start | bytes 3538952 | tf_op jit(solution)/shard_map/ppermute | solution.py:393
  148.7 9.6 %collective-permute-start.17 = (bf16[768,768]{1,0:T(8,128)(2,1)S(1)}, bf16[768,768]{1,0:T(8,128)(2,1)S(1)}, u32[]{:S(2)}, u32[]{:S(2)}) collective-permute-start(bf16[768,768]{1,0:T(8,128)(2,1)S(1)} %copy-done.22), channel_id=1, source_target_pairs={{0,1},{1,0},{2,3},{3,2},{4,5},{5,4},{6,7},{7,6},{8,9},{9,8},{10,11... | collective-permute-start | bytes 3538952 | tf_op jit(solution)/shard_map/ppermute | solution.py:393
  151.8 4.3 collective-permute-start.16
  155.5 13.0 %collective-permute-start.14 = (bf16[17,32,384]{2,1,0:T(8,128)(2,1)S(1)}, bf16[17,32,384]{2,1,0:T(8,128)(2,1)S(1)}, u32[]{:S(2)}, u32[]{:S(2)}) collective-permute-start(bf16[17,32,384]{2,1,0:T(8,128)(2,1)S(1)} %get-tuple-element.301), channel_id=1, source_target_pairs={{0,12},{4,0},{8,4},{12,8},{1,13},{5,1},{9,5},{13,9},{2,14},{6,2},{... | collective-permute-start | bytes 1253384 | tf_op jit(solution)/shard_map/ppermute | solution.py:399
  155.5 37.3 %collective-permute-start.13 = (bf16[17,32,384]{2,1,0:T(8,128)(2,1)S(1)}, bf16[17,32,384]{2,1,0:T(8,128)(2,1)S(1)}, u32[]{:S(2)}, u32[]{:S(2)}) collective-permute-start(bf16[17,32,384]{2,1,0:T(8,128)(2,1)S(1)} %get-tuple-element.302), channel_id=1, source_target_pairs={{0,8},{4,12},{8,0},{12,4},{1,9},{5,13},{9,1},{13,5},{2,10},{6,14},... | collective-permute-start | bytes 1253384 | tf_op jit(solution)/shard_map/ppermute | solution.py:399
  156.1 36.7 %collective-permute-start.12 = (bf16[17,32,384]{2,1,0:T(8,128)(2,1)S(1)}, bf16[17,32,384]{2,1,0:T(8,128)(2,1)S(1)}, u32[]{:S(2)}, u32[]{:S(2)}) collective-permute-start(bf16[17,32,384]{2,1,0:T(8,128)(2,1)S(1)} %get-tuple-element.303), channel_id=1, source_target_pairs={{0,4},{4,8},{8,12},{12,0},{1,5},{5,9},{9,13},{13,1},{2,6},{6,10},{... | collective-permute-start | bytes 1253384 | tf_op jit(solution)/shard_map/ppermute | solution.py:399
  158.2 141.3 %copy-start.4 = (bf16[768,1536]{1,0:T(8,128)(2,1)}, bf16[768,1536]{1,0:T(8,128)(2,1)S(1)}, u32[]{:S(2)}) copy-start(bf16[768,1536]{1,0:T(8,128)(2,1)S(1)} %pad_maximum_fusion.w_in_ref) | copy-start | bytes 7077892
  168.5 24.3 %copy-start.40 = (bf16[17,32,384]{2,1,0:T(8,128)(2,1)}, bf16[17,32,384]{2,1,0:T(8,128)(2,1)S(1)}, u32[]{:S(2)}) copy-start(bf16[17,32,384]{2,1,0:T(8,128)(2,1)S(1)} %collective-permute-done.14.refs_11_.refs_23_) | copy-start | bytes 1253380
  209.9 14.5 %collective-permute-start.18 = (bf16[17,32,384]{2,1,0:T(8,128)(2,1)S(1)}, bf16[17,32,384]{2,1,0:T(8,128)(2,1)S(1)}, u32[]{:S(2)}, u32[]{:S(2)}) collective-permute-start(bf16[17,32,384]{2,1,0:T(8,128)(2,1)S(1)} %get-tuple-element.234), channel_id=1, source_target_pairs={{0,4},{4,8},{8,12},{12,0},{1,5},{5,9},{9,13},{13,1},{2,6},{6,10},{... | collective-permute-start | bytes 1253384 | tf_op jit(solution)/shard_map/ppermute | solution.py:399
  210.1 30.9 %collective-permute-start.19 = (bf16[17,32,384]{2,1,0:T(8,128)(2,1)S(1)}, bf16[17,32,384]{2,1,0:T(8,128)(2,1)S(1)}, u32[]{:S(2)}, u32[]{:S(2)}) collective-permute-start(bf16[17,32,384]{2,1,0:T(8,128)(2,1)S(1)} %get-tuple-element.235), channel_id=1, source_target_pairs={{0,8},{4,12},{8,0},{12,4},{1,9},{5,13},{9,1},{13,5},{2,10},{6,14},... | collective-permute-start | bytes 1253384 | tf_op jit(solution)/shard_map/ppermute | solution.py:399
  212.1 28.9 %collective-permute-start.20 = (bf16[17,32,384]{2,1,0:T(8,128)(2,1)S(1)}, bf16[17,32,384]{2,1,0:T(8,128)(2,1)S(1)}, u32[]{:S(2)}, u32[]{:S(2)}) collective-permute-start(bf16[17,32,384]{2,1,0:T(8,128)(2,1)S(1)} %get-tuple-element.236), channel_id=1, source_target_pairs={{0,12},{4,0},{8,4},{12,8},{1,13},{5,1},{9,5},{13,9},{2,14},{6,2},{... | collective-permute-start | bytes 1253384 | tf_op jit(solution)/shard_map/ppermute | solution.py:399
  241.3 38.6 %collective-permute-start.24 = (bf16[4,17,32,384]{3,2,1,0:T(8,128)(2,1)S(1)}, bf16[4,17,32,384]{3,2,1,0:T(8,128)(2,1)S(1)}, u32[]{:S(2)}, u32[]{:S(2)}) collective-permute-start(bf16[4,17,32,384]{3,2,1,0:T(8,128)(2,1)S(1)} %pad_maximum_fusion.2.own_ref), channel_id=1, source_target_pairs={{0,2},{2,0},{1,3},{3,1},{4,6},{6,4},{5,7},{7,5},{8,10},{10,8},{9,1... | collective-permute-start | bytes 5013512 | tf_op jit(solution)/shard_map/ppermute | solution.py:393
  242.5 21.3 %collective-permute-start.21 = (bf16[17,32,384]{2,1,0:T(8,128)(2,1)S(1)}, bf16[17,32,384]{2,1,0:T(8,128)(2,1)S(1)}, u32[]{:S(2)}, u32[]{:S(2)}) collective-permute-start(bf16[17,32,384]{2,1,0:T(8,128)(2,1)S(1)} %get-tuple-element.247), channel_id=1, source_target_pairs={{0,4},{4,8},{8,12},{12,0},{1,5},{5,9},{9,13},{13,1},{2,6},{6,10},{... | collective-permute-start | bytes 1253384 | tf_op jit(solution)/shard_map/ppermute | solution.py:399
  251.5 28.3 %collective-permute-start.22 = (bf16[17,32,384]{2,1,0:T(8,128)(2,1)S(1)}, bf16[17,32,384]{2,1,0:T(8,128)(2,1)S(1)}, u32[]{:S(2)}, u32[]{:S(2)}) collective-permute-start(bf16[17,32,384]{2,1,0:T(8,128)(2,1)S(1)} %get-tuple-element.248), channel_id=1, source_target_pairs={{0,8},{4,12},{8,0},{12,4},{1,9},{5,13},{9,1},{13,5},{2,10},{6,14},... | collective-permute-start | bytes 1253384 | tf_op jit(solution)/shard_map/ppermute | solution.py:399
  253.7 26.2 %collective-permute-start.23 = (bf16[17,32,384]{2,1,0:T(8,128)(2,1)S(1)}, bf16[17,32,384]{2,1,0:T(8,128)(2,1)S(1)}, u32[]{:S(2)}, u32[]{:S(2)}) collective-permute-start(bf16[17,32,384]{2,1,0:T(8,128)(2,1)S(1)} %get-tuple-element.249), channel_id=1, source_target_pairs={{0,12},{4,0},{8,4},{12,8},{1,13},{5,1},{9,5},{13,9},{2,14},{6,2},{... | collective-permute-start | bytes 1253384 | tf_op jit(solution)/shard_map/ppermute | solution.py:399
  286.8 12.8 %collective-permute-start.29 = (bf16[4,16,32,384]{3,2,1,0:T(8,128)(2,1)S(1)}, bf16[4,16,32,384]{3,2,1,0:T(8,128)(2,1)S(1)}, u32[]{:S(2)}, u32[]{:S(2)}) collective-permute-start(bf16[4,16,32,384]{3,2,1,0:T(8,128)(2,1)S(1)} %get-tuple-element.272), channel_id=1, source_target_pairs={{0,1},{1,0},{2,3},{3,2},{4,5},{5,4},{6,7},{7,6},{8,9},{9,8},{10,11... | collective-permute-start | bytes 4718600 | tf_op jit(solution)/shard_map/ppermute | solution.py:393
  287.1 28.2 %copy-start = (bf16[4,17,32,384]{3,2,1,0:T(8,128)(2,1)}, bf16[4,17,32,384]{3,2,1,0:T(8,128)(2,1)S(1)}, u32[]{:S(2)}) copy-start(bf16[4,17,32,384]{3,2,1,0:T(8,128)(2,1)S(1)} %pad_maximum_fusion.3.own_ref) | copy-start | bytes 5013508
  287.1 39.0 %collective-permute-start.28 = (bf16[4,17,32,384]{3,2,1,0:T(8,128)(2,1)S(1)}, bf16[4,17,32,384]{3,2,1,0:T(8,128)(2,1)S(1)}, u32[]{:S(2)}, u32[]{:S(2)}) collective-permute-start(bf16[4,17,32,384]{3,2,1,0:T(8,128)(2,1)S(1)} %pad_maximum_fusion.3.own_ref), channel_id=1, source_target_pairs={{0,2},{2,0},{1,3},{3,1},{4,6},{6,4},{5,7},{7,5},{8,10},{10,8},{9,1... | collective-permute-start | bytes 5013512 | tf_op jit(solution)/shard_map/ppermute | solution.py:393
  287.7 27.5 %collective-permute-start.25 = (bf16[17,32,384]{2,1,0:T(8,128)(2,1)S(1)}, bf16[17,32,384]{2,1,0:T(8,128)(2,1)S(1)}, u32[]{:S(2)}, u32[]{:S(2)}) collective-permute-start(bf16[17,32,384]{2,1,0:T(8,128)(2,1)S(1)} %get-tuple-element.260), channel_id=1, source_target_pairs={{0,4},{4,8},{8,12},{12,0},{1,5},{5,9},{9,13},{13,1},{2,6},{6,10},{... | collective-permute-start | bytes 1253384 | tf_op jit(solution)/shard_map/ppermute | solution.py:399
  297.2 28.9 %collective-permute-start.26 = (bf16[17,32,384]{2,1,0:T(8,128)(2,1)S(1)}, bf16[17,32,384]{2,1,0:T(8,128)(2,1)S(1)}, u32[]{:S(2)}, u32[]{:S(2)}) collective-permute-start(bf16[17,32,384]{2,1,0:T(8,128)(2,1)S(1)} %get-tuple-element.261), channel_id=1, source_target_pairs={{0,8},{4,12},{8,0},{12,4},{1,9},{5,13},{9,1},{13,5},{2,10},{6,14},... | collective-permute-start | bytes 1253384 | tf_op jit(solution)/shard_map/ppermute | solution.py:399
  298.6 27.5 %collective-permute-start.27 = (bf16[17,32,384]{2,1,0:T(8,128)(2,1)S(1)}, bf16[17,32,384]{2,1,0:T(8,128)(2,1)S(1)}, u32[]{:S(2)}, u32[]{:S(2)}) collective-permute-start(bf16[17,32,384]{2,1,0:T(8,128)(2,1)S(1)} %get-tuple-element.262), channel_id=1, source_target_pairs={{0,12},{4,0},{8,4},{12,8},{1,13},{5,1},{9,5},{13,9},{2,14},{6,2},{... | collective-permute-start | bytes 1253384 | tf_op jit(solution)/shard_map/ppermute | solution.py:399
  328.2 83.2 %all-to-all-start = ((bf16[8,16,32,384]{3,2,1,0:T(8,128)(2,1)}), bf16[8,16,32,384]{3,2,1,0:T(8,128)(2,1)}, u32[]{:S(2)}, u32[]{:S(2)}) async-start(bf16[8,16,32,384]{3,2,1,0:T(8,128)(2,1)} %bitcast.135), calls=%async_computation | async-start | bytes 6291456 | tf_op jit(solution)/shard_map/all_to_all | solution.py:505
  342.7 7.6 %copy-start.24 = (bf16[17,32,384]{2,1,0:T(8,128)(2,1)S(1)}, bf16[17,32,384]{2,1,0:T(8,128)(2,1)}, u32[]{:S(2)}) copy-start(bf16[17,32,384]{2,1,0:T(8,128)(2,1)} %copy-done.23) | copy-start | bytes 1253380
  342.7 7.6 %copy-start.26 = (bf16[17,32,384]{2,1,0:T(8,128)(2,1)S(1)}, bf16[17,32,384]{2,1,0:T(8,128)(2,1)}, u32[]{:S(2)}) copy-start(bf16[17,32,384]{2,1,0:T(8,128)(2,1)} %copy-done.25) | copy-start | bytes 1253380
  349.7 3.6 copy-start.5
  349.7 3.6 collective-permute-start.31
  350.5 18.5 %copy-start.2 = (bf16[4,17,32,384]{3,2,1,0:T(8,128)(2,1)}, bf16[4,17,32,384]{3,2,1,0:T(8,128)(2,1)S(1)}, u32[]{:S(2)}) copy-start(bf16[4,17,32,384]{3,2,1,0:T(8,128)(2,1)S(1)} %pad_maximum_fusion.4.own_ref) | copy-start | bytes 5013508
  350.5 38.5 %collective-permute-start.30 = (bf16[4,17,32,384]{3,2,1,0:T(8,128)(2,1)S(1)}, bf16[4,17,32,384]{3,2,1,0:T(8,128)(2,1)S(1)}, u32[]{:S(2)}, u32[]{:S(2)}) collective-permute-start(bf16[4,17,32,384]{3,2,1,0:T(8,128)(2,1)S(1)} %pad_maximum_fusion.4.own_ref), channel_id=1, source_target_pairs={{0,2},{2,0},{1,3},{3,1},{4,6},{6,4},{5,7},{7,5},{8,10},{10,8},{9,1... | collective-permute-start | bytes 5013512 | tf_op jit(solution)/shard_map/ppermute | solution.py:393
  411.4 76.2 %all-to-all-start.1 = ((bf16[8,16,32,384]{3,2,1,0:T(8,128)(2,1)}), bf16[8,16,32,384]{3,2,1,0:T(8,128)(2,1)}, u32[]{:S(2)}, u32[]{:S(2)}) async-start(bf16[8,16,32,384]{3,2,1,0:T(8,128)(2,1)} %bitcast.136), calls=%async_computation.1 | async-start | bytes 6291456 | tf_op jit(solution)/shard_map/all_to_all | solution.py:505
  427.9 4.9 copy-start.6
  427.9 4.9 collective-permute-start.32
  487.7 75.1 %all-to-all-start.2 = ((bf16[8,16,32,384]{3,2,1,0:T(8,128)(2,1)}), bf16[8,16,32,384]{3,2,1,0:T(8,128)(2,1)S(1)}, u32[]{:S(2)}, u32[]{:S(2)}) async-start(bf16[8,16,32,384]{3,2,1,0:T(8,128)(2,1)} %bitcast.137), calls=%async_computation.2 | async-start | bytes 6291456 | tf_op jit(solution)/shard_map/all_to_all | solution.py:505
  (21 other events, 34.4 us)

commit v5 on v4

--- a/solution.py
+++ b/solution.py
@@ -185,42 +185,66 @@
     forward_ref, inverse_ref, w_in_ref, b_in_ref, w_out_ref, b_out_ref = refs[
         2 * inputs : 2 * inputs + 6
     ]
-    out_refs = refs[2 * inputs + 6 :]
+    out_refs, spare_ref = refs[2 * inputs + 6 : -1], refs[-1]
     width = pair_refs[0].shape[-1]
+    per_step = pair_refs[0].shape[0] // 2
     step = pl.program_id(0)
-    pairs = pl.num_programs(0)
-    pair_id = first_pair_ref[0] + step
+    last_row = 2 * per_step * pl.num_programs(0)
+    pair_id = first_pair_ref[0] + step * per_step
     special = pair_id == 0
     keep = KEEP_LON
 
     def columns(refs, row):
         return jnp.concatenate([ref[row] for ref in refs], axis=0)
 
-    both = jnp.concatenate([columns(pair_refs, 0), columns(pair_refs, 1)], axis=1)
+    @pl.when(special)
+    def _():
+        spare_ref[...] = jnp.dot(
+            forward_ref[...], columns(spare_refs, 0), preferred_element_type=F32
+        )
+
+    both = jnp.concatenate([columns(pair_refs, r) for r in range(2 * per_step)], axis=1)
     spectrum = jnp.dot(forward_ref[...], both, preferred_element_type=F32)
-    a_re, a_im = spectrum[:keep, :width], spectrum[keep:, :width]
-    b_re, b_im = spectrum[:keep, width:], spectrum[keep:, width:]
-
-    def filtered(plus_re, plus_im, minus_re, minus_im):
-        banded = jnp.concatenate(
-            [
-                jnp.concatenate([plus_re, plus_im], axis=1),
-                jnp.concatenate([minus_re, minus_im], axis=1),
-            ],
-            axis=0,
-        ).astype(BF)
-        first = jnp.dot(banded, w_in_ref[...], preferred_element_type=F32) + b_in_ref[...]
-        first = jnp.maximum(first, 0.0).astype(BF)
-        second = jnp.dot(first, w_out_ref[...], preferred_element_type=F32) + b_out_ref[...]
-        shrunk = second - jnp.clip(second, -shrink_level, shrink_level)
-        freq = lax.broadcasted_iota(jnp.int32, (keep, 2 * width), 0)
-        lon_ok = freq < lon_keep_ref[...]
-        plus_ok = lon_ok & (pair_id < lat_keep_ref[...])
-        minus_id = jnp.where(special, MLAT, pair_id)
+    banded = []
+    for q in range(per_step):
+        a = spectrum[:, 2 * q * width : (2 * q + 1) * width]
+        b = spectrum[:, (2 * q + 1) * width : (2 * q + 2) * width]
+        a_re, a_im, b_re, b_im = a[:keep], a[keep:], b[:keep], b[keep:]
+        plus = [a_re - b_im, a_im + b_re]
+        minus = [a_re + b_im, a_im - b_re]
+        if q == 0:
+            plus = [jnp.where(special, a_re, plus[0]), jnp.where(special, a_im, plus[1])]
+            minus = [
+                jnp.where(special, b_re + spare_ref[keep:], minus[0]),
+                jnp.where(special, b_im - spare_ref[:keep], minus[1]),
+            ]
+        banded += [jnp.concatenate(plus, axis=1), jnp.concatenate(minus, axis=1)]
+    banded = jnp.concatenate(banded, axis=0).astype(BF)
+    first = jnp.dot(banded, w_in_ref[...], preferred_element_type=F32) + b_in_ref[...]
+    first = jnp.maximum(first, 0.0).astype(BF)
+    second = jnp.dot(first, w_out_ref[...], preferred_element_type=F32) + b_out_ref[...]
+    shrunk = second - jnp.clip(second, -shrink_level, shrink_level)
+    freq = lax.broadcasted_iota(jnp.int32, (keep, 2 * width), 0)
+    lon_ok = freq < lon_keep_ref[...]
+    upper, lower = [], []
+    for q in range(per_step):
+        plus_ok = lon_ok & (pair_id + q < lat_keep_ref[...])
+        minus_id = jnp.where(special, MLAT, pair_id) if q == 0 else pair_id + q
         minus_ok = lon_ok & (minus_id <= lat_keep_ref[...])
-        plus = jnp.where(plus_ok, shrunk[:keep], 0.0)
-        minus = jnp.where(minus_ok, shrunk[keep:], 0.0)
-        return plus[:, :width], plus[:, width:], minus[:, :width], minus[:, width:]
+        plus = jnp.where(plus_ok, shrunk[2 * q * keep : (2 * q + 1) * keep], 0.0)
+        minus = jnp.where(minus_ok, shrunk[(2 * q + 1) * keep : (2 * q + 2) * keep], 0.0)
+        p_re, p_im, m_re, m_im = plus[:, :width], plus[:, width:], minus[:, :width], minus[:, width:]
+        tops = [p_re + m_re, p_im - m_im]
+        bottoms = [p_im + m_im, m_re - p_re]
+        if q == 0:
+            tops = [jnp.where(special, p_re, tops[0]), jnp.where(special, m_re, tops[1])]
+            bottoms = [jnp.where(special, p_im, bottoms[0]), jnp.where(special, m_im, bottoms[1])]
+            loose = jnp.concatenate([-m_im, m_re], axis=0).astype(BF)
+        upper += tops
+        lower += bottoms
+    values = jnp.concatenate(
+        [jnp.concatenate(upper, axis=1), jnp.concatenate(lower, axis=1)], axis=0
+    ).astype(BF)
 
     def back(values, row):
         grid_values = jnp.dot(inverse_ref[...], values, preferred_element_type=F32).astype(BF)
@@ -231,33 +255,16 @@
                 ref[row + r] = grid_values[start : start + cols, r * width : (r + 1) * width]
             start += cols
 
+    back(values, 2 * per_step * step)
+
     @pl.when(special)
     def _():
-        spare = jnp.dot(forward_ref[...], columns(spare_refs, 0), preferred_element_type=F32)
-        e_re, e_im = spare[:keep], spare[keep:]
-        p_re, p_im, m_re, m_im = filtered(a_re, a_im, b_re + e_im, b_im - e_re)
-        values = jnp.concatenate(
-            [jnp.concatenate([p_re, m_re], axis=1), jnp.concatenate([p_im, m_im], axis=1)], axis=0
-        ).astype(BF)
-        back(values, 2 * step)
-        back(jnp.concatenate([-m_im, m_re], axis=0).astype(BF), 2 * pairs)
-
-    @pl.when(jnp.logical_not(special))
-    def _():
-        p_re, p_im, m_re, m_im = filtered(a_re - b_im, a_im + b_re, a_re + b_im, a_im - b_re)
-        values = jnp.concatenate(
-            [
-                jnp.concatenate([p_re + m_re, p_im - m_im], axis=1),
-                jnp.concatenate([p_im + m_im, m_re - p_re], axis=1),
-            ],
-            axis=0,
-        ).astype(BF)
-        back(values, 2 * step)
+        back(loose, last_row)
 
     @pl.when(jnp.logical_and(step == 0, jnp.logical_not(special)))
     def _():
         for ref in out_refs:
-            ref[2 * pairs] = jnp.zeros(ref.shape[1:], BF)
+            ref[last_row] = jnp.zeros(ref.shape[1:], BF)
 
 
 def modes(received, first_pair, lat_keep, lon_keep, forward, inverse, w_in, b_in, w_out, b_out):
@@ -265,22 +272,24 @@
     flat = [values for chunk in received for values in chunk]
     slots, _, width = flat[0].shape
     pairs = slots // 2
-    pair_specs = [pl.BlockSpec((2, r.shape[1], width), lambda i: (i, 0, 0)) for r in flat]
+    per_step = 2 if pairs % 2 == 0 else 1
+    pair_specs = [pl.BlockSpec((2 * per_step, r.shape[1], width), lambda i: (i, 0, 0)) for r in flat]
     spare_specs = [pl.BlockSpec((1, r.shape[1], width), lambda i: (slots - 1, 0, 0)) for r in flat]
     whole = lambda array: pl.BlockSpec(array.shape, lambda i: (0,) * array.ndim)
     out = pl.pallas_call(
         functools.partial(modes_kernel, len(flat)),
-        grid=(pairs,),
+        grid=(pairs // per_step,),
         in_specs=[pl.BlockSpec(memory_space=pltpu.SMEM), whole(lat_keep), whole(lon_keep)]
         + pair_specs
         + spare_specs
         + [whole(forward), whole(inverse), whole(w_in), whole(b_in), whole(w_out), whole(b_out)],
         out_specs=[pl.BlockSpec(r.shape, lambda i: (0, 0, 0)) for r in flat],
         out_shape=[jax.ShapeDtypeStruct(r.shape, BF) for r in flat],
+        scratch_shapes=[pltpu.VMEM((2 * KEEP_LON, width), F32)],
         compiler_params=pltpu.CompilerParams(vmem_limit_bytes=48 << 20),
         cost_estimate=pl.CostEstimate(
-            flops=pairs * 2 * (2 * 2 * KEEP_LON * W * 2 * width + 4 * KEEP_LON * 4 * width * width) // COST_SHARE,
-            bytes_accessed=4 * slots * W * width // COST_SHARE,
+            flops=pairs * 2 * (2 * 2 * KEEP_LON * W * 2 * width + 4 * KEEP_LON * 4 * width * width),
+            bytes_accessed=4 * slots * W * width,
             transcendentals=0,
         ),
         name="modes",

time: 577 us -> 574 us (level)
  no operation moved by 1% of the time
where the time goes in v5:
time: 574 us; the launch traced here: 566 us
  waiting for transfers between devices  318 us (55%)
  Pallas kernels  111 us (19%)
  starting transfers between devices  70.9 us (12%)
  other arithmetic  35 us (6%)
  local copies, waits for them, and re-layouts  27.8 us (5%)
    ppermute x18, waiting for transfers between devices, shift(): lax.ppermute(values, 'lon', [(z, (z + steps) % lon_count) for z in range(...  145 us
    all_to_all x3, waiting for transfers between devices, outward(): return lax.all_to_all(flat, ('lon', 'ch'), 0, 0, tiled=True).reshape(shape)  126 us
    pallas_call x3, Pallas kernels, mlp(): pl.pallas_call(mlp_kernel, grid_spec=pltpu.PrefetchScalarGridSpec(num_sca...  47.4 us
    ppermute x15, waiting for transfers between devices, swap(): return lax.ppermute(values, axis, [(0, 1), (1, 0)])  47.1 us
    ppermute x18, starting transfers between devices, shift(): lax.ppermute(values, 'lon', [(z, (z + steps) % lon_count) for z in range(...  40.3 us
    pallas_call x3, Pallas kernels, lat_inverse(): pl.pallas_call(lat_inverse_kernel, grid=(cols // 16,), in_specs=[pl.Block...  21.6 us
    all_to_all x3, starting transfers between devices, outward(): return lax.all_to_all(flat, ('lon', 'ch'), 0, 0, tiled=True).reshape(shape)  19.9 us
    pallas_call x3, Pallas kernels, lat_forward(): pl.pallas_call(lat_forward_kernel, grid=(cols // 16,), in_specs=[pl.Block...  16.1 us
  transfers between devices with their start and end apart: 36, of which 17 were waited for; matrix products, arithmetic and copies ran while one was open for 6% of the time, Pallas kernels for 14%

profile of v5, /device:TPU:0, one launch (start us, length us, event | category | flops | bytes accessed | tf_op | source)
XLA Modules:
  0.0 565.7 jit_solution(11611055604800581765)
XLA Ops:
  0.0 2.5 convert_reduce_fusion.2
  2.6 2.9 fusion.1
  6.2 1.8 dynamic-slice_bitcast_fusion.1.table_ref
  8.2 4.5 fusion.5.cells_ref
  12.8 5.6 lat_forward.3
  19.1 2.6 collective-permute-start.1
  21.6 1.5 fusion.7
  24.7 4.5 fusion.11.cells_ref
  29.2 4.9 lat_forward.4
  34.2 24.9 %collective-permute-done.1 = bf16[4,17,32,384]{3,2,1,0:T(8,128)(2,1)} collective-permute-done((bf16[4,17,32,384]{3,2,1,0:T(8,128)(2,1)}, bf16[4,17,32,384]{3,2,1,0:T(8,128)(2,1)}, u32[]{:S(2)}, u32[]{:S(2)}) %collective-permute-start.1) | collective-permute-done | bytes 1671200 | tf_op jit(solution)/shard_map/ppermute | solution.py:402
  59.8 1.8 collective-permute-start.3
  61.6 1.6 fusion.13
  63.3 1.9 fusion.21
  65.2 3.7 collective-permute-start.7
  70.0 1.7 fusion.17.cells_ref
  71.7 5.6 lat_forward.5
  77.3 1.5 collective-permute-done.7.refs_3_.refs_15_
  78.9 26.4 %collective-permute-done.6.refs_2_.refs_14_ = bf16[17,32,384]{2,1,0:T(8,128)(2,1)} collective-permute-done((bf16[17,32,384]{2,1,0:T(8,128)(2,1)S(1)}, bf16[17,32,384]{2,1,0:T(8,128)(2,1)}, u32[]{:S(2)}, u32[]{:S(2)}) %collective-permute-start.6) | collective-permute-done | bytes 417824 | tf_op jit(solution)/shard_map/ppermute | solution.py:408
  106.6 1.5 fusion.49
  108.1 1.6 fusion.25
  109.7 2.8 collective-permute-start.10
  112.5 2.0 collective-permute-start.9
  118.7 2.0 squeeze.46
  122.8 2.3 maximum_maximum_fusion.1.refs_28_
  125.1 2.2 maximum_maximum_fusion.refs_26_
  127.3 21.3 %collective-permute-done.10.refs_6_.refs_18_ = bf16[17,32,384]{2,1,0:T(8,128)(2,1)} collective-permute-done((bf16[17,32,384]{2,1,0:T(8,128)(2,1)}, bf16[17,32,384]{2,1,0:T(8,128)(2,1)}, u32[]{:S(2)}, u32[]{:S(2)}) %collective-permute-start.10) | collective-permute-done | bytes 417824 | tf_op jit(solution)/shard_map/ppermute | solution.py:408
  149.8 2.0 dynamic-slice_bitcast_fusion.table_ref
  153.7 1.8 all-gather
  156.1 1.9 collective-permute-start.12
  158.3 1.7 pad_maximum_fusion.1.w_out_ref
  160.0 8.5 %collective-permute-done.14.refs_11_.refs_23_ = bf16[17,32,384]{2,1,0:T(8,128)(2,1)S(1)} collective-permute-done((bf16[17,32,384]{2,1,0:T(8,128)(2,1)S(1)}, bf16[17,32,384]{2,1,0:T(8,128)(2,1)S(1)}, u32[]{:S(2)}, u32[]{:S(2)}) %collective-permute-start.14) | collective-permute-done | bytes 417824 | tf_op jit(solution)/shard_map/ppermute | solution.py:408
  168.5 24.3 %collective-permute-done.13.refs_10_.refs_22_ = bf16[17,32,384]{2,1,0:T(8,128)(2,1)S(1)} collective-permute-done((bf16[17,32,384]{2,1,0:T(8,128)(2,1)S(1)}, bf16[17,32,384]{2,1,0:T(8,128)(2,1)S(1)}, u32[]{:S(2)}, u32[]{:S(2)}) %collective-permute-start.13) | collective-permute-done | bytes 417824 | tf_op jit(solution)/shard_map/ppermute | solution.py:408
  193.7 13.0 %modes.1 = (bf16[17,32,384]{2,1,0:T(8,128)(2,1)S(1)}, bf16[17,32,384]{2,1,0:T(8,128)(2,1)S(1)}, bf16[17,32,384]{2,1,0:T(8,128)(2,1)S(1)}, bf16[17,32,384]{2,1,0:...) custom-call(s32[1]{0:T(128)} %bitcast.23.first_pair_ref, ...), custom_call_target="tpu_custom_call" | custom-call | flops 7247757312 | bytes 10027008 | tf_op jit(solution)/shard_map/modes/pallas_call | solution.py:279
  206.7 1.9 collective-permute-start.19
  208.7 2.8 collective-permute-start.20
  211.5 9.7 %collective-permute-done.18 = bf16[17,32,384]{2,1,0:T(8,128)(2,1)S(1)} collective-permute-done((bf16[17,32,384]{2,1,0:T(8,128)(2,1)S(1)}, bf16[17,32,384]{2,1,0:T(8,128)(2,1)S(1)}, u32[]{:S(2)}, u32[]{:S(2)}) %collective-permute-start.18) | collective-permute-done | bytes 417824 | tf_op jit(solution)/shard_map/ppermute | solution.py:408
  221.2 16.6 %collective-permute-done.19 = bf16[17,32,384]{2,1,0:T(8,128)(2,1)S(1)} collective-permute-done((bf16[17,32,384]{2,1,0:T(8,128)(2,1)S(1)}, bf16[17,32,384]{2,1,0:T(8,128)(2,1)S(1)}, u32[]{:S(2)}, u32[]{:S(2)}) %collective-permute-start.19) | collective-permute-done | bytes 417824 | tf_op jit(solution)/shard_map/ppermute | solution.py:408
  239.1 9.0 %collective-permute-start.21 = (bf16[17,32,384]{2,1,0:T(8,128)(2,1)S(1)}, bf16[17,32,384]{2,1,0:T(8,128)(2,1)S(1)}, u32[]{:S(2)}, u32[]{:S(2)}) collective-permute-start(bf16[17,32,384]{2,1,0:T(8,128)(2,1)S(1)} %get-tuple-element.247), channel_id=1, source_target_pairs={{0,4},{4,8},{8,12},{12,0},{1,5},{5,9},{9,13},{13,1},{2,6},{6,10},{... | collective-permute-start | bytes 1253384 | tf_op jit(solution)/shard_map/ppermute | solution.py:408
  248.1 2.2 collective-permute-start.22
  250.7 9.7 %collective-permute-done.21 = bf16[17,32,384]{2,1,0:T(8,128)(2,1)S(1)} collective-permute-done((bf16[17,32,384]{2,1,0:T(8,128)(2,1)S(1)}, bf16[17,32,384]{2,1,0:T(8,128)(2,1)S(1)}, u32[]{:S(2)}, u32[]{:S(2)}) %collective-permute-start.21) | collective-permute-done | bytes 417824 | tf_op jit(solution)/shard_map/ppermute | solution.py:408
  260.4 16.0 %collective-permute-done.22 = bf16[17,32,384]{2,1,0:T(8,128)(2,1)S(1)} collective-permute-done((bf16[17,32,384]{2,1,0:T(8,128)(2,1)S(1)}, bf16[17,32,384]{2,1,0:T(8,128)(2,1)S(1)}, u32[]{:S(2)}, u32[]{:S(2)}) %collective-permute-start.22) | collective-permute-done | bytes 417824 | tf_op jit(solution)/shard_map/ppermute | solution.py:408
  276.5 6.9 %lat_inverse.3 = (bf16[4,16,32,384]{3,2,1,0:T(8,128)(2,1)S(1)}, bf16[4,16,32,384]{3,2,1,0:T(8,128)(2,1)S(1)}) custom-call(s32[2]{0:T(128)S(1)} %pad_add_fusion.where_ref, bf16[4,17,32,384]{3,2,1,0:T(8,128)(2,1)S(1)} %pad_maximum_fusion.2.own_ref, bf16[4,17,32,384]{3,2,1,0:T(8,128)(2,1)S(1)} %collective-permute-done.24.other_ref, ...), custom_call_target="tpu_custom_call" | custom-call | flops 3623878656 | bytes 9437184 | tf_op jit(solution)/shard_map/lat_inverse/pallas_call | solution.py:157
  284.3 9.4 %collective-permute-start.25 = (bf16[17,32,384]{2,1,0:T(8,128)(2,1)S(1)}, bf16[17,32,384]{2,1,0:T(8,128)(2,1)S(1)}, u32[]{:S(2)}, u32[]{:S(2)}) collective-permute-start(bf16[17,32,384]{2,1,0:T(8,128)(2,1)S(1)} %get-tuple-element.260), channel_id=1, source_target_pairs={{0,4},{4,8},{8,12},{12,0},{1,5},{5,9},{9,13},{13,1},{2,6},{6,10},{... | collective-permute-start | bytes 1253384 | tf_op jit(solution)/shard_map/ppermute | solution.py:408
  293.7 1.5 collective-permute-start.26
  296.1 15.8 %channel_mlp.3 = bf16[4,2,16,32,384]{4,3,2,1,0:T(8,128)(2,1)} custom-call(s32[2]{0:T(128)S(1)} %pad_add_fusion.where_ref, bf16[4,16,32,384]{3,2,1,0:T(8,128)(2,1)S(1)} %get-tuple-element.271.own_ref, bf16[4,16,32,384]{3,2,1,0:T(8,128)(2,1)S(1)} %collective-permute-done.29.other_ref, f32[1,768]{1,0:T(1,128)S(1)} %reshape.285.gain_ref, ...), custom_call_target="tpu_custom_call" | custom-call | flops 9663676416 | bytes 6291456 | tf_op jit(solution)/shard_map/channel_mlp/pallas_call | solution.py:332
  311.9 10.8 %collective-permute-done.26 = bf16[17,32,384]{2,1,0:T(8,128)(2,1)S(1)} collective-permute-done((bf16[17,32,384]{2,1,0:T(8,128)(2,1)S(1)}, bf16[17,32,384]{2,1,0:T(8,128)(2,1)S(1)}, u32[]{:S(2)}, u32[]{:S(2)}) %collective-permute-start.26) | collective-permute-done | bytes 417824 | tf_op jit(solution)/shard_map/ppermute | solution.py:408
  324.8 11.6 %all-to-all-start = ((bf16[8,16,32,384]{3,2,1,0:T(8,128)(2,1)}), bf16[8,16,32,384]{3,2,1,0:T(8,128)(2,1)}, u32[]{:S(2)}, u32[]{:S(2)}) async-start(bf16[8,16,32,384]{3,2,1,0:T(8,128)(2,1)} %bitcast.135), calls=%async_computation | async-start | bytes 6291456 | tf_op jit(solution)/shard_map/all_to_all | solution.py:514
  337.8 1.4 copy-done.8
  339.3 7.0 %lat_inverse.4 = (bf16[4,16,32,384]{3,2,1,0:T(8,128)(2,1)S(1)}, bf16[4,16,32,384]{3,2,1,0:T(8,128)(2,1)S(1)}) custom-call(s32[2]{0:T(128)S(1)} %pad_add_fusion.where_ref, bf16[4,17,32,384]{3,2,1,0:T(8,128)(2,1)S(1)} %copy-done.1, bf16[4,17,32,384]{3,2,1,0:T(8,128)(2,1)S(1)} %copy-done.8, bf16[1024,1152]{1,0:T(8,128)(2,1)S(1)} %dynamic-slice_bitcast_fusion.table_ref, ...), custom_call_target="tpu_custom_call" | custom-call | flops 3623878656 | bytes 9437184 | tf_op jit(solution)/shard_map/lat_inverse/pallas_call | solution.py:157
  347.1 1.6 collective-permute-start.30
  349.9 15.8 %channel_mlp.4 = bf16[4,2,16,32,384]{4,3,2,1,0:T(8,128)(2,1)} custom-call(s32[2]{0:T(128)S(1)} %pad_add_fusion.where_ref, bf16[4,16,32,384]{3,2,1,0:T(8,128)(2,1)S(1)} %get-tuple-element.287.own_ref, bf16[4,16,32,384]{3,2,1,0:T(8,128)(2,1)S(1)} %collective-permute-done.31.other_ref, f32[1,768]{1,0:T(1,128)S(1)} %reshape.285.gain_ref, ...), custom_call_target="tpu_custom_call" | custom-call | flops 9663676416 | bytes 6291456 | tf_op jit(solution)/shard_map/channel_mlp/pallas_call | solution.py:332
  365.6 20.0 %collective-permute-done.30.other_ref = bf16[4,17,32,384]{3,2,1,0:T(8,128)(2,1)S(1)} collective-permute-done((bf16[4,17,32,384]{3,2,1,0:T(8,128)(2,1)S(1)}, bf16[4,17,32,384]{3,2,1,0:T(8,128)(2,1)S(1)}, u32[]{:S(2)}, u32[]{:S(2)}) %collective-permute-start.30) | collective-permute-done | bytes 1671200 | tf_op jit(solution)/shard_map/ppermute | solution.py:402
  386.8 21.2 %all-to-all-done = bf16[8,16,32,384]{3,2,1,0:T(8,128)(2,1)} async-done(((bf16[8,16,32,384]{3,2,1,0:T(8,128)(2,1)}), bf16[8,16,32,384]{3,2,1,0:T(8,128)(2,1)}, u32[]{:S(2)}, u32[]{:S(2)}) %all-to-all-start) | async-done | bytes 3145760 | tf_op jit(solution)/shard_map/all_to_all | solution.py:514
  408.0 4.7 all-to-all-start.1
  414.2 1.4 copy-done.10
  415.6 7.7 %lat_inverse.5 = (bf16[4,16,32,384]{3,2,1,0:T(8,128)(2,1)S(1)}, bf16[4,16,32,384]{3,2,1,0:T(8,128)(2,1)}) custom-call(s32[2]{0:T(128)S(1)} %pad_add_fusion.where_ref, bf16[4,17,32,384]{3,2,1,0:T(8,128)(2,1)S(1)} %copy-done.3, bf16[4,17,32,384]{3,2,1,0:T(8,128)(2,1)S(1)} %copy-done.10, bf16[1024,1152]{1,0:T(8,128)(2,1)S(1)} %dynamic-slice_bitcast_fusion.table_ref, ...), custom_call_target="tpu_custom_call" | custom-call | flops 3623878656 | bytes 9437184 | tf_op jit(solution)/shard_map/lat_inverse/pallas_call | solution.py:157
  424.9 4.4 assemble.3.refs_0_
  430.8 15.9 %channel_mlp.5 = bf16[4,2,16,32,384]{4,3,2,1,0:T(8,128)(2,1)} custom-call(s32[2]{0:T(128)S(1)} %pad_add_fusion.where_ref, bf16[4,16,32,384]{3,2,1,0:T(8,128)(2,1)S(1)} %copy-done.16, bf16[4,16,32,384]{3,2,1,0:T(8,128)(2,1)} %collective-permute-done.32.other_ref, f32[1,768]{1,0:T(1,128)S(1)} %reshape.285.gain_ref, f32[1,768]{1,0:T(1,128)S(1)} %reshape.286.bias_ref, ...), custom_call_target="tpu_custom_call" | custom-call | flops 9663676416 | bytes 6291456 | tf_op jit(solution)/shard_map/channel_mlp/pallas_call | solution.py:332
  446.7 37.6 %all-to-all-done.1 = bf16[8,16,32,384]{3,2,1,0:T(8,128)(2,1)} async-done(((bf16[8,16,32,384]{3,2,1,0:T(8,128)(2,1)}), bf16[8,16,32,384]{3,2,1,0:T(8,128)(2,1)}, u32[]{:S(2)}, u32[]{:S(2)}) %all-to-all-start.1) | async-done | bytes 3145760 | tf_op jit(solution)/shard_map/all_to_all | solution.py:514
  484.3 3.6 all-to-all-start.2
  487.9 4.2 assemble.4.refs_0_
  492.2 67.2 %all-to-all-done.2 = bf16[8,16,32,384]{3,2,1,0:T(8,128)(2,1)S(1)} async-done(((bf16[8,16,32,384]{3,2,1,0:T(8,128)(2,1)}), bf16[8,16,32,384]{3,2,1,0:T(8,128)(2,1)S(1)}, u32[]{:S(2)}, u32[]{:S(2)}) %all-to-all-start.2) | async-done | bytes 3145760 | tf_op jit(solution)/shard_map/all_to_all | solution.py:514
  559.4 1.6 copy-done.17
  561.0 4.2 assemble.5
  (185 shorter events, 32.2 us)
Async XLA Ops:
  2.5 3.5 copy-start.37
  2.5 3.7 copy-start.32
  5.5 2.6 collective-permute-start
  8.2 10.2 %slice-start = ((s8[9437184]{0:T(1024)(128)(4,1)}), s8[4194304]{0:T(1024)(128)(4,1)S(1)}, s32[]{:S(2)}) async-start(s8[9437184]{0:T(1024)(128)(4,1)} %bitcast.130), calls=%async_computation.3 | async-start | bytes 8388608
  8.2 10.2 %slice-start.1 = ((s8[9437184]{0:T(1024)(128)(4,1)}), s8[4194304]{0:T(1024)(128)(4,1)S(1)}, s32[]{:S(2)}) async-start(s8[9437184]{0:T(1024)(128)(4,1)} %bitcast.130), calls=%async_computation.4 | async-start | bytes 8388608
  12.8 5.6 slice-start.2
  18.4 4.8 copy-start.13
  19.0 4.5 copy-start.33
  19.0 4.5 copy-start.38
  19.1 40.0 %collective-permute-start.1 = (bf16[4,17,32,384]{3,2,1,0:T(8,128)(2,1)}, bf16[4,17,32,384]{3,2,1,0:T(8,128)(2,1)}, u32[]{:S(2)}, u32[]{:S(2)}) collective-permute-start(bf16[4,17,32,384]{3,2,1,0:T(8,128)(2,1)} %get-tuple-element.157), channel_id=1, source_target_pairs={{0,2},{2,0},{1,3},{3,1},{4,6},{6,4},{5,7},{7,5},{8,10},{10,8},{9,1... | collective-permute-start | bytes 5013512 | tf_op jit(solution)/shard_map/ppermute | solution.py:402
  23.2 1.4 collective-permute-start.2
  24.7 34.4 %slice-start.3 = ((s8[9437184]{0:T(1024)(128)(4,1)}), s8[4194304]{0:T(1024)(128)(4,1)S(1)}, s32[]{:S(2)}) async-start(s8[9437184]{0:T(1024)(128)(4,1)} %bitcast.132), calls=%async_computation.6 | async-start | bytes 8388608
  24.7 34.4 %slice-start.4 = ((s8[9437184]{0:T(1024)(128)(4,1)}), s8[4194304]{0:T(1024)(128)(4,1)S(1)}, s32[]{:S(2)}) async-start(s8[9437184]{0:T(1024)(128)(4,1)} %bitcast.132), calls=%async_computation.7 | async-start | bytes 8388608
  29.2 29.9 %slice-start.5 = ((s8[9437184]{0:T(1024)(128)(4,1)}), s8[1048576]{0:T(1024)(128)(4,1)S(1)}, s32[]{:S(2)}) async-start(s8[9437184]{0:T(1024)(128)(4,1)} %bitcast.132), calls=%async_computation.8 | async-start | bytes 2097152
  59.8 3.5 copy-start.14
  59.8 45.4 %collective-permute-start.3 = (bf16[4,17,32,384]{3,2,1,0:T(8,128)(2,1)S(1)}, bf16[4,17,32,384]{3,2,1,0:T(8,128)(2,1)S(1)}, u32[]{:S(2)}, u32[]{:S(2)}) collective-permute-start(bf16[4,17,32,384]{3,2,1,0:T(8,128)(2,1)S(1)} %get-tuple-element.166), channel_id=1, source_target_pairs={{0,2},{2,0},{1,3},{3,1},{4,6},{6,4},{5,7},{7,5},{8,10},{10,8},{9,1... | collective-permute-start | bytes 5013512 | tf_op jit(solution)/shard_map/ppermute | solution.py:402
  63.2 6.8 %collective-permute-start.4 = (f32[2,128,32]{2,1,0:T(8,128)S(1)}, f32[2,128,32]{2,1,0:T(8,128)S(1)}, u32[]{:S(2)}, u32[]{:S(2)}) collective-permute-start(f32[2,128,32]{2,1,0:T(8,128)S(1)} %pad_maximum_fusion.7), channel_id=1, source_target_pairs={{0,1},{1,0},{2,3},{3,2},{4,5},{5,4},{6,7},{7,6},{8,9},{9,8},{10,11... | collective-permute-start | bytes 98312 | tf_op jit(solution)/shard_map/ppermute | solution.py:402
  65.2 13.7 %collective-permute-start.7 = (bf16[17,32,384]{2,1,0:T(8,128)(2,1)S(1)}, bf16[17,32,384]{2,1,0:T(8,128)(2,1)S(1)}, u32[]{:S(2)}, u32[]{:S(2)}) collective-permute-start(bf16[17,32,384]{2,1,0:T(8,128)(2,1)S(1)} %get-tuple-element.309), channel_id=1, source_target_pairs={{0,12},{4,0},{8,4},{12,8},{1,13},{5,1},{9,5},{13,9},{2,14},{6,2},{... | collective-permute-start | bytes 1253384 | tf_op jit(solution)/shard_map/ppermute | solution.py:408
  68.8 36.4 %collective-permute-start.6 = (bf16[17,32,384]{2,1,0:T(8,128)(2,1)S(1)}, bf16[17,32,384]{2,1,0:T(8,128)(2,1)}, u32[]{:S(2)}, u32[]{:S(2)}) collective-permute-start(bf16[17,32,384]{2,1,0:T(8,128)(2,1)S(1)} %get-tuple-element.310), channel_id=1, source_target_pairs={{0,8},{4,12},{8,0},{12,4},{1,9},{5,13},{9,1},{13,5},{2,10},{6,14},... | collective-permute-start | bytes 1253384 | tf_op jit(solution)/shard_map/ppermute | solution.py:408
  68.8 36.4 %collective-permute-start.5 = (bf16[17,32,384]{2,1,0:T(8,128)(2,1)S(1)}, bf16[17,32,384]{2,1,0:T(8,128)(2,1)}, u32[]{:S(2)}, u32[]{:S(2)}) collective-permute-start(bf16[17,32,384]{2,1,0:T(8,128)(2,1)S(1)} %get-tuple-element.311), channel_id=1, source_target_pairs={{0,4},{4,8},{8,12},{12,0},{1,5},{5,9},{9,13},{13,1},{2,6},{6,10},{... | collective-permute-start | bytes 1253384 | tf_op jit(solution)/shard_map/ppermute | solution.py:408
  71.7 34.1 %copy-start.27 = (bf16[2,4,96,96]{3,2,1,0:T(8,128)(2,1)S(1)}, bf16[2,4,96,96]{3,2,1,0:T(8,128)(2,1)}, u32[]{:S(2)}) copy-start(bf16[2,4,96,96]{3,2,1,0:T(8,128)(2,1)} %param.24) | copy-start | bytes 442372
  71.7 34.1 %copy-start.28 = (bf16[2,4,96,96]{3,2,1,0:T(8,128)(2,1)S(1)}, bf16[2,4,96,96]{3,2,1,0:T(8,128)(2,1)}, u32[]{:S(2)}) copy-start(bf16[2,4,96,96]{3,2,1,0:T(8,128)(2,1)} %param.22) | copy-start | bytes 442372
  77.3 30.8 %copy-start.11 = (bf16[4,17,32,384]{3,2,1,0:T(8,128)(2,1)}, bf16[4,17,32,384]{3,2,1,0:T(8,128)(2,1)S(1)}, u32[]{:S(2)}) copy-start(bf16[4,17,32,384]{3,2,1,0:T(8,128)(2,1)S(1)} %get-tuple-element.197) | copy-start | bytes 5013508
  78.9 29.3 %copy-start.39 = (bf16[17,32,384]{2,1,0:T(8,128)(2,1)}, bf16[17,32,384]{2,1,0:T(8,128)(2,1)S(1)}, u32[]{:S(2)}) copy-start(bf16[17,32,384]{2,1,0:T(8,128)(2,1)S(1)} %collective-permute-done.7.refs_3_.refs_15_) | copy-start | bytes 1253380
  105.2 43.3 %collective-permute-start.8 = (bf16[4,17,32,384]{3,2,1,0:T(8,128)(2,1)}, bf16[4,17,32,384]{3,2,1,0:T(8,128)(2,1)S(1)}, u32[]{:S(2)}, u32[]{:S(2)}) collective-permute-start(bf16[4,17,32,384]{3,2,1,0:T(8,128)(2,1)} %get-tuple-element.177), channel_id=1, source_target_pairs={{0,2},{2,0},{1,3},{3,1},{4,6},{6,4},{5,7},{7,5},{8,10},{10,8},{9,1... | collective-permute-start | bytes 5013512 | tf_op jit(solution)/shard_map/ppermute | solution.py:402
  109.7 17.6 %collective-permute-start.11 = (bf16[17,32,384]{2,1,0:T(8,128)(2,1)}, bf16[17,32,384]{2,1,0:T(8,128)(2,1)}, u32[]{:S(2)}, u32[]{:S(2)}) collective-permute-start(bf16[17,32,384]{2,1,0:T(8,128)(2,1)} %get-tuple-element.305), channel_id=1, source_target_pairs={{0,12},{4,0},{8,4},{12,8},{1,13},{5,1},{9,5},{13,9},{2,14},{6,2},{... | collective-permute-start | bytes 1253384 | tf_op jit(solution)/shard_map/ppermute | solution.py:408
  109.7 38.9 %collective-permute-start.10 = (bf16[17,32,384]{2,1,0:T(8,128)(2,1)}, bf16[17,32,384]{2,1,0:T(8,128)(2,1)}, u32[]{:S(2)}, u32[]{:S(2)}) collective-permute-start(bf16[17,32,384]{2,1,0:T(8,128)(2,1)} %get-tuple-element.306), channel_id=1, source_target_pairs={{0,8},{4,12},{8,0},{12,4},{1,9},{5,13},{9,1},{13,5},{2,10},{6,14},... | collective-permute-start | bytes 1253384 | tf_op jit(solution)/shard_map/ppermute | solution.py:408
  112.5 36.1 %collective-permute-start.9 = (bf16[17,32,384]{2,1,0:T(8,128)(2,1)}, bf16[17,32,384]{2,1,0:T(8,128)(2,1)}, u32[]{:S(2)}, u32[]{:S(2)}) collective-permute-start(bf16[17,32,384]{2,1,0:T(8,128)(2,1)} %get-tuple-element.307), channel_id=1, source_target_pairs={{0,4},{4,8},{8,12},{12,0},{1,5},{5,9},{9,13},{13,1},{2,6},{6,10},{... | collective-permute-start | bytes 1253384 | tf_op jit(solution)/shard_map/ppermute | solution.py:408
  121.7 27.5 %copy-start.29 = (bf16[768]{0:T(1024)(128)(2,1)S(1)}, bf16[768]{0:T(1024)(128)(2,1)}, u32[]{:S(2)}) copy-start(bf16[768]{0:T(1024)(128)(2,1)} %param.28) | copy-start | bytes 4612
  121.7 28.1 %copy-start.30 = (bf16[768]{0:T(1024)(128)(2,1)S(1)}, bf16[768]{0:T(1024)(128)(2,1)}, u32[]{:S(2)}) copy-start(bf16[768]{0:T(1024)(128)(2,1)} %param.29) | copy-start | bytes 4612
  121.7 26.9 %copy-start.21 = (bf16[768,768]{1,0:T(8,128)(2,1)S(1)}, bf16[768,768]{1,0:T(8,128)(2,1)}, u32[]{:S(2)}) copy-start(bf16[768,768]{1,0:T(8,128)(2,1)} %param.30) | copy-start | bytes 3538948
  121.7 27.0 %copy-start.22 = (bf16[768,768]{1,0:T(8,128)(2,1)S(1)}, bf16[768,768]{1,0:T(8,128)(2,1)}, u32[]{:S(2)}) copy-start(bf16[768,768]{1,0:T(8,128)(2,1)} %param.32) | copy-start | bytes 3538948
  148.6 9.5 %collective-permute-start.15 = (bf16[768,768]{1,0:T(8,128)(2,1)S(1)}, bf16[768,768]{1,0:T(8,128)(2,1)S(1)}, u32[]{:S(2)}, u32[]{:S(2)}) collective-permute-start(bf16[768,768]{1,0:T(8,128)(2,1)S(1)} %copy-done.21), channel_id=1, source_target_pairs={{0,1},{1,0},{2,3},{3,2},{4,5},{5,4},{6,7},{7,6},{8,9},{9,8},{10,11... | collective-permute-start | bytes 3538952 | tf_op jit(solution)/shard_map/ppermute | solution.py:402
  148.7 9.6 %collective-permute-start.17 = (bf16[768,768]{1,0:T(8,128)(2,1)S(1)}, bf16[768,768]{1,0:T(8,128)(2,1)S(1)}, u32[]{:S(2)}, u32[]{:S(2)}) collective-permute-start(bf16[768,768]{1,0:T(8,128)(2,1)S(1)} %copy-done.22), channel_id=1, source_target_pairs={{0,1},{1,0},{2,3},{3,2},{4,5},{5,4},{6,7},{7,6},{8,9},{9,8},{10,11... | collective-permute-start | bytes 3538952 | tf_op jit(solution)/shard_map/ppermute | solution.py:402
  151.8 4.3 collective-permute-start.16
  155.5 13.0 %collective-permute-start.14 = (bf16[17,32,384]{2,1,0:T(8,128)(2,1)S(1)}, bf16[17,32,384]{2,1,0:T(8,128)(2,1)S(1)}, u32[]{:S(2)}, u32[]{:S(2)}) collective-permute-start(bf16[17,32,384]{2,1,0:T(8,128)(2,1)S(1)} %get-tuple-element.301), channel_id=1, source_target_pairs={{0,12},{4,0},{8,4},{12,8},{1,13},{5,1},{9,5},{13,9},{2,14},{6,2},{... | collective-permute-start | bytes 1253384 | tf_op jit(solution)/shard_map/ppermute | solution.py:408
  155.5 37.3 %collective-permute-start.13 = (bf16[17,32,384]{2,1,0:T(8,128)(2,1)S(1)}, bf16[17,32,384]{2,1,0:T(8,128)(2,1)S(1)}, u32[]{:S(2)}, u32[]{:S(2)}) collective-permute-start(bf16[17,32,384]{2,1,0:T(8,128)(2,1)S(1)} %get-tuple-element.302), channel_id=1, source_target_pairs={{0,8},{4,12},{8,0},{12,4},{1,9},{5,13},{9,1},{13,5},{2,10},{6,14},... | collective-permute-start | bytes 1253384 | tf_op jit(solution)/shard_map/ppermute | solution.py:408
  156.1 36.7 %collective-permute-start.12 = (bf16[17,32,384]{2,1,0:T(8,128)(2,1)S(1)}, bf16[17,32,384]{2,1,0:T(8,128)(2,1)S(1)}, u32[]{:S(2)}, u32[]{:S(2)}) collective-permute-start(bf16[17,32,384]{2,1,0:T(8,128)(2,1)S(1)} %get-tuple-element.303), channel_id=1, source_target_pairs={{0,4},{4,8},{8,12},{12,0},{1,5},{5,9},{9,13},{13,1},{2,6},{6,10},{... | collective-permute-start | bytes 1253384 | tf_op jit(solution)/shard_map/ppermute | solution.py:408
  158.2 137.9 %copy-start.4 = (bf16[768,1536]{1,0:T(8,128)(2,1)}, bf16[768,1536]{1,0:T(8,128)(2,1)S(1)}, u32[]{:S(2)}) copy-start(bf16[768,1536]{1,0:T(8,128)(2,1)S(1)} %pad_maximum_fusion.w_in_ref) | copy-start | bytes 7077892
  168.5 24.3 %copy-start.40 = (bf16[17,32,384]{2,1,0:T(8,128)(2,1)}, bf16[17,32,384]{2,1,0:T(8,128)(2,1)S(1)}, u32[]{:S(2)}) copy-start(bf16[17,32,384]{2,1,0:T(8,128)(2,1)S(1)} %collective-permute-done.14.refs_11_.refs_23_) | copy-start | bytes 1253380
  206.7 14.5 %collective-permute-start.18 = (bf16[17,32,384]{2,1,0:T(8,128)(2,1)S(1)}, bf16[17,32,384]{2,1,0:T(8,128)(2,1)S(1)}, u32[]{:S(2)}, u32[]{:S(2)}) collective-permute-start(bf16[17,32,384]{2,1,0:T(8,128)(2,1)S(1)} %get-tuple-element.234), channel_id=1, source_target_pairs={{0,4},{4,8},{8,12},{12,0},{1,5},{5,9},{9,13},{13,1},{2,6},{6,10},{... | collective-permute-start | bytes 1253384 | tf_op jit(solution)/shard_map/ppermute | solution.py:408
  206.7 31.1 %collective-permute-start.19 = (bf16[17,32,384]{2,1,0:T(8,128)(2,1)S(1)}, bf16[17,32,384]{2,1,0:T(8,128)(2,1)S(1)}, u32[]{:S(2)}, u32[]{:S(2)}) collective-permute-start(bf16[17,32,384]{2,1,0:T(8,128)(2,1)S(1)} %get-tuple-element.235), channel_id=1, source_target_pairs={{0,8},{4,12},{8,0},{12,4},{1,9},{5,13},{9,1},{13,5},{2,10},{6,14},... | collective-permute-start | bytes 1253384 | tf_op jit(solution)/shard_map/ppermute | solution.py:408
  208.7 29.2 %collective-permute-start.20 = (bf16[17,32,384]{2,1,0:T(8,128)(2,1)S(1)}, bf16[17,32,384]{2,1,0:T(8,128)(2,1)S(1)}, u32[]{:S(2)}, u32[]{:S(2)}) collective-permute-start(bf16[17,32,384]{2,1,0:T(8,128)(2,1)S(1)} %get-tuple-element.236), channel_id=1, source_target_pairs={{0,12},{4,0},{8,4},{12,8},{1,13},{5,1},{9,5},{13,9},{2,14},{6,2},{... | collective-permute-start | bytes 1253384 | tf_op jit(solution)/shard_map/ppermute | solution.py:408
  238.1 38.4 %collective-permute-start.24 = (bf16[4,17,32,384]{3,2,1,0:T(8,128)(2,1)S(1)}, bf16[4,17,32,384]{3,2,1,0:T(8,128)(2,1)S(1)}, u32[]{:S(2)}, u32[]{:S(2)}) collective-permute-start(bf16[4,17,32,384]{3,2,1,0:T(8,128)(2,1)S(1)} %pad_maximum_fusion.2.own_ref), channel_id=1, source_target_pairs={{0,2},{2,0},{1,3},{3,1},{4,6},{6,4},{5,7},{7,5},{8,10},{10,8},{9,1... | collective-permute-start | bytes 5013512 | tf_op jit(solution)/shard_map/ppermute | solution.py:402
  239.1 21.3 %collective-permute-start.21 = (bf16[17,32,384]{2,1,0:T(8,128)(2,1)S(1)}, bf16[17,32,384]{2,1,0:T(8,128)(2,1)S(1)}, u32[]{:S(2)}, u32[]{:S(2)}) collective-permute-start(bf16[17,32,384]{2,1,0:T(8,128)(2,1)S(1)} %get-tuple-element.247), channel_id=1, source_target_pairs={{0,4},{4,8},{8,12},{12,0},{1,5},{5,9},{9,13},{13,1},{2,6},{6,10},{... | collective-permute-start | bytes 1253384 | tf_op jit(solution)/shard_map/ppermute | solution.py:408
  248.1 28.3 %collective-permute-start.22 = (bf16[17,32,384]{2,1,0:T(8,128)(2,1)S(1)}, bf16[17,32,384]{2,1,0:T(8,128)(2,1)S(1)}, u32[]{:S(2)}, u32[]{:S(2)}) collective-permute-start(bf16[17,32,384]{2,1,0:T(8,128)(2,1)S(1)} %get-tuple-element.248), channel_id=1, source_target_pairs={{0,8},{4,12},{8,0},{12,4},{1,9},{5,13},{9,1},{13,5},{2,10},{6,14},... | collective-permute-start | bytes 1253384 | tf_op jit(solution)/shard_map/ppermute | solution.py:408
  250.3 26.2 %collective-permute-start.23 = (bf16[17,32,384]{2,1,0:T(8,128)(2,1)S(1)}, bf16[17,32,384]{2,1,0:T(8,128)(2,1)S(1)}, u32[]{:S(2)}, u32[]{:S(2)}) collective-permute-start(bf16[17,32,384]{2,1,0:T(8,128)(2,1)S(1)} %get-tuple-element.249), channel_id=1, source_target_pairs={{0,12},{4,0},{8,4},{12,8},{1,13},{5,1},{9,5},{13,9},{2,14},{6,2},{... | collective-permute-start | bytes 1253384 | tf_op jit(solution)/shard_map/ppermute | solution.py:408
  283.4 12.7 %collective-permute-start.29 = (bf16[4,16,32,384]{3,2,1,0:T(8,128)(2,1)S(1)}, bf16[4,16,32,384]{3,2,1,0:T(8,128)(2,1)S(1)}, u32[]{:S(2)}, u32[]{:S(2)}) collective-permute-start(bf16[4,16,32,384]{3,2,1,0:T(8,128)(2,1)S(1)} %get-tuple-element.272), channel_id=1, source_target_pairs={{0,1},{1,0},{2,3},{3,2},{4,5},{5,4},{6,7},{7,6},{8,9},{9,8},{10,11... | collective-permute-start | bytes 4718600 | tf_op jit(solution)/shard_map/ppermute | solution.py:402
  283.7 28.2 %copy-start = (bf16[4,17,32,384]{3,2,1,0:T(8,128)(2,1)}, bf16[4,17,32,384]{3,2,1,0:T(8,128)(2,1)S(1)}, u32[]{:S(2)}) copy-start(bf16[4,17,32,384]{3,2,1,0:T(8,128)(2,1)S(1)} %pad_maximum_fusion.3.own_ref) | copy-start | bytes 5013508
  283.7 39.0 %collective-permute-start.28 = (bf16[4,17,32,384]{3,2,1,0:T(8,128)(2,1)S(1)}, bf16[4,17,32,384]{3,2,1,0:T(8,128)(2,1)S(1)}, u32[]{:S(2)}, u32[]{:S(2)}) collective-permute-start(bf16[4,17,32,384]{3,2,1,0:T(8,128)(2,1)S(1)} %pad_maximum_fusion.3.own_ref), channel_id=1, source_target_pairs={{0,2},{2,0},{1,3},{3,1},{4,6},{6,4},{5,7},{7,5},{8,10},{10,8},{9,1... | collective-permute-start | bytes 5013512 | tf_op jit(solution)/shard_map/ppermute | solution.py:402
  284.3 27.5 %collective-permute-start.25 = (bf16[17,32,384]{2,1,0:T(8,128)(2,1)S(1)}, bf16[17,32,384]{2,1,0:T(8,128)(2,1)S(1)}, u32[]{:S(2)}, u32[]{:S(2)}) collective-permute-start(bf16[17,32,384]{2,1,0:T(8,128)(2,1)S(1)} %get-tuple-element.260), channel_id=1, source_target_pairs={{0,4},{4,8},{8,12},{12,0},{1,5},{5,9},{9,13},{13,1},{2,6},{6,10},{... | collective-permute-start | bytes 1253384 | tf_op jit(solution)/shard_map/ppermute | solution.py:408
  293.7 28.9 %collective-permute-start.26 = (bf16[17,32,384]{2,1,0:T(8,128)(2,1)S(1)}, bf16[17,32,384]{2,1,0:T(8,128)(2,1)S(1)}, u32[]{:S(2)}, u32[]{:S(2)}) collective-permute-start(bf16[17,32,384]{2,1,0:T(8,128)(2,1)S(1)} %get-tuple-element.261), channel_id=1, source_target_pairs={{0,8},{4,12},{8,0},{12,4},{1,9},{5,13},{9,1},{13,5},{2,10},{6,14},... | collective-permute-start | bytes 1253384 | tf_op jit(solution)/shard_map/ppermute | solution.py:408
  295.2 27.5 %collective-permute-start.27 = (bf16[17,32,384]{2,1,0:T(8,128)(2,1)S(1)}, bf16[17,32,384]{2,1,0:T(8,128)(2,1)S(1)}, u32[]{:S(2)}, u32[]{:S(2)}) collective-permute-start(bf16[17,32,384]{2,1,0:T(8,128)(2,1)S(1)} %get-tuple-element.262), channel_id=1, source_target_pairs={{0,12},{4,0},{8,4},{12,8},{1,13},{5,1},{9,5},{13,9},{2,14},{6,2},{... | collective-permute-start | bytes 1253384 | tf_op jit(solution)/shard_map/ppermute | solution.py:408
  324.8 83.2 %all-to-all-start = ((bf16[8,16,32,384]{3,2,1,0:T(8,128)(2,1)}), bf16[8,16,32,384]{3,2,1,0:T(8,128)(2,1)}, u32[]{:S(2)}, u32[]{:S(2)}) async-start(bf16[8,16,32,384]{3,2,1,0:T(8,128)(2,1)} %bitcast.135), calls=%async_computation | async-start | bytes 6291456 | tf_op jit(solution)/shard_map/all_to_all | solution.py:514
  339.3 7.6 %copy-start.24 = (bf16[17,32,384]{2,1,0:T(8,128)(2,1)S(1)}, bf16[17,32,384]{2,1,0:T(8,128)(2,1)}, u32[]{:S(2)}) copy-start(bf16[17,32,384]{2,1,0:T(8,128)(2,1)} %copy-done.23) | copy-start | bytes 1253380
  339.3 7.6 %copy-start.26 = (bf16[17,32,384]{2,1,0:T(8,128)(2,1)S(1)}, bf16[17,32,384]{2,1,0:T(8,128)(2,1)}, u32[]{:S(2)}) copy-start(bf16[17,32,384]{2,1,0:T(8,128)(2,1)} %copy-done.25) | copy-start | bytes 1253380
  346.3 3.6 copy-start.5
  346.3 3.6 collective-permute-start.31
  347.1 18.5 %copy-start.2 = (bf16[4,17,32,384]{3,2,1,0:T(8,128)(2,1)}, bf16[4,17,32,384]{3,2,1,0:T(8,128)(2,1)S(1)}, u32[]{:S(2)}) copy-start(bf16[4,17,32,384]{3,2,1,0:T(8,128)(2,1)S(1)} %pad_maximum_fusion.4.own_ref) | copy-start | bytes 5013508
  347.1 38.5 %collective-permute-start.30 = (bf16[4,17,32,384]{3,2,1,0:T(8,128)(2,1)S(1)}, bf16[4,17,32,384]{3,2,1,0:T(8,128)(2,1)S(1)}, u32[]{:S(2)}, u32[]{:S(2)}) collective-permute-start(bf16[4,17,32,384]{3,2,1,0:T(8,128)(2,1)S(1)} %pad_maximum_fusion.4.own_ref), channel_id=1, source_target_pairs={{0,2},{2,0},{1,3},{3,1},{4,6},{6,4},{5,7},{7,5},{8,10},{10,8},{9,1... | collective-permute-start | bytes 5013512 | tf_op jit(solution)/shard_map/ppermute | solution.py:402
  408.0 76.2 %all-to-all-start.1 = ((bf16[8,16,32,384]{3,2,1,0:T(8,128)(2,1)}), bf16[8,16,32,384]{3,2,1,0:T(8,128)(2,1)}, u32[]{:S(2)}, u32[]{:S(2)}) async-start(bf16[8,16,32,384]{3,2,1,0:T(8,128)(2,1)} %bitcast.136), calls=%async_computation.1 | async-start | bytes 6291456 | tf_op jit(solution)/shard_map/all_to_all | solution.py:514
  424.5 4.9 copy-start.6
  424.5 4.9 collective-permute-start.32
  484.3 75.1 %all-to-all-start.2 = ((bf16[8,16,32,384]{3,2,1,0:T(8,128)(2,1)}), bf16[8,16,32,384]{3,2,1,0:T(8,128)(2,1)S(1)}, u32[]{:S(2)}, u32[]{:S(2)}) async-start(bf16[8,16,32,384]{3,2,1,0:T(8,128)(2,1)} %bitcast.137), calls=%async_computation.2 | async-start | bytes 6291456 | tf_op jit(solution)/shard_map/all_to_all | solution.py:514
  (21 other events, 34.4 us)

commit v6 on v5

--- a/solution.py
+++ b/solution.py
@@ -529,9 +529,12 @@
             sent, kept = row_transform(step, patches)
         elif step == chunks:
             filter_args = filter_operands()
-        else:
-            weights = mlp_weights(*dense)
-            inverse_lat = lax.dynamic_index_in_dim(jnp.asarray(np.stack(inverse_all)), lat_id, 0, False)
+        if step == 1:
+            (tied, tied_lat), _ = fence(((dense, lat_id), kept))
+            weights = mlp_weights(*tied)
+            inverse_lat = lax.dynamic_index_in_dim(
+                jnp.asarray(np.stack(inverse_all)), tied_lat, 0, False
+            )
         patches, arrived, sent, kept, received, filter_args, weights, inverse_lat, dense = fence(
             (patches, arrived, sent, kept, received, filter_args, weights, inverse_lat, dense)
         )

time: 574 us -> 574 us (level)
  waiting for transfers between devices: 318 us -> 308 us
  other arithmetic: 35 us -> 43.9 us
    ppermute x15, waiting for transfers between devices: 47.1 us -> 38.2 us  [swap(): return lax.ppermute(values, axis, [(0, 1), (1, 0)])]
    unnamed x105 -> x109, local copies, waits for them, and re-layouts: 15.5 us -> 16.9 us
  transfers between devices with their start and end apart: 36 -> 36, of which waited for: 17 -> 15; matrix products, arithmetic and copies ran while one was open for 6% -> 7% of each run, Pallas kernels for 14% -> 14%
where the time goes in v6:
time: 574 us; the launch traced here: 565 us
  waiting for transfers between devices  308 us (54%)
  Pallas kernels  110 us (19%)
  starting transfers between devices  69.3 us (12%)
  other arithmetic  43.9 us (8%)
  local copies, waits for them, and re-layouts  30.8 us (5%)
    ppermute x18, waiting for transfers between devices, shift(): lax.ppermute(values, 'lon', [(z, (z + steps) % lon_count) for z in range(...  143 us
    all_to_all x3, waiting for transfers between devices, outward(): return lax.all_to_all(flat, ('lon', 'ch'), 0, 0, tiled=True).reshape(shape)  126 us
    pallas_call x3, Pallas kernels, mlp(): pl.pallas_call(mlp_kernel, grid_spec=pltpu.PrefetchScalarGridSpec(num_sca...  46.7 us
    ppermute x18, starting transfers between devices, shift(): lax.ppermute(values, 'lon', [(z, (z + steps) % lon_count) for z in range(...  39 us
    ppermute x15, waiting for transfers between devices, swap(): return lax.ppermute(values, axis, [(0, 1), (1, 0)])  38.2 us
    pallas_call x3, Pallas kernels, lat_inverse(): pl.pallas_call(lat_inverse_kernel, grid=(cols // 16,), in_specs=[pl.Block...  21.4 us
    all_to_all x3, starting transfers between devices, outward(): return lax.all_to_all(flat, ('lon', 'ch'), 0, 0, tiled=True).reshape(shape)  19.4 us
    unnamed x109, local copies, waits for them, and re-layouts  16.9 us
  transfers between devices with their start and end apart: 36, of which 15 were waited for; matrix products, arithmetic and copies ran while one was open for 7% of the time, Pallas kernels for 14%

profile of v6, /device:TPU:0, one launch (start us, length us, event | category | flops | bytes accessed | tf_op | source)
XLA Modules:
  0.0 565.0 jit_solution(3987716088987870821)
XLA Ops:
  0.0 2.5 convert_reduce_fusion.2
  2.6 2.9 fusion.1
  6.1 1.8 dynamic-slice_bitcast_fusion.1.table_ref
  8.1 5.1 fusion.5.cells_ref
  13.1 5.6 lat_forward.3
  19.4 1.6 fusion.7
  21.1 2.9 collective-permute-start.1
  24.1 1.7 fusion.11.cells_ref
  25.9 4.9 lat_forward.4
  34.4 1.9 dynamic-slice_bitcast_fusion.table_ref
  36.2 1.9 all-gather
  38.2 3.2 pad_maximum_fusion.w_in_ref
  41.4 3.2 pad_maximum_fusion.1.w_out_ref
  44.6 16.5 %collective-permute-done.1 = bf16[4,17,32,384]{3,2,1,0:T(8,128)(2,1)} collective-permute-done((bf16[4,17,32,384]{3,2,1,0:T(8,128)(2,1)}, bf16[4,17,32,384]{3,2,1,0:T(8,128)(2,1)}, u32[]{:S(2)}, u32[]{:S(2)}) %collective-permute-start.1) | collective-permute-done | bytes 1671200 | tf_op jit(solution)/shard_map/ppermute | solution.py:402
  61.1 2.5 convert_reduce_fusion
  63.7 1.8 collective-permute-start.6
  65.5 2.9 fusion.13
  68.5 1.8 fusion.21
  70.4 3.7 collective-permute-start.10
  75.2 3.8 fusion.17.cells_ref
  79.1 5.6 lat_forward.5
  84.6 25.7 %collective-permute-done.9.refs_2_.refs_14_ = bf16[17,32,384]{2,1,0:T(8,128)(2,1)S(1)} collective-permute-done((bf16[17,32,384]{2,1,0:T(8,128)(2,1)S(1)}, bf16[17,32,384]{2,1,0:T(8,128)(2,1)S(1)}, u32[]{:S(2)}, u32[]{:S(2)}) %collective-permute-start.9) | collective-permute-done | bytes 417824 | tf_op jit(solution)/shard_map/ppermute | solution.py:408
  111.8 1.5 fusion.49
  113.4 1.5 fusion.25
  114.9 2.7 collective-permute-start.13
  117.6 2.0 collective-permute-start.12
  123.7 1.7 neg.7
  125.5 2.0 squeeze.48
  127.5 2.0 squeeze.46
  130.6 2.4 maximum_maximum_fusion.1.refs_28_
  134.2 19.5 %collective-permute-done.13.refs_6_.refs_18_ = bf16[17,32,384]{2,1,0:T(8,128)(2,1)} collective-permute-done((bf16[17,32,384]{2,1,0:T(8,128)(2,1)}, bf16[17,32,384]{2,1,0:T(8,128)(2,1)}, u32[]{:S(2)}, u32[]{:S(2)}) %collective-permute-start.13) | collective-permute-done | bytes 417824 | tf_op jit(solution)/shard_map/ppermute | solution.py:408
  153.7 2.6 fusion.29
  156.8 2.0 collective-permute-start.15
  158.9 7.7 %collective-permute-done.17.refs_11_.refs_23_ = bf16[17,32,384]{2,1,0:T(8,128)(2,1)S(1)} collective-permute-done((bf16[17,32,384]{2,1,0:T(8,128)(2,1)S(1)}, bf16[17,32,384]{2,1,0:T(8,128)(2,1)S(1)}, u32[]{:S(2)}, u32[]{:S(2)}) %collective-permute-start.17) | collective-permute-done | bytes 417824 | tf_op jit(solution)/shard_map/ppermute | solution.py:408
  166.6 26.9 %collective-permute-done.16.refs_10_.refs_22_ = bf16[17,32,384]{2,1,0:T(8,128)(2,1)S(1)} collective-permute-done((bf16[17,32,384]{2,1,0:T(8,128)(2,1)S(1)}, bf16[17,32,384]{2,1,0:T(8,128)(2,1)S(1)}, u32[]{:S(2)}, u32[]{:S(2)}) %collective-permute-start.16) | collective-permute-done | bytes 417824 | tf_op jit(solution)/shard_map/ppermute | solution.py:408
  194.4 13.0 %modes.1 = (bf16[17,32,384]{2,1,0:T(8,128)(2,1)S(1)}, bf16[17,32,384]{2,1,0:T(8,128)(2,1)S(1)}, bf16[17,32,384]{2,1,0:T(8,128)(2,1)S(1)}, bf16[17,32,384]{2,1,0:...) custom-call(s32[1]{0:T(128)} %bitcast.25.first_pair_ref, ...), custom_call_target="tpu_custom_call" | custom-call | flops 7247757312 | bytes 10027008 | tf_op jit(solution)/shard_map/modes/pallas_call | solution.py:279
  207.8 3.5 collective-permute-start.20
  211.3 10.7 %collective-permute-done.18 = bf16[17,32,384]{2,1,0:T(8,128)(2,1)S(1)} collective-permute-done((bf16[17,32,384]{2,1,0:T(8,128)(2,1)S(1)}, bf16[17,32,384]{2,1,0:T(8,128)(2,1)S(1)}, u32[]{:S(2)}, u32[]{:S(2)}) %collective-permute-start.18) | collective-permute-done | bytes 417824 | tf_op jit(solution)/shard_map/ppermute | solution.py:408
  221.9 16.5 %collective-permute-done.19 = bf16[17,32,384]{2,1,0:T(8,128)(2,1)S(1)} collective-permute-done((bf16[17,32,384]{2,1,0:T(8,128)(2,1)S(1)}, bf16[17,32,384]{2,1,0:T(8,128)(2,1)S(1)}, u32[]{:S(2)}, u32[]{:S(2)}) %collective-permute-start.19) | collective-permute-done | bytes 417824 | tf_op jit(solution)/shard_map/ppermute | solution.py:408
  239.7 8.5 %collective-permute-start.21 = (bf16[17,32,384]{2,1,0:T(8,128)(2,1)S(1)}, bf16[17,32,384]{2,1,0:T(8,128)(2,1)S(1)}, u32[]{:S(2)}, u32[]{:S(2)}) collective-permute-start(bf16[17,32,384]{2,1,0:T(8,128)(2,1)S(1)} %get-tuple-element.275), channel_id=1, source_target_pairs={{0,4},{4,8},{8,12},{12,0},{1,5},{5,9},{9,13},{13,1},{2,6},{6,10},{... | collective-permute-start | bytes 1253384 | tf_op jit(solution)/shard_map/ppermute | solution.py:408
  250.8 8.7 %collective-permute-done.21 = bf16[17,32,384]{2,1,0:T(8,128)(2,1)S(1)} collective-permute-done((bf16[17,32,384]{2,1,0:T(8,128)(2,1)S(1)}, bf16[17,32,384]{2,1,0:T(8,128)(2,1)S(1)}, u32[]{:S(2)}, u32[]{:S(2)}) %collective-permute-start.21) | collective-permute-done | bytes 417824 | tf_op jit(solution)/shard_map/ppermute | solution.py:408
  259.6 16.0 %collective-permute-done.22 = bf16[17,32,384]{2,1,0:T(8,128)(2,1)S(1)} collective-permute-done((bf16[17,32,384]{2,1,0:T(8,128)(2,1)S(1)}, bf16[17,32,384]{2,1,0:T(8,128)(2,1)S(1)}, u32[]{:S(2)}, u32[]{:S(2)}) %collective-permute-start.22) | collective-permute-done | bytes 417824 | tf_op jit(solution)/shard_map/ppermute | solution.py:408
  275.6 6.9 %lat_inverse.3 = (bf16[4,16,32,384]{3,2,1,0:T(8,128)(2,1)S(1)}, bf16[4,16,32,384]{3,2,1,0:T(8,128)(2,1)S(1)}) custom-call(s32[2]{0:T(128)S(1)} %pad_add_fusion.where_ref, bf16[4,17,32,384]{3,2,1,0:T(8,128)(2,1)S(1)} %pad_maximum_fusion.2.own_ref, bf16[4,17,32,384]{3,2,1,0:T(8,128)(2,1)S(1)} %collective-permute-done.24.other_ref, ...), custom_call_target="tpu_custom_call" | custom-call | flops 3623878656 | bytes 9437184 | tf_op jit(solution)/shard_map/lat_inverse/pallas_call | solution.py:157
  283.6 9.5 %collective-permute-start.25 = (bf16[17,32,384]{2,1,0:T(8,128)(2,1)S(1)}, bf16[17,32,384]{2,1,0:T(8,128)(2,1)S(1)}, u32[]{:S(2)}, u32[]{:S(2)}) collective-permute-start(bf16[17,32,384]{2,1,0:T(8,128)(2,1)S(1)} %get-tuple-element.288), channel_id=1, source_target_pairs={{0,4},{4,8},{8,12},{12,0},{1,5},{5,9},{9,13},{13,1},{2,6},{6,10},{... | collective-permute-start | bytes 1253384 | tf_op jit(solution)/shard_map/ppermute | solution.py:408
  293.1 2.0 collective-permute-start.26
  295.5 15.5 %channel_mlp.3 = bf16[4,2,16,32,384]{4,3,2,1,0:T(8,128)(2,1)} custom-call(s32[2]{0:T(128)S(1)} %pad_add_fusion.where_ref, bf16[4,16,32,384]{3,2,1,0:T(8,128)(2,1)S(1)} %get-tuple-element.299.own_ref, bf16[4,16,32,384]{3,2,1,0:T(8,128)(2,1)S(1)} %collective-permute-done.29.other_ref, f32[1,768]{1,0:T(1,128)S(1)} %reshape.283.gain_ref, ...), custom_call_target="tpu_custom_call" | custom-call | flops 9663676416 | bytes 6291456 | tf_op jit(solution)/shard_map/channel_mlp/pallas_call | solution.py:332
  311.0 11.6 %collective-permute-done.26 = bf16[17,32,384]{2,1,0:T(8,128)(2,1)S(1)} collective-permute-done((bf16[17,32,384]{2,1,0:T(8,128)(2,1)S(1)}, bf16[17,32,384]{2,1,0:T(8,128)(2,1)S(1)}, u32[]{:S(2)}, u32[]{:S(2)}) %collective-permute-start.26) | collective-permute-done | bytes 417824 | tf_op jit(solution)/shard_map/ppermute | solution.py:408
  324.7 11.1 %all-to-all-start = ((bf16[8,16,32,384]{3,2,1,0:T(8,128)(2,1)}), bf16[8,16,32,384]{3,2,1,0:T(8,128)(2,1)}, u32[]{:S(2)}, u32[]{:S(2)}) async-start(bf16[8,16,32,384]{3,2,1,0:T(8,128)(2,1)} %bitcast.133), calls=%async_computation | async-start | bytes 6291456 | tf_op jit(solution)/shard_map/all_to_all | solution.py:514
  337.2 1.4 copy-done.10
  338.6 6.9 %lat_inverse.4 = (bf16[4,16,32,384]{3,2,1,0:T(8,128)(2,1)S(1)}, bf16[4,16,32,384]{3,2,1,0:T(8,128)(2,1)S(1)}) custom-call(s32[2]{0:T(128)S(1)} %pad_add_fusion.where_ref, bf16[4,17,32,384]{3,2,1,0:T(8,128)(2,1)S(1)} %copy-done.1, bf16[4,17,32,384]{3,2,1,0:T(8,128)(2,1)S(1)} %copy-done.10, bf16[1024,1152]{1,0:T(8,128)(2,1)S(1)} %dynamic-slice_bitcast_fusion.table_ref, ...), custom_call_target="tpu_custom_call" | custom-call | flops 3623878656 | bytes 9437184 | tf_op jit(solution)/shard_map/lat_inverse/pallas_call | solution.py:157
  347.7 1.4 collective-permute-done.31.other_ref
  349.2 15.5 %channel_mlp.4 = bf16[4,2,16,32,384]{4,3,2,1,0:T(8,128)(2,1)} custom-call(s32[2]{0:T(128)S(1)} %pad_add_fusion.where_ref, bf16[4,16,32,384]{3,2,1,0:T(8,128)(2,1)S(1)} %get-tuple-element.315.own_ref, bf16[4,16,32,384]{3,2,1,0:T(8,128)(2,1)S(1)} %collective-permute-done.31.other_ref, f32[1,768]{1,0:T(1,128)S(1)} %reshape.283.gain_ref, ...), custom_call_target="tpu_custom_call" | custom-call | flops 9663676416 | bytes 6291456 | tf_op jit(solution)/shard_map/channel_mlp/pallas_call | solution.py:332
  364.7 20.2 %collective-permute-done.30.other_ref = bf16[4,17,32,384]{3,2,1,0:T(8,128)(2,1)S(1)} collective-permute-done((bf16[4,17,32,384]{3,2,1,0:T(8,128)(2,1)S(1)}, bf16[4,17,32,384]{3,2,1,0:T(8,128)(2,1)S(1)}, u32[]{:S(2)}, u32[]{:S(2)}) %collective-permute-start.30) | collective-permute-done | bytes 1671200 | tf_op jit(solution)/shard_map/ppermute | solution.py:402
  386.2 21.2 %all-to-all-done = bf16[8,16,32,384]{3,2,1,0:T(8,128)(2,1)} async-done(((bf16[8,16,32,384]{3,2,1,0:T(8,128)(2,1)}), bf16[8,16,32,384]{3,2,1,0:T(8,128)(2,1)}, u32[]{:S(2)}, u32[]{:S(2)}) %all-to-all-start) | async-done | bytes 3145760 | tf_op jit(solution)/shard_map/all_to_all | solution.py:514
  407.4 4.7 all-to-all-start.1
  415.0 7.6 %lat_inverse.5 = (bf16[4,16,32,384]{3,2,1,0:T(8,128)(2,1)S(1)}, bf16[4,16,32,384]{3,2,1,0:T(8,128)(2,1)}) custom-call(s32[2]{0:T(128)S(1)} %pad_add_fusion.where_ref, bf16[4,17,32,384]{3,2,1,0:T(8,128)(2,1)S(1)} %copy-done.3, bf16[4,17,32,384]{3,2,1,0:T(8,128)(2,1)S(1)} %copy-done.12, bf16[1024,1152]{1,0:T(8,128)(2,1)S(1)} %dynamic-slice_bitcast_fusion.table_ref, ...), custom_call_target="tpu_custom_call" | custom-call | flops 3623878656 | bytes 9437184 | tf_op jit(solution)/shard_map/lat_inverse/pallas_call | solution.py:157
  424.2 4.4 assemble.3.refs_0_
  430.1 15.7 %channel_mlp.5 = bf16[4,2,16,32,384]{4,3,2,1,0:T(8,128)(2,1)} custom-call(s32[2]{0:T(128)S(1)} %pad_add_fusion.where_ref, bf16[4,16,32,384]{3,2,1,0:T(8,128)(2,1)S(1)} %copy-done.22, bf16[4,16,32,384]{3,2,1,0:T(8,128)(2,1)} %collective-permute-done.32.other_ref, f32[1,768]{1,0:T(1,128)S(1)} %reshape.283.gain_ref, f32[1,768]{1,0:T(1,128)S(1)} %reshape.284.bias_ref, ...), custom_call_target="tpu_custom_call" | custom-call | flops 9663676416 | bytes 6291456 | tf_op jit(solution)/shard_map/channel_mlp/pallas_call | solution.py:332
  445.7 37.9 %all-to-all-done.1 = bf16[8,16,32,384]{3,2,1,0:T(8,128)(2,1)} async-done(((bf16[8,16,32,384]{3,2,1,0:T(8,128)(2,1)}), bf16[8,16,32,384]{3,2,1,0:T(8,128)(2,1)}, u32[]{:S(2)}, u32[]{:S(2)}) %all-to-all-start.1) | async-done | bytes 3145760 | tf_op jit(solution)/shard_map/all_to_all | solution.py:514
  483.6 3.6 all-to-all-start.2
  487.3 4.2 assemble.4.refs_0_
  491.5 67.2 %all-to-all-done.2 = bf16[8,16,32,384]{3,2,1,0:T(8,128)(2,1)S(1)} async-done(((bf16[8,16,32,384]{3,2,1,0:T(8,128)(2,1)}), bf16[8,16,32,384]{3,2,1,0:T(8,128)(2,1)S(1)}, u32[]{:S(2)}, u32[]{:S(2)}) %all-to-all-start.2) | async-done | bytes 3145760 | tf_op jit(solution)/shard_map/all_to_all | solution.py:514
  558.8 1.6 copy-done.23
  560.4 4.2 assemble.5
  (188 shorter events, 34.2 us)
Async XLA Ops:
  5.5 2.4 collective-permute-start
  7.9 17.9 %copy-start.7 = (bf16[1088,1024]{1,0:T(8,128)(2,1)}, bf16[1088,1024]{1,0:T(8,128)(2,1)S(1)}, u32[]{:S(2)}) copy-start(bf16[1088,1024]{1,0:T(8,128)(2,1)S(1)} %dynamic-slice_bitcast_fusion.1.table_ref) | copy-start | bytes 6684676
  8.0 10.7 %slice-start = ((s8[9437184]{0:T(1024)(128)(4,1)}), s8[4194304]{0:T(1024)(128)(4,1)S(1)}, s32[]{:S(2)}) async-start(s8[9437184]{0:T(1024)(128)(4,1)} %bitcast.130), calls=%async_computation.3 | async-start | bytes 8388608
  8.0 10.7 %slice-start.1 = ((s8[9437184]{0:T(1024)(128)(4,1)}), s8[4194304]{0:T(1024)(128)(4,1)S(1)}, s32[]{:S(2)}) async-start(s8[9437184]{0:T(1024)(128)(4,1)} %bitcast.130), calls=%async_computation.4 | async-start | bytes 8388608
  13.1 5.6 slice-start.2
  21.0 3.1 collective-permute-start.2
  21.1 40.0 %collective-permute-start.1 = (bf16[4,17,32,384]{3,2,1,0:T(8,128)(2,1)}, bf16[4,17,32,384]{3,2,1,0:T(8,128)(2,1)}, u32[]{:S(2)}, u32[]{:S(2)}) collective-permute-start(bf16[4,17,32,384]{3,2,1,0:T(8,128)(2,1)} %get-tuple-element.171), channel_id=1, source_target_pairs={{0,2},{2,0},{1,3},{3,1},{4,6},{6,4},{5,7},{7,5},{8,10},{10,8},{9,1... | collective-permute-start | bytes 5013512 | tf_op jit(solution)/shard_map/ppermute | solution.py:402
  25.8 7.5 %copy-start.35 = (bf16[2,384]{1,0:T(2,128)(2,1)S(1)}, bf16[2,384]{1,0:T(2,128)(2,1)}, u32[]{:S(2)}) copy-start(bf16[2,384]{1,0:T(2,128)(2,1)} %param.23) | copy-start | bytes 4612
  25.8 8.0 %copy-start.36 = (bf16[2,384]{1,0:T(2,128)(2,1)S(1)}, bf16[2,384]{1,0:T(2,128)(2,1)}, u32[]{:S(2)}) copy-start(bf16[2,384]{1,0:T(2,128)(2,1)} %param.25) | copy-start | bytes 4612
  25.8 8.0 %copy-start.40 = (s32[4]{0:T(128)S(1)}, s32[4]{0:T(128)}, u32[]{:S(2)}) copy-start(s32[4]{0:T(128)} %param.26) | copy-start | bytes 52
  25.8 8.2 %copy-start.41 = (s32[4]{0:T(128)S(1)}, s32[4]{0:T(128)}, u32[]{:S(2)}) copy-start(s32[4]{0:T(128)} %param.27) | copy-start | bytes 52
  25.9 8.3 %copy-start.32 = (bf16[768]{0:T(1024)(128)(2,1)S(1)}, bf16[768]{0:T(1024)(128)(2,1)}, u32[]{:S(2)}) copy-start(bf16[768]{0:T(1024)(128)(2,1)} %param.28) | copy-start | bytes 4612
  25.9 8.3 %copy-start.33 = (bf16[768]{0:T(1024)(128)(2,1)S(1)}, bf16[768]{0:T(1024)(128)(2,1)}, u32[]{:S(2)}) copy-start(bf16[768]{0:T(1024)(128)(2,1)} %param.29) | copy-start | bytes 4612
  25.9 8.3 %copy-start.34 = (bf16[768]{0:T(1024)(128)(2,1)S(1)}, bf16[768]{0:T(1024)(128)(2,1)}, u32[]{:S(2)}) copy-start(bf16[768]{0:T(1024)(128)(2,1)} %param.31) | copy-start | bytes 4612
  33.3 4.9 collective-permute-start.3
  33.3 8.1 %collective-permute-start.5 = (bf16[768,768]{1,0:T(8,128)(2,1)}, bf16[768,768]{1,0:T(8,128)(2,1)}, u32[]{:S(2)}, u32[]{:S(2)}) collective-permute-start(bf16[768,768]{1,0:T(8,128)(2,1)} %param.32), channel_id=1, source_target_pairs={{0,1},{1,0},{2,3},{3,2},{4,5},{5,4},{6,7},{7,6},{8,9},{9,8},{10,11... | collective-permute-start | bytes 3538952 | tf_op jit(solution)/shard_map/ppermute | solution.py:402
  34.2 4.0 collective-permute-start.4
  44.6 19.1 %copy-start.20 = (bf16[4,17,32,384]{3,2,1,0:T(8,128)(2,1)S(1)}, bf16[4,17,32,384]{3,2,1,0:T(8,128)(2,1)}, u32[]{:S(2)}) copy-start(bf16[4,17,32,384]{3,2,1,0:T(8,128)(2,1)} %copy-done.19) | copy-start | bytes 5013508
  63.7 4.9 copy-start.16
  63.7 46.6 %collective-permute-start.6 = (bf16[4,17,32,384]{3,2,1,0:T(8,128)(2,1)S(1)}, bf16[4,17,32,384]{3,2,1,0:T(8,128)(2,1)S(1)}, u32[]{:S(2)}, u32[]{:S(2)}) collective-permute-start(bf16[4,17,32,384]{3,2,1,0:T(8,128)(2,1)S(1)} %copy-done.20), channel_id=1, source_target_pairs={{0,2},{2,0},{1,3},{3,1},{4,6},{6,4},{5,7},{7,5},{8,10},{10,8},{9,1... | collective-permute-start | bytes 5013512 | tf_op jit(solution)/shard_map/ppermute | solution.py:402
  68.4 6.7 %collective-permute-start.7 = (f32[2,128,32]{2,1,0:T(8,128)S(1)}, f32[2,128,32]{2,1,0:T(8,128)S(1)}, u32[]{:S(2)}, u32[]{:S(2)}) collective-permute-start(f32[2,128,32]{2,1,0:T(8,128)S(1)} %pad_maximum_fusion.7), channel_id=1, source_target_pairs={{0,1},{1,0},{2,3},{3,2},{4,5},{5,4},{6,7},{7,6},{8,9},{9,8},{10,11... | collective-permute-start | bytes 98312 | tf_op jit(solution)/shard_map/ppermute | solution.py:402
  70.4 14.3 %collective-permute-start.10 = (bf16[17,32,384]{2,1,0:T(8,128)(2,1)S(1)}, bf16[17,32,384]{2,1,0:T(8,128)(2,1)S(1)}, u32[]{:S(2)}, u32[]{:S(2)}) collective-permute-start(bf16[17,32,384]{2,1,0:T(8,128)(2,1)S(1)} %get-tuple-element.337), channel_id=1, source_target_pairs={{0,12},{4,0},{8,4},{12,8},{1,13},{5,1},{9,5},{13,9},{2,14},{6,2},{... | collective-permute-start | bytes 1253384 | tf_op jit(solution)/shard_map/ppermute | solution.py:408
  74.0 36.3 %collective-permute-start.9 = (bf16[17,32,384]{2,1,0:T(8,128)(2,1)S(1)}, bf16[17,32,384]{2,1,0:T(8,128)(2,1)S(1)}, u32[]{:S(2)}, u32[]{:S(2)}) collective-permute-start(bf16[17,32,384]{2,1,0:T(8,128)(2,1)S(1)} %get-tuple-element.338), channel_id=1, source_target_pairs={{0,8},{4,12},{8,0},{12,4},{1,9},{5,13},{9,1},{13,5},{2,10},{6,14},... | collective-permute-start | bytes 1253384 | tf_op jit(solution)/shard_map/ppermute | solution.py:408
  74.0 36.3 %collective-permute-start.8 = (bf16[17,32,384]{2,1,0:T(8,128)(2,1)S(1)}, bf16[17,32,384]{2,1,0:T(8,128)(2,1)S(1)}, u32[]{:S(2)}, u32[]{:S(2)}) collective-permute-start(bf16[17,32,384]{2,1,0:T(8,128)(2,1)S(1)} %get-tuple-element.339), channel_id=1, source_target_pairs={{0,4},{4,8},{8,12},{12,0},{1,5},{5,9},{9,13},{13,1},{2,6},{6,10},{... | collective-permute-start | bytes 1253384 | tf_op jit(solution)/shard_map/ppermute | solution.py:408
  75.2 3.8 copy-start.8
  79.0 31.9 %copy-start.30 = (bf16[2,4,96,96]{3,2,1,0:T(8,128)(2,1)S(1)}, bf16[2,4,96,96]{3,2,1,0:T(8,128)(2,1)}, u32[]{:S(2)}) copy-start(bf16[2,4,96,96]{3,2,1,0:T(8,128)(2,1)} %param.24) | copy-start | bytes 442372
  79.0 31.9 %copy-start.31 = (bf16[2,4,96,96]{3,2,1,0:T(8,128)(2,1)S(1)}, bf16[2,4,96,96]{3,2,1,0:T(8,128)(2,1)}, u32[]{:S(2)}) copy-start(bf16[2,4,96,96]{3,2,1,0:T(8,128)(2,1)} %param.22) | copy-start | bytes 442372
  84.6 28.7 %copy-start.17 = (bf16[4,17,32,384]{3,2,1,0:T(8,128)(2,1)}, bf16[4,17,32,384]{3,2,1,0:T(8,128)(2,1)S(1)}, u32[]{:S(2)}) copy-start(bf16[4,17,32,384]{3,2,1,0:T(8,128)(2,1)S(1)} %get-tuple-element.222) | copy-start | bytes 5013508
  84.6 28.7 %copy-start.42 = (bf16[17,32,384]{2,1,0:T(8,128)(2,1)}, bf16[17,32,384]{2,1,0:T(8,128)(2,1)S(1)}, u32[]{:S(2)}) copy-start(bf16[17,32,384]{2,1,0:T(8,128)(2,1)S(1)} %collective-permute-done.10.refs_3_.refs_15_) | copy-start | bytes 1253380
  110.3 43.4 %collective-permute-start.11 = (bf16[4,17,32,384]{3,2,1,0:T(8,128)(2,1)}, bf16[4,17,32,384]{3,2,1,0:T(8,128)(2,1)}, u32[]{:S(2)}, u32[]{:S(2)}) collective-permute-start(bf16[4,17,32,384]{3,2,1,0:T(8,128)(2,1)} %get-tuple-element.199), channel_id=1, source_target_pairs={{0,2},{2,0},{1,3},{3,1},{4,6},{6,4},{5,7},{7,5},{8,10},{10,8},{9,1... | collective-permute-start | bytes 5013512 | tf_op jit(solution)/shard_map/ppermute | solution.py:402
  114.9 19.3 %collective-permute-start.14 = (bf16[17,32,384]{2,1,0:T(8,128)(2,1)}, bf16[17,32,384]{2,1,0:T(8,128)(2,1)}, u32[]{:S(2)}, u32[]{:S(2)}) collective-permute-start(bf16[17,32,384]{2,1,0:T(8,128)(2,1)} %get-tuple-element.333), channel_id=1, source_target_pairs={{0,12},{4,0},{8,4},{12,8},{1,13},{5,1},{9,5},{13,9},{2,14},{6,2},{... | collective-permute-start | bytes 1253384 | tf_op jit(solution)/shard_map/ppermute | solution.py:408
  114.9 38.8 %collective-permute-start.13 = (bf16[17,32,384]{2,1,0:T(8,128)(2,1)}, bf16[17,32,384]{2,1,0:T(8,128)(2,1)}, u32[]{:S(2)}, u32[]{:S(2)}) collective-permute-start(bf16[17,32,384]{2,1,0:T(8,128)(2,1)} %get-tuple-element.334), channel_id=1, source_target_pairs={{0,8},{4,12},{8,0},{12,4},{1,9},{5,13},{9,1},{13,5},{2,10},{6,14},... | collective-permute-start | bytes 1253384 | tf_op jit(solution)/shard_map/ppermute | solution.py:408
  117.6 36.1 %collective-permute-start.12 = (bf16[17,32,384]{2,1,0:T(8,128)(2,1)}, bf16[17,32,384]{2,1,0:T(8,128)(2,1)}, u32[]{:S(2)}, u32[]{:S(2)}) collective-permute-start(bf16[17,32,384]{2,1,0:T(8,128)(2,1)} %get-tuple-element.335), channel_id=1, source_target_pairs={{0,4},{4,8},{8,12},{12,0},{1,5},{5,9},{9,13},{13,1},{2,6},{6,10},{... | collective-permute-start | bytes 1253384 | tf_op jit(solution)/shard_map/ppermute | solution.py:408
  129.5 3.5 copy-start.25
  129.5 24.2 %copy-start.18 = (bf16[4,17,32,384]{3,2,1,0:T(8,128)(2,1)S(1)}, bf16[4,17,32,384]{3,2,1,0:T(8,128)(2,1)}, u32[]{:S(2)}) copy-start(bf16[4,17,32,384]{3,2,1,0:T(8,128)(2,1)} %copy-done.17) | copy-start | bytes 5013508
  156.3 10.3 %collective-permute-start.17 = (bf16[17,32,384]{2,1,0:T(8,128)(2,1)S(1)}, bf16[17,32,384]{2,1,0:T(8,128)(2,1)S(1)}, u32[]{:S(2)}, u32[]{:S(2)}) collective-permute-start(bf16[17,32,384]{2,1,0:T(8,128)(2,1)S(1)} %get-tuple-element.329), channel_id=1, source_target_pairs={{0,12},{4,0},{8,4},{12,8},{1,13},{5,1},{9,5},{13,9},{2,14},{6,2},{... | collective-permute-start | bytes 1253384 | tf_op jit(solution)/shard_map/ppermute | solution.py:408
  156.3 37.2 %collective-permute-start.16 = (bf16[17,32,384]{2,1,0:T(8,128)(2,1)S(1)}, bf16[17,32,384]{2,1,0:T(8,128)(2,1)S(1)}, u32[]{:S(2)}, u32[]{:S(2)}) collective-permute-start(bf16[17,32,384]{2,1,0:T(8,128)(2,1)S(1)} %get-tuple-element.330), channel_id=1, source_target_pairs={{0,8},{4,12},{8,0},{12,4},{1,9},{5,13},{9,1},{13,5},{2,10},{6,14},... | collective-permute-start | bytes 1253384 | tf_op jit(solution)/shard_map/ppermute | solution.py:408
  156.8 36.7 %collective-permute-start.15 = (bf16[17,32,384]{2,1,0:T(8,128)(2,1)S(1)}, bf16[17,32,384]{2,1,0:T(8,128)(2,1)S(1)}, u32[]{:S(2)}, u32[]{:S(2)}) collective-permute-start(bf16[17,32,384]{2,1,0:T(8,128)(2,1)S(1)} %get-tuple-element.331), channel_id=1, source_target_pairs={{0,4},{4,8},{8,12},{12,0},{1,5},{5,9},{9,13},{13,1},{2,6},{6,10},{... | collective-permute-start | bytes 1253384 | tf_op jit(solution)/shard_map/ppermute | solution.py:408
  166.6 26.9 %copy-start.45 = (bf16[17,32,384]{2,1,0:T(8,128)(2,1)}, bf16[17,32,384]{2,1,0:T(8,128)(2,1)S(1)}, u32[]{:S(2)}) copy-start(bf16[17,32,384]{2,1,0:T(8,128)(2,1)S(1)} %collective-permute-done.17.refs_11_.refs_23_) | copy-start | bytes 1253380
  207.4 14.5 %collective-permute-start.18 = (bf16[17,32,384]{2,1,0:T(8,128)(2,1)S(1)}, bf16[17,32,384]{2,1,0:T(8,128)(2,1)S(1)}, u32[]{:S(2)}, u32[]{:S(2)}) collective-permute-start(bf16[17,32,384]{2,1,0:T(8,128)(2,1)S(1)} %get-tuple-element.262), channel_id=1, source_target_pairs={{0,4},{4,8},{8,12},{12,0},{1,5},{5,9},{9,13},{13,1},{2,6},{6,10},{... | collective-permute-start | bytes 1253384 | tf_op jit(solution)/shard_map/ppermute | solution.py:408
  207.5 30.9 %collective-permute-start.19 = (bf16[17,32,384]{2,1,0:T(8,128)(2,1)S(1)}, bf16[17,32,384]{2,1,0:T(8,128)(2,1)S(1)}, u32[]{:S(2)}, u32[]{:S(2)}) collective-permute-start(bf16[17,32,384]{2,1,0:T(8,128)(2,1)S(1)} %get-tuple-element.263), channel_id=1, source_target_pairs={{0,8},{4,12},{8,0},{12,4},{1,9},{5,13},{9,1},{13,5},{2,10},{6,14},... | collective-permute-start | bytes 1253384 | tf_op jit(solution)/shard_map/ppermute | solution.py:408
  207.8 30.6 %collective-permute-start.20 = (bf16[17,32,384]{2,1,0:T(8,128)(2,1)S(1)}, bf16[17,32,384]{2,1,0:T(8,128)(2,1)S(1)}, u32[]{:S(2)}, u32[]{:S(2)}) collective-permute-start(bf16[17,32,384]{2,1,0:T(8,128)(2,1)S(1)} %get-tuple-element.264), channel_id=1, source_target_pairs={{0,12},{4,0},{8,4},{12,8},{1,13},{5,1},{9,5},{13,9},{2,14},{6,2},{... | collective-permute-start | bytes 1253384 | tf_op jit(solution)/shard_map/ppermute | solution.py:408
  238.7 36.9 %collective-permute-start.24 = (bf16[4,17,32,384]{3,2,1,0:T(8,128)(2,1)S(1)}, bf16[4,17,32,384]{3,2,1,0:T(8,128)(2,1)S(1)}, u32[]{:S(2)}, u32[]{:S(2)}) collective-permute-start(bf16[4,17,32,384]{3,2,1,0:T(8,128)(2,1)S(1)} %pad_maximum_fusion.2.own_ref), channel_id=1, source_target_pairs={{0,2},{2,0},{1,3},{3,1},{4,6},{6,4},{5,7},{7,5},{8,10},{10,8},{9,1... | collective-permute-start | bytes 5013512 | tf_op jit(solution)/shard_map/ppermute | solution.py:402
  239.7 19.8 %collective-permute-start.21 = (bf16[17,32,384]{2,1,0:T(8,128)(2,1)S(1)}, bf16[17,32,384]{2,1,0:T(8,128)(2,1)S(1)}, u32[]{:S(2)}, u32[]{:S(2)}) collective-permute-start(bf16[17,32,384]{2,1,0:T(8,128)(2,1)S(1)} %get-tuple-element.275), channel_id=1, source_target_pairs={{0,4},{4,8},{8,12},{12,0},{1,5},{5,9},{9,13},{13,1},{2,6},{6,10},{... | collective-permute-start | bytes 1253384 | tf_op jit(solution)/shard_map/ppermute | solution.py:408
  248.3 27.3 %collective-permute-start.22 = (bf16[17,32,384]{2,1,0:T(8,128)(2,1)S(1)}, bf16[17,32,384]{2,1,0:T(8,128)(2,1)S(1)}, u32[]{:S(2)}, u32[]{:S(2)}) collective-permute-start(bf16[17,32,384]{2,1,0:T(8,128)(2,1)S(1)} %get-tuple-element.276), channel_id=1, source_target_pairs={{0,8},{4,12},{8,0},{12,4},{1,9},{5,13},{9,1},{13,5},{2,10},{6,14},... | collective-permute-start | bytes 1253384 | tf_op jit(solution)/shard_map/ppermute | solution.py:408
  249.4 26.2 %collective-permute-start.23 = (bf16[17,32,384]{2,1,0:T(8,128)(2,1)S(1)}, bf16[17,32,384]{2,1,0:T(8,128)(2,1)S(1)}, u32[]{:S(2)}, u32[]{:S(2)}) collective-permute-start(bf16[17,32,384]{2,1,0:T(8,128)(2,1)S(1)} %get-tuple-element.277), channel_id=1, source_target_pairs={{0,12},{4,0},{8,4},{12,8},{1,13},{5,1},{9,5},{13,9},{2,14},{6,2},{... | collective-permute-start | bytes 1253384 | tf_op jit(solution)/shard_map/ppermute | solution.py:408
  282.5 13.0 %copy-start.4 = (bf16[768,1536]{1,0:T(8,128)(2,1)S(1)}, bf16[768,1536]{1,0:T(8,128)(2,1)}, u32[]{:S(2)}) copy-start(bf16[768,1536]{1,0:T(8,128)(2,1)} %pad_maximum_fusion.w_in_ref) | copy-start | bytes 7077892
  282.5 13.0 %collective-permute-start.29 = (bf16[4,16,32,384]{3,2,1,0:T(8,128)(2,1)S(1)}, bf16[4,16,32,384]{3,2,1,0:T(8,128)(2,1)S(1)}, u32[]{:S(2)}, u32[]{:S(2)}) collective-permute-start(bf16[4,16,32,384]{3,2,1,0:T(8,128)(2,1)S(1)} %get-tuple-element.300), channel_id=1, source_target_pairs={{0,1},{1,0},{2,3},{3,2},{4,5},{5,4},{6,7},{7,6},{8,9},{9,8},{10,11... | collective-permute-start | bytes 4718600 | tf_op jit(solution)/shard_map/ppermute | solution.py:402
  282.8 28.2 %copy-start = (bf16[4,17,32,384]{3,2,1,0:T(8,128)(2,1)}, bf16[4,17,32,384]{3,2,1,0:T(8,128)(2,1)S(1)}, u32[]{:S(2)}) copy-start(bf16[4,17,32,384]{3,2,1,0:T(8,128)(2,1)S(1)} %pad_maximum_fusion.3.own_ref) | copy-start | bytes 5013508
  282.8 39.7 %collective-permute-start.28 = (bf16[4,17,32,384]{3,2,1,0:T(8,128)(2,1)S(1)}, bf16[4,17,32,384]{3,2,1,0:T(8,128)(2,1)S(1)}, u32[]{:S(2)}, u32[]{:S(2)}) collective-permute-start(bf16[4,17,32,384]{3,2,1,0:T(8,128)(2,1)S(1)} %pad_maximum_fusion.3.own_ref), channel_id=1, source_target_pairs={{0,2},{2,0},{1,3},{3,1},{4,6},{6,4},{5,7},{7,5},{8,10},{10,8},{9,1... | collective-permute-start | bytes 5013512 | tf_op jit(solution)/shard_map/ppermute | solution.py:402
  283.6 27.4 %collective-permute-start.25 = (bf16[17,32,384]{2,1,0:T(8,128)(2,1)S(1)}, bf16[17,32,384]{2,1,0:T(8,128)(2,1)S(1)}, u32[]{:S(2)}, u32[]{:S(2)}) collective-permute-start(bf16[17,32,384]{2,1,0:T(8,128)(2,1)S(1)} %get-tuple-element.288), channel_id=1, source_target_pairs={{0,4},{4,8},{8,12},{12,0},{1,5},{5,9},{9,13},{13,1},{2,6},{6,10},{... | collective-permute-start | bytes 1253384 | tf_op jit(solution)/shard_map/ppermute | solution.py:408
  293.1 29.5 %collective-permute-start.26 = (bf16[17,32,384]{2,1,0:T(8,128)(2,1)S(1)}, bf16[17,32,384]{2,1,0:T(8,128)(2,1)S(1)}, u32[]{:S(2)}, u32[]{:S(2)}) collective-permute-start(bf16[17,32,384]{2,1,0:T(8,128)(2,1)S(1)} %get-tuple-element.289), channel_id=1, source_target_pairs={{0,8},{4,12},{8,0},{12,4},{1,9},{5,13},{9,1},{13,5},{2,10},{6,14},... | collective-permute-start | bytes 1253384 | tf_op jit(solution)/shard_map/ppermute | solution.py:408
  295.0 27.5 %collective-permute-start.27 = (bf16[17,32,384]{2,1,0:T(8,128)(2,1)S(1)}, bf16[17,32,384]{2,1,0:T(8,128)(2,1)S(1)}, u32[]{:S(2)}, u32[]{:S(2)}) collective-permute-start(bf16[17,32,384]{2,1,0:T(8,128)(2,1)S(1)} %get-tuple-element.290), channel_id=1, source_target_pairs={{0,12},{4,0},{8,4},{12,8},{1,13},{5,1},{9,5},{13,9},{2,14},{6,2},{... | collective-permute-start | bytes 1253384 | tf_op jit(solution)/shard_map/ppermute | solution.py:408
  324.7 82.7 %all-to-all-start = ((bf16[8,16,32,384]{3,2,1,0:T(8,128)(2,1)}), bf16[8,16,32,384]{3,2,1,0:T(8,128)(2,1)}, u32[]{:S(2)}, u32[]{:S(2)}) async-start(bf16[8,16,32,384]{3,2,1,0:T(8,128)(2,1)} %bitcast.133), calls=%async_computation | async-start | bytes 6291456 | tf_op jit(solution)/shard_map/all_to_all | solution.py:514
  338.6 7.5 %copy-start.27 = (bf16[17,32,384]{2,1,0:T(8,128)(2,1)S(1)}, bf16[17,32,384]{2,1,0:T(8,128)(2,1)}, u32[]{:S(2)}) copy-start(bf16[17,32,384]{2,1,0:T(8,128)(2,1)} %copy-done.26) | copy-start | bytes 1253380
  338.6 7.5 %copy-start.29 = (bf16[17,32,384]{2,1,0:T(8,128)(2,1)S(1)}, bf16[17,32,384]{2,1,0:T(8,128)(2,1)}, u32[]{:S(2)}) copy-start(bf16[17,32,384]{2,1,0:T(8,128)(2,1)} %copy-done.28) | copy-start | bytes 1253380
  345.6 3.6 copy-start.5
  345.6 3.6 collective-permute-start.31
  346.4 18.3 %copy-start.2 = (bf16[4,17,32,384]{3,2,1,0:T(8,128)(2,1)}, bf16[4,17,32,384]{3,2,1,0:T(8,128)(2,1)S(1)}, u32[]{:S(2)}) copy-start(bf16[4,17,32,384]{3,2,1,0:T(8,128)(2,1)S(1)} %pad_maximum_fusion.4.own_ref) | copy-start | bytes 5013508
  346.4 38.5 %collective-permute-start.30 = (bf16[4,17,32,384]{3,2,1,0:T(8,128)(2,1)S(1)}, bf16[4,17,32,384]{3,2,1,0:T(8,128)(2,1)S(1)}, u32[]{:S(2)}, u32[]{:S(2)}) collective-permute-start(bf16[4,17,32,384]{3,2,1,0:T(8,128)(2,1)S(1)} %pad_maximum_fusion.4.own_ref), channel_id=1, source_target_pairs={{0,2},{2,0},{1,3},{3,1},{4,6},{6,4},{5,7},{7,5},{8,10},{10,8},{9,1... | collective-permute-start | bytes 5013512 | tf_op jit(solution)/shard_map/ppermute | solution.py:402
  407.4 76.2 %all-to-all-start.1 = ((bf16[8,16,32,384]{3,2,1,0:T(8,128)(2,1)}), bf16[8,16,32,384]{3,2,1,0:T(8,128)(2,1)}, u32[]{:S(2)}, u32[]{:S(2)}) async-start(bf16[8,16,32,384]{3,2,1,0:T(8,128)(2,1)} %bitcast.134), calls=%async_computation.1 | async-start | bytes 6291456 | tf_op jit(solution)/shard_map/all_to_all | solution.py:514
  423.8 4.9 copy-start.6
  423.8 4.9 collective-permute-start.32
  483.6 75.1 %all-to-all-start.2 = ((bf16[8,16,32,384]{3,2,1,0:T(8,128)(2,1)}), bf16[8,16,32,384]{3,2,1,0:T(8,128)(2,1)S(1)}, u32[]{:S(2)}, u32[]{:S(2)}) async-start(bf16[8,16,32,384]{3,2,1,0:T(8,128)(2,1)} %bitcast.135), calls=%async_computation.2 | async-start | bytes 6291456 | tf_op jit(solution)/shard_map/all_to_all | solution.py:514
  (23 other events, 39.2 us)

commit v7 on v5

--- a/solution.py
+++ b/solution.py
@@ -516,6 +516,7 @@
     received, summed, sent, kept = [], None, None, None
     weights = None
     filter_args = None
+    ahead = None
     dense = (dense_in, dense_in_bias, dense_out, dense_out_bias)
     for step in range(chunks + 2):
         arrived = None
@@ -525,15 +526,19 @@
         if summed is not None:
             received.append(along_lon(summed))
             summed = None
-        if step < chunks:
+        if ahead is not None:
+            (sent, kept), ahead = ahead, None
+        elif step < chunks:
             sent, kept = row_transform(step, patches)
-        elif step == chunks:
+        if step == chunks:
             filter_args = filter_operands()
-        else:
+        if step == 1 and chunks > 2:
+            ahead = row_transform(2, fence((patches, kept))[0])
+        if step > chunks:
             weights = mlp_weights(*dense)
             inverse_lat = lax.dynamic_index_in_dim(jnp.asarray(np.stack(inverse_all)), lat_id, 0, False)
-        patches, arrived, sent, kept, received, filter_args, weights, inverse_lat, dense = fence(
-            (patches, arrived, sent, kept, received, filter_args, weights, inverse_lat, dense)
+        patches, arrived, sent, kept, received, filter_args, weights, inverse_lat, ahead, dense = fence(
+            (patches, arrived, sent, kept, received, filter_args, weights, inverse_lat, ahead, dense)
         )
         if arrived is not None:
             summed = [

time: 574 us -> 576 us (level)
    ppermute x18, waiting for transfers between devices: 145 us -> 153 us  [shift(): lax.ppermute(values, 'lon', [(z, (z + steps) % lon_count) for z in range(...]
    ppermute x15, waiting for transfers between devices: 47.1 us -> 40.2 us  [swap(): return lax.ppermute(values, axis, [(0, 1), (1, 0)])]
    unnamed x105 -> x95, local copies, waits for them, and re-layouts: 15.5 us -> 17 us
where the time goes in v7:
time: 576 us; the launch traced here: 567 us
  waiting for transfers between devices  319 us (55%)
  Pallas kernels  111 us (19%)
  starting transfers between devices  71.6 us (12%)
  other arithmetic  35.4 us (6%)
  local copies, waits for them, and re-layouts  26.4 us (5%)
    ppermute x18, waiting for transfers between devices, shift(): lax.ppermute(values, 'lon', [(z, (z + steps) % lon_count) for z in range(...  153 us
    all_to_all x3, waiting for transfers between devices, outward(): return lax.all_to_all(flat, ('lon', 'ch'), 0, 0, tiled=True).reshape(shape)  126 us
    pallas_call x3, Pallas kernels, mlp(): pl.pallas_call(mlp_kernel, grid_spec=pltpu.PrefetchScalarGridSpec(num_sca...  47.4 us
    ppermute x18, starting transfers between devices, shift(): lax.ppermute(values, 'lon', [(z, (z + steps) % lon_count) for z in range(...  41.3 us
    ppermute x15, waiting for transfers between devices, swap(): return lax.ppermute(values, axis, [(0, 1), (1, 0)])  40.2 us
    pallas_call x3, Pallas kernels, lat_inverse(): pl.pallas_call(lat_inverse_kernel, grid=(cols // 16,), in_specs=[pl.Block...  21.5 us
    all_to_all x3, starting transfers between devices, outward(): return lax.all_to_all(flat, ('lon', 'ch'), 0, 0, tiled=True).reshape(shape)  19.9 us
    unnamed x95, local copies, waits for them, and re-layouts  17 us
  transfers between devices with their start and end apart: 36, of which 17 were waited for; matrix products, arithmetic and copies ran while one was open for 6% of the time, Pallas kernels for 14%

profile of v7, /device:TPU:0, one launch (start us, length us, event | category | flops | bytes accessed | tf_op | source)
XLA Modules:
  0.0 566.7 jit_solution(8113538316328616911)
XLA Ops:
  0.0 2.5 convert_reduce_fusion.2
  2.6 2.9 fusion.1
  6.0 1.8 dynamic-slice_bitcast_fusion.1.table_ref
  8.0 4.5 fusion.5.cells_ref
  12.6 4.9 lat_forward.3
  18.2 1.6 fusion.7
  19.9 2.9 collective-permute-start.1
  22.9 1.7 fusion.11.cells_ref
  24.6 5.7 lat_forward.4
  30.9 1.6 fusion.13
  33.9 1.7 fusion.17.cells_ref
  35.6 5.6 lat_forward.5
  42.5 17.1 %collective-permute-done.1 = bf16[4,17,32,384]{3,2,1,0:T(8,128)(2,1)S(1)} collective-permute-done((bf16[4,17,32,384]{3,2,1,0:T(8,128)(2,1)S(1)}, bf16[4,17,32,384]{3,2,1,0:T(8,128)(2,1)S(1)}, u32[]{:S(2)}, u32[]{:S(2)}) %collective-permute-start.1) | collective-permute-done | bytes 1671200 | tf_op jit(solution)/shard_map/ppermute | solution.py:402
  60.8 1.7 collective-permute-start.4
  62.9 2.7 fusion.21
  65.6 3.6 collective-permute-start.7
  70.4 9.0 %collective-permute-done.7.refs_3_.refs_15_ = bf16[17,32,384]{2,1,0:T(8,128)(2,1)S(1)} collective-permute-done((bf16[17,32,384]{2,1,0:T(8,128)(2,1)S(1)}, bf16[17,32,384]{2,1,0:T(8,128)(2,1)S(1)}, u32[]{:S(2)}, u32[]{:S(2)}) %collective-permute-start.7) | collective-permute-done | bytes 417824 | tf_op jit(solution)/shard_map/ppermute | solution.py:408
  79.3 24.6 %collective-permute-done.6.refs_2_.refs_14_ = bf16[17,32,384]{2,1,0:T(8,128)(2,1)S(1)} collective-permute-done((bf16[17,32,384]{2,1,0:T(8,128)(2,1)S(1)}, bf16[17,32,384]{2,1,0:T(8,128)(2,1)S(1)}, u32[]{:S(2)}, u32[]{:S(2)}) %collective-permute-start.6) | collective-permute-done | bytes 417824 | tf_op jit(solution)/shard_map/ppermute | solution.py:408
  107.0 2.9 fusion.25
  110.0 2.8 collective-permute-start.10
  112.7 2.0 collective-permute-start.9
  121.2 27.7 %collective-permute-done.10.refs_6_.refs_18_ = bf16[17,32,384]{2,1,0:T(8,128)(2,1)} collective-permute-done((bf16[17,32,384]{2,1,0:T(8,128)(2,1)}, bf16[17,32,384]{2,1,0:T(8,128)(2,1)}, u32[]{:S(2)}, u32[]{:S(2)}) %collective-permute-start.10) | collective-permute-done | bytes 417824 | tf_op jit(solution)/shard_map/ppermute | solution.py:408
  149.5 2.0 dynamic-slice_bitcast_fusion.table_ref
  151.6 2.7 fusion.29
  154.3 1.9 all-gather
  156.3 2.0 collective-permute-start.12
  158.3 1.4 pad_maximum_fusion.w_in_ref
  159.8 3.7 pad_maximum_fusion.1.w_out_ref
  163.5 5.9 %collective-permute-done.14.refs_11_.refs_23_ = bf16[17,32,384]{2,1,0:T(8,128)(2,1)S(1)} collective-permute-done((bf16[17,32,384]{2,1,0:T(8,128)(2,1)S(1)}, bf16[17,32,384]{2,1,0:T(8,128)(2,1)S(1)}, u32[]{:S(2)}, u32[]{:S(2)}) %collective-permute-start.14) | collective-permute-done | bytes 417824 | tf_op jit(solution)/shard_map/ppermute | solution.py:408
  169.4 23.4 %collective-permute-done.13.refs_10_.refs_22_ = bf16[17,32,384]{2,1,0:T(8,128)(2,1)S(1)} collective-permute-done((bf16[17,32,384]{2,1,0:T(8,128)(2,1)S(1)}, bf16[17,32,384]{2,1,0:T(8,128)(2,1)S(1)}, u32[]{:S(2)}, u32[]{:S(2)}) %collective-permute-start.13) | collective-permute-done | bytes 417824 | tf_op jit(solution)/shard_map/ppermute | solution.py:408
  193.7 12.9 %modes.1 = (bf16[17,32,384]{2,1,0:T(8,128)(2,1)S(1)}, bf16[17,32,384]{2,1,0:T(8,128)(2,1)S(1)}, bf16[17,32,384]{2,1,0:T(8,128)(2,1)S(1)}, bf16[17,32,384]{2,1,0:...) custom-call(s32[1]{0:T(128)} %bitcast.23.first_pair_ref, ...), custom_call_target="tpu_custom_call" | custom-call | flops 7247757312 | bytes 10027008 | tf_op jit(solution)/shard_map/modes/pallas_call | solution.py:279
  207.6 2.0 collective-permute-start.19
  209.5 2.8 collective-permute-start.20
  212.4 8.7 %collective-permute-done.18 = bf16[17,32,384]{2,1,0:T(8,128)(2,1)S(1)} collective-permute-done((bf16[17,32,384]{2,1,0:T(8,128)(2,1)S(1)}, bf16[17,32,384]{2,1,0:T(8,128)(2,1)S(1)}, u32[]{:S(2)}, u32[]{:S(2)}) %collective-permute-start.18) | collective-permute-done | bytes 417824 | tf_op jit(solution)/shard_map/ppermute | solution.py:408
  221.1 16.7 %collective-permute-done.19 = bf16[17,32,384]{2,1,0:T(8,128)(2,1)S(1)} collective-permute-done((bf16[17,32,384]{2,1,0:T(8,128)(2,1)S(1)}, bf16[17,32,384]{2,1,0:T(8,128)(2,1)S(1)}, u32[]{:S(2)}, u32[]{:S(2)}) %collective-permute-start.19) | collective-permute-done | bytes 417824 | tf_op jit(solution)/shard_map/ppermute | solution.py:408
  238.7 9.4 %collective-permute-start.21 = (bf16[17,32,384]{2,1,0:T(8,128)(2,1)S(1)}, bf16[17,32,384]{2,1,0:T(8,128)(2,1)S(1)}, u32[]{:S(2)}, u32[]{:S(2)}) collective-permute-start(bf16[17,32,384]{2,1,0:T(8,128)(2,1)S(1)} %get-tuple-element.253), channel_id=1, source_target_pairs={{0,4},{4,8},{8,12},{12,0},{1,5},{5,9},{9,13},{13,1},{2,6},{6,10},{... | collective-permute-start | bytes 1253384 | tf_op jit(solution)/shard_map/ppermute | solution.py:408
  248.1 2.6 collective-permute-start.22
  250.7 10.1 %collective-permute-done.21 = bf16[17,32,384]{2,1,0:T(8,128)(2,1)S(1)} collective-permute-done((bf16[17,32,384]{2,1,0:T(8,128)(2,1)S(1)}, bf16[17,32,384]{2,1,0:T(8,128)(2,1)S(1)}, u32[]{:S(2)}, u32[]{:S(2)}) %collective-permute-start.21) | collective-permute-done | bytes 417824 | tf_op jit(solution)/shard_map/ppermute | solution.py:408
  260.8 16.1 %collective-permute-done.22 = bf16[17,32,384]{2,1,0:T(8,128)(2,1)S(1)} collective-permute-done((bf16[17,32,384]{2,1,0:T(8,128)(2,1)S(1)}, bf16[17,32,384]{2,1,0:T(8,128)(2,1)S(1)}, u32[]{:S(2)}, u32[]{:S(2)}) %collective-permute-start.22) | collective-permute-done | bytes 417824 | tf_op jit(solution)/shard_map/ppermute | solution.py:408
  276.9 6.9 %lat_inverse.3 = (bf16[4,16,32,384]{3,2,1,0:T(8,128)(2,1)S(1)}, bf16[4,16,32,384]{3,2,1,0:T(8,128)(2,1)S(1)}) custom-call(s32[2]{0:T(128)S(1)} %pad_add_fusion.where_ref, bf16[4,17,32,384]{3,2,1,0:T(8,128)(2,1)S(1)} %pad_maximum_fusion.2.own_ref, bf16[4,17,32,384]{3,2,1,0:T(8,128)(2,1)S(1)} %collective-permute-done.24.other_ref, ...), custom_call_target="tpu_custom_call" | custom-call | flops 3623878656 | bytes 9437184 | tf_op jit(solution)/shard_map/lat_inverse/pallas_call | solution.py:157
  285.3 9.4 %collective-permute-start.25 = (bf16[17,32,384]{2,1,0:T(8,128)(2,1)S(1)}, bf16[17,32,384]{2,1,0:T(8,128)(2,1)S(1)}, u32[]{:S(2)}, u32[]{:S(2)}) collective-permute-start(bf16[17,32,384]{2,1,0:T(8,128)(2,1)S(1)} %get-tuple-element.266), channel_id=1, source_target_pairs={{0,4},{4,8},{8,12},{12,0},{1,5},{5,9},{9,13},{13,1},{2,6},{6,10},{... | collective-permute-start | bytes 1253384 | tf_op jit(solution)/shard_map/ppermute | solution.py:408
  294.7 1.5 collective-permute-start.26
  297.3 15.8 %channel_mlp.3 = bf16[4,2,16,32,384]{4,3,2,1,0:T(8,128)(2,1)} custom-call(s32[2]{0:T(128)S(1)} %pad_add_fusion.where_ref, bf16[4,16,32,384]{3,2,1,0:T(8,128)(2,1)S(1)} %get-tuple-element.277.own_ref, bf16[4,16,32,384]{3,2,1,0:T(8,128)(2,1)S(1)} %collective-permute-done.29.other_ref, f32[1,768]{1,0:T(1,128)S(1)} %reshape.285.gain_ref, ...), custom_call_target="tpu_custom_call" | custom-call | flops 9663676416 | bytes 6291456 | tf_op jit(solution)/shard_map/channel_mlp/pallas_call | solution.py:332
  313.0 10.7 %collective-permute-done.26 = bf16[17,32,384]{2,1,0:T(8,128)(2,1)S(1)} collective-permute-done((bf16[17,32,384]{2,1,0:T(8,128)(2,1)S(1)}, bf16[17,32,384]{2,1,0:T(8,128)(2,1)S(1)}, u32[]{:S(2)}, u32[]{:S(2)}) %collective-permute-start.26) | collective-permute-done | bytes 417824 | tf_op jit(solution)/shard_map/ppermute | solution.py:408
  325.9 11.5 %all-to-all-start = ((bf16[8,16,32,384]{3,2,1,0:T(8,128)(2,1)}), bf16[8,16,32,384]{3,2,1,0:T(8,128)(2,1)}, u32[]{:S(2)}, u32[]{:S(2)}) async-start(bf16[8,16,32,384]{3,2,1,0:T(8,128)(2,1)} %bitcast.133), calls=%async_computation | async-start | bytes 6291456 | tf_op jit(solution)/shard_map/all_to_all | solution.py:514
  337.4 1.4 copy-done.1
  338.8 1.4 copy-done.8
  340.3 7.0 %lat_inverse.4 = (bf16[4,16,32,384]{3,2,1,0:T(8,128)(2,1)S(1)}, bf16[4,16,32,384]{3,2,1,0:T(8,128)(2,1)S(1)}) custom-call(s32[2]{0:T(128)S(1)} %pad_add_fusion.where_ref, bf16[4,17,32,384]{3,2,1,0:T(8,128)(2,1)S(1)} %copy-done.1, bf16[4,17,32,384]{3,2,1,0:T(8,128)(2,1)S(1)} %copy-done.8, bf16[1024,1152]{1,0:T(8,128)(2,1)S(1)} %dynamic-slice_bitcast_fusion.table_ref, ...), custom_call_target="tpu_custom_call" | custom-call | flops 3623878656 | bytes 9437184 | tf_op jit(solution)/shard_map/lat_inverse/pallas_call | solution.py:157
  349.1 1.7 collective-permute-done.31.other_ref
  350.9 15.8 %channel_mlp.4 = bf16[4,2,16,32,384]{4,3,2,1,0:T(8,128)(2,1)} custom-call(s32[2]{0:T(128)S(1)} %pad_add_fusion.where_ref, bf16[4,16,32,384]{3,2,1,0:T(8,128)(2,1)S(1)} %get-tuple-element.293.own_ref, bf16[4,16,32,384]{3,2,1,0:T(8,128)(2,1)S(1)} %collective-permute-done.31.other_ref, f32[1,768]{1,0:T(1,128)S(1)} %reshape.285.gain_ref, ...), custom_call_target="tpu_custom_call" | custom-call | flops 9663676416 | bytes 6291456 | tf_op jit(solution)/shard_map/channel_mlp/pallas_call | solution.py:332
  366.6 20.0 %collective-permute-done.30.other_ref = bf16[4,17,32,384]{3,2,1,0:T(8,128)(2,1)S(1)} collective-permute-done((bf16[4,17,32,384]{3,2,1,0:T(8,128)(2,1)S(1)}, bf16[4,17,32,384]{3,2,1,0:T(8,128)(2,1)S(1)}, u32[]{:S(2)}, u32[]{:S(2)}) %collective-permute-start.30) | collective-permute-done | bytes 1671200 | tf_op jit(solution)/shard_map/ppermute | solution.py:402
  387.8 21.2 %all-to-all-done = bf16[8,16,32,384]{3,2,1,0:T(8,128)(2,1)} async-done(((bf16[8,16,32,384]{3,2,1,0:T(8,128)(2,1)}), bf16[8,16,32,384]{3,2,1,0:T(8,128)(2,1)}, u32[]{:S(2)}, u32[]{:S(2)}) %all-to-all-start) | async-done | bytes 3145760 | tf_op jit(solution)/shard_map/all_to_all | solution.py:514
  409.0 4.7 all-to-all-start.1
  413.7 1.4 copy-done.3
  415.2 1.4 copy-done.10
  416.6 7.6 %lat_inverse.5 = (bf16[4,16,32,384]{3,2,1,0:T(8,128)(2,1)S(1)}, bf16[4,16,32,384]{3,2,1,0:T(8,128)(2,1)}) custom-call(s32[2]{0:T(128)S(1)} %pad_add_fusion.where_ref, bf16[4,17,32,384]{3,2,1,0:T(8,128)(2,1)S(1)} %copy-done.3, bf16[4,17,32,384]{3,2,1,0:T(8,128)(2,1)S(1)} %copy-done.10, bf16[1024,1152]{1,0:T(8,128)(2,1)S(1)} %dynamic-slice_bitcast_fusion.table_ref, ...), custom_call_target="tpu_custom_call" | custom-call | flops 3623878656 | bytes 9437184 | tf_op jit(solution)/shard_map/lat_inverse/pallas_call | solution.py:157
  425.9 4.4 assemble.3.refs_0_
  431.7 15.9 %channel_mlp.5 = bf16[4,2,16,32,384]{4,3,2,1,0:T(8,128)(2,1)} custom-call(s32[2]{0:T(128)S(1)} %pad_add_fusion.where_ref, bf16[4,16,32,384]{3,2,1,0:T(8,128)(2,1)S(1)} %copy-done.15, bf16[4,16,32,384]{3,2,1,0:T(8,128)(2,1)} %collective-permute-done.32.other_ref, f32[1,768]{1,0:T(1,128)S(1)} %reshape.285.gain_ref, f32[1,768]{1,0:T(1,128)S(1)} %reshape.286.bias_ref, ...), custom_call_target="tpu_custom_call" | custom-call | flops 9663676416 | bytes 6291456 | tf_op jit(solution)/shard_map/channel_mlp/pallas_call | solution.py:332
  447.6 37.6 %all-to-all-done.1 = bf16[8,16,32,384]{3,2,1,0:T(8,128)(2,1)} async-done(((bf16[8,16,32,384]{3,2,1,0:T(8,128)(2,1)}), bf16[8,16,32,384]{3,2,1,0:T(8,128)(2,1)}, u32[]{:S(2)}, u32[]{:S(2)}) %all-to-all-start.1) | async-done | bytes 3145760 | tf_op jit(solution)/shard_map/all_to_all | solution.py:514
  485.3 3.6 all-to-all-start.2
  488.9 4.2 assemble.4.refs_0_
  493.1 67.2 %all-to-all-done.2 = bf16[8,16,32,384]{3,2,1,0:T(8,128)(2,1)S(1)} async-done(((bf16[8,16,32,384]{3,2,1,0:T(8,128)(2,1)}), bf16[8,16,32,384]{3,2,1,0:T(8,128)(2,1)S(1)}, u32[]{:S(2)}, u32[]{:S(2)}) %all-to-all-start.2) | async-done | bytes 3145760 | tf_op jit(solution)/shard_map/all_to_all | solution.py:514
  560.4 1.6 copy-done.16
  562.0 4.2 assemble.5
  (174 shorter events, 31.1 us)
Async XLA Ops:
  5.5 2.5 copy-start.29
  5.5 2.5 copy-start.30
  5.5 2.4 collective-permute-start
  8.0 9.5 %slice-start = ((s8[9437184]{0:T(1024)(128)(4,1)}), s8[4194304]{0:T(1024)(128)(4,1)S(1)}, s32[]{:S(2)}) async-start(s8[9437184]{0:T(1024)(128)(4,1)} %bitcast.130), calls=%async_computation.3 | async-start | bytes 8388608
  8.0 9.5 %slice-start.1 = ((s8[9437184]{0:T(1024)(128)(4,1)}), s8[4194304]{0:T(1024)(128)(4,1)S(1)}, s32[]{:S(2)}) async-start(s8[9437184]{0:T(1024)(128)(4,1)} %bitcast.130), calls=%async_computation.4 | async-start | bytes 8388608
  12.5 5.0 slice-start.2
  19.8 3.1 collective-permute-start.2
  19.9 39.7 %collective-permute-start.1 = (bf16[4,17,32,384]{3,2,1,0:T(8,128)(2,1)S(1)}, bf16[4,17,32,384]{3,2,1,0:T(8,128)(2,1)S(1)}, u32[]{:S(2)}, u32[]{:S(2)}) collective-permute-start(bf16[4,17,32,384]{3,2,1,0:T(8,128)(2,1)S(1)} %get-tuple-element.160), channel_id=1, source_target_pairs={{0,2},{2,0},{1,3},{3,1},{4,6},{6,4},{5,7},{7,5},{8,10},{10,8},{9,1... | collective-permute-start | bytes 5013512 | tf_op jit(solution)/shard_map/ppermute | solution.py:402
  32.5 1.4 collective-permute-start.3
  35.6 26.9 %copy-start.32 = (s32[4]{0:T(128)S(1)}, s32[4]{0:T(128)}, u32[]{:S(2)}) copy-start(s32[4]{0:T(128)} %param.26) | copy-start | bytes 52
  35.6 27.1 %copy-start.33 = (s32[4]{0:T(128)S(1)}, s32[4]{0:T(128)}, u32[]{:S(2)}) copy-start(s32[4]{0:T(128)} %param.27) | copy-start | bytes 52
  35.6 27.2 %copy-start.27 = (bf16[2,384]{1,0:T(2,128)(2,1)S(1)}, bf16[2,384]{1,0:T(2,128)(2,1)}, u32[]{:S(2)}) copy-start(bf16[2,384]{1,0:T(2,128)(2,1)} %param.23) | copy-start | bytes 4612
  60.8 43.2 %collective-permute-start.4 = (bf16[4,17,32,384]{3,2,1,0:T(8,128)(2,1)}, bf16[4,17,32,384]{3,2,1,0:T(8,128)(2,1)}, u32[]{:S(2)}, u32[]{:S(2)}) collective-permute-start(bf16[4,17,32,384]{3,2,1,0:T(8,128)(2,1)} %get-tuple-element.172), channel_id=1, source_target_pairs={{0,2},{2,0},{1,3},{3,1},{4,6},{6,4},{5,7},{7,5},{8,10},{10,8},{9,1... | collective-permute-start | bytes 5013512 | tf_op jit(solution)/shard_map/ppermute | solution.py:402
  62.8 7.5 %copy-start.28 = (bf16[2,384]{1,0:T(2,128)(2,1)S(1)}, bf16[2,384]{1,0:T(2,128)(2,1)}, u32[]{:S(2)}) copy-start(bf16[2,384]{1,0:T(2,128)(2,1)} %param.25) | copy-start | bytes 4612
  62.8 42.0 %copy-start.22 = (bf16[2,4,96,96]{3,2,1,0:T(8,128)(2,1)S(1)}, bf16[2,4,96,96]{3,2,1,0:T(8,128)(2,1)}, u32[]{:S(2)}) copy-start(bf16[2,4,96,96]{3,2,1,0:T(8,128)(2,1)} %param.24) | copy-start | bytes 442372
  62.8 42.0 %copy-start.23 = (bf16[2,4,96,96]{3,2,1,0:T(8,128)(2,1)S(1)}, bf16[2,4,96,96]{3,2,1,0:T(8,128)(2,1)}, u32[]{:S(2)}) copy-start(bf16[2,4,96,96]{3,2,1,0:T(8,128)(2,1)} %param.22) | copy-start | bytes 442372
  65.6 13.7 %collective-permute-start.7 = (bf16[17,32,384]{2,1,0:T(8,128)(2,1)S(1)}, bf16[17,32,384]{2,1,0:T(8,128)(2,1)S(1)}, u32[]{:S(2)}, u32[]{:S(2)}) collective-permute-start(bf16[17,32,384]{2,1,0:T(8,128)(2,1)S(1)} %get-tuple-element.315), channel_id=1, source_target_pairs={{0,12},{4,0},{8,4},{12,8},{1,13},{5,1},{9,5},{13,9},{2,14},{6,2},{... | collective-permute-start | bytes 1253384 | tf_op jit(solution)/shard_map/ppermute | solution.py:408
  69.2 34.8 %collective-permute-start.6 = (bf16[17,32,384]{2,1,0:T(8,128)(2,1)S(1)}, bf16[17,32,384]{2,1,0:T(8,128)(2,1)S(1)}, u32[]{:S(2)}, u32[]{:S(2)}) collective-permute-start(bf16[17,32,384]{2,1,0:T(8,128)(2,1)S(1)} %get-tuple-element.316), channel_id=1, source_target_pairs={{0,8},{4,12},{8,0},{12,4},{1,9},{5,13},{9,1},{13,5},{2,10},{6,14},... | collective-permute-start | bytes 1253384 | tf_op jit(solution)/shard_map/ppermute | solution.py:408
  69.2 34.8 %collective-permute-start.5 = (bf16[17,32,384]{2,1,0:T(8,128)(2,1)S(1)}, bf16[17,32,384]{2,1,0:T(8,128)(2,1)S(1)}, u32[]{:S(2)}, u32[]{:S(2)}) collective-permute-start(bf16[17,32,384]{2,1,0:T(8,128)(2,1)S(1)} %get-tuple-element.317), channel_id=1, source_target_pairs={{0,4},{4,8},{8,12},{12,0},{1,5},{5,9},{9,13},{13,1},{2,6},{6,10},{... | collective-permute-start | bytes 1253384 | tf_op jit(solution)/shard_map/ppermute | solution.py:408
  79.3 27.7 %copy-start.34 = (bf16[17,32,384]{2,1,0:T(8,128)(2,1)}, bf16[17,32,384]{2,1,0:T(8,128)(2,1)S(1)}, u32[]{:S(2)}) copy-start(bf16[17,32,384]{2,1,0:T(8,128)(2,1)S(1)} %collective-permute-done.7.refs_3_.refs_15_) | copy-start | bytes 1253380
  104.0 1.7 copy-start.35
  104.0 44.9 %collective-permute-start.8 = (bf16[4,17,32,384]{3,2,1,0:T(8,128)(2,1)}, bf16[4,17,32,384]{3,2,1,0:T(8,128)(2,1)}, u32[]{:S(2)}, u32[]{:S(2)}) collective-permute-start(bf16[4,17,32,384]{3,2,1,0:T(8,128)(2,1)} %get-tuple-element.183), channel_id=1, source_target_pairs={{0,2},{2,0},{1,3},{3,1},{4,6},{6,4},{5,7},{7,5},{8,10},{10,8},{9,1... | collective-permute-start | bytes 5013512 | tf_op jit(solution)/shard_map/ppermute | solution.py:402
  110.0 11.3 %collective-permute-start.11 = (bf16[17,32,384]{2,1,0:T(8,128)(2,1)}, bf16[17,32,384]{2,1,0:T(8,128)(2,1)S(1)}, u32[]{:S(2)}, u32[]{:S(2)}) collective-permute-start(bf16[17,32,384]{2,1,0:T(8,128)(2,1)} %get-tuple-element.311), channel_id=1, source_target_pairs={{0,12},{4,0},{8,4},{12,8},{1,13},{5,1},{9,5},{13,9},{2,14},{6,2},{... | collective-permute-start | bytes 1253384 | tf_op jit(solution)/shard_map/ppermute | solution.py:408
  110.0 39.0 %collective-permute-start.10 = (bf16[17,32,384]{2,1,0:T(8,128)(2,1)}, bf16[17,32,384]{2,1,0:T(8,128)(2,1)}, u32[]{:S(2)}, u32[]{:S(2)}) collective-permute-start(bf16[17,32,384]{2,1,0:T(8,128)(2,1)} %get-tuple-element.312), channel_id=1, source_target_pairs={{0,8},{4,12},{8,0},{12,4},{1,9},{5,13},{9,1},{13,5},{2,10},{6,14},... | collective-permute-start | bytes 1253384 | tf_op jit(solution)/shard_map/ppermute | solution.py:408
  112.7 36.2 %collective-permute-start.9 = (bf16[17,32,384]{2,1,0:T(8,128)(2,1)}, bf16[17,32,384]{2,1,0:T(8,128)(2,1)}, u32[]{:S(2)}, u32[]{:S(2)}) collective-permute-start(bf16[17,32,384]{2,1,0:T(8,128)(2,1)} %get-tuple-element.313), channel_id=1, source_target_pairs={{0,4},{4,8},{8,12},{12,0},{1,5},{5,9},{9,13},{13,1},{2,6},{6,10},{... | collective-permute-start | bytes 1253384 | tf_op jit(solution)/shard_map/ppermute | solution.py:408
  118.0 31.4 %copy-start.24 = (bf16[768]{0:T(1024)(128)(2,1)S(1)}, bf16[768]{0:T(1024)(128)(2,1)}, u32[]{:S(2)}) copy-start(bf16[768]{0:T(1024)(128)(2,1)} %param.28) | copy-start | bytes 4612
  118.0 31.4 %copy-start.25 = (bf16[768]{0:T(1024)(128)(2,1)S(1)}, bf16[768]{0:T(1024)(128)(2,1)}, u32[]{:S(2)}) copy-start(bf16[768]{0:T(1024)(128)(2,1)} %param.29) | copy-start | bytes 4612
  121.2 28.2 %copy-start.37 = (bf16[17,32,384]{2,1,0:T(8,128)(2,1)}, bf16[17,32,384]{2,1,0:T(8,128)(2,1)S(1)}, u32[]{:S(2)}) copy-start(bf16[17,32,384]{2,1,0:T(8,128)(2,1)S(1)} %collective-permute-done.11.refs_7_.refs_19_) | copy-start | bytes 1253380
  148.9 9.4 %collective-permute-start.15 = (bf16[768,768]{1,0:T(8,128)(2,1)}, bf16[768,768]{1,0:T(8,128)(2,1)S(1)}, u32[]{:S(2)}, u32[]{:S(2)}) collective-permute-start(bf16[768,768]{1,0:T(8,128)(2,1)} %param.30), channel_id=1, source_target_pairs={{0,1},{1,0},{2,3},{3,2},{4,5},{5,4},{6,7},{7,6},{8,9},{9,8},{10,11... | collective-permute-start | bytes 3538952 | tf_op jit(solution)/shard_map/ppermute | solution.py:402
  148.9 10.9 %collective-permute-start.17 = (bf16[768,768]{1,0:T(8,128)(2,1)}, bf16[768,768]{1,0:T(8,128)(2,1)S(1)}, u32[]{:S(2)}, u32[]{:S(2)}) collective-permute-start(bf16[768,768]{1,0:T(8,128)(2,1)} %param.32), channel_id=1, source_target_pairs={{0,1},{1,0},{2,3},{3,2},{4,5},{5,4},{6,7},{7,6},{8,9},{9,8},{10,11... | collective-permute-start | bytes 3538952 | tf_op jit(solution)/shard_map/ppermute | solution.py:402
  149.5 2.0 copy-start.26
  149.5 2.2 copy-start.12
  151.5 2.8 copy-start.31
  151.5 4.8 collective-permute-start.16
  156.2 13.2 %collective-permute-start.14 = (bf16[17,32,384]{2,1,0:T(8,128)(2,1)S(1)}, bf16[17,32,384]{2,1,0:T(8,128)(2,1)S(1)}, u32[]{:S(2)}, u32[]{:S(2)}) collective-permute-start(bf16[17,32,384]{2,1,0:T(8,128)(2,1)S(1)} %get-tuple-element.307), channel_id=1, source_target_pairs={{0,12},{4,0},{8,4},{12,8},{1,13},{5,1},{9,5},{13,9},{2,14},{6,2},{... | collective-permute-start | bytes 1253384 | tf_op jit(solution)/shard_map/ppermute | solution.py:408
  156.2 36.6 %collective-permute-start.13 = (bf16[17,32,384]{2,1,0:T(8,128)(2,1)S(1)}, bf16[17,32,384]{2,1,0:T(8,128)(2,1)S(1)}, u32[]{:S(2)}, u32[]{:S(2)}) collective-permute-start(bf16[17,32,384]{2,1,0:T(8,128)(2,1)S(1)} %get-tuple-element.308), channel_id=1, source_target_pairs={{0,8},{4,12},{8,0},{12,4},{1,9},{5,13},{9,1},{13,5},{2,10},{6,14},... | collective-permute-start | bytes 1253384 | tf_op jit(solution)/shard_map/ppermute | solution.py:408
  156.3 36.5 %collective-permute-start.12 = (bf16[17,32,384]{2,1,0:T(8,128)(2,1)S(1)}, bf16[17,32,384]{2,1,0:T(8,128)(2,1)S(1)}, u32[]{:S(2)}, u32[]{:S(2)}) collective-permute-start(bf16[17,32,384]{2,1,0:T(8,128)(2,1)S(1)} %get-tuple-element.309), channel_id=1, source_target_pairs={{0,4},{4,8},{8,12},{12,0},{1,5},{5,9},{9,13},{13,1},{2,6},{6,10},{... | collective-permute-start | bytes 1253384 | tf_op jit(solution)/shard_map/ppermute | solution.py:408
  159.8 137.5 %copy-start.4 = (bf16[768,1536]{1,0:T(8,128)(2,1)}, bf16[768,1536]{1,0:T(8,128)(2,1)S(1)}, u32[]{:S(2)}) copy-start(bf16[768,1536]{1,0:T(8,128)(2,1)S(1)} %pad_maximum_fusion.w_in_ref) | copy-start | bytes 7077892
  159.8 33.9 %copy-start.13 = (bf16[17,32,384]{2,1,0:T(8,128)(2,1)S(1)}, bf16[17,32,384]{2,1,0:T(8,128)(2,1)}, u32[]{:S(2)}) copy-start(bf16[17,32,384]{2,1,0:T(8,128)(2,1)} %get-tuple-element.222.refs_0_.refs_12_) | copy-start | bytes 1253380
  169.4 23.4 %copy-start.38 = (bf16[17,32,384]{2,1,0:T(8,128)(2,1)}, bf16[17,32,384]{2,1,0:T(8,128)(2,1)S(1)}, u32[]{:S(2)}) copy-start(bf16[17,32,384]{2,1,0:T(8,128)(2,1)S(1)} %collective-permute-done.14.refs_11_.refs_23_) | copy-start | bytes 1253380
  206.6 14.5 %collective-permute-start.18 = (bf16[17,32,384]{2,1,0:T(8,128)(2,1)S(1)}, bf16[17,32,384]{2,1,0:T(8,128)(2,1)S(1)}, u32[]{:S(2)}, u32[]{:S(2)}) collective-permute-start(bf16[17,32,384]{2,1,0:T(8,128)(2,1)S(1)} %get-tuple-element.240), channel_id=1, source_target_pairs={{0,4},{4,8},{8,12},{12,0},{1,5},{5,9},{9,13},{13,1},{2,6},{6,10},{... | collective-permute-start | bytes 1253384 | tf_op jit(solution)/shard_map/ppermute | solution.py:408
  207.6 30.3 %collective-permute-start.19 = (bf16[17,32,384]{2,1,0:T(8,128)(2,1)S(1)}, bf16[17,32,384]{2,1,0:T(8,128)(2,1)S(1)}, u32[]{:S(2)}, u32[]{:S(2)}) collective-permute-start(bf16[17,32,384]{2,1,0:T(8,128)(2,1)S(1)} %get-tuple-element.241), channel_id=1, source_target_pairs={{0,8},{4,12},{8,0},{12,4},{1,9},{5,13},{9,1},{13,5},{2,10},{6,14},... | collective-permute-start | bytes 1253384 | tf_op jit(solution)/shard_map/ppermute | solution.py:408
  209.5 28.3 %collective-permute-start.20 = (bf16[17,32,384]{2,1,0:T(8,128)(2,1)S(1)}, bf16[17,32,384]{2,1,0:T(8,128)(2,1)S(1)}, u32[]{:S(2)}, u32[]{:S(2)}) collective-permute-start(bf16[17,32,384]{2,1,0:T(8,128)(2,1)S(1)} %get-tuple-element.242), channel_id=1, source_target_pairs={{0,12},{4,0},{8,4},{12,8},{1,13},{5,1},{9,5},{13,9},{2,14},{6,2},{... | collective-permute-start | bytes 1253384 | tf_op jit(solution)/shard_map/ppermute | solution.py:408
  238.1 38.8 %collective-permute-start.24 = (bf16[4,17,32,384]{3,2,1,0:T(8,128)(2,1)S(1)}, bf16[4,17,32,384]{3,2,1,0:T(8,128)(2,1)S(1)}, u32[]{:S(2)}, u32[]{:S(2)}) collective-permute-start(bf16[4,17,32,384]{3,2,1,0:T(8,128)(2,1)S(1)} %pad_maximum_fusion.2.own_ref), channel_id=1, source_target_pairs={{0,2},{2,0},{1,3},{3,1},{4,6},{6,4},{5,7},{7,5},{8,10},{10,8},{9,1... | collective-permute-start | bytes 5013512 | tf_op jit(solution)/shard_map/ppermute | solution.py:402
  238.7 22.2 %collective-permute-start.21 = (bf16[17,32,384]{2,1,0:T(8,128)(2,1)S(1)}, bf16[17,32,384]{2,1,0:T(8,128)(2,1)S(1)}, u32[]{:S(2)}, u32[]{:S(2)}) collective-permute-start(bf16[17,32,384]{2,1,0:T(8,128)(2,1)S(1)} %get-tuple-element.253), channel_id=1, source_target_pairs={{0,4},{4,8},{8,12},{12,0},{1,5},{5,9},{9,13},{13,1},{2,6},{6,10},{... | collective-permute-start | bytes 1253384 | tf_op jit(solution)/shard_map/ppermute | solution.py:408
  248.1 28.8 %collective-permute-start.22 = (bf16[17,32,384]{2,1,0:T(8,128)(2,1)S(1)}, bf16[17,32,384]{2,1,0:T(8,128)(2,1)S(1)}, u32[]{:S(2)}, u32[]{:S(2)}) collective-permute-start(bf16[17,32,384]{2,1,0:T(8,128)(2,1)S(1)} %get-tuple-element.254), channel_id=1, source_target_pairs={{0,8},{4,12},{8,0},{12,4},{1,9},{5,13},{9,1},{13,5},{2,10},{6,14},... | collective-permute-start | bytes 1253384 | tf_op jit(solution)/shard_map/ppermute | solution.py:408
  250.7 26.2 %collective-permute-start.23 = (bf16[17,32,384]{2,1,0:T(8,128)(2,1)S(1)}, bf16[17,32,384]{2,1,0:T(8,128)(2,1)S(1)}, u32[]{:S(2)}, u32[]{:S(2)}) collective-permute-start(bf16[17,32,384]{2,1,0:T(8,128)(2,1)S(1)} %get-tuple-element.255), channel_id=1, source_target_pairs={{0,12},{4,0},{8,4},{12,8},{1,13},{5,1},{9,5},{13,9},{2,14},{6,2},{... | collective-permute-start | bytes 1253384 | tf_op jit(solution)/shard_map/ppermute | solution.py:408
  283.8 13.4 %collective-permute-start.29 = (bf16[4,16,32,384]{3,2,1,0:T(8,128)(2,1)S(1)}, bf16[4,16,32,384]{3,2,1,0:T(8,128)(2,1)S(1)}, u32[]{:S(2)}, u32[]{:S(2)}) collective-permute-start(bf16[4,16,32,384]{3,2,1,0:T(8,128)(2,1)S(1)} %get-tuple-element.278), channel_id=1, source_target_pairs={{0,1},{1,0},{2,3},{3,2},{4,5},{5,4},{6,7},{7,6},{8,9},{9,8},{10,11... | collective-permute-start | bytes 4718600 | tf_op jit(solution)/shard_map/ppermute | solution.py:402
  284.2 28.8 %copy-start = (bf16[4,17,32,384]{3,2,1,0:T(8,128)(2,1)}, bf16[4,17,32,384]{3,2,1,0:T(8,128)(2,1)S(1)}, u32[]{:S(2)}) copy-start(bf16[4,17,32,384]{3,2,1,0:T(8,128)(2,1)S(1)} %pad_maximum_fusion.3.own_ref) | copy-start | bytes 5013508
  284.2 39.5 %collective-permute-start.28 = (bf16[4,17,32,384]{3,2,1,0:T(8,128)(2,1)S(1)}, bf16[4,17,32,384]{3,2,1,0:T(8,128)(2,1)S(1)}, u32[]{:S(2)}, u32[]{:S(2)}) collective-permute-start(bf16[4,17,32,384]{3,2,1,0:T(8,128)(2,1)S(1)} %pad_maximum_fusion.3.own_ref), channel_id=1, source_target_pairs={{0,2},{2,0},{1,3},{3,1},{4,6},{6,4},{5,7},{7,5},{8,10},{10,8},{9,1... | collective-permute-start | bytes 5013512 | tf_op jit(solution)/shard_map/ppermute | solution.py:402
  285.3 27.7 %collective-permute-start.25 = (bf16[17,32,384]{2,1,0:T(8,128)(2,1)S(1)}, bf16[17,32,384]{2,1,0:T(8,128)(2,1)S(1)}, u32[]{:S(2)}, u32[]{:S(2)}) collective-permute-start(bf16[17,32,384]{2,1,0:T(8,128)(2,1)S(1)} %get-tuple-element.266), channel_id=1, source_target_pairs={{0,4},{4,8},{8,12},{12,0},{1,5},{5,9},{9,13},{13,1},{2,6},{6,10},{... | collective-permute-start | bytes 1253384 | tf_op jit(solution)/shard_map/ppermute | solution.py:408
  294.7 29.0 %collective-permute-start.26 = (bf16[17,32,384]{2,1,0:T(8,128)(2,1)S(1)}, bf16[17,32,384]{2,1,0:T(8,128)(2,1)S(1)}, u32[]{:S(2)}, u32[]{:S(2)}) collective-permute-start(bf16[17,32,384]{2,1,0:T(8,128)(2,1)S(1)} %get-tuple-element.267), channel_id=1, source_target_pairs={{0,8},{4,12},{8,0},{12,4},{1,9},{5,13},{9,1},{13,5},{2,10},{6,14},... | collective-permute-start | bytes 1253384 | tf_op jit(solution)/shard_map/ppermute | solution.py:408
  296.2 27.5 %collective-permute-start.27 = (bf16[17,32,384]{2,1,0:T(8,128)(2,1)S(1)}, bf16[17,32,384]{2,1,0:T(8,128)(2,1)S(1)}, u32[]{:S(2)}, u32[]{:S(2)}) collective-permute-start(bf16[17,32,384]{2,1,0:T(8,128)(2,1)S(1)} %get-tuple-element.268), channel_id=1, source_target_pairs={{0,12},{4,0},{8,4},{12,8},{1,13},{5,1},{9,5},{13,9},{2,14},{6,2},{... | collective-permute-start | bytes 1253384 | tf_op jit(solution)/shard_map/ppermute | solution.py:408
  325.9 83.1 %all-to-all-start = ((bf16[8,16,32,384]{3,2,1,0:T(8,128)(2,1)}), bf16[8,16,32,384]{3,2,1,0:T(8,128)(2,1)}, u32[]{:S(2)}, u32[]{:S(2)}) async-start(bf16[8,16,32,384]{3,2,1,0:T(8,128)(2,1)} %bitcast.133), calls=%async_computation | async-start | bytes 6291456 | tf_op jit(solution)/shard_map/all_to_all | solution.py:514
  340.3 7.6 %copy-start.19 = (bf16[17,32,384]{2,1,0:T(8,128)(2,1)S(1)}, bf16[17,32,384]{2,1,0:T(8,128)(2,1)}, u32[]{:S(2)}) copy-start(bf16[17,32,384]{2,1,0:T(8,128)(2,1)} %copy-done.18) | copy-start | bytes 1253380
  340.3 7.6 %copy-start.21 = (bf16[17,32,384]{2,1,0:T(8,128)(2,1)S(1)}, bf16[17,32,384]{2,1,0:T(8,128)(2,1)}, u32[]{:S(2)}) copy-start(bf16[17,32,384]{2,1,0:T(8,128)(2,1)} %copy-done.20) | copy-start | bytes 1253380
  347.2 3.6 copy-start.5
  347.2 3.6 collective-permute-start.31
  348.1 18.5 %copy-start.2 = (bf16[4,17,32,384]{3,2,1,0:T(8,128)(2,1)}, bf16[4,17,32,384]{3,2,1,0:T(8,128)(2,1)S(1)}, u32[]{:S(2)}) copy-start(bf16[4,17,32,384]{3,2,1,0:T(8,128)(2,1)S(1)} %pad_maximum_fusion.4.own_ref) | copy-start | bytes 5013508
  348.1 38.5 %collective-permute-start.30 = (bf16[4,17,32,384]{3,2,1,0:T(8,128)(2,1)S(1)}, bf16[4,17,32,384]{3,2,1,0:T(8,128)(2,1)S(1)}, u32[]{:S(2)}, u32[]{:S(2)}) collective-permute-start(bf16[4,17,32,384]{3,2,1,0:T(8,128)(2,1)S(1)} %pad_maximum_fusion.4.own_ref), channel_id=1, source_target_pairs={{0,2},{2,0},{1,3},{3,1},{4,6},{6,4},{5,7},{7,5},{8,10},{10,8},{9,1... | collective-permute-start | bytes 5013512 | tf_op jit(solution)/shard_map/ppermute | solution.py:402
  409.0 76.2 %all-to-all-start.1 = ((bf16[8,16,32,384]{3,2,1,0:T(8,128)(2,1)}), bf16[8,16,32,384]{3,2,1,0:T(8,128)(2,1)}, u32[]{:S(2)}, u32[]{:S(2)}) async-start(bf16[8,16,32,384]{3,2,1,0:T(8,128)(2,1)} %bitcast.134), calls=%async_computation.1 | async-start | bytes 6291456 | tf_op jit(solution)/shard_map/all_to_all | solution.py:514
  425.4 4.9 copy-start.6
  425.4 4.9 collective-permute-start.32
  485.3 75.1 %all-to-all-start.2 = ((bf16[8,16,32,384]{3,2,1,0:T(8,128)(2,1)}), bf16[8,16,32,384]{3,2,1,0:T(8,128)(2,1)S(1)}, u32[]{:S(2)}, u32[]{:S(2)}) async-start(bf16[8,16,32,384]{3,2,1,0:T(8,128)(2,1)} %bitcast.135), calls=%async_computation.2 | async-start | bytes 6291456 | tf_op jit(solution)/shard_map/all_to_all | solution.py:514
  (16 other events, 18.9 us)

commit v8 on v7

--- a/solution.py
+++ b/solution.py
@@ -534,9 +534,6 @@
             filter_args = filter_operands()
         if step == 1 and chunks > 2:
             ahead = row_transform(2, fence((patches, kept))[0])
-        if step > chunks:
-            weights = mlp_weights(*dense)
-            inverse_lat = lax.dynamic_index_in_dim(jnp.asarray(np.stack(inverse_all)), lat_id, 0, False)
         patches, arrived, sent, kept, received, filter_args, weights, inverse_lat, ahead, dense = fence(
             (patches, arrived, sent, kept, received, filter_args, weights, inverse_lat, ahead, dense)
         )
@@ -558,7 +555,13 @@
             others[step - 1] = swap(owns[step - 1], "lat")
         if step >= 2:
             outputs[step - 2] = row_result(step - 2, owns[step - 2], others[step - 2])
-        patches, filtered, owns, others, outputs = fence((patches, filtered, owns, others, outputs))
+        if step == 0:
+            dense = fence((dense, owns[0][lon_count // 2]))[0]
+            weights = mlp_weights(*dense)
+            inverse_lat = lax.dynamic_index_in_dim(jnp.asarray(np.stack(inverse_all)), lat_id, 0, False)
+        patches, filtered, owns, others, outputs, weights, inverse_lat = fence(
+            (patches, filtered, owns, others, outputs, weights, inverse_lat)
+        )
 
     result = None
     pieces = None

time: 576 us -> 576 us (level)
  starting transfers between devices: 71.6 us -> 52.7 us
  waiting for transfers between devices: 319 us -> 336 us
    ppermute x18, starting transfers between devices: 41.3 us -> 27.9 us  [shift(): lax.ppermute(values, 'lon', [(z, (z + steps) % lon_count) for z in range(...]
    ppermute x15, waiting for transfers between devices: 40.2 us -> 53.4 us  [swap(): return lax.ppermute(values, axis, [(0, 1), (1, 0)])]
    unnamed x95 -> x105, local copies, waits for them, and re-layouts: 17 us -> 15 us
  transfers between devices with their start and end apart: 36 -> 36, of which waited for: 17 -> 20; matrix products, arithmetic and copies ran while one was open for 6% -> 6% of each run, Pallas kernels for 14% -> 14%
where the time goes in v8:
time: 576 us; the launch traced here: 566 us
  waiting for transfers between devices  336 us (58%)
  Pallas kernels  111 us (19%)
  starting transfers between devices  52.7 us (9%)
  other arithmetic  37.4 us (6%)
  local copies, waits for them, and re-layouts  25.6 us (4%)
    ppermute x18, waiting for transfers between devices, shift(): lax.ppermute(values, 'lon', [(z, (z + steps) % lon_count) for z in range(...  157 us
    all_to_all x3, waiting for transfers between devices, outward(): return lax.all_to_all(flat, ('lon', 'ch'), 0, 0, tiled=True).reshape(shape)  126 us
    ppermute x15, waiting for transfers between devices, swap(): return lax.ppermute(values, axis, [(0, 1), (1, 0)])  53.4 us
    pallas_call x3, Pallas kernels, mlp(): pl.pallas_call(mlp_kernel, grid_spec=pltpu.PrefetchScalarGridSpec(num_sca...  47.4 us
    ppermute x18, starting transfers between devices, shift(): lax.ppermute(values, 'lon', [(z, (z + steps) % lon_count) for z in range(...  27.9 us
    pallas_call x3, Pallas kernels, lat_inverse(): pl.pallas_call(lat_inverse_kernel, grid=(cols // 16,), in_specs=[pl.Block...  21.5 us
    pallas_call x3, Pallas kernels, lat_forward(): pl.pallas_call(lat_forward_kernel, grid=(cols // 16,), in_specs=[pl.Block...  16.2 us
    unnamed x105, local copies, waits for them, and re-layouts  15 us
  transfers between devices with their start and end apart: 36, of which 20 were waited for; matrix products, arithmetic and copies ran while one was open for 6% of the time, Pallas kernels for 14%

profile of v8, /device:TPU:0, one launch (start us, length us, event | category | flops | bytes accessed | tf_op | source)
XLA Modules:
  0.0 566.0 jit_solution(4463057665026141959)
XLA Ops:
  0.0 2.5 convert_reduce_fusion.2
  2.6 2.9 fusion.1
  6.0 1.8 dynamic-slice_bitcast_fusion.1.table_ref
  8.0 4.5 fusion.5.cells_ref
  12.6 4.9 lat_forward.3
  18.2 1.6 fusion.7
  19.9 2.9 collective-permute-start.1
  22.9 1.7 fusion.11.cells_ref
  24.6 5.6 lat_forward.4
  30.9 1.6 fusion.13
  33.9 1.7 fusion.17.cells_ref
  35.6 5.7 %lat_forward.5 = (bf16[4,17,32,384]{3,2,1,0:T(8,128)(2,1)}, bf16[4,17,32,384]{3,2,1,0:T(8,128)(2,1)S(1)}) custom-call(s32[2]{0:T(128)S(1)} %pad_add_fusion.where_ref, bf16[128,32,384]{2,1,0:T(8,128)(2,1)S(1)} %fusion.17.cells_ref, bf16[1088,1024]{1,0:T(8,128)(2,1)S(1)} %dynamic-slice_bitcast_fusion.1.table_ref), custom_call_target="tpu_custom_call" | custom-call | flops 3422552064 | bytes 6291456 | tf_op jit(solution)/shard_map/lat_forward/pallas_call | solution.py:95
  41.3 18.3 %collective-permute-done.1 = bf16[4,17,32,384]{3,2,1,0:T(8,128)(2,1)S(1)} collective-permute-done((bf16[4,17,32,384]{3,2,1,0:T(8,128)(2,1)S(1)}, bf16[4,17,32,384]{3,2,1,0:T(8,128)(2,1)S(1)}, u32[]{:S(2)}, u32[]{:S(2)}) %collective-permute-start.1) | collective-permute-done | bytes 1671200 | tf_op jit(solution)/shard_map/ppermute | solution.py:402
  60.8 1.7 collective-permute-start.4
  62.9 3.2 fusion.21
  66.1 3.6 collective-permute-start.7
  70.9 9.0 %collective-permute-done.7.refs_3_.refs_15_ = bf16[17,32,384]{2,1,0:T(8,128)(2,1)S(1)} collective-permute-done((bf16[17,32,384]{2,1,0:T(8,128)(2,1)S(1)}, bf16[17,32,384]{2,1,0:T(8,128)(2,1)S(1)}, u32[]{:S(2)}, u32[]{:S(2)}) %collective-permute-start.7) | collective-permute-done | bytes 417824 | tf_op jit(solution)/shard_map/ppermute | solution.py:408
  79.8 24.6 %collective-permute-done.6.refs_2_.refs_14_ = bf16[17,32,384]{2,1,0:T(8,128)(2,1)S(1)} collective-permute-done((bf16[17,32,384]{2,1,0:T(8,128)(2,1)S(1)}, bf16[17,32,384]{2,1,0:T(8,128)(2,1)S(1)}, u32[]{:S(2)}, u32[]{:S(2)}) %collective-permute-start.6) | collective-permute-done | bytes 417824 | tf_op jit(solution)/shard_map/ppermute | solution.py:408
  106.3 1.7 fusion.49
  107.9 3.0 fusion.25
  110.9 2.7 collective-permute-start.10
  113.6 2.0 collective-permute-start.9
  123.7 2.3 maximum_maximum_fusion.1.refs_28_
  127.2 22.6 %collective-permute-done.10.refs_6_.refs_18_ = bf16[17,32,384]{2,1,0:T(8,128)(2,1)} collective-permute-done((bf16[17,32,384]{2,1,0:T(8,128)(2,1)}, bf16[17,32,384]{2,1,0:T(8,128)(2,1)}, u32[]{:S(2)}, u32[]{:S(2)}) %collective-permute-start.10) | collective-permute-done | bytes 417824 | tf_op jit(solution)/shard_map/ppermute | solution.py:408
  149.8 2.8 fusion.29
  152.6 2.0 collective-permute-start.12
  154.6 9.1 %collective-permute-done.14.refs_11_.refs_23_ = bf16[17,32,384]{2,1,0:T(8,128)(2,1)S(1)} collective-permute-done((bf16[17,32,384]{2,1,0:T(8,128)(2,1)S(1)}, bf16[17,32,384]{2,1,0:T(8,128)(2,1)S(1)}, u32[]{:S(2)}, u32[]{:S(2)}) %collective-permute-start.14) | collective-permute-done | bytes 417824 | tf_op jit(solution)/shard_map/ppermute | solution.py:408
  163.7 24.6 %collective-permute-done.13.refs_10_.refs_22_ = bf16[17,32,384]{2,1,0:T(8,128)(2,1)S(1)} collective-permute-done((bf16[17,32,384]{2,1,0:T(8,128)(2,1)S(1)}, bf16[17,32,384]{2,1,0:T(8,128)(2,1)S(1)}, u32[]{:S(2)}, u32[]{:S(2)}) %collective-permute-start.13) | collective-permute-done | bytes 417824 | tf_op jit(solution)/shard_map/ppermute | solution.py:408
  189.3 13.1 %modes.1 = (bf16[17,32,384]{2,1,0:T(8,128)(2,1)S(1)}, bf16[17,32,384]{2,1,0:T(8,128)(2,1)S(1)}, bf16[17,32,384]{2,1,0:T(8,128)(2,1)S(1)}, bf16[17,32,384]{2,1,0:...) custom-call(s32[1]{0:T(128)} %bitcast.23.first_pair_ref, ...), custom_call_target="tpu_custom_call" | custom-call | flops 7247757312 | bytes 10027008 | tf_op jit(solution)/shard_map/modes/pallas_call | solution.py:279
  202.4 1.8 collective-permute-start.16
  204.3 18.8 %collective-permute-done.16 = bf16[17,32,384]{2,1,0:T(8,128)(2,1)S(1)} collective-permute-done((bf16[17,32,384]{2,1,0:T(8,128)(2,1)S(1)}, bf16[17,32,384]{2,1,0:T(8,128)(2,1)S(1)}, u32[]{:S(2)}, u32[]{:S(2)}) %collective-permute-start.16) | collective-permute-done | bytes 417824 | tf_op jit(solution)/shard_map/ppermute | solution.py:408
  223.9 3.8 collective-permute-start.17
  227.7 1.8 all-gather
  229.8 3.7 pad_maximum_fusion.1.w_out_ref
  233.5 4.7 collective-permute-done.15
  238.2 6.8 %collective-permute-done.17 = bf16[17,32,384]{2,1,0:T(8,128)(2,1)S(1)} collective-permute-done((bf16[17,32,384]{2,1,0:T(8,128)(2,1)S(1)}, bf16[17,32,384]{2,1,0:T(8,128)(2,1)S(1)}, u32[]{:S(2)}, u32[]{:S(2)}) %collective-permute-start.17) | collective-permute-done | bytes 417824 | tf_op jit(solution)/shard_map/ppermute | solution.py:408
  246.0 2.6 collective-permute-start.22
  248.6 2.7 collective-permute-start.23
  251.3 9.2 %collective-permute-done.21 = bf16[17,32,384]{2,1,0:T(8,128)(2,1)S(1)} collective-permute-done((bf16[17,32,384]{2,1,0:T(8,128)(2,1)S(1)}, bf16[17,32,384]{2,1,0:T(8,128)(2,1)S(1)}, u32[]{:S(2)}, u32[]{:S(2)}) %collective-permute-start.21) | collective-permute-done | bytes 417824 | tf_op jit(solution)/shard_map/ppermute | solution.py:408
  260.5 16.4 %collective-permute-done.22 = bf16[17,32,384]{2,1,0:T(8,128)(2,1)S(1)} collective-permute-done((bf16[17,32,384]{2,1,0:T(8,128)(2,1)S(1)}, bf16[17,32,384]{2,1,0:T(8,128)(2,1)S(1)}, u32[]{:S(2)}, u32[]{:S(2)}) %collective-permute-start.22) | collective-permute-done | bytes 417824 | tf_op jit(solution)/shard_map/ppermute | solution.py:408
  276.9 6.5 %collective-permute-done.24.other_ref = bf16[4,17,32,384]{3,2,1,0:T(8,128)(2,1)S(1)} collective-permute-done((bf16[4,17,32,384]{3,2,1,0:T(8,128)(2,1)S(1)}, bf16[4,17,32,384]{3,2,1,0:T(8,128)(2,1)S(1)}, u32[]{:S(2)}, u32[]{:S(2)}) %collective-permute-start.24) | collective-permute-done | bytes 1671200 | tf_op jit(solution)/shard_map/ppermute | solution.py:402
  283.4 6.9 %lat_inverse.3 = (bf16[4,16,32,384]{3,2,1,0:T(8,128)(2,1)S(1)}, bf16[4,16,32,384]{3,2,1,0:T(8,128)(2,1)S(1)}) custom-call(s32[2]{0:T(128)S(1)} %pad_add_fusion.where_ref, bf16[4,17,32,384]{3,2,1,0:T(8,128)(2,1)S(1)} %pad_maximum_fusion.2.own_ref, bf16[4,17,32,384]{3,2,1,0:T(8,128)(2,1)S(1)} %collective-permute-done.24.other_ref, ...), custom_call_target="tpu_custom_call" | custom-call | flops 3623878656 | bytes 9437184 | tf_op jit(solution)/shard_map/lat_inverse/pallas_call | solution.py:157
  291.4 2.5 collective-permute-start.25
  294.0 2.3 collective-permute-start.26
  296.9 15.8 %channel_mlp.3 = bf16[4,2,16,32,384]{4,3,2,1,0:T(8,128)(2,1)} custom-call(s32[2]{0:T(128)S(1)} %pad_add_fusion.where_ref, bf16[4,16,32,384]{3,2,1,0:T(8,128)(2,1)S(1)} %get-tuple-element.314.own_ref, bf16[4,16,32,384]{3,2,1,0:T(8,128)(2,1)S(1)} %collective-permute-done.29.other_ref, f32[1,768]{1,0:T(1,128)S(1)} %reshape.285.gain_ref, ...), custom_call_target="tpu_custom_call" | custom-call | flops 9663676416 | bytes 6291456 | tf_op jit(solution)/shard_map/channel_mlp/pallas_call | solution.py:332
  312.7 11.1 %collective-permute-done.26 = bf16[17,32,384]{2,1,0:T(8,128)(2,1)S(1)} collective-permute-done((bf16[17,32,384]{2,1,0:T(8,128)(2,1)S(1)}, bf16[17,32,384]{2,1,0:T(8,128)(2,1)S(1)}, u32[]{:S(2)}, u32[]{:S(2)}) %collective-permute-start.26) | collective-permute-done | bytes 417824 | tf_op jit(solution)/shard_map/ppermute | solution.py:408
  323.8 5.8 %collective-permute-done.28.other_ref = bf16[4,17,32,384]{3,2,1,0:T(8,128)(2,1)S(1)} collective-permute-done((bf16[4,17,32,384]{3,2,1,0:T(8,128)(2,1)S(1)}, bf16[4,17,32,384]{3,2,1,0:T(8,128)(2,1)S(1)}, u32[]{:S(2)}, u32[]{:S(2)}) %collective-permute-start.28) | collective-permute-done | bytes 1671200 | tf_op jit(solution)/shard_map/ppermute | solution.py:402
  330.9 5.9 %all-to-all-start = ((bf16[8,16,32,384]{3,2,1,0:T(8,128)(2,1)}), bf16[8,16,32,384]{3,2,1,0:T(8,128)(2,1)}, u32[]{:S(2)}, u32[]{:S(2)}) async-start(bf16[8,16,32,384]{3,2,1,0:T(8,128)(2,1)} %bitcast.133), calls=%async_computation | async-start | bytes 6291456 | tf_op jit(solution)/shard_map/all_to_all | solution.py:514
  338.2 1.4 copy-done.8
  339.6 7.0 %lat_inverse.4 = (bf16[4,16,32,384]{3,2,1,0:T(8,128)(2,1)S(1)}, bf16[4,16,32,384]{3,2,1,0:T(8,128)(2,1)S(1)}) custom-call(s32[2]{0:T(128)S(1)} %pad_add_fusion.where_ref, bf16[4,17,32,384]{3,2,1,0:T(8,128)(2,1)S(1)} %copy-done.1, bf16[4,17,32,384]{3,2,1,0:T(8,128)(2,1)S(1)} %copy-done.8, bf16[1024,1152]{1,0:T(8,128)(2,1)S(1)} %dynamic-slice_bitcast_fusion.table_ref, ...), custom_call_target="tpu_custom_call" | custom-call | flops 3623878656 | bytes 9437184 | tf_op jit(solution)/shard_map/lat_inverse/pallas_call | solution.py:157
  350.2 15.7 %channel_mlp.4 = bf16[4,2,16,32,384]{4,3,2,1,0:T(8,128)(2,1)} custom-call(s32[2]{0:T(128)S(1)} %pad_add_fusion.where_ref, bf16[4,16,32,384]{3,2,1,0:T(8,128)(2,1)S(1)} %get-tuple-element.331.own_ref, bf16[4,16,32,384]{3,2,1,0:T(8,128)(2,1)S(1)} %collective-permute-done.31.other_ref, f32[1,768]{1,0:T(1,128)S(1)} %reshape.285.gain_ref, ...), custom_call_target="tpu_custom_call" | custom-call | flops 9663676416 | bytes 6291456 | tf_op jit(solution)/shard_map/channel_mlp/pallas_call | solution.py:332
  366.0 20.0 %collective-permute-done.30.other_ref = bf16[4,17,32,384]{3,2,1,0:T(8,128)(2,1)S(1)} collective-permute-done((bf16[4,17,32,384]{3,2,1,0:T(8,128)(2,1)S(1)}, bf16[4,17,32,384]{3,2,1,0:T(8,128)(2,1)S(1)}, u32[]{:S(2)}, u32[]{:S(2)}) %collective-permute-start.30) | collective-permute-done | bytes 1671200 | tf_op jit(solution)/shard_map/ppermute | solution.py:402
  387.2 21.2 %all-to-all-done = bf16[8,16,32,384]{3,2,1,0:T(8,128)(2,1)} async-done(((bf16[8,16,32,384]{3,2,1,0:T(8,128)(2,1)}), bf16[8,16,32,384]{3,2,1,0:T(8,128)(2,1)}, u32[]{:S(2)}, u32[]{:S(2)}) %all-to-all-start) | async-done | bytes 3145760 | tf_op jit(solution)/shard_map/all_to_all | solution.py:514
  408.4 4.7 all-to-all-start.1
  414.5 1.4 copy-done.10
  416.0 7.6 %lat_inverse.5 = (bf16[4,16,32,384]{3,2,1,0:T(8,128)(2,1)S(1)}, bf16[4,16,32,384]{3,2,1,0:T(8,128)(2,1)}) custom-call(s32[2]{0:T(128)S(1)} %pad_add_fusion.where_ref, bf16[4,17,32,384]{3,2,1,0:T(8,128)(2,1)S(1)} %copy-done.3, bf16[4,17,32,384]{3,2,1,0:T(8,128)(2,1)S(1)} %copy-done.10, bf16[1024,1152]{1,0:T(8,128)(2,1)S(1)} %dynamic-slice_bitcast_fusion.table_ref, ...), custom_call_target="tpu_custom_call" | custom-call | flops 3623878656 | bytes 9437184 | tf_op jit(solution)/shard_map/lat_inverse/pallas_call | solution.py:157
  425.2 4.4 assemble.3.refs_0_
  431.1 15.9 %channel_mlp.5 = bf16[4,2,16,32,384]{4,3,2,1,0:T(8,128)(2,1)} custom-call(s32[2]{0:T(128)S(1)} %pad_add_fusion.where_ref, bf16[4,16,32,384]{3,2,1,0:T(8,128)(2,1)S(1)} %copy-done.14, bf16[4,16,32,384]{3,2,1,0:T(8,128)(2,1)} %collective-permute-done.32.other_ref, f32[1,768]{1,0:T(1,128)S(1)} %reshape.285.gain_ref, f32[1,768]{1,0:T(1,128)S(1)} %reshape.286.bias_ref, ...), custom_call_target="tpu_custom_call" | custom-call | flops 9663676416 | bytes 6291456 | tf_op jit(solution)/shard_map/channel_mlp/pallas_call | solution.py:332
  447.0 37.6 %all-to-all-done.1 = bf16[8,16,32,384]{3,2,1,0:T(8,128)(2,1)} async-done(((bf16[8,16,32,384]{3,2,1,0:T(8,128)(2,1)}), bf16[8,16,32,384]{3,2,1,0:T(8,128)(2,1)}, u32[]{:S(2)}, u32[]{:S(2)}) %all-to-all-start.1) | async-done | bytes 3145760 | tf_op jit(solution)/shard_map/all_to_all | solution.py:514
  484.6 3.6 all-to-all-start.2
  488.3 4.2 assemble.4.refs_0_
  492.5 67.2 %all-to-all-done.2 = bf16[8,16,32,384]{3,2,1,0:T(8,128)(2,1)S(1)} async-done(((bf16[8,16,32,384]{3,2,1,0:T(8,128)(2,1)}), bf16[8,16,32,384]{3,2,1,0:T(8,128)(2,1)S(1)}, u32[]{:S(2)}, u32[]{:S(2)}) %all-to-all-start.2) | async-done | bytes 3145760 | tf_op jit(solution)/shard_map/all_to_all | solution.py:514
  559.7 1.6 copy-done.15
  561.4 4.2 assemble.5
  (185 shorter events, 34.1 us)
Async XLA Ops:
  5.5 2.4 collective-permute-start
  8.0 9.5 %slice-start = ((s8[9437184]{0:T(1024)(128)(4,1)}), s8[4194304]{0:T(1024)(128)(4,1)S(1)}, s32[]{:S(2)}) async-start(s8[9437184]{0:T(1024)(128)(4,1)} %bitcast.130), calls=%async_computation.3 | async-start | bytes 8388608
  8.0 9.5 %slice-start.1 = ((s8[9437184]{0:T(1024)(128)(4,1)}), s8[4194304]{0:T(1024)(128)(4,1)S(1)}, s32[]{:S(2)}) async-start(s8[9437184]{0:T(1024)(128)(4,1)} %bitcast.130), calls=%async_computation.4 | async-start | bytes 8388608
  12.5 5.0 slice-start.2
  19.8 3.1 collective-permute-start.2
  19.9 39.7 %collective-permute-start.1 = (bf16[4,17,32,384]{3,2,1,0:T(8,128)(2,1)S(1)}, bf16[4,17,32,384]{3,2,1,0:T(8,128)(2,1)S(1)}, u32[]{:S(2)}, u32[]{:S(2)}) collective-permute-start(bf16[4,17,32,384]{3,2,1,0:T(8,128)(2,1)S(1)} %get-tuple-element.182), channel_id=1, source_target_pairs={{0,2},{2,0},{1,3},{3,1},{4,6},{6,4},{5,7},{7,5},{8,10},{10,8},{9,1... | collective-permute-start | bytes 5013512 | tf_op jit(solution)/shard_map/ppermute | solution.py:402
  32.5 1.4 collective-permute-start.3
  35.6 26.9 %copy-start.36 = (s32[4]{0:T(128)S(1)}, s32[4]{0:T(128)}, u32[]{:S(2)}) copy-start(s32[4]{0:T(128)} %param.26) | copy-start | bytes 52
  35.6 27.1 %copy-start.37 = (s32[4]{0:T(128)S(1)}, s32[4]{0:T(128)}, u32[]{:S(2)}) copy-start(s32[4]{0:T(128)} %param.27) | copy-start | bytes 52
  35.6 27.2 %copy-start.31 = (bf16[2,384]{1,0:T(2,128)(2,1)S(1)}, bf16[2,384]{1,0:T(2,128)(2,1)}, u32[]{:S(2)}) copy-start(bf16[2,384]{1,0:T(2,128)(2,1)} %param.23) | copy-start | bytes 4612
  60.8 43.7 %collective-permute-start.4 = (bf16[4,17,32,384]{3,2,1,0:T(8,128)(2,1)}, bf16[4,17,32,384]{3,2,1,0:T(8,128)(2,1)}, u32[]{:S(2)}, u32[]{:S(2)}) collective-permute-start(bf16[4,17,32,384]{3,2,1,0:T(8,128)(2,1)} %get-tuple-element.194), channel_id=1, source_target_pairs={{0,2},{2,0},{1,3},{3,1},{4,6},{6,4},{5,7},{7,5},{8,10},{10,8},{9,1... | collective-permute-start | bytes 5013512 | tf_op jit(solution)/shard_map/ppermute | solution.py:402
  62.8 8.0 %copy-start.32 = (bf16[2,384]{1,0:T(2,128)(2,1)S(1)}, bf16[2,384]{1,0:T(2,128)(2,1)}, u32[]{:S(2)}) copy-start(bf16[2,384]{1,0:T(2,128)(2,1)} %param.25) | copy-start | bytes 4612
  62.9 42.6 %copy-start.26 = (bf16[2,4,96,96]{3,2,1,0:T(8,128)(2,1)S(1)}, bf16[2,4,96,96]{3,2,1,0:T(8,128)(2,1)}, u32[]{:S(2)}) copy-start(bf16[2,4,96,96]{3,2,1,0:T(8,128)(2,1)} %param.24) | copy-start | bytes 442372
  62.9 42.6 %copy-start.27 = (bf16[2,4,96,96]{3,2,1,0:T(8,128)(2,1)S(1)}, bf16[2,4,96,96]{3,2,1,0:T(8,128)(2,1)}, u32[]{:S(2)}) copy-start(bf16[2,4,96,96]{3,2,1,0:T(8,128)(2,1)} %param.22) | copy-start | bytes 442372
  66.1 13.7 %collective-permute-start.7 = (bf16[17,32,384]{2,1,0:T(8,128)(2,1)S(1)}, bf16[17,32,384]{2,1,0:T(8,128)(2,1)S(1)}, u32[]{:S(2)}, u32[]{:S(2)}) collective-permute-start(bf16[17,32,384]{2,1,0:T(8,128)(2,1)S(1)} %get-tuple-element.359), channel_id=1, source_target_pairs={{0,12},{4,0},{8,4},{12,8},{1,13},{5,1},{9,5},{13,9},{2,14},{6,2},{... | collective-permute-start | bytes 1253384 | tf_op jit(solution)/shard_map/ppermute | solution.py:408
  69.7 34.8 %collective-permute-start.6 = (bf16[17,32,384]{2,1,0:T(8,128)(2,1)S(1)}, bf16[17,32,384]{2,1,0:T(8,128)(2,1)S(1)}, u32[]{:S(2)}, u32[]{:S(2)}) collective-permute-start(bf16[17,32,384]{2,1,0:T(8,128)(2,1)S(1)} %get-tuple-element.360), channel_id=1, source_target_pairs={{0,8},{4,12},{8,0},{12,4},{1,9},{5,13},{9,1},{13,5},{2,10},{6,14},... | collective-permute-start | bytes 1253384 | tf_op jit(solution)/shard_map/ppermute | solution.py:408
  69.7 34.8 %collective-permute-start.5 = (bf16[17,32,384]{2,1,0:T(8,128)(2,1)S(1)}, bf16[17,32,384]{2,1,0:T(8,128)(2,1)S(1)}, u32[]{:S(2)}, u32[]{:S(2)}) collective-permute-start(bf16[17,32,384]{2,1,0:T(8,128)(2,1)S(1)} %get-tuple-element.361), channel_id=1, source_target_pairs={{0,4},{4,8},{8,12},{12,0},{1,5},{5,9},{9,13},{13,1},{2,6},{6,10},{... | collective-permute-start | bytes 1253384 | tf_op jit(solution)/shard_map/ppermute | solution.py:408
  79.8 25.3 %copy-start.38 = (bf16[17,32,384]{2,1,0:T(8,128)(2,1)}, bf16[17,32,384]{2,1,0:T(8,128)(2,1)S(1)}, u32[]{:S(2)}) copy-start(bf16[17,32,384]{2,1,0:T(8,128)(2,1)S(1)} %collective-permute-done.7.refs_3_.refs_15_) | copy-start | bytes 1253380
  104.5 45.2 %collective-permute-start.8 = (bf16[4,17,32,384]{3,2,1,0:T(8,128)(2,1)}, bf16[4,17,32,384]{3,2,1,0:T(8,128)(2,1)}, u32[]{:S(2)}, u32[]{:S(2)}) collective-permute-start(bf16[4,17,32,384]{3,2,1,0:T(8,128)(2,1)} %get-tuple-element.205), channel_id=1, source_target_pairs={{0,2},{2,0},{1,3},{3,1},{4,6},{6,4},{5,7},{7,5},{8,10},{10,8},{9,1... | collective-permute-start | bytes 5013512 | tf_op jit(solution)/shard_map/ppermute | solution.py:402
  110.9 9.8 %copy-start.18 = (bf16[1,4,96,4,96]{4,3,2,1,0:T(4,128)(2,1)S(1)}, bf16[1,4,96,4,96]{4,3,2,1,0:T(4,128)(2,1)}, u32[]{:S(2)}) copy-start(bf16[1,4,96,4,96]{4,3,2,1,0:T(4,128)(2,1)} %get-tuple-element.364) | copy-start | bytes 884740
  110.9 10.8 %copy-start.17 = (bf16[1,4,96,4,96]{4,3,2,1,0:T(4,128)(2,1)S(1)}, bf16[1,4,96,4,96]{4,3,2,1,0:T(4,128)(2,1)}, u32[]{:S(2)}) copy-start(bf16[1,4,96,4,96]{4,3,2,1,0:T(4,128)(2,1)} %get-tuple-element.381) | copy-start | bytes 884740
  110.9 16.2 %collective-permute-start.11 = (bf16[17,32,384]{2,1,0:T(8,128)(2,1)}, bf16[17,32,384]{2,1,0:T(8,128)(2,1)}, u32[]{:S(2)}, u32[]{:S(2)}) collective-permute-start(bf16[17,32,384]{2,1,0:T(8,128)(2,1)} %get-tuple-element.355), channel_id=1, source_target_pairs={{0,12},{4,0},{8,4},{12,8},{1,13},{5,1},{9,5},{13,9},{2,14},{6,2},{... | collective-permute-start | bytes 1253384 | tf_op jit(solution)/shard_map/ppermute | solution.py:408
  110.9 38.8 %collective-permute-start.10 = (bf16[17,32,384]{2,1,0:T(8,128)(2,1)}, bf16[17,32,384]{2,1,0:T(8,128)(2,1)}, u32[]{:S(2)}, u32[]{:S(2)}) collective-permute-start(bf16[17,32,384]{2,1,0:T(8,128)(2,1)} %get-tuple-element.356), channel_id=1, source_target_pairs={{0,8},{4,12},{8,0},{12,4},{1,9},{5,13},{9,1},{13,5},{2,10},{6,14},... | collective-permute-start | bytes 1253384 | tf_op jit(solution)/shard_map/ppermute | solution.py:408
  113.6 36.1 %collective-permute-start.9 = (bf16[17,32,384]{2,1,0:T(8,128)(2,1)}, bf16[17,32,384]{2,1,0:T(8,128)(2,1)}, u32[]{:S(2)}, u32[]{:S(2)}) collective-permute-start(bf16[17,32,384]{2,1,0:T(8,128)(2,1)} %get-tuple-element.357), channel_id=1, source_target_pairs={{0,4},{4,8},{8,12},{12,0},{1,5},{5,9},{9,13},{13,1},{2,6},{6,10},{... | collective-permute-start | bytes 1253384 | tf_op jit(solution)/shard_map/ppermute | solution.py:408
  149.7 39.5 %copy-start.12 = (bf16[17,32,384]{2,1,0:T(8,128)(2,1)S(1)}, bf16[17,32,384]{2,1,0:T(8,128)(2,1)}, u32[]{:S(2)}) copy-start(bf16[17,32,384]{2,1,0:T(8,128)(2,1)} %get-tuple-element.244.refs_0_.refs_12_) | copy-start | bytes 1253380
  149.7 73.8 %slice-start.3 = ((s8[4718592]{0:T(1024)(128)(4,1)}), s8[4194304]{0:T(1024)(128)(4,1)S(1)}, s32[]{:S(2)}) async-start(s8[4718592]{0:T(1024)(128)(4,1)} %bitcast.136), calls=%async_computation.6 | async-start | bytes 8388608
  152.6 11.2 %collective-permute-start.14 = (bf16[17,32,384]{2,1,0:T(8,128)(2,1)S(1)}, bf16[17,32,384]{2,1,0:T(8,128)(2,1)S(1)}, u32[]{:S(2)}, u32[]{:S(2)}) collective-permute-start(bf16[17,32,384]{2,1,0:T(8,128)(2,1)S(1)} %get-tuple-element.351), channel_id=1, source_target_pairs={{0,12},{4,0},{8,4},{12,8},{1,13},{5,1},{9,5},{13,9},{2,14},{6,2},{... | collective-permute-start | bytes 1253384 | tf_op jit(solution)/shard_map/ppermute | solution.py:408
  152.6 35.8 %collective-permute-start.13 = (bf16[17,32,384]{2,1,0:T(8,128)(2,1)S(1)}, bf16[17,32,384]{2,1,0:T(8,128)(2,1)S(1)}, u32[]{:S(2)}, u32[]{:S(2)}) collective-permute-start(bf16[17,32,384]{2,1,0:T(8,128)(2,1)S(1)} %get-tuple-element.352), channel_id=1, source_target_pairs={{0,8},{4,12},{8,0},{12,4},{1,9},{5,13},{9,1},{13,5},{2,10},{6,14},... | collective-permute-start | bytes 1253384 | tf_op jit(solution)/shard_map/ppermute | solution.py:408
  152.6 35.8 %collective-permute-start.12 = (bf16[17,32,384]{2,1,0:T(8,128)(2,1)S(1)}, bf16[17,32,384]{2,1,0:T(8,128)(2,1)S(1)}, u32[]{:S(2)}, u32[]{:S(2)}) collective-permute-start(bf16[17,32,384]{2,1,0:T(8,128)(2,1)S(1)} %get-tuple-element.353), channel_id=1, source_target_pairs={{0,4},{4,8},{8,12},{12,0},{1,5},{5,9},{9,13},{13,1},{2,6},{6,10},{... | collective-permute-start | bytes 1253384 | tf_op jit(solution)/shard_map/ppermute | solution.py:408
  163.7 24.7 %copy-start.41 = (bf16[17,32,384]{2,1,0:T(8,128)(2,1)}, bf16[17,32,384]{2,1,0:T(8,128)(2,1)S(1)}, u32[]{:S(2)}) copy-start(bf16[17,32,384]{2,1,0:T(8,128)(2,1)S(1)} %collective-permute-done.14.refs_11_.refs_23_) | copy-start | bytes 1253380
  189.3 33.8 %copy-start.20 = (bf16[768,768]{1,0:T(8,128)(2,1)S(1)}, bf16[768,768]{1,0:T(8,128)(2,1)}, u32[]{:S(2)}) copy-start(bf16[768,768]{1,0:T(8,128)(2,1)} %param.30) | copy-start | bytes 3538948
  189.3 34.3 %copy-start.30 = (bf16[768]{0:T(1024)(128)(2,1)S(1)}, bf16[768]{0:T(1024)(128)(2,1)}, u32[]{:S(2)}) copy-start(bf16[768]{0:T(1024)(128)(2,1)} %param.31) | copy-start | bytes 4612
  189.3 34.3 %slice-start.4 = ((s8[4718592]{0:T(1024)(128)(4,1)}), s8[524288]{0:T(1024)(128)(4,1)S(1)}, s32[]{:S(2)}) async-start(s8[4718592]{0:T(1024)(128)(4,1)} %bitcast.136), calls=%async_computation.7 | async-start | bytes 1048576
  202.4 21.4 %copy-start.28 = (bf16[768]{0:T(1024)(128)(2,1)S(1)}, bf16[768]{0:T(1024)(128)(2,1)}, u32[]{:S(2)}) copy-start(bf16[768]{0:T(1024)(128)(2,1)} %param.28) | copy-start | bytes 4612
  202.4 21.4 %copy-start.29 = (bf16[768]{0:T(1024)(128)(2,1)S(1)}, bf16[768]{0:T(1024)(128)(2,1)}, u32[]{:S(2)}) copy-start(bf16[768]{0:T(1024)(128)(2,1)} %param.29) | copy-start | bytes 4612
  202.4 25.3 %copy-start.35 = (bf16[384]{0:T(512)(128)(2,1)S(1)}, bf16[384]{0:T(512)(128)(2,1)}, u32[]{:S(2)}) copy-start(bf16[384]{0:T(512)(128)(2,1)} %param.33) | copy-start | bytes 2308
  202.4 20.6 %collective-permute-start.16 = (bf16[17,32,384]{2,1,0:T(8,128)(2,1)S(1)}, bf16[17,32,384]{2,1,0:T(8,128)(2,1)S(1)}, u32[]{:S(2)}, u32[]{:S(2)}) collective-permute-start(bf16[17,32,384]{2,1,0:T(8,128)(2,1)S(1)} %get-tuple-element.263), channel_id=1, source_target_pairs={{0,8},{4,12},{8,0},{12,4},{1,9},{5,13},{9,1},{13,5},{2,10},{6,14},... | collective-permute-start | bytes 1253384 | tf_op jit(solution)/shard_map/ppermute | solution.py:408
  223.1 6.5 %collective-permute-start.18 = (bf16[768,768]{1,0:T(8,128)(2,1)S(1)}, bf16[768,768]{1,0:T(8,128)(2,1)S(1)}, u32[]{:S(2)}, u32[]{:S(2)}) collective-permute-start(bf16[768,768]{1,0:T(8,128)(2,1)S(1)} %copy-done.20), channel_id=1, source_target_pairs={{0,1},{1,0},{2,3},{3,2},{4,5},{5,4},{6,7},{7,6},{8,9},{9,8},{10,11... | collective-permute-start | bytes 3538952 | tf_op jit(solution)/shard_map/ppermute | solution.py:402
  223.1 6.7 %collective-permute-start.20 = (bf16[768,768]{1,0:T(8,128)(2,1)}, bf16[768,768]{1,0:T(8,128)(2,1)S(1)}, u32[]{:S(2)}, u32[]{:S(2)}) collective-permute-start(bf16[768,768]{1,0:T(8,128)(2,1)} %param.32), channel_id=1, source_target_pairs={{0,1},{1,0},{2,3},{3,2},{4,5},{5,4},{6,7},{7,6},{8,9},{9,8},{10,11... | collective-permute-start | bytes 3538952 | tf_op jit(solution)/shard_map/ppermute | solution.py:402
  223.6 5.9 %collective-permute-start.19 = (bf16[768]{0:T(1024)(128)(2,1)S(1)}, bf16[768]{0:T(1024)(128)(2,1)S(1)}, u32[]{:S(2)}, u32[]{:S(2)}) collective-permute-start(bf16[768]{0:T(1024)(128)(2,1)S(1)} %copy-done.30), channel_id=1, source_target_pairs={{0,1},{1,0},{2,3},{3,2},{4,5},{5,4},{6,7},{7,6},{8,9},{9,8},{10,11... | collective-permute-start | bytes 4616 | tf_op jit(solution)/shard_map/ppermute | solution.py:402
  223.8 14.3 %collective-permute-start.15 = (bf16[17,32,384]{2,1,0:T(8,128)(2,1)S(1)}, bf16[17,32,384]{2,1,0:T(8,128)(2,1)S(1)}, u32[]{:S(2)}, u32[]{:S(2)}) collective-permute-start(bf16[17,32,384]{2,1,0:T(8,128)(2,1)S(1)} %get-tuple-element.262), channel_id=1, source_target_pairs={{0,4},{4,8},{8,12},{12,0},{1,5},{5,9},{9,13},{13,1},{2,6},{6,10},{... | collective-permute-start | bytes 1253384 | tf_op jit(solution)/shard_map/ppermute | solution.py:408
  223.9 21.0 %collective-permute-start.17 = (bf16[17,32,384]{2,1,0:T(8,128)(2,1)S(1)}, bf16[17,32,384]{2,1,0:T(8,128)(2,1)S(1)}, u32[]{:S(2)}, u32[]{:S(2)}) collective-permute-start(bf16[17,32,384]{2,1,0:T(8,128)(2,1)S(1)} %get-tuple-element.264), channel_id=1, source_target_pairs={{0,12},{4,0},{8,4},{12,8},{1,13},{5,1},{9,5},{13,9},{2,14},{6,2},{... | collective-permute-start | bytes 1253384 | tf_op jit(solution)/shard_map/ppermute | solution.py:408
  229.8 67.2 %copy-start.4 = (bf16[768,1536]{1,0:T(8,128)(2,1)}, bf16[768,1536]{1,0:T(8,128)(2,1)S(1)}, u32[]{:S(2)}) copy-start(bf16[768,1536]{1,0:T(8,128)(2,1)S(1)} %pad_maximum_fusion.w_in_ref) | copy-start | bytes 7077892
  245.2 38.2 %collective-permute-start.24 = (bf16[4,17,32,384]{3,2,1,0:T(8,128)(2,1)S(1)}, bf16[4,17,32,384]{3,2,1,0:T(8,128)(2,1)S(1)}, u32[]{:S(2)}, u32[]{:S(2)}) collective-permute-start(bf16[4,17,32,384]{3,2,1,0:T(8,128)(2,1)S(1)} %pad_maximum_fusion.2.own_ref), channel_id=1, source_target_pairs={{0,2},{2,0},{1,3},{3,1},{4,6},{6,4},{5,7},{7,5},{8,10},{10,8},{9,1... | collective-permute-start | bytes 5013512 | tf_op jit(solution)/shard_map/ppermute | solution.py:402
  246.0 14.5 %collective-permute-start.21 = (bf16[17,32,384]{2,1,0:T(8,128)(2,1)S(1)}, bf16[17,32,384]{2,1,0:T(8,128)(2,1)S(1)}, u32[]{:S(2)}, u32[]{:S(2)}) collective-permute-start(bf16[17,32,384]{2,1,0:T(8,128)(2,1)S(1)} %get-tuple-element.283), channel_id=1, source_target_pairs={{0,4},{4,8},{8,12},{12,0},{1,5},{5,9},{9,13},{13,1},{2,6},{6,10},{... | collective-permute-start | bytes 1253384 | tf_op jit(solution)/shard_map/ppermute | solution.py:408
  246.0 30.9 %collective-permute-start.22 = (bf16[17,32,384]{2,1,0:T(8,128)(2,1)S(1)}, bf16[17,32,384]{2,1,0:T(8,128)(2,1)S(1)}, u32[]{:S(2)}, u32[]{:S(2)}) collective-permute-start(bf16[17,32,384]{2,1,0:T(8,128)(2,1)S(1)} %get-tuple-element.284), channel_id=1, source_target_pairs={{0,8},{4,12},{8,0},{12,4},{1,9},{5,13},{9,1},{13,5},{2,10},{6,14},... | collective-permute-start | bytes 1253384 | tf_op jit(solution)/shard_map/ppermute | solution.py:408
  248.6 28.3 %collective-permute-start.23 = (bf16[17,32,384]{2,1,0:T(8,128)(2,1)S(1)}, bf16[17,32,384]{2,1,0:T(8,128)(2,1)S(1)}, u32[]{:S(2)}, u32[]{:S(2)}) collective-permute-start(bf16[17,32,384]{2,1,0:T(8,128)(2,1)S(1)} %get-tuple-element.285), channel_id=1, source_target_pairs={{0,12},{4,0},{8,4},{12,8},{1,13},{5,1},{9,5},{13,9},{2,14},{6,2},{... | collective-permute-start | bytes 1253384 | tf_op jit(solution)/shard_map/ppermute | solution.py:408
  290.3 6.6 %collective-permute-start.29 = (bf16[4,16,32,384]{3,2,1,0:T(8,128)(2,1)S(1)}, bf16[4,16,32,384]{3,2,1,0:T(8,128)(2,1)S(1)}, u32[]{:S(2)}, u32[]{:S(2)}) collective-permute-start(bf16[4,16,32,384]{3,2,1,0:T(8,128)(2,1)S(1)} %get-tuple-element.315), channel_id=1, source_target_pairs={{0,1},{1,0},{2,3},{3,2},{4,5},{5,4},{6,7},{7,6},{8,9},{9,8},{10,11... | collective-permute-start | bytes 4718600 | tf_op jit(solution)/shard_map/ppermute | solution.py:402
  290.6 22.1 %copy-start = (bf16[4,17,32,384]{3,2,1,0:T(8,128)(2,1)}, bf16[4,17,32,384]{3,2,1,0:T(8,128)(2,1)S(1)}, u32[]{:S(2)}) copy-start(bf16[4,17,32,384]{3,2,1,0:T(8,128)(2,1)S(1)} %pad_maximum_fusion.3.own_ref) | copy-start | bytes 5013508
  290.6 39.0 %collective-permute-start.28 = (bf16[4,17,32,384]{3,2,1,0:T(8,128)(2,1)S(1)}, bf16[4,17,32,384]{3,2,1,0:T(8,128)(2,1)S(1)}, u32[]{:S(2)}, u32[]{:S(2)}) collective-permute-start(bf16[4,17,32,384]{3,2,1,0:T(8,128)(2,1)S(1)} %pad_maximum_fusion.3.own_ref), channel_id=1, source_target_pairs={{0,2},{2,0},{1,3},{3,1},{4,6},{6,4},{5,7},{7,5},{8,10},{10,8},{9,1... | collective-permute-start | bytes 5013512 | tf_op jit(solution)/shard_map/ppermute | solution.py:402
  291.4 21.2 %collective-permute-start.25 = (bf16[17,32,384]{2,1,0:T(8,128)(2,1)S(1)}, bf16[17,32,384]{2,1,0:T(8,128)(2,1)S(1)}, u32[]{:S(2)}, u32[]{:S(2)}) collective-permute-start(bf16[17,32,384]{2,1,0:T(8,128)(2,1)S(1)} %get-tuple-element.303), channel_id=1, source_target_pairs={{0,4},{4,8},{8,12},{12,0},{1,5},{5,9},{9,13},{13,1},{2,6},{6,10},{... | collective-permute-start | bytes 1253384 | tf_op jit(solution)/shard_map/ppermute | solution.py:408
  294.0 29.8 %collective-permute-start.26 = (bf16[17,32,384]{2,1,0:T(8,128)(2,1)S(1)}, bf16[17,32,384]{2,1,0:T(8,128)(2,1)S(1)}, u32[]{:S(2)}, u32[]{:S(2)}) collective-permute-start(bf16[17,32,384]{2,1,0:T(8,128)(2,1)S(1)} %get-tuple-element.304), channel_id=1, source_target_pairs={{0,8},{4,12},{8,0},{12,4},{1,9},{5,13},{9,1},{13,5},{2,10},{6,14},... | collective-permute-start | bytes 1253384 | tf_op jit(solution)/shard_map/ppermute | solution.py:408
  296.3 27.5 %collective-permute-start.27 = (bf16[17,32,384]{2,1,0:T(8,128)(2,1)S(1)}, bf16[17,32,384]{2,1,0:T(8,128)(2,1)S(1)}, u32[]{:S(2)}, u32[]{:S(2)}) collective-permute-start(bf16[17,32,384]{2,1,0:T(8,128)(2,1)S(1)} %get-tuple-element.305), channel_id=1, source_target_pairs={{0,12},{4,0},{8,4},{12,8},{1,13},{5,1},{9,5},{13,9},{2,14},{6,2},{... | collective-permute-start | bytes 1253384 | tf_op jit(solution)/shard_map/ppermute | solution.py:408
  323.8 5.8 %copy-start.22 = (bf16[17,32,384]{2,1,0:T(8,128)(2,1)}, bf16[17,32,384]{2,1,0:T(8,128)(2,1)S(1)}, u32[]{:S(2)}) copy-start(bf16[17,32,384]{2,1,0:T(8,128)(2,1)S(1)} %collective-permute-done.26) | copy-start | bytes 1253380
  323.8 5.8 %copy-start.24 = (bf16[17,32,384]{2,1,0:T(8,128)(2,1)}, bf16[17,32,384]{2,1,0:T(8,128)(2,1)S(1)}, u32[]{:S(2)}) copy-start(bf16[17,32,384]{2,1,0:T(8,128)(2,1)S(1)} %collective-permute-done.27) | copy-start | bytes 1253380
  330.9 77.5 %all-to-all-start = ((bf16[8,16,32,384]{3,2,1,0:T(8,128)(2,1)}), bf16[8,16,32,384]{3,2,1,0:T(8,128)(2,1)}, u32[]{:S(2)}, u32[]{:S(2)}) async-start(bf16[8,16,32,384]{3,2,1,0:T(8,128)(2,1)} %bitcast.133), calls=%async_computation | async-start | bytes 6291456 | tf_op jit(solution)/shard_map/all_to_all | solution.py:514
  339.6 7.6 %copy-start.23 = (bf16[17,32,384]{2,1,0:T(8,128)(2,1)S(1)}, bf16[17,32,384]{2,1,0:T(8,128)(2,1)}, u32[]{:S(2)}) copy-start(bf16[17,32,384]{2,1,0:T(8,128)(2,1)} %copy-done.22) | copy-start | bytes 1253380
  339.6 7.6 %copy-start.25 = (bf16[17,32,384]{2,1,0:T(8,128)(2,1)S(1)}, bf16[17,32,384]{2,1,0:T(8,128)(2,1)}, u32[]{:S(2)}) copy-start(bf16[17,32,384]{2,1,0:T(8,128)(2,1)} %copy-done.24) | copy-start | bytes 1253380
  346.6 3.6 collective-permute-start.31
  347.5 18.5 %copy-start.2 = (bf16[4,17,32,384]{3,2,1,0:T(8,128)(2,1)}, bf16[4,17,32,384]{3,2,1,0:T(8,128)(2,1)S(1)}, u32[]{:S(2)}) copy-start(bf16[4,17,32,384]{3,2,1,0:T(8,128)(2,1)S(1)} %pad_maximum_fusion.4.own_ref) | copy-start | bytes 5013508
  347.5 38.5 %collective-permute-start.30 = (bf16[4,17,32,384]{3,2,1,0:T(8,128)(2,1)S(1)}, bf16[4,17,32,384]{3,2,1,0:T(8,128)(2,1)S(1)}, u32[]{:S(2)}, u32[]{:S(2)}) collective-permute-start(bf16[4,17,32,384]{3,2,1,0:T(8,128)(2,1)S(1)} %pad_maximum_fusion.4.own_ref), channel_id=1, source_target_pairs={{0,2},{2,0},{1,3},{3,1},{4,6},{6,4},{5,7},{7,5},{8,10},{10,8},{9,1... | collective-permute-start | bytes 5013512 | tf_op jit(solution)/shard_map/ppermute | solution.py:402
  408.4 76.2 %all-to-all-start.1 = ((bf16[8,16,32,384]{3,2,1,0:T(8,128)(2,1)}), bf16[8,16,32,384]{3,2,1,0:T(8,128)(2,1)}, u32[]{:S(2)}, u32[]{:S(2)}) async-start(bf16[8,16,32,384]{3,2,1,0:T(8,128)(2,1)} %bitcast.134), calls=%async_computation.1 | async-start | bytes 6291456 | tf_op jit(solution)/shard_map/all_to_all | solution.py:514
  424.8 4.9 collective-permute-start.32
  484.6 75.1 %all-to-all-start.2 = ((bf16[8,16,32,384]{3,2,1,0:T(8,128)(2,1)}), bf16[8,16,32,384]{3,2,1,0:T(8,128)(2,1)S(1)}, u32[]{:S(2)}, u32[]{:S(2)}) async-start(bf16[8,16,32,384]{3,2,1,0:T(8,128)(2,1)} %bitcast.135), calls=%async_computation.2 | async-start | bytes 6291456 | tf_op jit(solution)/shard_map/all_to_all | solution.py:514
  (21 other events, 40.3 us)
